TPU v7x, 32 devices: a whole 2x2x4 slice. The times are simulated.
32 devices in a mesh: parts: 2 (over y), shard: 16 (over z, x, core).
Axes of the slice: x: 2, y: 2, z: 4, core: 2. Of those that a mesh axis runs over, the one named last changes fastest.
Arguments:
- entity_table: bfloat16 [32768, 200], P('shard'), may hold values from -6 to 6
- relation_table: bfloat16 [1387, 200], replicated, may hold values from -6 to 6
- filters: bfloat16 [48, 9, 9], replicated, may hold values from -0.625 to 0.625
- proj_weight: bfloat16 [19200, 200], replicated, may hold values from -0.046875 to 0.046875
- chequer_perm: int32 [400], replicated, may hold values from 0 to 399, each once
- head_owner: int32 [4096, 1], P(('parts', 'shard')), parts along dimension 0, may hold values from 0 to 15; in each aligned block of 128 rows (0 to 127, 128 to 255, ...) at most 16 rows name the same one
- head_row: int32 [4096], P(('parts', 'shard')), parts along dimension 0, may hold values from 0 to 2047
- rel_ids: int32 [4096], P(('parts', 'shard')), parts along dimension 0, may hold values from 0 to 1386
- pos_index: int32 [4096], P(('parts', 'shard')), parts along dimension 0, may hold values from 0 to 4095
- tail_owner: int32 [8192, 1], P('parts'), parts along dimension 0, may hold values from 0 to 15; in each aligned block of 4096 rows (0 to 4095, 4096 to 8191, ...) at most 512 rows name the same one
- tail_row: int32 [8192], P('parts'), parts along dimension 0, may hold values from 0 to 2047
Outputs:
- entity_grad: float32 [65536, 200], P(('parts', 'shard')), parts along dimension 0
- relation_grad: float32 [2774, 200], P('parts'), parts along dimension 0
- filter_grad: float32 [96, 9, 9], P('parts'), parts along dimension 0
- proj_grad: float32 [38400, 200], P(('parts', 'shard')), parts along dimension 0
There are 2 independent parts, one for each index of `parts`. A program takes and returns all parts, laid end to end along the dimension named above; an argument that names none is the same for every part. Nothing has to cross between parts.
Inputs may be any that keep to these rules, and one draw needn't show every extreme that they name: `head_owner`: the queries of one device name one owner at most 16 times; some device names some owner exactly 16 times. `tail_owner`: at most 512 candidates name one owner; some owner is named exactly 512 times. `chequer_perm`: each of 0 to 399 appears once.
All inputs are finite; a program needn't handle non-finite values.
Results may differ from a plain program's by a relative error of at most 0.0014.
Values may be sent and summed in bfloat16 or wider, within the bound.
No kernel may reach another device: no remote copies, remote signals or barrier semaphores. Data moves between devices by JAX's collectives and lax.ppermute only.
A program may use at most 192 MiB of HBM per device.

v0:
```python
import jax
import jax.numpy as jnp
from jax import lax
from jax.sharding import PartitionSpec as P

IMG_H = 20
IMG_W = 20


loss_weight = 0.015625
smooth = 0.1


def wrap_pad(pair_image, rim_width):
    return jnp.pad(
        pair_image, ((0, 0), (rim_width, rim_width), (rim_width, rim_width)), mode="wrap"
    )


def conv_forward(pair_image, filters):
    rim_width = filters.shape[-1] // 2
    padded = wrap_pad(pair_image, rim_width)[:, None]
    return lax.conv_general_dilated(
        padded,
        filters[:, None],
        (1, 1),
        "VALID",
        dimension_numbers=("NCHW", "OIHW", "NCHW"),
        preferred_element_type=jnp.float32,
    )


def conv_backward(pair_image, filters, feat_grad):
    kernel_size = filters.shape[-1]
    rim_width = kernel_size // 2
    img_height = pair_image.shape[1]
    img_width = pair_image.shape[2]
    padded = wrap_pad(pair_image, rim_width)
    filter_part = lax.conv_general_dilated(
        padded[None],
        feat_grad,
        (1, 1),
        "VALID",
        dimension_numbers=("NCHW", "IOHW", "NCHW"),
        preferred_element_type=jnp.float32,
    )[0]
    flipped = filters[:, ::-1, ::-1][None]
    spread = lax.conv_general_dilated(
        feat_grad,
        flipped,
        (1, 1),
        ((kernel_size - 1, kernel_size - 1), (kernel_size - 1, kernel_size - 1)),
        dimension_numbers=("NCHW", "OIHW", "NCHW"),
        preferred_element_type=jnp.float32,
    )[:, 0]
    row_block = spread[:, rim_width : rim_width + img_height]
    row_block = row_block.at[:, :rim_width].add(spread[:, rim_width + img_height :])
    row_block = row_block.at[:, img_height - rim_width :].add(spread[:, :rim_width])
    col_block = row_block[:, :, rim_width : rim_width + img_width]
    col_block = col_block.at[:, :, :rim_width].add(row_block[:, :, rim_width + img_width :])
    col_block = col_block.at[:, :, img_width - rim_width :].add(row_block[:, :, :rim_width])
    return (filter_part, col_block)


def make_image(head_vec, rel_vec, positions):
    joined = jnp.concatenate([head_vec, rel_vec], axis=1)
    return joined[:, positions].reshape(joined.shape[0], IMG_H, IMG_W)


def front(pair_image, filters, proj_weight):
    conv_pre = conv_forward(pair_image, filters)
    features = jax.nn.silu(conv_pre).astype(jnp.bfloat16).reshape(conv_pre.shape[0], -1)
    query_vec = jnp.dot(features, proj_weight, preferred_element_type=jnp.float32).astype(
        jnp.bfloat16
    )
    return (conv_pre, features, query_vec)


def feature_grad(query_grad, proj_weight, conv_pre):
    linear = lax.dot_general(
        query_grad, proj_weight, (((1,), (1,)), ((), ())), preferred_element_type=jnp.float32
    )
    gate_sig = jax.nn.sigmoid(conv_pre)
    slope = gate_sig * (1.0 + conv_pre * (1.0 - gate_sig))
    return (linear.reshape(conv_pre.shape) * slope).astype(jnp.bfloat16)


def slot_ranks(owner_ids, owner_count):
    onehot = (owner_ids[:, None] == jnp.arange(owner_count, dtype=jnp.int32)[None, :]).astype(
        jnp.int32
    )
    before = jnp.cumsum(onehot, axis=0) - onehot
    return jnp.sum(before * onehot, axis=1)


def shards(
    entity_table,
    relation_table,
    filters,
    proj_weight,
    chequer_perm,
    head_owner,
    head_row,
    rel_ids,
    pos_index,
    tail_owner,
    tail_row,
):
    owners = lax.axis_size("shard")
    my_index = lax.axis_index("shard")
    query_rows = head_row.shape[0]
    cand_count = tail_row.shape[0]
    model_width = entity_table.shape[1]
    table_rows = entity_table.shape[0]
    head_cap = 2 * query_rows // owners
    tail_cap = 2 * cand_count // owners
    head_owners = head_owner[:, 0]
    head_slot = head_owners * head_cap + slot_ranks(head_owners, owners)
    wanted = (
        jnp.zeros((owners * head_cap,), jnp.int32)
        .at[head_slot]
        .set(head_row)
        .reshape(owners, head_cap)
    )
    requested = lax.all_to_all(wanted, "shard", split_axis=0, concat_axis=0, tiled=True)
    found_rows = entity_table[requested]
    fetched, requested = (
        lax.all_to_all(found_rows, "shard", split_axis=0, concat_axis=0, tiled=True),
        requested,
    )
    head_vec = fetched.reshape(owners * head_cap, model_width)[head_slot]
    pair_image = make_image(head_vec, relation_table[rel_ids], chequer_perm)
    conv_pre, features, query_vec = front(pair_image, filters, proj_weight)
    tail_owners = tail_owner[:, 0]
    tail_slot = tail_owners * tail_cap + slot_ranks(tail_owners, owners)
    local_slot = jnp.where(tail_owners == my_index, tail_slot - my_index * tail_cap, tail_cap)
    slot_row = jnp.zeros((tail_cap,), jnp.int32).at[local_slot].set(tail_row, mode="drop")
    slot_live = jnp.zeros((tail_cap,), jnp.int32).at[local_slot].set(1, mode="drop")
    packed = jnp.where(slot_live[:, None] > 0, entity_table[slot_row], jnp.zeros((), jnp.bfloat16))
    all_slots = lax.all_gather(packed, "shard", axis=0, tiled=True)
    owned_rows = jnp.where(slot_live > 0, slot_row, table_rows)
    cand_index = jnp.arange(cand_count, dtype=jnp.int32)
    tail_vec = all_slots[tail_slot]
    score = lax.dot_general(
        query_vec, tail_vec, (((1,), (1,)), ((), ())), preferred_element_type=jnp.float32
    )
    target = smooth / cand_count + (1.0 - smooth) * (
        cand_index[None, :] == pos_index[:, None]
    ).astype(jnp.float32)
    score_grad = ((jax.nn.sigmoid(score) - target) * loss_weight).astype(jnp.bfloat16)
    query_grad = jnp.dot(score_grad, tail_vec, preferred_element_type=jnp.float32).astype(
        jnp.bfloat16
    )
    tail_part = lax.dot_general(
        score_grad, query_vec, (((0,), (0,)), ((), ())), preferred_element_type=jnp.float32
    )
    tail_part = jnp.concatenate([tail_part, jnp.zeros((1, model_width), jnp.float32)], axis=0)
    slot_cand = jnp.full((owners * tail_cap,), cand_count, jnp.int32).at[tail_slot].set(cand_index)
    tail_mine = lax.psum_scatter(tail_part[slot_cand], "shard", scatter_dimension=0, tiled=True)
    columns = lax.all_to_all(features, "shard", split_axis=1, concat_axis=0, tiled=True)
    empty = jnp.zeros((columns.shape[1], model_width), jnp.float32)
    part_rows = lax.all_gather(query_grad, "shard", axis=0, tiled=True)
    matched = lax.slice_in_dim(columns, 0, part_rows.shape[0], axis=0)
    proj_grad = empty + lax.dot_general(
        matched, part_rows, (((0,), (0,)), ((), ())), preferred_element_type=jnp.float32
    )
    feat_grad = feature_grad(query_grad, proj_weight, conv_pre)
    filter_part, image_grad = conv_backward(pair_image, filters, feat_grad)
    inverse = jnp.argsort(chequer_perm)
    pair_grad = image_grad.reshape(query_rows, -1)[:, inverse]
    rel_onehot = (
        rel_ids[:, None] == jnp.arange(relation_table.shape[0], dtype=jnp.int32)[None, :]
    ).astype(jnp.float32)
    rel_part = lax.dot_general(
        rel_onehot,
        pair_grad[:, model_width:],
        (((0,), (0,)), ((), ())),
        precision=lax.Precision.HIGHEST,
        preferred_element_type=jnp.float32,
    )
    relation_grad, filter_grad = lax.psum((rel_part, filter_part), "shard")
    outgoing = (
        jnp.zeros((owners * head_cap, model_width), jnp.float32)
        .at[head_slot]
        .set(pair_grad[:, :model_width])
    )
    incoming = lax.all_to_all(
        outgoing.reshape(owners, head_cap, model_width).astype(jnp.bfloat16),
        "shard",
        split_axis=0,
        concat_axis=0,
        tiled=True,
    ).astype(jnp.float32)
    entity_grad = (
        jnp.zeros((table_rows, model_width), jnp.float32)
        .at[requested.reshape(-1)]
        .add(incoming.reshape(-1, model_width))
    )
    entity_grad = entity_grad.at[owned_rows].add(tail_mine, mode="drop")
    return (entity_grad, relation_grad, filter_grad, proj_grad)


def solution(mesh):
    placed = (
        P("shard", None),
        P(),
        P(),
        P(),
        P(),
        P(("parts", "shard"), None),
        P(("parts", "shard")),
        P(("parts", "shard")),
        P(("parts", "shard")),
        P("parts", None),
        P("parts"),
    )
    return jax.shard_map(
        shards,
        mesh=mesh,
        in_specs=placed,
        out_specs=(
            P(("parts", "shard"), None),
            P("parts", None),
            P("parts", None, None),
            P(("parts", "shard"), None),
        ),
        check_vma=False,
    )
```

profile of v0, /device:TPU:0, one launch (start us, length us, event | category | flops | bytes accessed | tf_op | source)
XLA Modules:
  0.0 575.6 jit_solution(18341511149278213776)
XLA Ops:
  8.1 4.6 reduce-window.6
  15.2 15.5 %scatter_custom_fusion.1 = s32[512]{0:T(512)S(1)} fusion(s32[4096]{0:T(1024)S(1)} %bitcast.108, s32[4096]{0:T(1024)S(1)} %broadcast.193, s32[]{:T(128)} %constant.151.clone.1), kind=kCustom, calls=%fused_computation.104 | custom fusion | bytes 2052 | tf_op jit(solution)/shard_map/scatter | solution.py:138
  30.7 15.7 %scatter_custom_fusion.2 = s32[512]{0:T(512)S(1)} fusion(s32[4096]{0:T(1024)S(1)} %bitcast.109, s32[4096]{0:T(1024)} %param.29, s32[]{:T(128)} %constant.151.clone.1), kind=kCustom, calls=%fused_computation.101 | custom fusion | bytes 2560 | tf_op jit(solution)/shard_map/scatter | solution.py:137
  47.9 2.0 gather_fusion.4
  53.0 7.4 %all-to-all-start = ((s32[16,1,16]{2,1,0:T(1,128)}), s32[16,1,16]{2,1,0:T(1,128)S(1)}, u32[]{:S(2)}, u32[]{:S(2)}) async-start(s32[16,1,16]{2,1,0:T(1,128)} %all_to_all.28), calls=%async_computation | async-start | bytes 16384 | tf_op jit(solution)/shard_map/all_to_all | solution.py:125
  60.4 3.8 sort.17
  64.1 15.5 %scatter_custom_fusion.5 = s32[8192]{0:T(1024)S(1)} fusion(s32[4096]{0:T(1024)S(1)} %bitcast.104, s32[4096]{0:T(1024)S(1)} %iota.25, s32[]{:T(128)} %constant.166.clone.1), kind=kCustom, calls=%fused_computation.84 | custom fusion | bytes 32772 | tf_op jit(solution)/shard_map/scatter | solution.py:158
  81.1 1.8 gather_fusion
  82.9 6.0 %all-to-all-start.1 = ((bf16[16,16,200]{2,1,0:T(8,128)(2,1)}), bf16[16,16,200]{2,1,0:T(8,128)(2,1)S(1)}, u32[]{:S(2)}, u32[]{:S(2)}) async-start(bf16[16,16,200]{2,1,0:T(8,128)(2,1)} %bitcast.5), calls=%async_computation.1 | async-start | bytes 262144 | tf_op jit(solution)/shard_map/all_to_all | solution.py:128
  89.0 9.4 %all-to-all-done.1 = bf16[16,16,200]{2,1,0:T(8,128)(2,1)S(1)} async-done(((bf16[16,16,200]{2,1,0:T(8,128)(2,1)}), bf16[16,16,200]{2,1,0:T(8,128)(2,1)S(1)}, u32[]{:S(2)}, u32[]{:S(2)}) %all-to-all-start.1) | async-done | bytes 102432 | tf_op jit(solution)/shard_map/all_to_all | solution.py:128
  101.3 10.8 %multiply_convert_fusion = (bf16[128,48,20,20]{0,1,3,2:T(8,128)(2,1)S(1)}, f32[128,48,20,20]{0,1,3,2:T(8,128)}) fusion(bf16[48,1,9,9]{0,3,2,1:T(8,128)(2,1)S(1)} %bitcast.106, bf16[128,1,28,28]{0,3,2,1:T(8,128)(2,1)S(1)} %get-tuple-element.65), kind=kOutput, calls=%fused_computation.17 | convolution fusion | flops 410419200 | bytes 14954080 | tf_op jit(solution)/shard_map/conv_general_dilated | solution.py:23
  112.1 3.8 copy.43
  115.9 8.6 %reshape.242 = bf16[128,19200]{0,1:T(8,128)(2,1)} reshape(bf16[128,48,20,20]{0,3,2,1:T(8,128)(2,1)} %copy.43) | data formatting | bytes 9830400 | tf_op jit(solution)/shard_map/reshape | solution.py:72
  124.6 6.8 %convolution_convert_fusion.1 = bf16[128,200]{0,1:T(8,128)(2,1)S(1)} fusion(bf16[128,19200]{0,1:T(8,128)(2,1)} %reshape.242, bf16[19200,200]{0,1:T(8,128)(2,1)} %param.22), kind=kOutput, calls=%fused_computation.31 | convolution fusion | flops 983065600 | bytes 12646400 | tf_op jit(solution)/shard_map/dot_general | solution.py:73
  131.4 15.7 %gather_fusion.5 = bf16[4096,200]{1,0:T(8,128)(2,1)S(1)} fusion(bf16[8192,200]{1,0:T(8,128)(2,1)} %all-gather.2.cloned.1.call-done, s32[4096]{0:T(1024)S(1)} %broadcast_clamp_fusion), kind=kCustom, calls=%fused_computation.5 | custom fusion | bytes 3293184 | tf_op jit(solution)/shard_map/gather | solution.py:143
  150.0 2.3 concatenate.27.clone
  152.3 46.1 %gather_fusion.7 = f32[8192,200]{1,0:T(8,128)} fusion(f32[4097,200]{1,0:T(8,128)} %concatenate.27.clone, s32[8192]{0:T(1024)S(1)} %fusion.36), kind=kCustom, calls=%fused_computation.7 | custom fusion | bytes 13139968 | tf_op jit(solution)/shard_map/gather | solution.py:159
  198.4 11.4 %fusion.49 = f32[128,19200]{0,1:T(8,128)} fusion(bf16[128,200]{0,1:T(8,128)(2,1)S(1)} %convolution_convert_fusion, bf16[19200,200]{0,1:T(8,128)(2,1)} %param.22), kind=kOutput, calls=%fused_computation.113 | convolution fusion | flops 983040000 | bytes 17561600 | tf_op jit(solution)/shard_map/dot_general | solution.py:80
  209.8 12.1 %reshape.244 = f32[128,48,20,20]{0,3,2,1:T(8,128)} reshape(f32[128,19200]{0,1:T(8,128)} %fusion.49) | data formatting | bytes 19660800 | tf_op jit(solution)/shard_map/reshape | solution.py:85
  221.9 12.4 %fusion = bf16[128,48,20,20]{0,1,3,2:T(8,128)(2,1)S(1)} fusion(f32[128,48,20,20]{0,3,2,1:T(8,128)} %reshape.244, f32[128,48,20,20]{0,1,3,2:T(8,128)} %get-tuple-element.72), kind=kLoop, calls=%fused_computation.16 | loop fusion | flops 22118400 | bytes 24576000 | tf_op jit(solution)/shard_map/convert_element_type | solution.py:85
  234.3 104.9 %fusion.31 = f32[128,1,28,28]{0,1,3,2:T(1,128)S(1)} fusion(bf16[128,48,20,20]{0,1,3,2:T(8,128)(2,1)S(1)} %fusion, bf16[1,48,9,9]{1,3,2,0:T(8,128)(2,1)S(1)} %bitcast.99), kind=kOutput, calls=%fused_computation.75 | convolution fusion | flops 398131200 | bytes 5324384 | tf_op jit(solution)/shard_map/conv_general_dilated | solution.py:48
  342.7 3.8 all-to-all-start.2
  346.5 8.7 %all_to_all.33 = bf16[128,16,1200]{0,2,1:T(8,128)(2,1)} reshape(bf16[128,48,20,20]{0,3,2,1:T(8,128)(2,1)} %copy.43) | data formatting | bytes 9830400 | tf_op jit(solution)/shard_map/all_to_all | solution.py:160
  355.2 6.1 %all-to-all-start.3 = ((bf16[128,16,1200]{0,2,1:T(8,128)(2,1)}), bf16[128,16,1200]{0,2,1:T(8,128)(2,1)}, u32[]{:S(2)}, u32[]{:S(2)}) async-start(bf16[128,16,1200]{0,2,1:T(8,128)(2,1)} %all_to_all.33), calls=%async_computation.4 | async-start | bytes 9830400 | tf_op jit(solution)/shard_map/all_to_all | solution.py:160
  362.6 1.8 fusion.12
  364.4 9.0 %fusion.13 = f32[1,48,9,9]{1,0,3,2:T(1,128)S(1)} fusion(bf16[128,48,20,20]{0,1,3,2:T(8,128)(2,1)} %copy-done, bf16[1,128,28,28]{1,3,2,0:T(8,128)(2,1)S(1)} %get-tuple-element.64), kind=kOutput, calls=%fused_computation.37 | convolution fusion | flops 398131200 | bytes 5131456 | tf_op jit(solution)/shard_map/conv_general_dilated | solution.py:39
  373.4 98.0 %all_gather.7 = bf16[2048,200]{0,1:T(8,128)(2,1)S(1)} all-gather(bf16[128,200]{0,1:T(8,128)(2,1)S(1)} %convolution_convert_fusion), channel_id=1, replica_groups=mesh['parts'=2,'shard'=16] {'shard'}, dimensions={0}, use_global_device_ids=true | all-gather | bytes 870400 | tf_op jit(solution)/shard_map/all_gather | solution.py:162
  471.4 81.2 %psum.15 = f32[48,9,9]{0,2,1:T(8,128)} all-reduce(f32[48,9,9]{0,2,1:T(8,128)S(1)} %bitcast.98), channel_id=1, replica_groups=mesh['parts'=2,'shard'=16] {'shard'}, use_global_device_ids=true, to_apply=%region_15.16 | all-reduce | flops 3888 | bytes 31104 | tf_op jit(solution)/shard_map/psum | solution.py:181
  552.6 2.5 scatter_custom_fusion.4
  555.1 5.0 fusion.3
  560.1 4.6 scatter_fusion
  566.4 2.3 copy.90
  (89 shorter events, 21.4 us)
Async XLA Ops:
  7.2 43.5 %copy-start.4 = (s32[128,1]{0,1:T(1,128)S(1)}, s32[128,1]{0,1:T(1,128)}, u32[]{:S(2)}) copy-start(s32[128,1]{0,1:T(1,128)} %param.24) | copy-start | bytes 1540
  7.2 53.2 %copy-start.3 = (s32[400]{0:T(512)S(1)}, s32[400]{0:T(512)}, u32[]{:S(2)}) copy-start(s32[400]{0:T(512)} %param.23) | copy-start | bytes 4804
  7.2 72.6 %copy-start.5 = (s32[128]{0:T(128)S(1)}, s32[128]{0:T(128)}, u32[]{:S(2)}) copy-start(s32[128]{0:T(128)} %param.26) | copy-start | bytes 1540
  7.2 72.6 %copy-start.2 = (bf16[48,9,9]{0,2,1:T(8,128)(2,1)S(1)}, bf16[48,9,9]{0,2,1:T(8,128)(2,1)}, u32[]{:S(2)}) copy-start(bf16[48,9,9]{0,2,1:T(8,128)(2,1)} %param.21) | copy-start | bytes 23332
  7.2 72.7 %copy-start.1 = (bf16[1387,200]{0,1:T(8,128)(2,1)S(1)}, bf16[1387,200]{0,1:T(8,128)(2,1)}, u32[]{:S(2)}) copy-start(bf16[1387,200]{0,1:T(8,128)(2,1)} %param.20) | copy-start | bytes 1664404
  7.2 124.2 %all-gather.2.cloned.1.call-start = ((), (), s32[]{:S(2)}) async-start(), calls=%async_computation.5 | async-start | bytes 4456448 | tf_op jit(solution)/shard_map/all_gather | solution.py:140
  53.0 28.0 %all-to-all-start = ((s32[16,1,16]{2,1,0:T(1,128)}), s32[16,1,16]{2,1,0:T(1,128)S(1)}, u32[]{:S(2)}, u32[]{:S(2)}) async-start(s32[16,1,16]{2,1,0:T(1,128)} %all_to_all.28), calls=%async_computation | async-start | bytes 16384 | tf_op jit(solution)/shard_map/all_to_all | solution.py:125
  82.9 15.4 %all-to-all-start.1 = ((bf16[16,16,200]{2,1,0:T(8,128)(2,1)}), bf16[16,16,200]{2,1,0:T(8,128)(2,1)S(1)}, u32[]{:S(2)}, u32[]{:S(2)}) async-start(bf16[16,16,200]{2,1,0:T(8,128)(2,1)} %bitcast.5), calls=%async_computation.1 | async-start | bytes 262144 | tf_op jit(solution)/shard_map/all_to_all | solution.py:128
  88.9 471.2 %reduce-scatter.2.cloned.1.call-start = ((), (), s32[]{:S(2)}) async-start(), calls=%async_computation.6 | async-start | bytes 8912896 | tf_op jit(solution)/shard_map/reduce_scatter | solution.py:159
  131.4 15.8 %copy-start.6 = (s32[128]{0:T(128)S(1)}, s32[128]{0:T(128)}, u32[]{:S(2)}) copy-start(s32[128]{0:T(128)} %param.27) | copy-start | bytes 1540
  234.3 105.0 %copy-start = (bf16[128,48,20,20]{0,1,3,2:T(8,128)(2,1)}, bf16[128,48,20,20]{0,1,3,2:T(8,128)(2,1)S(1)}, u32[]{:S(2)}) copy-start(bf16[128,48,20,20]{0,1,3,2:T(8,128)(2,1)S(1)} %fusion) | copy-start | bytes 14745604
  342.7 12.5 %all-to-all-start.2 = ((bf16[16,16,200]{2,1,0:T(8,128)(2,1)}), bf16[16,16,200]{2,1,0:T(8,128)(2,1)S(1)}, u32[]{:S(2)}, u32[]{:S(2)}) async-start(bf16[16,16,200]{2,1,0:T(8,128)(2,1)} %bitcast.18), calls=%async_computation.2 | async-start | bytes 262144 | tf_op jit(solution)/shard_map/all_to_all | solution.py:187
  355.2 199.9 %all-to-all-start.3 = ((bf16[128,16,1200]{0,2,1:T(8,128)(2,1)}), bf16[128,16,1200]{0,2,1:T(8,128)(2,1)}, u32[]{:S(2)}, u32[]{:S(2)}) async-start(bf16[128,16,1200]{0,2,1:T(8,128)(2,1)} %all_to_all.33), calls=%async_computation.4 | async-start | bytes 9830400 | tf_op jit(solution)/shard_map/all_to_all | solution.py:160
  361.3 205.1 %all-reduce.3.cloned.1.call-start = ((), (), s32[]{:S(2)}) async-start(), calls=%async_computation.7 | async-start | bytes 2252800 | tf_op jit(solution)/shard_map/psum | solution.py:181
Sparse Core Ops, SparseCore 0:
  50.8 53.7 all-gather.1
  198.5 103.6 reduce-scatter.1
  366.1 166.0 all-reduce.2
where the time goes:
time: 583 us; the launch traced here: 576 us
  blocking collectives  179 us (31%)
  local copies, waits for them, and re-layouts  163 us (28%)
  matrix products  152 us (26%)
  other arithmetic  33.6 us (6%)
  starting transfers between devices  23.3 us (4%)
  between operations  14.7 us (3%)
  waiting for transfers between devices  9.45 us (2%)
    conv_general_dilated x1, matrix products, conv_backward(): lax.conv_general_dilated(feat_grad, flipped, (1, 1), ((kernel_size - 1, k...  105 us
    all_gather x1, blocking collectives, shards(): part_rows = lax.all_gather(query_grad, 'shard', axis=0, tiled=True)  98 us
    psum x1, blocking collectives, shards(): relation_grad, filter_grad = lax.psum((rel_part, filter_part), 'shard')  81.2 us
    gather x1, local copies, waits for them, and re-layouts, shards(): tail_part[slot_cand]  46.1 us
    gather x1, local copies, waits for them, and re-layouts, shards(): tail_vec = all_slots[tail_slot]  15.7 us
    scatter x1, local copies, waits for them, and re-layouts, shards(): jnp.zeros((tail_cap,), jnp.int32).at[local_slot].set(tail_row, mode='drop')  15.7 us
    scatter x1, local copies, waits for them, and re-layouts, shards(): jnp.full((owners * tail_cap,), cand_count, jnp.int32).at[tail_slot]  15.5 us
    scatter x1, local copies, waits for them, and re-layouts, shards(): jnp.zeros((tail_cap,), jnp.int32).at[local_slot].set(1, mode='drop')  15.5 us
  transfers between devices with their start and end apart: 7, of which 1 were waited for; matrix products, arithmetic and copies ran while one was open for 39% of the time, Pallas kernels for 0%

commit v1 on v0

v1 whole, which is shorter than its diff:
```python
import functools
import math

import jax
import jax.numpy as jnp
import numpy as np
from jax import lax
from jax.experimental import pallas as pl
from jax.experimental.pallas import tpu as pltpu
from jax.sharding import PartitionSpec as P

IMG = 20
BAND = 4
GROUPS = IMG // BAND
BAND_OUT = BAND * IMG
LANES = 256

loss_weight = 0.015625
smooth = 0.1

f32 = jnp.float32
bf16 = jnp.bfloat16
i32 = jnp.int32

NN = (((1,), (0,)), ((), ()))
NT = (((1,), (1,)), ((), ()))
TN = (((0,), (0,)), ((), ()))


def mm(a, b, dims=NN):
    return lax.dot_general(a, b, dims, preferred_element_type=f32)


def iota(shape, axis):
    return lax.broadcasted_iota(i32, shape, axis)


def onehot(mask):
    return jnp.where(mask, 1.0, 0.0).astype(bf16)


def split(value):
    high = value.astype(bf16)
    return high, (value - high.astype(f32)).astype(bf16)


def sigmoid(v):
    return 0.5 * jnp.tanh(0.5 * v) + 0.5


def params(*semantics, mib=40):
    return pltpu.CompilerParams(
        dimension_semantics=semantics or None, vmem_limit_bytes=mib << 20
    )


def cost(flops, nbytes, trans=0):
    return pl.CostEstimate(flops=int(flops), bytes_accessed=int(nbytes), transcendentals=int(trans))


def whole(shape):
    return pl.BlockSpec(shape, lambda *_: (0,) * len(shape))


SMEM = pl.BlockSpec(memory_space=pltpu.SMEM)


def band_codes(ks):
    codes = np.full((IMG, LANES), -1, np.int32)
    for j in range(IMG):
        for r in range(ks):
            for x in range(IMG):
                b = (x - j + ks // 2) % IMG
                if b < ks:
                    codes[j, r * IMG + x] = r * ks + b
    return codes


def band_kernel(codes_ref, filt_ref, out_ref, scr):
    count, taps = filt_ref.shape
    filt = filt_ref[...]
    for j in range(IMG):
        pick = onehot(iota((taps, LANES), 0) == codes_ref[j : j + 1, :])
        row = mm(filt, pick)
        for di in range(BAND):
            scr[:, di * IMG + j, :] = row if di == 0 else pltpu.roll(row, di * IMG, 1)
    out_ref[...] = scr[...].reshape(count * BAND_OUT, LANES).astype(bf16)


def build_band(filters):
    count, ks, _ = filters.shape
    codes = jnp.asarray(band_codes(ks))
    return pl.pallas_call(
        band_kernel,
        out_shape=jax.ShapeDtypeStruct((count * BAND_OUT, LANES), bf16),
        scratch_shapes=[pltpu.VMEM((count, BAND_OUT, LANES), f32)],
        compiler_params=params(),
        cost_estimate=cost(4e7, 4e6),
        name="band",
    )(codes, filters.reshape(count, ks * ks))


def pack_kernel(shift, me_ref, owner_ref, row_ref, table_ref, tails_ref, tails_t_ref, cand_ref, srow_ref):
    cap = tails_ref.shape[0]
    lines = owner_ref.shape[0]
    mine = owner_ref[...] == me_ref[0]
    mine_b = onehot(mine)
    before = onehot(iota((128, 128), 0) < iota((128, 128), 1))
    rank = mm(mine_b, before)
    totals = mm(mine_b, jnp.ones((128, 128), bf16))
    upper = jnp.where(iota((lines, lines), 1) < iota((lines, lines), 0), 1.0, 0.0).astype(bf16)
    offset = mm(upper, totals.astype(bf16))
    key = jnp.where(mine, (rank + offset).astype(i32), -1)
    code = row_ref[...] * (1 << shift) + iota((lines, 128), 0) * 128 + iota((lines, 128), 1) + 1
    code = code.astype(f32)
    slots = iota((cap, 128), 0)
    total = jnp.zeros((cap, 128), f32)
    for r in range(lines):
        total = total + jnp.where(slots == key[r : r + 1, :], code[r : r + 1, :], 0.0)
    found = jnp.sum(total, axis=1, keepdims=True).astype(i32) - 1
    live = found >= 0
    srow = jnp.where(live, lax.shift_right_arithmetic(found, shift), -1)
    cand_ref[...] = jnp.where(live, found & ((1 << shift) - 1), -1)
    srow_ref[...] = srow
    pick = onehot(iota((cap, table_ref.shape[0]), 1) == srow)
    tails = mm(pick, table_ref[...])
    tails_ref[...] = tails.astype(bf16)
    tails_t_ref[...] = tails.T.astype(bf16)


def pack_tails(me, tail_owners, tail_row, table, cap):
    cand = tail_row.shape[0]
    shift = int(math.log2(cand))
    assert 1 << shift == cand and cand * table.shape[0] < 1 << 24 and cand % 128 == 0
    width = table.shape[1]
    return pl.pallas_call(
        functools.partial(pack_kernel, shift),
        in_specs=[SMEM] + [pl.BlockSpec(memory_space=pltpu.VMEM)] * 3,
        out_shape=[
            jax.ShapeDtypeStruct((cap, width), bf16),
            jax.ShapeDtypeStruct((width, cap), bf16),
            jax.ShapeDtypeStruct((cap, 1), i32),
            jax.ShapeDtypeStruct((cap, 1), i32),
        ],
        compiler_params=params(),
        cost_estimate=cost(1e9, 2e6),
        name="pack_tails",
    )(me, tail_owners.reshape(-1, 128), tail_row.reshape(-1, 128), table)


def found_kernel(cap, me_ref, owner_ref, row_ref, table_ref, found_ref, want_ref, scr):
    count, queries = owner_ref.shape
    mine = owner_ref[...] == me_ref[0]
    before = onehot(iota((queries, queries), 0) < iota((queries, queries), 1))
    rank = mm(onehot(mine), before)
    key = jnp.where(mine, rank.astype(i32), -1)
    code = (row_ref[...] + 1).astype(f32)
    slots = iota((cap, queries), 0)
    for d in range(count):
        picked = jnp.where(slots == key[d : d + 1, :], code[d : d + 1, :], 0.0)
        scr[d * cap : (d + 1) * cap, :] = jnp.sum(picked, axis=1, keepdims=True)
    want = scr[...].astype(i32) - 1
    want_ref[...] = want
    pick = onehot(iota((count * cap, table_ref.shape[0]), 1) == want)
    found_ref[...] = mm(pick, table_ref[...]).astype(bf16)


def find_heads(me, owners, rows, table, cap):
    count = owners.shape[0]
    width = table.shape[1]
    return pl.pallas_call(
        functools.partial(found_kernel, cap),
        in_specs=[SMEM] + [pl.BlockSpec(memory_space=pltpu.VMEM)] * 3,
        out_shape=[
            jax.ShapeDtypeStruct((count * cap, width), bf16),
            jax.ShapeDtypeStruct((count * cap, 1), i32),
        ],
        scratch_shapes=[pltpu.VMEM((count * cap, 1), f32)],
        compiler_params=params(),
        cost_estimate=cost(3e8, 2e6),
        name="find_heads",
    )(me, owners, rows, table)


def pos_kernel(cap, core_ref, owner_ref, pos_ref, out_ref):
    cand = owner_ref.shape[1]
    pos = pos_ref[...]
    queries = pos.shape[0]
    step = min(512, cand)
    owner = jnp.zeros((queries, 1), f32)
    for c in range(0, cand, step):
        here = iota((queries, step), 1) + c
        value = owner_ref[:, c : c + step].astype(f32)
        owner = owner + jnp.sum(jnp.where(here == pos, value, 0.0), axis=1, keepdims=True)
    owner = owner.astype(i32)
    ahead = jnp.zeros((queries, 1), f32)
    for c in range(0, cand, step):
        here = iota((queries, step), 1) + c
        same = (owner_ref[:, c : c + step] == owner) & (here < pos)
        ahead = ahead + jnp.sum(jnp.where(same, 1.0, 0.0), axis=1, keepdims=True)
    slot = lax.shift_right_arithmetic(owner, 1) * cap + ahead.astype(i32)
    out_ref[...] = jnp.where((owner & 1) == core_ref[0], slot, -1)


def pos_slots(core, tail_owners, pos_col, cap):
    return pl.pallas_call(
        functools.partial(pos_kernel, cap),
        in_specs=[SMEM] + [pl.BlockSpec(memory_space=pltpu.VMEM)] * 2,
        out_shape=jax.ShapeDtypeStruct(pos_col.shape, i32),
        compiler_params=params(),
        cost_estimate=cost(1e7, 1e5),
        name="pos_slots",
    )(core, tail_owners.reshape(1, -1), pos_col)


def front_kernel(
    cap, fetched_ref, ocol_ref, orow_ref, rel_ref, rtab_ref, win_ref, band_ref, w_ref,
    pre_ref, pwin_ref, qv_ref, hvt_ref, qvt_ref, hv, rv, acc,
):
    g = pl.program_id(0)
    queries, width = hv.shape

    @pl.when(g == 0)
    def _():
        ocol = ocol_ref[...]
        same = (ocol == orow_ref[...]) & (iota((queries, queries), 1) < iota((queries, queries), 0))
        rank = jnp.sum(jnp.where(same, 1.0, 0.0), axis=1, keepdims=True)
        slot = ocol * cap + rank.astype(i32)
        pick = onehot(iota((queries, fetched_ref.shape[0]), 1) == slot)
        head = mm(pick, fetched_ref[...])
        hv[...] = head.astype(bf16)
        hvt_ref[...] = head.T.astype(bf16)
        rpick = onehot(iota((queries, rtab_ref.shape[0]), 1) == rel_ref[...])
        rv[...] = mm(rpick, rtab_ref[...]).astype(bf16)
        acc[...] = jnp.zeros_like(acc)

    win = win_ref[0]
    entry = iota((width, LANES), 0)
    image = mm(hv[...], onehot(entry == win)) + mm(rv[...], onehot(entry + width == win))
    image = image.astype(bf16)
    pwin_ref[0] = image
    count = w_ref.shape[0]
    chunk = math.gcd(count, 16)
    total = acc[...]
    for c in range(0, count, chunk):
        rows = pl.ds(c * BAND_OUT, chunk * BAND_OUT)
        pre = mm(image, band_ref[rows, :], NT)
        pre_ref[0, :, rows] = pre
        feats = (pre * sigmoid(pre)).astype(bf16)
        weight = w_ref[c : c + chunk, 0].reshape(chunk * BAND_OUT, width)
        total = total + mm(feats, weight)
    acc[...] = total

    @pl.when(g == GROUPS - 1)
    def _():
        query = acc[...]
        qv_ref[...] = query.astype(bf16)
        qvt_ref[...] = query.T.astype(bf16)


def front(fetched, ocol, orow, rel_col, relation_table, windows, band, weight, cap):
    queries = ocol.shape[0]
    width = weight.shape[-1]
    count = weight.shape[0]
    lanes = count * BAND_OUT
    return pl.pallas_call(
        functools.partial(front_kernel, cap),
        grid=(GROUPS,),
        in_specs=[
            whole(fetched.shape),
            whole(ocol.shape),
            whole(orow.shape),
            whole(rel_col.shape),
            whole(relation_table.shape),
            pl.BlockSpec((1, 1, LANES), lambda g: (g, 0, 0)),
            whole(band.shape),
            pl.BlockSpec((count, 1, BAND_OUT, width), lambda g: (0, g, 0, 0)),
        ],
        out_specs=[
            pl.BlockSpec((1, queries, lanes), lambda g: (g, 0, 0)),
            pl.BlockSpec((1, queries, LANES), lambda g: (g, 0, 0)),
            whole((queries, width)),
            whole((width, queries)),
            whole((width, queries)),
        ],
        out_shape=[
            jax.ShapeDtypeStruct((GROUPS, queries, lanes), f32),
            jax.ShapeDtypeStruct((GROUPS, queries, LANES), bf16),
            jax.ShapeDtypeStruct((queries, width), bf16),
            jax.ShapeDtypeStruct((width, queries), bf16),
            jax.ShapeDtypeStruct((width, queries), bf16),
        ],
        scratch_shapes=[
            pltpu.VMEM((queries, width), bf16),
            pltpu.VMEM((queries, width), bf16),
            pltpu.VMEM((queries, width), f32),
        ],
        compiler_params=params("arbitrary"),
        cost_estimate=cost(4e9, 2.4e7, 2.5e6),
        name="front",
    )(fetched, ocol, orow, rel_col, relation_table, windows, band, weight)


def score_kernel(cand, qv_ref, pos_ref, tails_ref, own_ref, other_ref, acc):
    step = pl.program_id(0)

    @pl.when(step == 0)
    def _():
        acc[...] = jnp.zeros_like(acc)

    blocks, _, cap = tails_ref.shape
    qv = qv_ref[...]
    queries = qv.shape[0]
    total = acc[...]
    for b in range(blocks):
        tails = tails_ref[b]
        score = mm(qv, tails)
        here = iota((queries, cap), 1) + (step * blocks + b) * cap
        target = jnp.where(here == pos_ref[...], 1.0 - smooth + smooth / cand, smooth / cand)
        grad = ((sigmoid(score) - target) * loss_weight).astype(bf16)
        total = total + mm(grad, tails, NT)
    acc[...] = total

    @pl.when(step == pl.num_programs(0) - 1)
    def _():
        own_ref[...] = acc[: queries // 2, :]
        other_ref[...] = acc[queries // 2 :, :]


def score_part(qv2, pos2, tails, cand):
    owners, width, cap = tails.shape
    queries = qv2.shape[0]
    blocks = math.gcd(owners, max(1, 2048 // cap))
    half = jax.ShapeDtypeStruct((queries // 2, width), f32)
    return pl.pallas_call(
        functools.partial(score_kernel, cand),
        grid=(owners // blocks,),
        in_specs=[
            whole(qv2.shape),
            whole(pos2.shape),
            pl.BlockSpec((blocks, width, cap), lambda s: (s, 0, 0)),
        ],
        out_specs=[whole(half.shape), whole(half.shape)],
        out_shape=[half, half],
        scratch_shapes=[pltpu.VMEM((queries, width), f32)],
        compiler_params=params("arbitrary"),
        cost_estimate=cost(1e9, 2e6, 1e6),
        name="score",
    )(qv2, pos2, tails)


def back_kernel(
    cap, qg_ref, ocol_ref, orow_ref, win_ref, band_ref, w_ref, pre_ref, pwin_ref,
    relt_ref, out_ref, corr_ref, hacc, racc,
):
    g = pl.program_id(0)
    queries, width = hacc.shape

    @pl.when(g == 0)
    def _():
        hacc[...] = jnp.zeros_like(hacc)
        racc[...] = jnp.zeros_like(racc)
        corr_ref[...] = jnp.zeros_like(corr_ref)

    qg = qg_ref[...]
    image = pwin_ref[0]
    count = w_ref.shape[0]
    chunk = math.gcd(count, 16)
    spread = jnp.zeros((queries, LANES), f32)
    for c in range(0, count, chunk):
        rows = pl.ds(c * BAND_OUT, chunk * BAND_OUT)
        weight = w_ref[c : c + chunk, 0].reshape(chunk * BAND_OUT, width)
        linear = mm(qg, weight, NT)
        v = pre_ref[0, :, rows]
        s = sigmoid(v)
        grad = (linear * (s * (1.0 + v * (1.0 - s)))).astype(bf16)
        spread = spread + mm(grad, band_ref[rows, :])
        corr_ref[:, rows] += mm(image, grad, TN)
    win = win_ref[0]
    entry = iota((width, LANES), 0)
    hpick = onehot(entry == win)
    rpick = onehot(entry + width == win)
    high, low = split(spread)
    hacc[...] += mm(high, hpick, NT) + mm(low, hpick, NT)
    racc[...] += mm(rpick, high, NT) + mm(rpick, low, NT)

    @pl.when(g == GROUPS - 1)
    def _():
        relt_ref[...] = racc[...]
        orow = orow_ref[...]
        same = (ocol_ref[...] == orow) & (iota((queries, queries), 0) < iota((queries, queries), 1))
        rank = jnp.sum(jnp.where(same, 1.0, 0.0), axis=0, keepdims=True)
        slot = orow * cap + rank.astype(i32)
        pick = onehot(iota((out_ref.shape[0], queries), 0) == slot)
        out_ref[...] = mm(pick, hacc[...].astype(bf16)).astype(bf16)


def back(qg, ocol, orow, windows, band, weight, pre, pwin, slots, cap):
    queries, width = qg.shape
    count = weight.shape[0]
    lanes = count * BAND_OUT
    return pl.pallas_call(
        functools.partial(back_kernel, cap),
        grid=(GROUPS,),
        in_specs=[
            whole(qg.shape),
            whole(ocol.shape),
            whole(orow.shape),
            pl.BlockSpec((1, 1, LANES), lambda g: (g, 0, 0)),
            whole(band.shape),
            pl.BlockSpec((count, 1, BAND_OUT, width), lambda g: (0, g, 0, 0)),
            pl.BlockSpec((1, queries, lanes), lambda g: (g, 0, 0)),
            pl.BlockSpec((1, queries, LANES), lambda g: (g, 0, 0)),
        ],
        out_specs=[
            whole((width, queries)),
            whole((slots, width)),
            whole((LANES, lanes)),
        ],
        out_shape=[
            jax.ShapeDtypeStruct((width, queries), f32),
            jax.ShapeDtypeStruct((slots, width), bf16),
            jax.ShapeDtypeStruct((LANES, lanes), f32),
        ],
        scratch_shapes=[pltpu.VMEM((queries, width), f32), pltpu.VMEM((width, queries), f32)],
        compiler_params=params("arbitrary", mib=48),
        cost_estimate=cost(6e9, 2.8e7, 2.5e6),
        name="back",
    )(qg, ocol, orow, windows, band, weight, pre, pwin)


def diag_kernel(ks, corr_ref, out_ref, scr):
    lanes = corr_ref.shape[1]
    count = out_ref.shape[1]
    lane = iota((1, lanes), 1)
    unit = lane - (lane // BAND_OUT) * BAND_OUT
    di = unit // IMG
    j = unit - di * IMG
    xs = iota((IMG, lanes), 0)
    near = [((j + (b - ks // 2) + IMG) % IMG) == xs for b in range(ks)]
    for a in range(ks):
        rows = jnp.zeros((IMG, lanes), f32)
        for d in range(BAND):
            first = (d + a) * IMG
            rows = jnp.where(di == d, corr_ref[first : first + IMG, :], rows)
        for b in range(ks):
            scr[a * ks + b : a * ks + b + 1, :] = jnp.sum(
                jnp.where(near[b], rows, 0.0), axis=0, keepdims=True
            )
    member = onehot(iota((lanes, count), 0) // BAND_OUT == iota((lanes, count), 1))
    high, low = split(scr[...])
    out_ref[...] = mm(high, member) + mm(low, member)


def filter_sums(corr, count, ks):
    lanes = corr.shape[1]
    return pl.pallas_call(
        functools.partial(diag_kernel, ks),
        out_shape=jax.ShapeDtypeStruct((ks * ks, count), f32),
        scratch_shapes=[pltpu.VMEM((ks * ks, lanes), f32)],
        compiler_params=params(mib=48),
        cost_estimate=cost(3e7, 4e6),
        name="filter_sums",
    )(corr)


def tail_kernel(cand, tails_ref, scand_ref, qvt_ref, pos_ref, own_ref, other_ref, acc):
    step = pl.program_id(0)

    @pl.when(step == 0)
    def _():
        acc[...] = jnp.zeros_like(acc)

    blocks = qvt_ref.shape[0]
    qvt = jnp.concatenate([qvt_ref[b, 0] for b in range(blocks)], axis=1)
    pos = jnp.concatenate([pos_ref[b] for b in range(blocks)], axis=1)
    score = mm(tails_ref[...], qvt)
    target = jnp.where(scand_ref[...] == pos, 1.0 - smooth + smooth / cand, smooth / cand)
    grad = ((sigmoid(score) - target) * loss_weight).astype(bf16)
    acc[...] += mm(grad, qvt, NT)

    @pl.when(step == pl.num_programs(0) - 1)
    def _():
        cap = own_ref.shape[0]
        own_ref[...] = acc[:cap, :]
        other_ref[...] = acc[cap:, :]


def tail_part(tails2, scand2, gathered, which, pos, cand):
    owners, _, width, queries = gathered.shape
    cap = tails2.shape[0] // 2
    blocks = 2 if owners % 2 == 0 else 1
    half = jax.ShapeDtypeStruct((cap, width), f32)
    return pl.pallas_call(
        functools.partial(tail_kernel, cand),
        grid=(owners // blocks,),
        in_specs=[
            whole(tails2.shape),
            whole(scand2.shape),
            pl.BlockSpec((blocks, 1, width, queries), lambda s: (s, which, 0, 0)),
            pl.BlockSpec((blocks, 1, queries), lambda s: (s, 0, 0)),
        ],
        out_specs=[whole(half.shape), whole(half.shape)],
        out_shape=[half, half],
        scratch_shapes=[pltpu.VMEM((2 * cap, width), f32)],
        compiler_params=params("arbitrary"),
        cost_estimate=cost(2e9, 3e6, 1e6),
        name="tail_grad",
    )(tails2, scand2, gathered, pos)


def proj_kernel(
    rtab_ref, win_ref, band_ref, hvt_ref, qgt_ref, rel_ref, own_ref, other_ref, hmat, rmat, acc
):
    step = pl.program_id(0)
    width = rtab_ref.shape[0]
    rels = rtab_ref.shape[1]

    @pl.when(step == 0)
    def _():
        acc[...] = jnp.zeros_like(acc)
        entry = iota((width, LANES), 0)
        for g in range(GROUPS):
            hmat[g] = mm(band_ref[...], onehot(entry == win_ref[g]), NT).astype(bf16)
            rmat[g] = mm(band_ref[...], onehot(entry + width == win_ref[g]), NT).astype(bf16)

    blocks = hvt_ref.shape[0]
    hvt = jnp.concatenate([hvt_ref[b, 0] for b in range(blocks)], axis=1)
    qgt = jnp.concatenate([qgt_ref[b, 0] for b in range(blocks)], axis=1)
    rel = jnp.concatenate([rel_ref[b] for b in range(blocks)], axis=1)
    rvt = mm(rtab_ref[...], onehot(iota((rels, rel.shape[1]), 0) == rel)).astype(bf16)
    for g in range(GROUPS):
        pre = mm(hmat[g], hvt) + mm(rmat[g], rvt)
        feats = (pre * sigmoid(pre)).astype(bf16)
        acc[g] += mm(feats, qgt, NT)

    @pl.when(step == pl.num_programs(0) - 1)
    def _():
        half = own_ref.shape[0]
        for f in range(half):
            for g in range(GROUPS):
                own_ref[f, g] = acc[g, f * BAND_OUT : (f + 1) * BAND_OUT, :]
                other_ref[f, g] = acc[g, (half + f) * BAND_OUT : (half + f + 1) * BAND_OUT, :]


def proj_part(rtab_t, windows, band2, gathered, rel_rows):
    owners, _, width, queries = gathered.shape
    rows = band2.shape[0]
    blocks = 2 if owners % 2 == 0 else 1
    half = jax.ShapeDtypeStruct((rows // BAND_OUT // 2, GROUPS, BAND_OUT, width), f32)
    return pl.pallas_call(
        proj_kernel,
        grid=(owners // blocks,),
        in_specs=[
            whole(rtab_t.shape),
            whole(windows.shape),
            whole(band2.shape),
            pl.BlockSpec((blocks, 1, width, queries), lambda s: (s, 0, 0, 0)),
            pl.BlockSpec((blocks, 1, width, queries), lambda s: (s, 2, 0, 0)),
            pl.BlockSpec((blocks, 1, queries), lambda s: (s, 0, 0)),
        ],
        out_specs=[whole(half.shape), whole(half.shape)],
        out_shape=[half, half],
        scratch_shapes=[
            pltpu.VMEM((GROUPS, rows, width), bf16),
            pltpu.VMEM((GROUPS, rows, width), bf16),
            pltpu.VMEM((GROUPS, rows, width), f32),
        ],
        compiler_params=params("arbitrary"),
        cost_estimate=cost(6e9, 6e6, 2.5e6),
        name="proj_grad",
    )(rtab_t, windows, band2, gathered, gathered, rel_rows)


def proj_columns(first, cols, filters, chequer_perm, relation_table, gathered, rel_rows):
    ks = filters.shape[-1]
    rim = ks // 2
    flat = IMG * IMG
    column = first + jnp.arange(cols, dtype=i32)
    f = column // flat
    i = (column % flat) // IMG
    j = column % IMG
    spot = jnp.arange(flat, dtype=i32)
    a = (spot[:, None] // IMG - i[None, :] + rim) % IMG
    b = (spot[:, None] % IMG - j[None, :] + rim) % IMG
    tap = filters[f[None, :], jnp.minimum(a, ks - 1), jnp.minimum(b, ks - 1)]
    matrix = jnp.where((a < ks) & (b < ks), tap, jnp.zeros((), bf16))
    owners, _, width, queries = gathered.shape
    head = gathered[:, 0].transpose(0, 2, 1).reshape(owners * queries, width)
    qg = gathered[:, 2].transpose(0, 2, 1).reshape(owners * queries, width)
    joined = jnp.concatenate([head, relation_table[rel_rows.reshape(-1)]], axis=1)
    pre = mm(joined[:, chequer_perm], matrix)
    return mm((pre * sigmoid(pre)).astype(bf16), qg, TN)


def rel_kernel(relt_ref, rel_ref, out_ref):
    step = pl.program_id(0)

    @pl.when(step == 0)
    def _():
        out_ref[...] = jnp.zeros_like(out_ref)

    blocks = relt_ref.shape[0]
    grads = jnp.concatenate([relt_ref[b] for b in range(blocks)], axis=1)
    rel = jnp.concatenate([rel_ref[b] for b in range(blocks)], axis=1)
    pick = onehot(iota((out_ref.shape[0], rel.shape[1]), 0) == rel)
    high, low = split(grads)
    out_ref[...] += mm(pick, high, NT) + mm(pick, low, NT)


def rel_part(relt, rel_rows, rels):
    owners, width, queries = relt.shape
    blocks = 2 if owners % 2 == 0 else 1
    return pl.pallas_call(
        rel_kernel,
        grid=(owners // blocks,),
        in_specs=[
            pl.BlockSpec((blocks, width, queries), lambda s: (s, 0, 0)),
            pl.BlockSpec((blocks, 1, queries), lambda s: (s, 0, 0)),
        ],
        out_specs=whole((rels, width)),
        out_shape=jax.ShapeDtypeStruct((rels, width), f32),
        compiler_params=params("arbitrary"),
        cost_estimate=cost(2e9, 3e6),
        name="rel_grad",
    )(relt, rel_rows)


def entity_kernel(want_ref, incoming_ref, srow_ref, own_ref, recv_ref, out_ref):
    rows = out_ref.shape[0]
    first = pl.program_id(0) * rows
    here = iota((rows, want_ref.shape[1]), 0) + first
    total = mm(onehot(here == want_ref[...]), incoming_ref[...])
    here = iota((rows, srow_ref.shape[1]), 0) + first
    pick = onehot(here == srow_ref[...])
    high, low = split(own_ref[...] + recv_ref[...])
    out_ref[...] = total + mm(pick, high) + mm(pick, low)


def entity_sum(want, incoming, srow, own, recv, rows):
    width = own.shape[1]
    block = math.gcd(rows, 512)
    return pl.pallas_call(
        entity_kernel,
        grid=(rows // block,),
        in_specs=[whole(want.shape), whole(incoming.shape), whole(srow.shape), whole(own.shape), whole(recv.shape)],
        out_specs=pl.BlockSpec((block, width), lambda s: (s, 0)),
        out_shape=jax.ShapeDtypeStruct((rows, width), f32),
        compiler_params=params("arbitrary"),
        cost_estimate=cost(1.5e9, 4e6),
        name="entity_grad",
    )(want, incoming, srow, own, recv)


def shards(
    entity_table,
    relation_table,
    filters,
    proj_weight,
    chequer_perm,
    head_owner,
    head_row,
    rel_ids,
    pos_index,
    tail_owner,
    tail_row,
):
    count = lax.axis_size("shard")
    me = lax.axis_index("shard")
    core = me & 1
    partner = me ^ 1
    queries = head_row.shape[0]
    cand = tail_row.shape[0]
    rows, width = entity_table.shape
    rels = relation_table.shape[0]
    filts, ks, _ = filters.shape
    head_cap = 2 * queries // count
    tail_cap = 2 * cand // count
    same_core = [list(range(c, count, 2)) for c in range(2)]
    swap = [(d, d ^ 1) for d in range(count)]

    def gather_core(x):
        return lax.all_gather(x, "shard", axis=0, axis_index_groups=same_core)

    def to_partner(x):
        return lax.ppermute(x, "shard", swap)

    me1 = me.reshape(1)
    heads = head_owner[:, 0]
    numbers = lax.all_gather(jnp.stack([heads, head_row, rel_ids, pos_index]), "shard", axis=0)
    tail_owners = tail_owner[:, 0]
    tails, tails_t, slot_cand, slot_row = pack_tails(me1, tail_owners, tail_row, entity_table, tail_cap)
    core_tails = gather_core(tails_t)
    tails2 = jnp.concatenate([tails, to_partner(tails)], axis=0)
    scand2 = jnp.concatenate([slot_cand, to_partner(slot_cand)], axis=0)

    found, want = find_heads(me1, numbers[:, 0], numbers[:, 1], entity_table, head_cap)
    fetched = lax.all_to_all(
        found.reshape(count, head_cap, width), "shard", split_axis=0, concat_axis=0, tiled=True
    ).reshape(count * head_cap, width)
    band = build_band(filters)
    extended = jnp.concatenate([chequer_perm[-BAND_OUT:], chequer_perm, chequer_perm[:BAND_OUT]])
    reach = BAND + ks - 1
    windows = jnp.stack([extended[g * BAND_OUT : g * BAND_OUT + reach * IMG] for g in range(GROUPS)])
    windows = jnp.pad(windows, ((0, 0), (0, LANES - reach * IMG)), constant_values=-1)[:, None]
    weight = proj_weight.reshape(filts, GROUPS, BAND_OUT, width)
    mates = numbers.reshape(count // 2, 2, 4, queries)
    core_numbers = lax.dynamic_index_in_dim(mates, core, 1, keepdims=False)
    rel_rows = core_numbers[:, 2:3]
    pos_rows = core_numbers[:, 3:4]
    pos2 = jnp.concatenate([pos_index, lax.dynamic_index_in_dim(numbers, partner, 0, keepdims=False)[3]])
    pos2 = pos_slots(core.reshape(1), tail_owners, pos2[:, None], tail_cap)
    ocol = heads[:, None]
    orow = heads[None, :]
    pre, pwin, qv, hvt, qvt = front(
        fetched, ocol, orow, rel_ids[:, None], relation_table, windows, band, weight, head_cap
    )

    qv2 = jnp.concatenate([qv, to_partner(qv)], axis=0)
    own, other = score_part(qv2, pos2, core_tails, cand)
    qg = (own + to_partner(other)).astype(bf16)
    gathered = gather_core(jnp.stack([hvt, qvt, qg.T]))

    relt, outgoing, corr = back(
        qg, ocol, orow, windows, band, weight, pre, pwin, count * head_cap, head_cap
    )
    incoming = lax.all_to_all(
        outgoing.reshape(count, head_cap, width), "shard", split_axis=0, concat_axis=0, tiled=True
    ).reshape(count * head_cap, width)
    relt_all = gather_core(relt)
    filter_grad = lax.psum(filter_sums(corr, filts, ks), "shard").T.reshape(filts, ks, ks)

    own, other = tail_part(tails2, scand2, gathered, 1, pos_rows, cand)
    entity_grad = entity_sum(
        want.reshape(1, -1), incoming, slot_row.reshape(1, -1), own, to_partner(other), rows
    )

    cols = filts * IMG * IMG // count
    if cols % (IMG * IMG) == 0:
        unit = cols // (IMG * IMG) * BAND_OUT
        band2 = jnp.concatenate(
            [lax.dynamic_slice_in_dim(band, d * unit, unit, axis=0) for d in (me, partner)]
        )
        own, other = proj_part(relation_table.T, windows, band2, gathered, rel_rows)
        own, other = own.reshape(cols, width), other.reshape(cols, width)
    else:
        own, other = (
            proj_columns(d * cols, cols, filters, chequer_perm, relation_table, gathered, rel_rows)
            for d in (me, partner)
        )
    proj_grad = own + to_partner(other)

    part = rel_part(relt_all, rel_rows, rels)
    relation_grad = part + to_partner(part)
    return (entity_grad, relation_grad, filter_grad, proj_grad)


def solution(mesh):
    placed = (
        P("shard", None),
        P(),
        P(),
        P(),
        P(),
        P(("parts", "shard"), None),
        P(("parts", "shard")),
        P(("parts", "shard")),
        P(("parts", "shard")),
        P("parts", None),
        P("parts"),
    )
    return jax.shard_map(
        shards,
        mesh=mesh,
        in_specs=placed,
        out_specs=(
            P(("parts", "shard"), None),
            P("parts", None),
            P("parts", None, None),
            P(("parts", "shard"), None),
        ),
        check_vma=False,
    )
```

time: 583 us -> 268 us (0.46); the launches traced: 576 us -> 267 us
  matrix products: 152 us -> 0 us
  local copies, waits for them, and re-layouts: 163 us -> 47.1 us
  Pallas kernels: 0 us -> 62.9 us
  blocking collectives: 179 us -> 121 us
  other arithmetic: 33.6 us -> 9.45 us
  starting transfers between devices: 23.3 us -> 11.1 us
  waiting for transfers between devices: 9.45 us -> 0.87 us
    conv_general_dilated x3 -> x0, matrix products: 125 us -> none  [the longest x1 105 us: conv_backward(): lax.conv_general_dilated(feat_grad, flipped, (1, 1), ((kernel_size - 1, k...]
    gather x8 -> x0, local copies, waits for them, and re-layouts: 70.3 us -> none  [the longest x1 46.1 us: shards(): tail_part[slot_cand]]
    pallas_call x0 -> x12, Pallas kernels: none -> 62.9 us  [the longest x1 14.2 us: back(): pl.pallas_call(functools.partial(back_kernel, cap), grid=(GROUPS,), in_sp...]
    scatter x5 -> x0, local copies, waits for them, and re-layouts: 48.9 us -> none  [the longest x1 15.7 us: shards(): jnp.zeros((tail_cap,), jnp.int32).at[local_slot].set(tail_row, mode='drop')]
    all_gather x1 -> x2, blocking collectives: 98 us -> 57.5 us  [the longest x1 34 us: gather_core(): return lax.all_gather(x, 'shard', axis=0, axis_index_groups=same_core)]
    unnamed x20 -> x74, local copies, waits for them, and re-layouts: 5.83 us -> 35.9 us
    dot_general x6 -> x0, matrix products: 27.1 us -> none  [the longest x1 11.4 us: feature_grad(): lax.dot_general(query_grad, proj_weight, (((1,), (1,)), ((), ())), prefer...]
    psum x1, blocking collectives: 81.2 us -> 63.3 us  [shards(): lax.psum(filter_sums(corr, filts, ks), 'shard').T.reshape(filts, ks, ks)]
  transfers between devices with their start and end apart: 7 -> 11, of which waited for: 1 -> 1; matrix products, arithmetic and copies ran while one was open for 39% -> 13% of each run, Pallas kernels for 0% -> 22%
where the time goes in v1:
time: 268 us; the launch traced here: 267 us
  blocking collectives  121 us (45%)
  Pallas kernels  62.9 us (23%)
  local copies, waits for them, and re-layouts  47.1 us (18%)
  between operations  14.5 us (5%)
  starting transfers between devices  11.1 us (4%)
  other arithmetic  9.45 us (4%)
    psum x1, blocking collectives, shards(): lax.psum(filter_sums(corr, filts, ks), 'shard').T.reshape(filts, ks, ks)  63.3 us
    unnamed x74, local copies, waits for them, and re-layouts  35.9 us
    all_gather x1, blocking collectives, gather_core(): return lax.all_gather(x, 'shard', axis=0, axis_index_groups=same_core)  34 us
    all_gather x1, blocking collectives, shards(): lax.all_gather(jnp.stack([heads, head_row, rel_ids, pos_index]), 'shard',...  23.5 us
    pallas_call x1, Pallas kernels, back(): pl.pallas_call(functools.partial(back_kernel, cap), grid=(GROUPS,), in_sp...  14.2 us
    pallas_call x1, Pallas kernels, proj_part(): pl.pallas_call(proj_kernel, grid=(owners // blocks,), in_specs=[whole(rta...  10.4 us
    pallas_call x1, Pallas kernels, front(): pl.pallas_call(functools.partial(front_kernel, cap), grid=(GROUPS,), in_s...  9.99 us
    pallas_call x1, Pallas kernels, filter_sums(): pl.pallas_call(functools.partial(diag_kernel, ks), out_shape=jax.ShapeDty...  9.17 us
  transfers between devices with their start and end apart: 11, of which 1 were waited for; matrix products, arithmetic and copies ran while one was open for 13% of the time, Pallas kernels for 22%

profile of v1, /device:TPU:0, one launch (start us, length us, event | category | flops | bytes accessed | tf_op | source)
XLA Modules:
  0.0 266.6 jit_solution(9105828070915649630)
XLA Ops:
  7.2 1.4 copy.75.table_ref
  8.8 3.2 %pack_tails.1 = (bf16[512,200]{1,0:T(8,128)(2,1)}, bf16[200,512]{1,0:T(8,128)(2,1)}, s32[512,1]{1,0:T(8,128)}, s32[512,1]{1,0:T(8,128)S(1)}) custom-call(s32[1]{0:T(128)} %bitcast.me_ref, s32[32,128]{1,0:T(8,128)S(1)} %bitcast.61, s32[32,128]{1,0:T(8,128)S(1)} %bitcast.74, bf16[2048,200]{1,0:T(8,128)(2,1)S(1)} %copy.75.table_ref), custom_call_target="tpu_custom_call" | custom-call | flops 1000000000 | bytes 2000000 | tf_op jit(solution)/shard_map/pack_tails/pallas_call | solution.py:136
  12.0 23.5 %all-gather.4 = s32[16,4,128]{2,1,0:T(4,128)S(1)} all-gather(s32[1,4,128]{2,1,0:T(4,128)S(1)} %add_bitcast_fusion), channel_id=2, replica_groups=mesh['parts'=2,'shard'=16] {'shard'}, dimensions={0}, use_global_device_ids=true | all-gather | bytes 34816 | tf_op jit(solution)/shard_map/all_gather | solution.py:690
  36.1 1.4 find_heads.1
  38.2 4.2 %all-to-all-start = ((bf16[16,16,200]{2,1,0:T(8,128)(2,1)}), bf16[16,16,200]{2,1,0:T(8,128)(2,1)}, u32[]{:S(2)}, u32[]{:S(2)}) async-start(bf16[16,16,200]{2,1,0:T(8,128)(2,1)} %bitcast.8), calls=%async_computation | async-start | bytes 262144 | tf_op jit(solution)/shard_map/all_to_all | solution.py:698
  44.8 11.8 %copy.77 = bf16[19200,200]{1,0:T(8,128)(2,1)} copy(bf16[19200,200]{0,1:T(8,128)(2,1)} %param.15) | data formatting | bytes 15360000 | tf_op args[3]
  56.6 2.4 band.1.band_ref
  61.4 10.0 %front.1 = (f32[5,128,3840]{2,1,0:T(8,128)S(1)}, bf16[5,128,256]{2,1,0:T(8,128)(2,1)S(1)}, bf16[128,200]{1,0:T(8,128)(2,1)}, bf16[200,128]{1,0:T(8,128)(2,1)S(1)}, bf16[200,128]{1,0:T(8,128)(2,1)S(1)}) custom-call(bf16[256,200]{1,0:T(8,128)(2,1)} %bitcast.9.fetched_ref, s32[128,1]{1,0:T(8,128)S(1)} %copy-done.6, s32[1,128]{1,0:T(1,128)S(1)} %bitcast.67, ...), custom_call_target="tpu_custom_call" | custom-call | flops 4000000000 | bytes 24000000 | tf_op jit(solution)/shard_map/front/pallas_call | solution.py:266
  72.6 3.7 %copy-done.21 = f32[5,128,3840]{2,1,0:T(8,128)} copy-done((f32[5,128,3840]{2,1,0:T(8,128)}, f32[5,128,3840]{2,1,0:T(8,128)S(1)}, u32[]{:S(2)}) %copy-start.21) | copy-done | bytes 9830424
  77.4 1.3 pos_slots.1.pos_ref
  79.6 1.4 copy-done.17
  81.0 2.0 score.1
  87.6 14.2 %back.1 = (f32[200,128]{1,0:T(8,128)S(1)}, bf16[256,200]{1,0:T(8,128)(2,1)}, f32[256,3840]{1,0:T(8,128)}) custom-call(bf16[128,200]{1,0:T(8,128)(2,1)S(1)} %add_convert_fusion.qg_ref, s32[128,1]{1,0:T(8,128)S(1)} %copy-done.7, s32[1,128]{1,0:T(1,128)S(1)} %bitcast.68, s32[5,1,256]{2,1,0:T(1,128)S(1)} %broadcast_in_dim.10.win_ref, ...), custom_call_target="tpu_custom_call" | custom-call | flops 6000000000 | bytes 28000000 | tf_op jit(solution)/shard_map/back/pallas_call | solution.py:402
  101.8 34.0 %all-gather.3 = f32[1600,128]{1,0:T(8,128)S(1)} all-gather(f32[200,128]{1,0:T(8,128)S(1)} %get-tuple-element.40), channel_id=5, replica_groups={{0,2,4,6,8,10,12,14},{1,3,5,7,9,11,13,15},{16,18,20,22,24,26,28,30},{17..., dimensions={0}, use_global_device_ids=true | all-gather | bytes 921600 | tf_op jit(solution)/shard_map/all_gather | solution.py:683
  135.8 2.4 rel_grad.1
  138.2 1.4 copy.88
  140.6 1.3 copy-done.18
  141.9 10.4 %proj_grad.1 = (f32[3,5,80,200]{3,2,1,0:T(8,128)S(1)}, f32[3,5,80,200]{3,2,1,0:T(8,128)S(1)}) custom-call(bf16[200,1387]{1,0:T(8,128)(2,1)S(1)} %bitcast.57, s32[5,1,256]{2,1,0:T(1,128)S(1)} %broadcast_in_dim.10.win_ref, bf16[480,256]{1,0:T(8,128)(2,1)S(1)} %copy-done.3, bf16[8,3,200,128]{3,2,1,0:T(8,128)(2,1)S(1)} %bitcast.71, ...), custom_call_target="tpu_custom_call" | custom-call | flops 6000000000 | bytes 6000000 | tf_op jit(solution)/shard_map/proj_grad/pallas_call | solution.py:551
  153.4 2.6 copy.90
  157.6 1.1 pad_maximum_fusion.tails_ref
  158.7 3.3 %tail_grad.1 = (f32[512,200]{1,0:T(8,128)S(1)}, f32[512,200]{1,0:T(8,128)}) custom-call(bf16[1024,200]{1,0:T(8,128)(2,1)S(1)} %pad_maximum_fusion.tails_ref, s32[1024,1]{1,0:T(8,128)S(1)} %pad_add_fusion.scand_ref, bf16[8,3,200,128]{3,2,1,0:T(8,128)(2,1)S(1)} %bitcast.73, s32[8,1,128]{2,1,0:T(1,128)S(1)} %get-tuple-element.65.pos_ref), custom_call_target="tpu_custom_call" | custom-call | flops 2000000000 | bytes 3000000 | tf_op jit(solution)/shard_map/tail_grad/pallas_call | solution.py:494
  162.9 4.9 %all-to-all-start.1 = ((bf16[16,16,200]{2,1,0:T(8,128)(2,1)}), bf16[16,16,200]{2,1,0:T(8,128)(2,1)S(1)}, u32[]{:S(2)}, u32[]{:S(2)}) async-start(bf16[16,16,200]{2,1,0:T(8,128)(2,1)} %bitcast.24), calls=%async_computation.1 | async-start | bytes 262144 | tf_op jit(solution)/shard_map/all_to_all | solution.py:727
  168.1 2.1 copy-done
  170.2 9.2 %filter_sums.1 = f32[81,48]{1,0:T(8,128)S(1)} custom-call(f32[256,3840]{1,0:T(8,128)S(1)} %copy-done), custom_call_target="tpu_custom_call" | custom-call | flops 30000000 | bytes 4000000 | tf_op jit(solution)/shard_map/filter_sums/pallas_call | solution.py:457
  179.4 63.3 %psum.7 = f32[48,9,9]{0,2,1:T(8,128)} all-reduce(f32[48,9,9]{0,2,1:T(8,128)S(1)} %reshape.67), channel_id=1, replica_groups=mesh['parts'=2,'shard'=16] {'shard'}, use_global_device_ids=true, to_apply=%region_0.1 | all-reduce | flops 3888 | bytes 31104 | tf_op jit(solution)/shard_map/psum | solution.py:731
  242.7 2.8 %copy.89 = f32[1387,200]{1,0:T(8,128)} copy(f32[1387,200]{0,1:T(8,128)} %collective-permute-done.5) | data formatting | bytes 2219200 | tf_op jit(solution)/shard_map/ppermute | solution.py:686
  245.4 2.7 %add.30 = f32[1387,200]{1,0:T(8,128)} add(f32[1387,200]{1,0:T(8,128)S(1)} %rel_grad.1, f32[1387,200]{1,0:T(8,128)} %copy.89) | non-fusion elementwise | flops 277400 | bytes 3328800 | tf_op jit(solution)/shard_map/add | solution.py:754
  248.1 2.8 %copy.93 = f32[1387,200]{0,1:T(8,128)} copy(f32[1387,200]{1,0:T(8,128)} %add.30) | data formatting | bytes 2219200
  250.9 1.3 copy.91
  252.3 3.2 %entity_grad.1 = f32[2048,200]{1,0:T(8,128)S(1)} custom-call(s32[1,256]{1,0:T(1,128)S(1)} %bitcast.69, bf16[256,200]{1,0:T(8,128)(2,1)S(1)} %bitcast.60, s32[1,512]{1,0:T(1,128)S(1)} %bitcast.65, f32[512,200]{1,0:T(8,128)S(1)} %copy-done.25, f32[512,200]{1,0:T(8,128)} %collective-permute-done.4.recv_ref), custom_call_target="tpu_custom_call" | custom-call | flops 1500000000 | bytes 4000000 | tf_op jit(solution)/shard_map/entity_grad/pallas_call | solution.py:643
  255.5 1.7 copy.92
  257.2 2.6 add.33
  (119 shorter events, 18.7 us)
Async XLA Ops:
  7.2 1.5 copy-start.14
  7.2 1.5 copy-start.20
  7.2 72.4 %all-gather.8.cloned.1.call-start = ((), (), s32[]{:S(2)}) async-start(), calls=%async_computation.2 | async-start | bytes 1843200 | tf_op jit(solution)/shard_map/all_gather | solution.py:683
  8.7 3.2 %copy-start.16 = (s32[128,1]{0,1:T(1,128)S(1)}, s32[128,1]{0,1:T(1,128)}, u32[]{:S(2)}) copy-start(s32[128,1]{0,1:T(1,128)} %param.17) | copy-start | bytes 1540
  8.7 3.2 %copy-start.30 = (s32[128]{0:T(128)S(1)}, s32[128]{0:T(128)}, u32[]{:S(2)}) copy-start(s32[128]{0:T(128)} %param.19) | copy-start | bytes 1540
  8.7 3.2 %copy-start.31 = (s32[128]{0:T(128)S(1)}, s32[128]{0:T(128)}, u32[]{:S(2)}) copy-start(s32[128]{0:T(128)} %param.20) | copy-start | bytes 1540
  8.7 3.2 %copy-start.33 = (s32[128]{0:T(128)S(1)}, s32[128]{0:T(128)}, u32[]{:S(2)}) copy-start(s32[128]{0:T(128)} %param.18) | copy-start | bytes 1540
  11.9 32.2 %copy-start.2 = (bf16[1387,200]{0,1:T(8,128)(2,1)S(1)}, bf16[1387,200]{0,1:T(8,128)(2,1)}, u32[]{:S(2)}) copy-start(bf16[1387,200]{0,1:T(8,128)(2,1)} %param.13) | copy-start | bytes 1664404
  11.9 32.4 %copy-start.29 = (s32[400]{0:T(512)S(1)}, s32[400]{0:T(512)}, u32[]{:S(2)}) copy-start(s32[400]{0:T(512)} %param.16) | copy-start | bytes 4804
  11.9 32.8 %copy-start.28 = (bf16[48,9,9]{0,2,1:T(8,128)(2,1)S(1)}, bf16[48,9,9]{0,2,1:T(8,128)(2,1)}, u32[]{:S(2)}) copy-start(bf16[48,9,9]{0,2,1:T(8,128)(2,1)} %param.14) | copy-start | bytes 23332
  38.2 21.5 %all-to-all-start = ((bf16[16,16,200]{2,1,0:T(8,128)(2,1)}), bf16[16,16,200]{2,1,0:T(8,128)(2,1)}, u32[]{:S(2)}, u32[]{:S(2)}) async-start(bf16[16,16,200]{2,1,0:T(8,128)(2,1)} %bitcast.8), calls=%async_computation | async-start | bytes 262144 | tf_op jit(solution)/shard_map/all_to_all | solution.py:698
  42.3 97.3 %all-gather.10.cloned.1.call-start = ((), (), s32[]{:S(2)}) async-start(), calls=%async_computation.3 | async-start | bytes 1382400 | tf_op jit(solution)/shard_map/all_gather | solution.py:683
  44.8 11.8 %copy-start.13 = (s32[20,256]{1,0:T(8,128)S(1)}, s32[20,256]{1,0:T(8,128)}, u32[]{:S(2)}) copy-start(s32[20,256]{1,0:T(8,128)} %constant.26.clone.codes_ref) | copy-start | bytes 61444
  61.4 15.8 %copy-start.32 = (s32[128]{0:T(128)S(1)}, s32[128]{0:T(128)}, u32[]{:S(2)}) copy-start(s32[128]{0:T(128)} %param.20) | copy-start | bytes 1540
  61.4 16.0 %copy-start.15 = (s32[4096,1]{0,1:T(1,128)S(1)}, s32[4096,1]{0,1:T(1,128)}, u32[]{:S(2)}) copy-start(s32[4096,1]{0,1:T(1,128)} %param.21) | copy-start | bytes 49156
  72.6 3.7 %copy-start.21 = (f32[5,128,3840]{2,1,0:T(8,128)}, f32[5,128,3840]{2,1,0:T(8,128)S(1)}, u32[]{:S(2)}) copy-start(f32[5,128,3840]{2,1,0:T(8,128)S(1)} %get-tuple-element.30.pre_ref) | copy-start | bytes 29491204
  77.0 1.6 collective-permute-start
  79.5 1.4 copy-start.17
  81.0 2.4 copy-start.12
  81.0 2.5 copy-start.10
  81.0 4.9 %copy-start.27 = (s32[16,4,128]{2,1,0:T(4,128)S(1)}, s32[16,4,128]{2,1,0:T(4,128)}, u32[]{:S(2)}) copy-start(s32[16,4,128]{2,1,0:T(4,128)} %copy-done.26) | copy-start | bytes 98308
  83.0 3.7 %copy-start.7 = (s32[128,1]{1,0:T(8,128)S(1)}, s32[128,1]{1,0:T(8,128)}, u32[]{:S(2)}) copy-start(s32[128,1]{1,0:T(8,128)} %copy.78.ocol_ref) | copy-start | bytes 1540
  83.0 1.4 collective-permute-start.1
  85.3 72.2 %collective-permute-start.2 = (bf16[512,200]{1,0:T(8,128)(2,1)}, bf16[512,200]{1,0:T(8,128)(2,1)}, u32[]{:S(2)}, u32[]{:S(2)}) collective-permute-start(bf16[512,200]{1,0:T(8,128)(2,1)} %get-tuple-element.34), channel_id=1, source_target_pairs={{0,1},{1,0},{2,3},{3,2},{4,5},{5,4},{6,7},{7,6},{8,9},{9,8},{10,11... | collective-permute-start | bytes 614408 | tf_op jit(solution)/shard_map/ppermute | solution.py:686
  85.7 70.8 %collective-permute-start.3 = (s32[512,1]{1,0:T(8,128)}, s32[512,1]{1,0:T(8,128)}, u32[]{:S(2)}, u32[]{:S(2)}) collective-permute-start(s32[512,1]{1,0:T(8,128)} %get-tuple-element.35), channel_id=1, source_target_pairs={{0,1},{1,0},{2,3},{3,2},{4,5},{5,4},{6,7},{7,6},{8,9},{9,8},{10,11... | collective-permute-start | bytes 6152 | tf_op jit(solution)/shard_map/ppermute | solution.py:686
  139.6 103.0 %collective-permute-start.5 = (f32[1387,200]{0,1:T(8,128)}, f32[1387,200]{0,1:T(8,128)}, u32[]{:S(2)}, u32[]{:S(2)}) collective-permute-start(f32[1387,200]{0,1:T(8,128)} %copy.88), channel_id=1, source_target_pairs={{0,1},{1,0},{2,3},{3,2},{4,5},{5,4},{6,7},{7,6},{8,9},{9,8},{10,11... | collective-permute-start | bytes 3328808 | tf_op jit(solution)/shard_map/ppermute | solution.py:686
  156.0 2.7 %copy-start.19 = (bf16[24,200,128]{2,1,0:T(8,128)(2,1)S(1)}, bf16[24,200,128]{2,1,0:T(8,128)(2,1)}, u32[]{:S(2)}) copy-start(bf16[24,200,128]{2,1,0:T(8,128)(2,1)} %all-gather.10.cloned.1.call-done) | copy-start | bytes 3686404
  156.0 101.2 %collective-permute-start.6 = (f32[1200,200]{0,1:T(8,128)}, f32[1200,200]{0,1:T(8,128)}, u32[]{:S(2)}, u32[]{:S(2)}) collective-permute-start(f32[1200,200]{0,1:T(8,128)} %copy.90), channel_id=1, source_target_pairs={{0,1},{1,0},{2,3},{3,2},{4,5},{5,4},{6,7},{7,6},{8,9},{9,8},{10,11... | collective-permute-start | bytes 2880008 | tf_op jit(solution)/shard_map/ppermute | solution.py:686
  158.7 9.1 %copy-start.5 = (s32[256,1]{1,0:T(8,128)S(1)}, s32[256,1]{1,0:T(8,128)}, u32[]{:S(2)}) copy-start(s32[256,1]{1,0:T(8,128)} %copy-done.4) | copy-start | bytes 3076
  162.8 89.4 %collective-permute-start.4 = (f32[512,200]{1,0:T(8,128)}, f32[512,200]{1,0:T(8,128)}, u32[]{:S(2)}, u32[]{:S(2)}) collective-permute-start(f32[512,200]{1,0:T(8,128)} %get-tuple-element.39), channel_id=1, source_target_pairs={{0,1},{1,0},{2,3},{3,2},{4,5},{5,4},{6,7},{7,6},{8,9},{9,8},{10,11... | collective-permute-start | bytes 1228808 | tf_op jit(solution)/shard_map/ppermute | solution.py:686
  162.9 89.3 %all-to-all-start.1 = ((bf16[16,16,200]{2,1,0:T(8,128)(2,1)}), bf16[16,16,200]{2,1,0:T(8,128)(2,1)S(1)}, u32[]{:S(2)}, u32[]{:S(2)}) async-start(bf16[16,16,200]{2,1,0:T(8,128)(2,1)} %bitcast.24), calls=%async_computation.1 | async-start | bytes 262144 | tf_op jit(solution)/shard_map/all_to_all | solution.py:727
  168.1 2.1 copy-start
  (13 other events, 11.3 us)
Sparse Core Ops, SparseCore 0:
  12.1 48.5 all-gather.7
  85.4 50.4 all-gather.9

commit v2 on v0

v2 whole, which is shorter than its diff:
```python
import functools
import math

import jax
import jax.numpy as jnp
import numpy as np
from jax import lax
from jax.experimental import pallas as pl
from jax.experimental.pallas import tpu as pltpu
from jax.sharding import PartitionSpec as P

IMG = 20
BAND = 4
GROUPS = IMG // BAND
BAND_OUT = BAND * IMG
LANES = 256

loss_weight = 0.015625
smooth = 0.1

f32 = jnp.float32
bf16 = jnp.bfloat16
i32 = jnp.int32

NN = (((1,), (0,)), ((), ()))
NT = (((1,), (1,)), ((), ()))
TN = (((0,), (0,)), ((), ()))


def mm(a, b, dims=NN):
    return lax.dot_general(a, b, dims, preferred_element_type=f32)


def iota(shape, axis):
    return lax.broadcasted_iota(i32, shape, axis)


def onehot(mask):
    return jnp.where(mask, 1.0, 0.0).astype(bf16)


def split(value):
    high = value.astype(bf16)
    return high, (value - high.astype(f32)).astype(bf16)


def sigmoid(v):
    return 0.5 * jnp.tanh(0.5 * v) + 0.5


def params(*semantics, mib=40):
    return pltpu.CompilerParams(
        dimension_semantics=semantics or None, vmem_limit_bytes=mib << 20
    )


def cost(flops, nbytes, trans=0):
    return pl.CostEstimate(flops=int(flops), bytes_accessed=int(nbytes), transcendentals=int(trans))


def whole(shape):
    return pl.BlockSpec(shape, lambda *_: (0,) * len(shape))


SMEM = pl.BlockSpec(memory_space=pltpu.SMEM)


def band_codes(ks):
    codes = np.full((IMG, LANES), -1, np.int32)
    for j in range(IMG):
        for r in range(ks):
            for x in range(IMG):
                b = (x - j + ks // 2) % IMG
                if b < ks:
                    codes[j, r * IMG + x] = r * ks + b
    return codes


def band_kernel(codes_ref, filt_ref, out_ref, out_t_ref, scr):
    count, taps = filt_ref.shape
    filt = filt_ref[...]
    for j in range(IMG):
        pick = onehot(iota((taps, LANES), 0) == codes_ref[j : j + 1, :])
        row = mm(filt, pick)
        for di in range(BAND):
            scr[:, di * IMG + j, :] = row if di == 0 else pltpu.roll(row, di * IMG, 1)
    full = scr[...].reshape(count * BAND_OUT, LANES)
    out_ref[...] = full.astype(bf16)
    out_t_ref[...] = full.T.astype(bf16)


def build_band(filters, codes):
    count, ks, _ = filters.shape
    return pl.pallas_call(
        band_kernel,
        out_shape=[
            jax.ShapeDtypeStruct((count * BAND_OUT, LANES), bf16),
            jax.ShapeDtypeStruct((LANES, count * BAND_OUT), bf16),
        ],
        scratch_shapes=[pltpu.VMEM((count, BAND_OUT, LANES), f32)],
        compiler_params=params(mib=24),
        cost_estimate=cost(4e7, 4e6),
        name="band",
    )(codes, filters.reshape(count, ks * ks))


VMEM = pl.BlockSpec(memory_space=pltpu.VMEM)


def pieces(refs):
    return [ref.at[i] for ref in refs for i in range(ref.shape[0])]


def pairs(blocks):
    step = 2 if len(blocks) % 2 == 0 else 1
    return [blocks[i : i + step] for i in range(0, len(blocks), step)]


def lanes_of(blocks, rows=slice(None)):
    return jnp.concatenate([b[rows, :] for b in blocks], axis=1)


def pack_kernel(shift, me_ref, owner_ref, row_ref, table_ref, tails_ref, tails_t_ref, cand_ref, srow_ref):
    cap = tails_ref.shape[0]
    lines = owner_ref.shape[0]
    mine = owner_ref[...] == me_ref[0]
    mine_b = onehot(mine)
    before = onehot(iota((128, 128), 0) < iota((128, 128), 1))
    rank = mm(mine_b, before)
    totals = mm(mine_b, jnp.ones((128, 128), bf16))
    upper = onehot(iota((lines, lines), 1) < iota((lines, lines), 0))
    offset = mm(upper, totals.astype(bf16))
    key = jnp.where(mine, (rank + offset).astype(i32), -1)
    code = row_ref[...] * (1 << shift) + iota((lines, 128), 0) * 128 + iota((lines, 128), 1) + 1
    code = code.astype(f32)
    slots = iota((cap, 128), 0)
    total = jnp.zeros((cap, 128), f32)
    for r in range(lines):
        total = total + jnp.where(slots == key[r : r + 1, :], code[r : r + 1, :], 0.0)
    found = jnp.sum(total, axis=1, keepdims=True).astype(i32) - 1
    live = found >= 0
    srow = jnp.where(live, lax.shift_right_arithmetic(found, shift), -1)
    cand_ref[...] = jnp.where(live, found & ((1 << shift) - 1), -1)
    srow_ref[...] = srow
    pick = onehot(iota((cap, table_ref.shape[1]), 1) == srow)
    tails_ref[...] = mm(pick, table_ref[...], NT).astype(bf16)
    tails_t_ref[0] = mm(table_ref[...], pick, NT).astype(bf16)


def pack_tails(me, tail_owners, tail_row, table_t, cap):
    cand = tail_row.shape[0]
    shift = int(math.log2(cand))
    width, rows = table_t.shape
    assert 1 << shift == cand and cand * rows < 1 << 24 and cand % 128 == 0
    return pl.pallas_call(
        functools.partial(pack_kernel, shift),
        in_specs=[SMEM] + [VMEM] * 3,
        out_shape=[
            jax.ShapeDtypeStruct((cap, width), bf16),
            jax.ShapeDtypeStruct((1, width, cap), bf16),
            jax.ShapeDtypeStruct((cap, 1), i32),
            jax.ShapeDtypeStruct((cap, 1), i32),
        ],
        compiler_params=params(mib=16),
        cost_estimate=cost(1e9, 2e6),
        name="pack_tails",
    )(me, tail_owners.reshape(-1, 128), tail_row.reshape(-1, 128), table_t)


def found_kernel(cap, count, me_ref, table_ref, *refs):
    outs, (want_ref, scr) = refs[count:-2], refs[-2:]
    numbers = pieces(refs[:count])
    queries = numbers[0].shape[1]
    owners = jnp.concatenate([b[0:1, :] for b in numbers], axis=0)
    mine = owners == me_ref[0]
    before = onehot(iota((queries, queries), 0) < iota((queries, queries), 1))
    rank = mm(onehot(mine), before)
    key = jnp.where(mine, rank.astype(i32), -1)
    slots = iota((cap, queries), 0)
    for d, block in enumerate(numbers):
        code = (block[1:2, :] + 1).astype(f32)
        picked = jnp.where(slots == key[d : d + 1, :], code, 0.0)
        scr[d * cap : (d + 1) * cap, :] = jnp.sum(picked, axis=1, keepdims=True)
    want = scr[...].astype(i32) - 1
    want_ref[...] = want
    pick = onehot(iota((len(numbers) * cap, table_ref.shape[1]), 1) == want)
    found = mm(pick, table_ref[...], NT).astype(bf16)
    for d, out in enumerate(pieces(outs)):
        out[...] = found[d * cap : (d + 1) * cap, :]


def find_heads(me, numbers, table_t, cap):
    width = table_t.shape[0]
    sizes = [x.shape[0] for x in numbers]
    slots = sum(sizes) * cap
    *found, want = pl.pallas_call(
        functools.partial(found_kernel, cap, len(numbers)),
        in_specs=[SMEM] + [VMEM] * (1 + len(numbers)),
        out_shape=[jax.ShapeDtypeStruct((s, cap, width), bf16) for s in sizes]
        + [jax.ShapeDtypeStruct((slots, 1), i32)],
        scratch_shapes=[pltpu.VMEM((slots, 1), f32)],
        compiler_params=params(mib=16),
        cost_estimate=cost(3e8, 2e6),
        name="find_heads",
    )(me, table_t, *numbers)
    return found, want


def pos_kernel(cap, me_ref, owner_ref, own_ref, other_ref, out_ref):
    cand = owner_ref.shape[1]
    queries = own_ref.shape[2]
    eye = iota((queries, queries), 0) == iota((queries, queries), 1)
    step = min(512, cand)
    for part, ref in enumerate((own_ref, other_ref)):
        row = ref[0, 3:4, :].astype(f32)
        pos = jnp.sum(jnp.where(eye, row, 0.0), axis=1, keepdims=True).astype(i32)
        owner = jnp.zeros((queries, step), f32)
        for c in range(0, cand, step):
            here = iota((queries, step), 1) + c
            value = owner_ref[:, c : c + step].astype(f32)
            owner = owner + jnp.where(here == pos, value, 0.0)
        owner = jnp.sum(owner, axis=1, keepdims=True).astype(i32)
        ahead = jnp.zeros((queries, step), f32)
        for c in range(0, cand, step):
            here = iota((queries, step), 1) + c
            same = (owner_ref[:, c : c + step] == owner) & (here < pos)
            ahead = ahead + jnp.where(same, 1.0, 0.0)
        ahead = jnp.sum(ahead, axis=1, keepdims=True).astype(i32)
        away = owner ^ me_ref[0]
        slot = lax.shift_right_arithmetic(away, 1) * cap + ahead
        out_ref[part * queries : (part + 1) * queries, :] = jnp.where((away & 1) == 0, slot, -1)


def pos_slots(me, tail_owners, own, other, cap):
    queries = own.shape[2]
    return pl.pallas_call(
        functools.partial(pos_kernel, cap),
        in_specs=[SMEM] + [VMEM] * 3,
        out_shape=jax.ShapeDtypeStruct((2 * queries, 1), i32),
        compiler_params=params(mib=8),
        cost_estimate=cost(1e7, 1e5),
        name="pos_slots",
    )(me, tail_owners.reshape(1, -1), own, other)


def slot_picks(cap, slots, me, orow):
    count = slots // cap
    queries = orow.shape[1]
    away = orow ^ me
    member = iota((count, queries), 0) == away
    before = onehot(iota((queries, queries), 0) < iota((queries, queries), 1))
    rank = mm(onehot(member), before)
    rank = jnp.sum(jnp.where(member, rank, 0.0), axis=0, keepdims=True).astype(i32)
    return onehot(iota((slots, queries), 0) == away * cap + rank)


def front_kernel(cap, count, me_ref, orow_ref, rel_ref, rtab_ref, ext_ref, band_ref, w_ref, *refs):
    fetched, (pre_ref, img_ref, qv_ref, hvt_ref, qvt_ref, feats, acc, ext) = refs[:count], refs[count:]
    s = pl.program_id(0)
    width, queries = acc.shape

    @pl.when(s == 0)
    def _():
        rows = jnp.concatenate([b[...] for b in pieces(fetched)], axis=0)
        pick = slot_picks(cap, rows.shape[0], me_ref[0], orow_ref[...])
        hvt = mm(rows, pick, TN).astype(bf16)
        hvt_ref[0] = hvt
        rels = rtab_ref.shape[1]
        rvt = mm(rtab_ref[...], onehot(iota((rels, queries), 0) == rel_ref[...])).astype(bf16)
        entry = iota((width, ext_ref.shape[1]), 0)
        image = mm(onehot(entry == ext_ref[...]), hvt, TN)
        image = image + mm(onehot(entry + width == ext_ref[...]), rvt, TN)
        ext[...] = image.astype(bf16)
        for g in range(GROUPS):
            img_ref[:, g * queries : (g + 1) * queries] = ext[g * BAND_OUT : g * BAND_OUT + LANES, :]
        acc[...] = jnp.zeros_like(acc)

    units = band_ref.shape[0] // BAND_OUT
    flat = GROUPS * BAND_OUT
    pre = mm(band_ref[...], img_ref[...])
    act = (pre * sigmoid(pre)).astype(bf16)
    for f in range(units):
        for g in range(GROUPS):
            rows = slice(f * flat + g * BAND_OUT, f * flat + (g + 1) * BAND_OUT)
            part = slice(f * BAND_OUT, (f + 1) * BAND_OUT)
            lanes = slice(g * queries, (g + 1) * queries)
            pre_ref[rows, :] = pre[part, lanes]
            feats[rows, :] = act[part, lanes]
    acc[...] += mm(w_ref[...], feats[...])

    @pl.when(s == pl.num_programs(0) - 1)
    def _():
        query = acc[...]
        qvt_ref[0] = query.astype(bf16)
        qv_ref[...] = query.T.astype(bf16)


def filter_block(filts):
    return math.gcd(filts, 8)


def front(me, fetched, orow, rel_row, rtab_t, ext, band, weight_t, cap):
    queries = orow.shape[1]
    width, flat = weight_t.shape
    filts = band.shape[0] // BAND_OUT
    units = filter_block(filts)
    cols = flat // filts * units
    return pl.pallas_call(
        functools.partial(front_kernel, cap, len(fetched)),
        grid=(filts // units,),
        in_specs=[
            SMEM,
            whole(orow.shape),
            whole(rel_row.shape),
            whole(rtab_t.shape),
            whole(ext.shape),
            pl.BlockSpec((units * BAND_OUT, LANES), lambda s: (s, 0)),
            pl.BlockSpec((width, cols), lambda s: (0, s)),
        ]
        + [whole(x.shape) for x in fetched],
        out_specs=[
            pl.BlockSpec((cols, queries), lambda s: (s, 0)),
            whole((LANES, GROUPS * queries)),
            whole((queries, width)),
            whole((1, width, queries)),
            whole((1, width, queries)),
        ],
        out_shape=[
            jax.ShapeDtypeStruct((flat, queries), f32),
            jax.ShapeDtypeStruct((LANES, GROUPS * queries), bf16),
            jax.ShapeDtypeStruct((queries, width), bf16),
            jax.ShapeDtypeStruct((1, width, queries), bf16),
            jax.ShapeDtypeStruct((1, width, queries), bf16),
        ],
        scratch_shapes=[
            pltpu.VMEM((cols, queries), bf16),
            pltpu.VMEM((width, queries), f32),
            pltpu.VMEM((ext.shape[1], queries), bf16),
        ],
        compiler_params=params("arbitrary", mib=24),
        cost_estimate=cost(4e9, 2.4e7, 2.5e6),
        name="front",
    )(me, orow, rel_row, rtab_t, ext, band, weight_t, *fetched)


def score_kernel(cand, count, pos_ref, mine_ref, mate_ref, *refs):
    tails, (own_ref, other_ref) = pieces(refs[:count]), refs[count:]
    qv = jnp.concatenate([mine_ref[...], mate_ref[...]], axis=0)
    queries = qv.shape[0]
    cap = tails[0].shape[1]
    total = jnp.zeros(qv.shape, f32)
    for b, ref in enumerate(tails):
        block = ref[...]
        score = mm(qv, block)
        here = iota((queries, cap), 1) + b * cap
        target = jnp.where(here == pos_ref[...], 1.0 - smooth + smooth / cand, smooth / cand)
        grad = ((sigmoid(score) - target) * loss_weight).astype(bf16)
        total = total + mm(grad, block, NT)
    own_ref[...] = total[: queries // 2, :]
    other_ref[...] = total[queries // 2 :, :]


def score_part(qv, mate, pos2, tails, cand):
    half = jax.ShapeDtypeStruct(qv.shape, f32)
    return pl.pallas_call(
        functools.partial(score_kernel, cand, len(tails)),
        out_shape=[half, half],
        compiler_params=params(mib=16),
        cost_estimate=cost(1e9, 2e6, 1e6),
        name="score",
    )(pos2, qv, mate, *tails)


def back_kernel(
    cap, taps, count, me_ref, orow_ref, ext_ref, codes_ref, own_ref, recv_ref, img_ref, bandt_ref, w_ref, pre_ref,
    *refs,
):
    outs, (qgt_out, sums_ref, qgt, fgrad, spread, corr, ext) = refs[:count], refs[count:]
    s = pl.program_id(0)
    width, queries = qgt.shape

    @pl.when(s == 0)
    def _():
        qgt[...] = (own_ref[...] + recv_ref[...]).T.astype(bf16)
        qgt_out[0] = qgt[...]
        spread[...] = jnp.zeros_like(spread)

    units = bandt_ref.shape[1] // BAND_OUT
    flat = GROUPS * BAND_OUT
    for f in range(units):
        cols = slice(f * flat, (f + 1) * flat)
        linear = mm(w_ref[:, cols], qgt[...], TN)
        v = pre_ref[cols, :]
        sig = sigmoid(v)
        grad = (linear * (sig * (1.0 + v * (1.0 - sig)))).astype(bf16)
        for g in range(GROUPS):
            fgrad[f * BAND_OUT : (f + 1) * BAND_OUT, g * queries : (g + 1) * queries] = grad[
                g * BAND_OUT : (g + 1) * BAND_OUT, :
            ]
    spread[...] += mm(bandt_ref[...], fgrad[...])
    corr[pl.ds(s * units, units)] = mm(fgrad[...], img_ref[...], NT).reshape(units, BAND_OUT, LANES)

    @pl.when(s == pl.num_programs(0) - 1)
    def _():
        filts = corr.shape[0]
        ext[...] = jnp.zeros_like(ext)
        for g in range(GROUPS):
            ext[g * BAND_OUT : g * BAND_OUT + LANES, :] += spread[:, g * queries : (g + 1) * queries]
        entry = iota((width, ext.shape[0]), 0)
        high, low = split(ext[...])
        hpick = onehot(entry == ext_ref[...])
        rpick = onehot(entry + width == ext_ref[...])
        hgrad = (mm(hpick, high) + mm(hpick, low)).astype(bf16)
        sums_ref[0, :width, :] = mm(rpick, high) + mm(rpick, low)
        total = jnp.zeros((taps, filts), f32)
        for j in range(IMG):
            rows = corr[:, j, :]
            for di in range(1, BAND):
                rows = rows + pltpu.roll(corr[:, di * IMG + j, :], LANES - di * IMG, 1)
            pick = onehot(iota((taps, LANES), 0) == codes_ref[j : j + 1, :])
            rhigh, rlow = split(rows)
            total = total + mm(pick, rhigh, NT) + mm(pick, rlow, NT)
        rest = sums_ref.shape[1] - width
        sums_ref[0, width:, :] = jnp.zeros((rest, queries), f32)
        sums_ref[0, width : width + taps, :filts] = total
        blocks = pieces(outs)
        pick = slot_picks(cap, len(blocks) * cap, me_ref[0], orow_ref[...])
        rows = mm(pick, hgrad, NT).astype(bf16)
        for d, out in enumerate(blocks):
            out[...] = rows[d * cap : (d + 1) * cap, :]


def sums_rows(width, taps):
    return -(-(width + taps) // 8) * 8


def back(me, own, recv, orow, ext, codes, img, band_t, weight_t, pre, sizes, cap, taps):
    queries, width = own.shape
    flat = weight_t.shape[1]
    filts = band_t.shape[1] // BAND_OUT
    units = filter_block(filts)
    cols = flat // filts * units
    rows = sums_rows(width, taps)
    assert filts <= queries
    *outgoing, qgt, sums = pl.pallas_call(
        functools.partial(back_kernel, cap, taps, len(sizes)),
        grid=(filts // units,),
        in_specs=[
            SMEM,
            whole(orow.shape),
            whole(ext.shape),
            whole(codes.shape),
            whole(own.shape),
            whole(recv.shape),
            whole(img.shape),
            pl.BlockSpec((LANES, units * BAND_OUT), lambda s: (0, s)),
            pl.BlockSpec((width, cols), lambda s: (0, s)),
            pl.BlockSpec((cols, queries), lambda s: (s, 0)),
        ],
        out_specs=[whole((n, cap, width)) for n in sizes]
        + [whole((1, width, queries)), whole((1, rows, queries))],
        out_shape=[jax.ShapeDtypeStruct((n, cap, width), bf16) for n in sizes]
        + [
            jax.ShapeDtypeStruct((1, width, queries), bf16),
            jax.ShapeDtypeStruct((1, rows, queries), f32),
        ],
        scratch_shapes=[
            pltpu.VMEM((width, queries), bf16),
            pltpu.VMEM((units * BAND_OUT, GROUPS * queries), bf16),
            pltpu.VMEM((LANES, GROUPS * queries), f32),
            pltpu.VMEM((filts, BAND_OUT, LANES), f32),
            pltpu.VMEM((ext.shape[1], queries), f32),
        ],
        compiler_params=params("arbitrary", mib=28),
        cost_estimate=cost(6e9, 2e7, 2.5e6),
        name="back",
    )(me, orow, ext, codes, own, recv, img, band_t, weight_t, pre)
    return outgoing, qgt, sums


def tail_kernel(cand, count, tails_ref, mate_ref, scand_ref, mcand_ref, *refs):
    numbers, vectors = pieces(refs[:count]), pieces(refs[count : 2 * count])
    own_ref, other_ref = refs[2 * count :]
    tails = jnp.concatenate([tails_ref[...], mate_ref[...]], axis=0)
    scand = jnp.concatenate([scand_ref[...], mcand_ref[...]], axis=0)
    cap = tails_ref.shape[0]
    own = jnp.zeros(own_ref.shape, f32)
    other = jnp.zeros(own_ref.shape, f32)
    for nums, vecs in zip(pairs(numbers), pairs(vectors)):
        qvt = lanes_of(vecs)
        pos = lanes_of(nums, slice(3, 4))
        score = mm(tails, qvt)
        target = jnp.where(scand == pos, 1.0 - smooth + smooth / cand, smooth / cand)
        grad = ((sigmoid(score) - target) * loss_weight).astype(bf16)
        own = own + mm(qvt, grad[:cap, :], NT)
        other = other + mm(qvt, grad[cap:, :], NT)
    own_ref[...] = own
    other_ref[...] = other


def tail_part(tails, mate, scand, mcand, numbers, vectors, cand):
    cap, width = tails.shape
    half = jax.ShapeDtypeStruct((width, cap), f32)
    return pl.pallas_call(
        functools.partial(tail_kernel, cand, len(numbers)),
        out_shape=[half, half],
        compiler_params=params(mib=24),
        cost_estimate=cost(2e9, 3e6, 1e6),
        name="tail_grad",
    )(tails, mate, scand, mcand, *numbers, *vectors)


def proj_kernel(count, rtab_ref, ext_ref, band_ref, mate_ref, *refs):
    numbers = pieces(refs[:count])
    heads = pieces(refs[count : 2 * count])
    grads = pieces(refs[2 * count : 3 * count])
    own_ref, other_ref, pick, hmat, rmat = refs[3 * count :]
    width, rels = rtab_ref.shape
    units = band_ref.shape[0] // BAND_OUT
    flat = GROUPS * BAND_OUT
    cols = units * flat
    entry = iota((width, ext_ref.shape[1]), 0)
    for part, mat in ((0, hmat), (width, rmat)):
        pick[...] = jnp.where(entry + part == ext_ref[...], 1.0, 0.0).T.astype(bf16)
        for k, source in enumerate((band_ref, mate_ref)):
            for g in range(GROUPS):
                rows = mm(source[...], pick[g * BAND_OUT : g * BAND_OUT + LANES, :]).astype(bf16)
                for f in range(units):
                    first = k * cols + f * flat + g * BAND_OUT
                    mat[first : first + BAND_OUT, :] = rows[f * BAND_OUT : (f + 1) * BAND_OUT, :]
    for k, out in enumerate((own_ref, other_ref)):
        out[...] = jnp.zeros_like(out)
    for nums, hs, gs in zip(pairs(numbers), pairs(heads), pairs(grads)):
        hvt = lanes_of(hs)
        qgt = lanes_of(gs)
        rel = lanes_of(nums, slice(2, 3))
        rvt = mm(rtab_ref[...], onehot(iota((rels, rel.shape[1]), 0) == rel)).astype(bf16)
        for k, out in enumerate((own_ref, other_ref)):
            rows = slice(k * cols, (k + 1) * cols)
            pre = mm(hmat[rows, :], hvt) + mm(rmat[rows, :], rvt)
            out[...] += mm(qgt, (pre * sigmoid(pre)).astype(bf16), NT)


def proj_part(rtab_t, ext, band, mate, numbers, heads, grads):
    width = rtab_t.shape[0]
    rows = band.shape[0]
    cols = rows * GROUPS
    half = jax.ShapeDtypeStruct((width, cols), f32)
    return pl.pallas_call(
        functools.partial(proj_kernel, len(numbers)),
        out_shape=[half, half],
        scratch_shapes=[
            pltpu.VMEM((ext.shape[1], width), bf16),
            pltpu.VMEM((2 * cols, width), bf16),
            pltpu.VMEM((2 * cols, width), bf16),
        ],
        compiler_params=params(mib=28),
        cost_estimate=cost(6e9, 6e6, 2.5e6),
        name="proj_grad",
    )(rtab_t, ext, band, mate, *numbers, *heads, *grads)


def proj_columns(first, cols, filters, chequer_perm, relation_table, numbers, heads, grads):
    ks = filters.shape[-1]
    rim = ks // 2
    flat = IMG * IMG
    column = first + jnp.arange(cols, dtype=i32)
    f = column // flat
    i = (column % flat) // IMG
    j = column % IMG
    spot = jnp.arange(flat, dtype=i32)
    a = (spot[:, None] // IMG - i[None, :] + rim) % IMG
    b = (spot[:, None] % IMG - j[None, :] + rim) % IMG
    tap = filters[f[None, :], jnp.minimum(a, ks - 1), jnp.minimum(b, ks - 1)]
    matrix = jnp.where((a < ks) & (b < ks), tap, jnp.zeros((), bf16))
    width = heads.shape[1]
    head = heads.transpose(0, 2, 1).reshape(-1, width)
    qg = grads.transpose(0, 2, 1).reshape(-1, width)
    joined = jnp.concatenate([head, relation_table[numbers[:, 2].reshape(-1)]], axis=1)
    pre = mm(joined[:, chequer_perm], matrix)
    return mm(qg, (pre * sigmoid(pre)).astype(bf16), TN)


def rel_kernel(count, width, taps, *refs):
    numbers, sums = pieces(refs[:count]), pieces(refs[count : 2 * count])
    rel_ref, filt_ref = refs[2 * count :]
    total = jnp.zeros(rel_ref.shape, f32)
    filt = jnp.zeros(filt_ref.shape, f32)
    for nums, parts in zip(pairs(numbers), pairs(sums)):
        rel = lanes_of(nums, slice(2, 3))
        pick = onehot(iota((rel_ref.shape[1], rel.shape[1]), 0) == rel)
        high, low = split(lanes_of(parts, slice(0, width)))
        total = total + mm(high, pick, NT) + mm(low, pick, NT)
        for part in parts:
            filt = filt + part[width:, :]
    rel_ref[...] = total
    filt_ref[...] = filt


def rel_part(numbers, sums, width, rels, taps):
    rows, queries = sums[0].shape[1:]
    return pl.pallas_call(
        functools.partial(rel_kernel, len(numbers), width, taps),
        out_shape=[
            jax.ShapeDtypeStruct((width, rels), f32),
            jax.ShapeDtypeStruct((rows - width, queries), f32),
        ],
        compiler_params=params(mib=24),
        cost_estimate=cost(2e9, 3e6),
        name="rel_grad",
    )(*numbers, *sums)


def entity_kernel(count, want_ref, srow_ref, own_ref, recv_ref, *refs):
    incoming, out_ref = refs[:count], refs[count]
    rows = out_ref.shape[1]
    grads = jnp.concatenate([b[...] for b in pieces(incoming)], axis=0)
    total = mm(grads, onehot(iota((want_ref.shape[0], rows), 1) == want_ref[...]), TN)
    pick = onehot(iota((srow_ref.shape[0], rows), 1) == srow_ref[...])
    high, low = split(own_ref[...] + recv_ref[...])
    out_ref[...] = total + mm(high, pick) + mm(low, pick)


def entity_sum(want, srow, own, recv, incoming, rows):
    return pl.pallas_call(
        functools.partial(entity_kernel, len(incoming)),
        out_shape=jax.ShapeDtypeStruct((own.shape[0], rows), f32),
        compiler_params=params(mib=24),
        cost_estimate=cost(1.5e9, 4e6),
        name="entity_grad",
    )(want, srow, own, recv, *incoming)


def shards(
    entity_table,
    relation_table,
    filters,
    proj_weight,
    chequer_perm,
    head_owner,
    head_row,
    rel_ids,
    pos_index,
    tail_owner,
    tail_row,
):
    count = lax.axis_size("shard")
    me = lax.axis_index("shard")
    assert count & (count - 1) == 0
    direct = count <= 16
    order = me ^ jnp.arange(count, dtype=i32)
    core_order = (me >> 1) ^ jnp.arange(count // 2, dtype=i32)
    queries = head_row.shape[0]
    cand = tail_row.shape[0]
    rows, width = entity_table.shape
    rels = relation_table.shape[0]
    filts, ks, _ = filters.shape
    head_cap = 2 * queries // count
    tail_cap = 2 * cand // count
    same_core = [list(range(c, count, 2)) for c in range(2)]

    def swap(x, r):
        return lax.ppermute(x, "shard", [(d, d ^ r) for d in range(count)])

    def gather_all(x):
        if direct:
            return [x] + [swap(x, r) for r in range(1, count)]
        return [lax.all_gather(x, "shard", axis=0, tiled=True)[order]]

    def gather_core(x):
        if direct:
            far = [x] + [swap(x, r) for r in range(4, count, 4)]
            return [b for block in far for b in (block, swap(block, 2))]
        every = lax.all_gather(x, "shard", axis=0, axis_index_groups=same_core, tiled=True)
        return [every[core_order]]

    def exchange(blocks):
        if direct:
            return blocks[:1] + [swap(b, r) for r, b in enumerate(blocks) if r]
        sent = lax.all_to_all(blocks[0][order], "shard", split_axis=0, concat_axis=0, tiled=True)
        return [sent[order]]

    me1 = me.reshape(1)
    heads = head_owner[:, 0]
    tail_owners = tail_owner[:, 0]
    table_t, rtab_t, weight_t = entity_table.T, relation_table.T, proj_weight.T
    numbers = gather_all(jnp.stack([heads, head_row, rel_ids, pos_index])[None])
    core_numbers = numbers[::2] if direct else [numbers[0][::2]]
    mate_numbers = numbers[1] if direct else numbers[0][1:2]
    own_numbers = numbers[0] if direct else numbers[0][:1]

    found, want = find_heads(me1, numbers, table_t, head_cap)
    fetched = exchange(found)
    tails, tails_t, slot_cand, slot_row = pack_tails(me1, tail_owners, tail_row, table_t, tail_cap)
    core_tails = gather_core(tails_t)
    mate_tails, mate_cand = swap(tails, 1), swap(slot_cand, 1)
    pos2 = pos_slots(me1, tail_owners, own_numbers, mate_numbers, tail_cap)

    codes = jnp.asarray(band_codes(ks))
    band, band_t = build_band(filters, codes)
    extra = BAND_OUT * (GROUPS - 1) + LANES - IMG * IMG - BAND_OUT
    ext = jnp.concatenate([chequer_perm[-BAND_OUT:], chequer_perm, chequer_perm[:extra]])[None]
    orow = heads[None, :]
    pre, img, qv, hvt, qvt = front(
        me1, fetched, orow, rel_ids[None, :], rtab_t, ext, band, weight_t, head_cap
    )

    own, other = score_part(qv, swap(qv, 1), pos2, core_tails, cand)
    outgoing, qgt, sums = back(
        me1, own, swap(other, 1), orow, ext, codes, img, band_t, weight_t, pre,
        [x.shape[0] for x in found], head_cap, ks * ks,
    )
    incoming = exchange(outgoing)
    core_sums = gather_core(sums)
    core_hvt, core_qvt, core_qgt = gather_core(hvt), gather_core(qvt), gather_core(qgt)

    own, other = tail_part(tails, mate_tails, slot_cand, mate_cand, core_numbers, core_qvt, cand)
    entity_grad = entity_sum(want, slot_row, own, swap(other, 1), incoming, rows).T

    cols = filts * IMG * IMG // count
    if direct and cols % (IMG * IMG) == 0:
        unit = cols // (IMG * IMG) * BAND_OUT
        mine, mate = (
            lax.dynamic_slice_in_dim(band, d * unit, unit, axis=0) for d in (me, me ^ 1)
        )
        own, other = proj_part(rtab_t, ext, mine, mate, core_numbers, core_hvt, core_qgt)
    else:
        own, other = (
            proj_columns(
                d * cols, cols, filters, chequer_perm, relation_table,
                jnp.concatenate(core_numbers), jnp.concatenate(core_hvt), jnp.concatenate(core_qgt),
            )
            for d in (me, me ^ 1)
        )
    proj_grad = (own + swap(other, 1)).T

    part, filt = rel_part(core_numbers, core_sums, width, rels, ks * ks)
    relation_grad = (part + swap(part, 1)).T
    filter_grad = (filt + swap(filt, 1))[: ks * ks, :filts].T.reshape(filts, ks, ks)
    return (entity_grad, relation_grad, filter_grad, proj_grad)


def solution(mesh):
    placed = (
        P("shard", None),
        P(),
        P(),
        P(),
        P(),
        P(("parts", "shard"), None),
        P(("parts", "shard")),
        P(("parts", "shard")),
        P(("parts", "shard")),
        P("parts", None),
        P("parts"),
    )
    return jax.shard_map(
        shards,
        mesh=mesh,
        in_specs=placed,
        out_specs=(
            P(("parts", "shard"), None),
            P("parts", None),
            P("parts", None, None),
            P(("parts", "shard"), None),
        ),
        check_vma=False,
    )
```

time: 583 us -> 264 us (0.45)
  blocking collectives: 179 us -> 0 us
  matrix products: 152 us -> 0 us
  local copies, waits for them, and re-layouts: 163 us -> 32.8 us
  waiting for transfers between devices: 9.45 us -> 81.7 us
  starting transfers between devices: 23.3 us -> 88.6 us
  Pallas kernels: 0 us -> 52.3 us
  other arithmetic: 33.6 us -> 5.47 us
  between operations: 14.7 us -> 1.32 us
    conv_general_dilated x3 -> x0, matrix products: 125 us -> none  [the longest x1 105 us: conv_backward(): lax.conv_general_dilated(feat_grad, flipped, (1, 1), ((kernel_size - 1, k...]
    all_gather x1 -> x0, blocking collectives: 98 us -> none  [shards(): part_rows = lax.all_gather(query_grad, 'shard', axis=0, tiled=True)]
    ppermute x0 -> x88, starting transfers between devices: none -> 88.6 us  [swap(): return lax.ppermute(x, 'shard', [(d, d ^ r) for d in range(count)])]
    ppermute x0 -> x88, waiting for transfers between devices: none -> 81.7 us  [swap(): return lax.ppermute(x, 'shard', [(d, d ^ r) for d in range(count)])]
    psum x1 -> x0, blocking collectives: 81.2 us -> none  [shards(): relation_grad, filter_grad = lax.psum((rel_part, filter_part), 'shard')]
    gather x8 -> x0, local copies, waits for them, and re-layouts: 70.3 us -> none  [the longest x1 46.1 us: shards(): tail_part[slot_cand]]
    pallas_call x0 -> x11, Pallas kernels: none -> 52.3 us  [the longest x1 15.9 us: back(): pl.pallas_call(functools.partial(back_kernel, cap, taps, len(sizes)), gri...]
    scatter x5 -> x0, local copies, waits for them, and re-layouts: 48.9 us -> none  [the longest x1 15.7 us: shards(): jnp.zeros((tail_cap,), jnp.int32).at[local_slot].set(tail_row, mode='drop')]
  transfers between devices with their start and end apart: 7 -> 88, of which waited for: 1 -> 35; matrix products, arithmetic and copies ran while one was open for 39% -> 1% of each run, Pallas kernels for 0% -> 20%
where the time goes in v2:
time: 264 us; the launch traced here: 262 us
  starting transfers between devices  88.6 us (34%)
  waiting for transfers between devices  81.7 us (31%)
  Pallas kernels  52.3 us (20%)
  local copies, waits for them, and re-layouts  32.8 us (12%)
  other arithmetic  5.47 us (2%)
    ppermute x88, starting transfers between devices, swap(): return lax.ppermute(x, 'shard', [(d, d ^ r) for d in range(count)])  88.6 us
    ppermute x88, waiting for transfers between devices, swap(): return lax.ppermute(x, 'shard', [(d, d ^ r) for d in range(count)])  81.7 us
    unnamed x192, local copies, waits for them, and re-layouts  31.9 us
    pallas_call x1, Pallas kernels, back(): pl.pallas_call(functools.partial(back_kernel, cap, taps, len(sizes)), gri...  15.9 us
    pallas_call x1, Pallas kernels, proj_part(): pl.pallas_call(functools.partial(proj_kernel, len(numbers)), out_shape=[h...  9.24 us
    pallas_call x1, Pallas kernels, front(): pl.pallas_call(functools.partial(front_kernel, cap, len(fetched)), grid=(...  7.17 us
  transfers between devices with their start and end apart: 88, of which 35 were waited for; matrix products, arithmetic and copies ran while one was open for 1% of the time, Pallas kernels for 20%

profile of v2, /device:TPU:0, one launch (start us, length us, event | category | flops | bytes accessed | tf_op | source)
XLA Modules:
  0.0 262.2 jit_solution(11605415175580136640)
XLA Ops:
  1.3 3.0 %collective-permute-start.1 = (s32[1,4,128]{2,1,0:T(4,128)S(1)}, s32[1,4,128]{2,1,0:T(4,128)S(1)}, u32[]{:S(2)}, u32[]{:S(2)}) collective-permute-start(s32[1,4,128]{2,1,0:T(4,128)S(1)} %add_bitcast_fusion.2.refs_0_.own_ref), channel_id=1, source_target_pairs={{0,2},{1,3},{2,0},{3,1},{4,6},{5,7},{6,4},{7,5},{8,10},{9,11},{10,... | collective-permute-start | bytes 6152 | tf_op jit(solution)/shard_map/ppermute | solution.py:663
  7.0 3.6 %pack_tails.1 = (bf16[512,200]{1,0:T(8,128)(2,1)S(1)}, bf16[1,200,512]{2,1,0:T(8,128)(2,1)}, s32[512,1]{1,0:T(8,128)S(1)}, s32[512,1]{1,0:T(8,128)S(1)}) custom-call(s32[1]{0:T(128)} %bitcast.me_ref, s32[32,128]{1,0:T(8,128)S(1)} %bitcast.24, s32[32,128]{1,0:T(8,128)S(1)} %bitcast.37, bf16[200,2048]{1,0:T(8,128)(2,1)S(1)} %bitcast.33), custom_call_target="tpu_custom_call" | custom-call | flops 1000000000 | bytes 2000000 | tf_op jit(solution)/shard_map/pack_tails/pallas_call | solution.py:155
  15.4 2.9 %collective-permute-start.46 = (bf16[1,200,512]{2,1,0:T(8,128)(2,1)}, bf16[1,200,512]{2,1,0:T(8,128)(2,1)}, u32[]{:S(2)}, u32[]{:S(2)}) collective-permute-start(bf16[1,200,512]{2,1,0:T(8,128)(2,1)} %get-tuple-element.83.refs_0_), channel_id=1, source_target_pairs={{0,12},{1,13},{2,14},{3,15},{4,8},{5,9},{6,10},{7,11},{8,4},{9,5},... | collective-permute-start | bytes 614408 | tf_op jit(solution)/shard_map/ppermute | solution.py:663
  21.6 7.3 %collective-permute-done.13.refs_14_.refs_7_ = s32[1,4,128]{2,1,0:T(4,128)S(1)} collective-permute-done((s32[1,4,128]{2,1,0:T(4,128)S(1)}, s32[1,4,128]{2,1,0:T(4,128)S(1)}, u32[]{:S(2)}, u32[]{:S(2)}) %collective-permute-start.13) | collective-permute-done | bytes 2080 | tf_op jit(solution)/shard_map/ppermute | solution.py:663
  28.9 8.2 %collective-permute-start.5 = (s32[1,4,128]{2,1,0:T(4,128)S(1)}, s32[1,4,128]{2,1,0:T(4,128)S(1)}, u32[]{:S(2)}, u32[]{:S(2)}) collective-permute-start(s32[1,4,128]{2,1,0:T(4,128)S(1)} %add_bitcast_fusion.2.refs_0_.own_ref), channel_id=1, source_target_pairs={{0,6},{1,7},{2,4},{3,5},{4,2},{5,3},{6,0},{7,1},{8,14},{9,15},{10,... | collective-permute-start | bytes 6152 | tf_op jit(solution)/shard_map/ppermute | solution.py:663
  38.7 2.8 %collective-permute-start.9 = (s32[1,4,128]{2,1,0:T(4,128)S(1)}, s32[1,4,128]{2,1,0:T(4,128)S(1)}, u32[]{:S(2)}, u32[]{:S(2)}) collective-permute-start(s32[1,4,128]{2,1,0:T(4,128)S(1)} %add_bitcast_fusion.2.refs_0_.own_ref), channel_id=1, source_target_pairs={{0,10},{1,11},{2,8},{3,9},{4,14},{5,15},{6,12},{7,13},{8,2},{9,3},... | collective-permute-start | bytes 6152 | tf_op jit(solution)/shard_map/ppermute | solution.py:663
  44.1 5.0 %collective-permute-start.12 = (s32[1,4,128]{2,1,0:T(4,128)S(1)}, s32[1,4,128]{2,1,0:T(4,128)S(1)}, u32[]{:S(2)}, u32[]{:S(2)}) collective-permute-start(s32[1,4,128]{2,1,0:T(4,128)S(1)} %add_bitcast_fusion.2.refs_0_.own_ref), channel_id=1, source_target_pairs={{0,13},{1,12},{2,15},{3,14},{4,9},{5,8},{6,11},{7,10},{8,5},{9,4},... | collective-permute-start | bytes 6152 | tf_op jit(solution)/shard_map/ppermute | solution.py:663
  52.0 2.8 %collective-permute-done.14.refs_15_ = s32[1,4,128]{2,1,0:T(4,128)S(1)} collective-permute-done((s32[1,4,128]{2,1,0:T(4,128)S(1)}, s32[1,4,128]{2,1,0:T(4,128)S(1)}, u32[]{:S(2)}, u32[]{:S(2)}) %collective-permute-start.14) | collective-permute-done | bytes 2080 | tf_op jit(solution)/shard_map/ppermute | solution.py:663
  58.7 3.0 %collective-permute-done.8.refs_9_ = s32[1,4,128]{2,1,0:T(4,128)S(1)} collective-permute-done((s32[1,4,128]{2,1,0:T(4,128)S(1)}, s32[1,4,128]{2,1,0:T(4,128)S(1)}, u32[]{:S(2)}, u32[]{:S(2)}) %collective-permute-start.8) | collective-permute-done | bytes 2080 | tf_op jit(solution)/shard_map/ppermute | solution.py:663
  67.0 3.0 %collective-permute-done.20.refs_4_ = bf16[1,16,200]{2,1,0:T(8,128)(2,1)S(1)} collective-permute-done((bf16[1,16,200]{2,1,0:T(8,128)(2,1)S(1)}, bf16[1,16,200]{2,1,0:T(8,128)(2,1)S(1)}, u32[]{:S(2)}, u32[]{:S(2)}) %collective-permute-start.20) | collective-permute-done | bytes 6432 | tf_op jit(solution)/shard_map/ppermute | solution.py:663
  70.9 3.7 %collective-permute-done.22.refs_6_ = bf16[1,16,200]{2,1,0:T(8,128)(2,1)S(1)} collective-permute-done((bf16[1,16,200]{2,1,0:T(8,128)(2,1)S(1)}, bf16[1,16,200]{2,1,0:T(8,128)(2,1)S(1)}, u32[]{:S(2)}, u32[]{:S(2)}) %collective-permute-start.22) | collective-permute-done | bytes 6432 | tf_op jit(solution)/shard_map/ppermute | solution.py:663
  75.3 3.8 %collective-permute-done.24.refs_8_ = bf16[1,16,200]{2,1,0:T(8,128)(2,1)S(1)} collective-permute-done((bf16[1,16,200]{2,1,0:T(8,128)(2,1)S(1)}, bf16[1,16,200]{2,1,0:T(8,128)(2,1)S(1)}, u32[]{:S(2)}, u32[]{:S(2)}) %collective-permute-start.24) | collective-permute-done | bytes 6432 | tf_op jit(solution)/shard_map/ppermute | solution.py:663
  80.7 3.8 %collective-permute-done.26.refs_10_ = bf16[1,16,200]{2,1,0:T(8,128)(2,1)S(1)} collective-permute-done((bf16[1,16,200]{2,1,0:T(8,128)(2,1)S(1)}, bf16[1,16,200]{2,1,0:T(8,128)(2,1)S(1)}, u32[]{:S(2)}, u32[]{:S(2)}) %collective-permute-start.26) | collective-permute-done | bytes 6432 | tf_op jit(solution)/shard_map/ppermute | solution.py:663
  86.5 3.5 %collective-permute-done.28.refs_12_ = bf16[1,16,200]{2,1,0:T(8,128)(2,1)S(1)} collective-permute-done((bf16[1,16,200]{2,1,0:T(8,128)(2,1)S(1)}, bf16[1,16,200]{2,1,0:T(8,128)(2,1)S(1)}, u32[]{:S(2)}, u32[]{:S(2)}) %collective-permute-start.28) | collective-permute-done | bytes 6432 | tf_op jit(solution)/shard_map/ppermute | solution.py:663
  92.9 2.8 %band.1 = (bf16[3840,256]{1,0:T(8,128)(2,1)S(1)}, bf16[256,3840]{1,0:T(8,128)(2,1)S(1)}) custom-call(s32[20,256]{1,0:T(8,128)S(1)} %copy-done.86, bf16[48,81]{1,0:T(8,128)(2,1)S(1)} %copy.17.filt_ref), custom_call_target="tpu_custom_call" | custom-call | flops 40000000 | bytes 4000000 | tf_op jit(solution)/shard_map/band/pallas_call | solution.py:94
  100.4 3.2 %copy-done.4 = bf16[19200,200]{0,1:T(8,128)(2,1)S(1)} copy-done((bf16[19200,200]{0,1:T(8,128)(2,1)S(1)}, bf16[19200,200]{0,1:T(8,128)(2,1)}, u32[]{:S(2)}) %copy-start.4) | copy-done | bytes 7680024
  103.6 7.2 %front.1 = (f32[19200,128]{1,0:T(8,128)S(1)}, bf16[256,640]{1,0:T(8,128)(2,1)S(1)}, bf16[128,200]{1,0:T(8,128)(2,1)S(1)}, bf16[1,200,128]{2,1,0:T(8,128)(2,1)S(1)}, bf16[1,200,128]{2,1,0:T(8,128)(2,1)S(1)}) custom-call(s32[1]{0:T(128)} %bitcast.me_ref, s32[1,128]{1,0:T(1,128)S(1)} %bitcast.29, s32[1,128]{1,0:T(1,128)S(1)} %bitcast.27, ...), custom_call_target="tpu_custom_call" | custom-call | flops 4000000000 | bytes 24000000 | tf_op jit(solution)/shard_map/front/pallas_call | solution.py:308
  112.8 4.3 %collective-permute-done.47.refs_7_ = bf16[1,200,512]{2,1,0:T(8,128)(2,1)S(1)} collective-permute-done((bf16[1,200,512]{2,1,0:T(8,128)(2,1)}, bf16[1,200,512]{2,1,0:T(8,128)(2,1)S(1)}, u32[]{:S(2)}, u32[]{:S(2)}) %collective-permute-start.47) | collective-permute-done | bytes 204832 | tf_op jit(solution)/shard_map/ppermute | solution.py:663
  117.1 2.9 %score.1 = (f32[128,200]{1,0:T(8,128)S(1)}, f32[128,200]{1,0:T(8,128)S(1)}) custom-call(s32[256,1]{1,0:T(8,128)S(1)} %pos_slots.1.pos_ref, bf16[128,200]{1,0:T(8,128)(2,1)S(1)} %get-tuple-element.82.mine_ref, bf16[128,200]{1,0:T(8,128)(2,1)S(1)} %collective-permute-done.40.mate_ref, bf16[1,200,512]{2,1,0:T(8,128)(2,1)} %get-tuple-element.83.refs_0_, ...), custom_call_target="tpu_custom_call" | custom-call | flops 1000000000 | bytes 2000000 | tf_op jit(solution)/shard_map/score/pallas_call | solution.py:365
  124.6 2.7 %collective-permute-done.76.refs_12_ = bf16[1,200,128]{2,1,0:T(8,128)(2,1)S(1)} collective-permute-done((bf16[1,200,128]{2,1,0:T(8,128)(2,1)S(1)}, bf16[1,200,128]{2,1,0:T(8,128)(2,1)S(1)}, u32[]{:S(2)}, u32[]{:S(2)}) %collective-permute-start.76) | collective-permute-done | bytes 51232 | tf_op jit(solution)/shard_map/ppermute | solution.py:663
  131.7 15.9 %back.1 = (bf16[1,16,200]{2,1,0:T(8,128)(2,1)S(1)}, bf16[1,16,200]{2,1,0:T(8,128)(2,1)S(1)}, bf16[1,16,200]{2,1,0:T(8,128)(2,1)S(1)}, bf16[1,16,200]{2,1,0:T(8,1...) custom-call(s32[1]{0:T(128)} %bitcast.me_ref, ...), custom_call_target="tpu_custom_call" | custom-call | flops 6000000000 | bytes 20000000 | tf_op jit(solution)/shard_map/back/pallas_call | solution.py:445
  190.3 9.2 %proj_grad.1 = (f32[200,1200]{1,0:T(8,128)S(1)}, f32[200,1200]{1,0:T(8,128)S(1)}) custom-call(bf16[200,1387]{1,0:T(8,128)(2,1)S(1)} %bitcast.36, s32[1,576]{1,0:T(1,128)S(1)} %broadcast_in_dim.8.ext_ref, bf16[240,256]{1,0:T(8,128)(2,1)S(1)} %get-tuple-element.113.band_ref, bf16[240,256]{1,0:T(8,128)(2,1)S(1)} %get-tuple-element.112.mate_ref, ...), custom_call_target="tpu_custom_call" | custom-call | flops 6000000000 | bytes 6000000 | tf_op jit(solution)/shard_map/proj_grad/pallas_call | solution.py:549
  203.8 2.8 %tail_grad.1 = (f32[200,512]{1,0:T(8,128)S(1)}, f32[200,512]{1,0:T(8,128)S(1)}) custom-call(bf16[512,200]{1,0:T(8,128)(2,1)S(1)} %get-tuple-element.60.tails_ref, bf16[512,200]{1,0:T(8,128)(2,1)S(1)} %collective-permute-done.15.mate_ref, s32[512,1]{1,0:T(8,128)S(1)} %copy-done.10, s32[512,1]{1,0:T(8,128)S(1)} %copy-done.12, ...), custom_call_target="tpu_custom_call" | custom-call | flops 2000000000 | bytes 3000000 | tf_op jit(solution)/shard_map/tail_grad/pallas_call | solution.py:504
  209.0 3.2 %collective-permute-done.68.refs_13_ = f32[1,288,128]{2,1,0:T(8,128)S(1)} collective-permute-done((f32[1,288,128]{2,1,0:T(8,128)S(1)}, f32[1,288,128]{2,1,0:T(8,128)S(1)}, u32[]{:S(2)}, u32[]{:S(2)}) %collective-permute-start.68) | collective-permute-done | bytes 147488 | tf_op jit(solution)/shard_map/ppermute | solution.py:663
  214.5 3.1 %rel_grad.1 = (f32[200,1387]{1,0:T(8,128)S(1)}, f32[88,128]{1,0:T(8,128)S(1)}) custom-call(s32[1,4,128]{2,1,0:T(4,128)S(1)} %add_bitcast_fusion.2.refs_0_.own_ref, s32[1,4,128]{2,1,0:T(4,128)S(1)} %collective-permute-done.1.refs_2_.refs_1_, s32[1,4,128]{2,1,0:T(4,128)S(1)} %copy-done.79, s32[1,4,128]{2,1,0:T(4,128)S(1)} %copy-done.81, ...), custom_call_target="tpu_custom_call" | custom-call | flops 2000000000 | bytes 3000000 | tf_op jit(solution)/shard_map/rel_grad/pallas_call | solution.py:602
  227.1 3.0 %collective-permute-done.54.refs_6_ = bf16[1,16,200]{2,1,0:T(8,128)(2,1)S(1)} collective-permute-done((bf16[1,16,200]{2,1,0:T(8,128)(2,1)S(1)}, bf16[1,16,200]{2,1,0:T(8,128)(2,1)S(1)}, u32[]{:S(2)}, u32[]{:S(2)}) %collective-permute-start.54) | collective-permute-done | bytes 6432 | tf_op jit(solution)/shard_map/ppermute | solution.py:663
  231.1 3.5 %collective-permute-done.56.refs_8_ = bf16[1,16,200]{2,1,0:T(8,128)(2,1)S(1)} collective-permute-done((bf16[1,16,200]{2,1,0:T(8,128)(2,1)S(1)}, bf16[1,16,200]{2,1,0:T(8,128)(2,1)S(1)}, u32[]{:S(2)}, u32[]{:S(2)}) %collective-permute-start.56) | collective-permute-done | bytes 6432 | tf_op jit(solution)/shard_map/ppermute | solution.py:663
  236.3 3.8 %collective-permute-done.58.refs_10_ = bf16[1,16,200]{2,1,0:T(8,128)(2,1)S(1)} collective-permute-done((bf16[1,16,200]{2,1,0:T(8,128)(2,1)S(1)}, bf16[1,16,200]{2,1,0:T(8,128)(2,1)S(1)}, u32[]{:S(2)}, u32[]{:S(2)}) %collective-permute-start.58) | collective-permute-done | bytes 6432 | tf_op jit(solution)/shard_map/ppermute | solution.py:663
  242.1 3.4 %collective-permute-done.60.refs_12_ = bf16[1,16,200]{2,1,0:T(8,128)(2,1)S(1)} collective-permute-done((bf16[1,16,200]{2,1,0:T(8,128)(2,1)S(1)}, bf16[1,16,200]{2,1,0:T(8,128)(2,1)S(1)}, u32[]{:S(2)}, u32[]{:S(2)}) %collective-permute-start.60) | collective-permute-done | bytes 6432 | tf_op jit(solution)/shard_map/ppermute | solution.py:663
  245.5 2.8 %collective-permute-start.62 = (bf16[1,16,200]{2,1,0:T(8,128)(2,1)S(1)}, bf16[1,16,200]{2,1,0:T(8,128)(2,1)S(1)}, u32[]{:S(2)}, u32[]{:S(2)}) collective-permute-start(bf16[1,16,200]{2,1,0:T(8,128)(2,1)S(1)} %copy-done.47), channel_id=1, source_target_pairs={{0,14},{1,15},{2,12},{3,13},{4,10},{5,11},{6,8},{7,9},{8,6},{9,7},... | collective-permute-start | bytes 19208 | tf_op jit(solution)/shard_map/ppermute | solution.py:663
  248.4 3.5 %collective-permute-done.62.refs_14_ = bf16[1,16,200]{2,1,0:T(8,128)(2,1)S(1)} collective-permute-done((bf16[1,16,200]{2,1,0:T(8,128)(2,1)S(1)}, bf16[1,16,200]{2,1,0:T(8,128)(2,1)S(1)}, u32[]{:S(2)}, u32[]{:S(2)}) %collective-permute-start.62) | collective-permute-done | bytes 6432 | tf_op jit(solution)/shard_map/ppermute | solution.py:663
  254.1 2.8 %entity_grad.1 = f32[200,2048]{1,0:T(8,128)} custom-call(s32[256,1]{1,0:T(8,128)S(1)} %copy-done.89, s32[512,1]{1,0:T(8,128)S(1)} %copy-done.91, f32[200,512]{1,0:T(8,128)S(1)} %get-tuple-element.80.own_ref, f32[200,512]{1,0:T(8,128)S(1)} %collective-permute-done.39.recv_ref, bf16[1,16,200]{2,1,0:T(8,128)(2,1)S(1)} %copy-done.93, ...), custom_call_target="tpu_custom_call" | custom-call | flops 1500000000 | bytes 4000000 | tf_op jit(solution)/shard_map/entity_grad/pallas_call | solution.py:625
  (360 shorter events, 124.5 us)
Async XLA Ops:
  1.3 17.0 %collective-permute-start.1 = (s32[1,4,128]{2,1,0:T(4,128)S(1)}, s32[1,4,128]{2,1,0:T(4,128)S(1)}, u32[]{:S(2)}, u32[]{:S(2)}) collective-permute-start(s32[1,4,128]{2,1,0:T(4,128)S(1)} %add_bitcast_fusion.2.refs_0_.own_ref), channel_id=1, source_target_pairs={{0,2},{1,3},{2,0},{3,1},{4,6},{5,7},{6,4},{7,5},{8,10},{9,11},{10,... | collective-permute-start | bytes 6152 | tf_op jit(solution)/shard_map/ppermute | solution.py:663
  11.2 85.6 %collective-permute-start.42 = (bf16[1,200,512]{2,1,0:T(8,128)(2,1)}, bf16[1,200,512]{2,1,0:T(8,128)(2,1)}, u32[]{:S(2)}, u32[]{:S(2)}) collective-permute-start(bf16[1,200,512]{2,1,0:T(8,128)(2,1)} %get-tuple-element.83.refs_0_), channel_id=1, source_target_pairs={{0,4},{1,5},{2,6},{3,7},{4,0},{5,1},{6,2},{7,3},{8,12},{9,13},{10,... | collective-permute-start | bytes 614408 | tf_op jit(solution)/shard_map/ppermute | solution.py:663
  12.8 8.8 %collective-permute-start.11 = (s32[1,4,128]{2,1,0:T(4,128)S(1)}, s32[1,4,128]{2,1,0:T(4,128)S(1)}, u32[]{:S(2)}, u32[]{:S(2)}) collective-permute-start(s32[1,4,128]{2,1,0:T(4,128)S(1)} %add_bitcast_fusion.2.refs_0_.own_ref), channel_id=1, source_target_pairs={{0,12},{1,13},{2,14},{3,15},{4,8},{5,9},{6,10},{7,11},{8,4},{9,5},... | collective-permute-start | bytes 6152 | tf_op jit(solution)/shard_map/ppermute | solution.py:663
  15.3 83.1 %collective-permute-start.44 = (bf16[1,200,512]{2,1,0:T(8,128)(2,1)}, bf16[1,200,512]{2,1,0:T(8,128)(2,1)}, u32[]{:S(2)}, u32[]{:S(2)}) collective-permute-start(bf16[1,200,512]{2,1,0:T(8,128)(2,1)} %get-tuple-element.83.refs_0_), channel_id=1, source_target_pairs={{0,8},{1,9},{2,10},{3,11},{4,12},{5,13},{6,14},{7,15},{8,0},{9,1},... | collective-permute-start | bytes 614408 | tf_op jit(solution)/shard_map/ppermute | solution.py:663
  15.4 83.5 %collective-permute-start.46 = (bf16[1,200,512]{2,1,0:T(8,128)(2,1)}, bf16[1,200,512]{2,1,0:T(8,128)(2,1)}, u32[]{:S(2)}, u32[]{:S(2)}) collective-permute-start(bf16[1,200,512]{2,1,0:T(8,128)(2,1)} %get-tuple-element.83.refs_0_), channel_id=1, source_target_pairs={{0,12},{1,13},{2,14},{3,15},{4,8},{5,9},{6,10},{7,11},{8,4},{9,5},... | collective-permute-start | bytes 614408 | tf_op jit(solution)/shard_map/ppermute | solution.py:663
  18.3 10.6 %collective-permute-start.13 = (s32[1,4,128]{2,1,0:T(4,128)S(1)}, s32[1,4,128]{2,1,0:T(4,128)S(1)}, u32[]{:S(2)}, u32[]{:S(2)}) collective-permute-start(s32[1,4,128]{2,1,0:T(4,128)S(1)} %add_bitcast_fusion.2.refs_0_.own_ref), channel_id=1, source_target_pairs={{0,14},{1,15},{2,12},{3,13},{4,10},{5,11},{6,8},{7,9},{8,6},{9,7},... | collective-permute-start | bytes 6152 | tf_op jit(solution)/shard_map/ppermute | solution.py:663
  21.6 15.5 %collective-permute-start.3 = (s32[1,4,128]{2,1,0:T(4,128)S(1)}, s32[1,4,128]{2,1,0:T(4,128)S(1)}, u32[]{:S(2)}, u32[]{:S(2)}) collective-permute-start(s32[1,4,128]{2,1,0:T(4,128)S(1)} %add_bitcast_fusion.2.refs_0_.own_ref), channel_id=1, source_target_pairs={{0,4},{1,5},{2,6},{3,7},{4,0},{5,1},{6,2},{7,3},{8,12},{9,13},{10,... | collective-permute-start | bytes 6152 | tf_op jit(solution)/shard_map/ppermute | solution.py:663
  28.9 9.8 %collective-permute-start.5 = (s32[1,4,128]{2,1,0:T(4,128)S(1)}, s32[1,4,128]{2,1,0:T(4,128)S(1)}, u32[]{:S(2)}, u32[]{:S(2)}) collective-permute-start(s32[1,4,128]{2,1,0:T(4,128)S(1)} %add_bitcast_fusion.2.refs_0_.own_ref), channel_id=1, source_target_pairs={{0,6},{1,7},{2,4},{3,5},{4,2},{5,3},{6,0},{7,1},{8,14},{9,15},{10,... | collective-permute-start | bytes 6152 | tf_op jit(solution)/shard_map/ppermute | solution.py:663
  91.5 8.9 %collective-permute-start.31 = (bf16[1,16,200]{2,1,0:T(8,128)(2,1)S(1)}, bf16[1,16,200]{2,1,0:T(8,128)(2,1)S(1)}, u32[]{:S(2)}, u32[]{:S(2)}) collective-permute-start(bf16[1,16,200]{2,1,0:T(8,128)(2,1)S(1)} %get-tuple-element.78), channel_id=1, source_target_pairs={{0,15},{1,14},{2,13},{3,12},{4,11},{5,10},{6,9},{7,8},{8,7},{9,6},... | collective-permute-start | bytes 19208 | tf_op jit(solution)/shard_map/ppermute | solution.py:663
  96.3 16.4 %collective-permute-start.41 = (bf16[1,200,512]{2,1,0:T(8,128)(2,1)}, bf16[1,200,512]{2,1,0:T(8,128)(2,1)S(1)}, u32[]{:S(2)}, u32[]{:S(2)}) collective-permute-start(bf16[1,200,512]{2,1,0:T(8,128)(2,1)} %get-tuple-element.83.refs_0_), channel_id=1, source_target_pairs={{0,2},{1,3},{2,0},{3,1},{4,6},{5,7},{6,4},{7,5},{8,10},{9,11},{10,... | collective-permute-start | bytes 614408 | tf_op jit(solution)/shard_map/ppermute | solution.py:663
  96.9 15.9 %collective-permute-start.43 = (bf16[1,200,512]{2,1,0:T(8,128)(2,1)}, bf16[1,200,512]{2,1,0:T(8,128)(2,1)S(1)}, u32[]{:S(2)}, u32[]{:S(2)}) collective-permute-start(bf16[1,200,512]{2,1,0:T(8,128)(2,1)} %collective-permute-done.42.refs_2_), channel_id=1, source_target_pairs={{0,2},{1,3},{2,0},{3,1},{4,6},{5,7},{6,4},{7,5},{8,10},{9,11},{10,... | collective-permute-start | bytes 614408 | tf_op jit(solution)/shard_map/ppermute | solution.py:663
  98.4 14.4 %collective-permute-start.45 = (bf16[1,200,512]{2,1,0:T(8,128)(2,1)}, bf16[1,200,512]{2,1,0:T(8,128)(2,1)S(1)}, u32[]{:S(2)}, u32[]{:S(2)}) collective-permute-start(bf16[1,200,512]{2,1,0:T(8,128)(2,1)} %collective-permute-done.44.refs_4_), channel_id=1, source_target_pairs={{0,2},{1,3},{2,0},{3,1},{4,6},{5,7},{6,4},{7,5},{8,10},{9,11},{10,... | collective-permute-start | bytes 614408 | tf_op jit(solution)/shard_map/ppermute | solution.py:663
  98.9 18.2 %collective-permute-start.47 = (bf16[1,200,512]{2,1,0:T(8,128)(2,1)}, bf16[1,200,512]{2,1,0:T(8,128)(2,1)S(1)}, u32[]{:S(2)}, u32[]{:S(2)}) collective-permute-start(bf16[1,200,512]{2,1,0:T(8,128)(2,1)} %collective-permute-done.46.refs_6_), channel_id=1, source_target_pairs={{0,2},{1,3},{2,0},{3,1},{4,6},{5,7},{6,4},{7,5},{8,10},{9,11},{10,... | collective-permute-start | bytes 614408 | tf_op jit(solution)/shard_map/ppermute | solution.py:663
  112.7 10.0 %collective-permute-start.74 = (bf16[1,200,128]{2,1,0:T(8,128)(2,1)S(1)}, bf16[1,200,128]{2,1,0:T(8,128)(2,1)S(1)}, u32[]{:S(2)}, u32[]{:S(2)}) collective-permute-start(bf16[1,200,128]{2,1,0:T(8,128)(2,1)S(1)} %get-tuple-element.108.refs_8_), channel_id=1, source_target_pairs={{0,4},{1,5},{2,6},{3,7},{4,0},{5,1},{6,2},{7,3},{8,12},{9,13},{10,... | collective-permute-start | bytes 153608 | tf_op jit(solution)/shard_map/ppermute | solution.py:663
  120.0 11.2 %collective-permute-start.48 = (f32[128,200]{1,0:T(8,128)S(1)}, f32[128,200]{1,0:T(8,128)S(1)}, u32[]{:S(2)}, u32[]{:S(2)}) collective-permute-start(f32[128,200]{1,0:T(8,128)S(1)} %get-tuple-element.85), channel_id=1, source_target_pairs={{0,1},{1,0},{2,3},{3,2},{4,5},{5,4},{6,7},{7,6},{8,9},{9,8},{10,11... | collective-permute-start | bytes 307208 | tf_op jit(solution)/shard_map/ppermute | solution.py:663
  127.3 29.8 %collective-permute-start.35 = (bf16[1,200,128]{2,1,0:T(8,128)(2,1)S(1)}, bf16[1,200,128]{2,1,0:T(8,128)(2,1)S(1)}, u32[]{:S(2)}, u32[]{:S(2)}) collective-permute-start(bf16[1,200,128]{2,1,0:T(8,128)(2,1)S(1)} %get-tuple-element.79.refs_8_), channel_id=1, source_target_pairs={{0,8},{1,9},{2,10},{3,11},{4,12},{5,13},{6,14},{7,15},{8,0},{9,1},... | collective-permute-start | bytes 153608 | tf_op jit(solution)/shard_map/ppermute | solution.py:663
  127.3 31.5 %collective-permute-start.37 = (bf16[1,200,128]{2,1,0:T(8,128)(2,1)S(1)}, bf16[1,200,128]{2,1,0:T(8,128)(2,1)}, u32[]{:S(2)}, u32[]{:S(2)}) collective-permute-start(bf16[1,200,128]{2,1,0:T(8,128)(2,1)S(1)} %get-tuple-element.79.refs_8_), channel_id=1, source_target_pairs={{0,12},{1,13},{2,14},{3,15},{4,8},{5,9},{6,10},{7,11},{8,4},{9,5},... | collective-permute-start | bytes 153608 | tf_op jit(solution)/shard_map/ppermute | solution.py:663
  129.2 30.0 %collective-permute-start.32 = (bf16[1,200,128]{2,1,0:T(8,128)(2,1)S(1)}, bf16[1,200,128]{2,1,0:T(8,128)(2,1)S(1)}, u32[]{:S(2)}, u32[]{:S(2)}) collective-permute-start(bf16[1,200,128]{2,1,0:T(8,128)(2,1)S(1)} %get-tuple-element.79.refs_8_), channel_id=1, source_target_pairs={{0,2},{1,3},{2,0},{3,1},{4,6},{5,7},{6,4},{7,5},{8,10},{9,11},{10,... | collective-permute-start | bytes 153608 | tf_op jit(solution)/shard_map/ppermute | solution.py:663
  129.6 31.8 %collective-permute-start.75 = (bf16[1,200,128]{2,1,0:T(8,128)(2,1)S(1)}, bf16[1,200,128]{2,1,0:T(8,128)(2,1)S(1)}, u32[]{:S(2)}, u32[]{:S(2)}) collective-permute-start(bf16[1,200,128]{2,1,0:T(8,128)(2,1)S(1)} %collective-permute-done.74.refs_10_), channel_id=1, source_target_pairs={{0,2},{1,3},{2,0},{3,1},{4,6},{5,7},{6,4},{7,5},{8,10},{9,11},{10,... | collective-permute-start | bytes 153608 | tf_op jit(solution)/shard_map/ppermute | solution.py:663
  131.2 31.2 %collective-permute-start.77 = (bf16[1,200,128]{2,1,0:T(8,128)(2,1)S(1)}, bf16[1,200,128]{2,1,0:T(8,128)(2,1)S(1)}, u32[]{:S(2)}, u32[]{:S(2)}) collective-permute-start(bf16[1,200,128]{2,1,0:T(8,128)(2,1)S(1)} %collective-permute-done.76.refs_12_), channel_id=1, source_target_pairs={{0,2},{1,3},{2,0},{3,1},{4,6},{5,7},{6,4},{7,5},{8,10},{9,11},{10,... | collective-permute-start | bytes 153608 | tf_op jit(solution)/shard_map/ppermute | solution.py:663
  161.4 7.7 %collective-permute-start.83 = (bf16[1,200,128]{2,1,0:T(8,128)(2,1)S(1)}, bf16[1,200,128]{2,1,0:T(8,128)(2,1)S(1)}, u32[]{:S(2)}, u32[]{:S(2)}) collective-permute-start(bf16[1,200,128]{2,1,0:T(8,128)(2,1)S(1)} %get-tuple-element.109.refs_16_), channel_id=1, source_target_pairs={{0,8},{1,9},{2,10},{3,11},{4,12},{5,13},{6,14},{7,15},{8,0},{9,1},... | collective-permute-start | bytes 153608 | tf_op jit(solution)/shard_map/ppermute | solution.py:663
  171.2 29.9 %collective-permute-start.15 = (bf16[512,200]{1,0:T(8,128)(2,1)S(1)}, bf16[512,200]{1,0:T(8,128)(2,1)S(1)}, u32[]{:S(2)}, u32[]{:S(2)}) collective-permute-start(bf16[512,200]{1,0:T(8,128)(2,1)S(1)} %get-tuple-element.60.tails_ref), channel_id=1, source_target_pairs={{0,1},{1,0},{2,3},{3,2},{4,5},{5,4},{6,7},{7,6},{8,9},{9,8},{10,11... | collective-permute-start | bytes 614408 | tf_op jit(solution)/shard_map/ppermute | solution.py:663
  171.3 28.3 %collective-permute-start.38 = (bf16[1,200,128]{2,1,0:T(8,128)(2,1)}, bf16[1,200,128]{2,1,0:T(8,128)(2,1)S(1)}, u32[]{:S(2)}, u32[]{:S(2)}) collective-permute-start(bf16[1,200,128]{2,1,0:T(8,128)(2,1)} %collective-permute-done.37.refs_14_), channel_id=1, source_target_pairs={{0,2},{1,3},{2,0},{3,1},{4,6},{5,7},{6,4},{7,5},{8,10},{9,11},{10,... | collective-permute-start | bytes 153608 | tf_op jit(solution)/shard_map/ppermute | solution.py:663
  171.8 29.3 %collective-permute-start.65 = (f32[1,288,128]{2,1,0:T(8,128)}, f32[1,288,128]{2,1,0:T(8,128)S(1)}, u32[]{:S(2)}, u32[]{:S(2)}) collective-permute-start(f32[1,288,128]{2,1,0:T(8,128)} %get-tuple-element.105.refs_8_), channel_id=1, source_target_pairs={{0,4},{1,5},{2,6},{3,7},{4,0},{5,1},{6,2},{7,3},{8,12},{9,13},{10,... | collective-permute-start | bytes 442376 | tf_op jit(solution)/shard_map/ppermute | solution.py:663
  173.2 28.5 %collective-permute-start.67 = (f32[1,288,128]{2,1,0:T(8,128)}, f32[1,288,128]{2,1,0:T(8,128)S(1)}, u32[]{:S(2)}, u32[]{:S(2)}) collective-permute-start(f32[1,288,128]{2,1,0:T(8,128)} %get-tuple-element.105.refs_8_), channel_id=1, source_target_pairs={{0,8},{1,9},{2,10},{3,11},{4,12},{5,13},{6,14},{7,15},{8,0},{9,1},... | collective-permute-start | bytes 442376 | tf_op jit(solution)/shard_map/ppermute | solution.py:663
  174.3 28.9 %collective-permute-start.69 = (f32[1,288,128]{2,1,0:T(8,128)}, f32[1,288,128]{2,1,0:T(8,128)S(1)}, u32[]{:S(2)}, u32[]{:S(2)}) collective-permute-start(f32[1,288,128]{2,1,0:T(8,128)} %get-tuple-element.105.refs_8_), channel_id=1, source_target_pairs={{0,12},{1,13},{2,14},{3,15},{4,8},{5,9},{6,10},{7,11},{8,4},{9,5},... | collective-permute-start | bytes 442376 | tf_op jit(solution)/shard_map/ppermute | solution.py:663
  201.1 56.5 %collective-permute-start.87 = (f32[200,1200]{1,0:T(8,128)S(1)}, f32[200,1200]{1,0:T(8,128)}, u32[]{:S(2)}, u32[]{:S(2)}) collective-permute-start(f32[200,1200]{1,0:T(8,128)S(1)} %get-tuple-element.111), channel_id=1, source_target_pairs={{0,1},{1,0},{2,3},{3,2},{4,5},{5,4},{6,7},{7,6},{8,9},{9,8},{10,11... | collective-permute-start | bytes 2880008 | tf_op jit(solution)/shard_map/ppermute | solution.py:663
  201.1 7.9 %collective-permute-start.66 = (f32[1,288,128]{2,1,0:T(8,128)S(1)}, f32[1,288,128]{2,1,0:T(8,128)S(1)}, u32[]{:S(2)}, u32[]{:S(2)}) collective-permute-start(f32[1,288,128]{2,1,0:T(8,128)S(1)} %collective-permute-done.65.refs_10_), channel_id=1, source_target_pairs={{0,2},{1,3},{2,0},{3,1},{4,6},{5,7},{6,4},{7,5},{8,10},{9,11},{10,... | collective-permute-start | bytes 442376 | tf_op jit(solution)/shard_map/ppermute | solution.py:663
  201.8 10.4 %collective-permute-start.68 = (f32[1,288,128]{2,1,0:T(8,128)S(1)}, f32[1,288,128]{2,1,0:T(8,128)S(1)}, u32[]{:S(2)}, u32[]{:S(2)}) collective-permute-start(f32[1,288,128]{2,1,0:T(8,128)S(1)} %collective-permute-done.67.refs_12_), channel_id=1, source_target_pairs={{0,2},{1,3},{2,0},{3,1},{4,6},{5,7},{6,4},{7,5},{8,10},{9,11},{10,... | collective-permute-start | bytes 442376 | tf_op jit(solution)/shard_map/ppermute | solution.py:663
  203.2 11.3 %collective-permute-start.70 = (f32[1,288,128]{2,1,0:T(8,128)S(1)}, f32[1,288,128]{2,1,0:T(8,128)S(1)}, u32[]{:S(2)}, u32[]{:S(2)}) collective-permute-start(f32[1,288,128]{2,1,0:T(8,128)S(1)} %collective-permute-done.69.refs_14_), channel_id=1, source_target_pairs={{0,2},{1,3},{2,0},{3,1},{4,6},{5,7},{6,4},{7,5},{8,10},{9,11},{10,... | collective-permute-start | bytes 442376 | tf_op jit(solution)/shard_map/ppermute | solution.py:663
  206.8 47.3 %collective-permute-start.39 = (f32[200,512]{1,0:T(8,128)S(1)}, f32[200,512]{1,0:T(8,128)S(1)}, u32[]{:S(2)}, u32[]{:S(2)}) collective-permute-start(f32[200,512]{1,0:T(8,128)S(1)} %get-tuple-element.81), channel_id=1, source_target_pairs={{0,1},{1,0},{2,3},{3,2},{4,5},{5,4},{6,7},{7,6},{8,9},{9,8},{10,11... | collective-permute-start | bytes 1228808 | tf_op jit(solution)/shard_map/ppermute | solution.py:663
  217.6 42.3 %collective-permute-start.71 = (f32[200,1387]{1,0:T(8,128)S(1)}, f32[200,1387]{1,0:T(8,128)}, u32[]{:S(2)}, u32[]{:S(2)}) collective-permute-start(f32[200,1387]{1,0:T(8,128)S(1)} %get-tuple-element.106), channel_id=1, source_target_pairs={{0,1},{1,0},{2,3},{3,2},{4,5},{5,4},{6,7},{7,6},{8,9},{9,8},{10,11... | collective-permute-start | bytes 3328808 | tf_op jit(solution)/shard_map/ppermute | solution.py:663
  (153 other events, 2291.1 us)

commit v3 on v2

v3 whole, which is shorter than its diff:
```python
import functools
import math

import jax
import jax.numpy as jnp
import numpy as np
from jax import lax
from jax.experimental import pallas as pl
from jax.experimental.pallas import tpu as pltpu
from jax.sharding import PartitionSpec as P

IMG = 20
BAND = 4
GROUPS = IMG // BAND
BAND_OUT = BAND * IMG
LANES = 256

loss_weight = 0.015625
smooth = 0.1

f32 = jnp.float32
bf16 = jnp.bfloat16
i32 = jnp.int32

NN = (((1,), (0,)), ((), ()))
NT = (((1,), (1,)), ((), ()))
TN = (((0,), (0,)), ((), ()))


def mm(a, b, dims=NN):
    return lax.dot_general(a, b, dims, preferred_element_type=f32)


def iota(shape, axis):
    return lax.broadcasted_iota(i32, shape, axis)


def onehot(mask):
    return jnp.where(mask, 1.0, 0.0).astype(bf16)


def split(value):
    high = value.astype(bf16)
    return high, (value - high.astype(f32)).astype(bf16)


def sigmoid(v):
    return 0.5 * jnp.tanh(0.5 * v) + 0.5


def params(*semantics, mib=40):
    return pltpu.CompilerParams(
        dimension_semantics=semantics or None, vmem_limit_bytes=mib << 20
    )


def cost(flops, nbytes, trans=0):
    return pl.CostEstimate(flops=int(flops), bytes_accessed=int(nbytes), transcendentals=int(trans))


def whole(shape):
    return pl.BlockSpec(shape, lambda *_: (0,) * len(shape))


SMEM = pl.BlockSpec(memory_space=pltpu.SMEM)


def band_codes(ks):
    codes = np.full((IMG, LANES), -1, np.int32)
    for j in range(IMG):
        for r in range(ks):
            for x in range(IMG):
                b = (x - j + ks // 2) % IMG
                if b < ks:
                    codes[j, r * IMG + x] = r * ks + b
    return codes


def band_kernel(codes_ref, filt_ref, out_ref, out_t_ref, scr):
    count, taps = filt_ref.shape
    filt = filt_ref[...]
    for j in range(IMG):
        pick = onehot(iota((taps, LANES), 0) == codes_ref[j : j + 1, :])
        row = mm(filt, pick)
        for di in range(BAND):
            scr[:, di * IMG + j, :] = row if di == 0 else pltpu.roll(row, di * IMG, 1)
    full = scr[...].reshape(count * BAND_OUT, LANES)
    out_ref[...] = full.astype(bf16)
    out_t_ref[...] = full.T.astype(bf16)


def build_band(filters, codes):
    count, ks, _ = filters.shape
    return pl.pallas_call(
        band_kernel,
        out_shape=[
            jax.ShapeDtypeStruct((count * BAND_OUT, LANES), bf16),
            jax.ShapeDtypeStruct((LANES, count * BAND_OUT), bf16),
        ],
        scratch_shapes=[pltpu.VMEM((count, BAND_OUT, LANES), f32)],
        compiler_params=params(mib=24),
        cost_estimate=cost(4e7, 4e6),
        name="band",
    )(codes, filters.reshape(count, ks * ks))


VMEM = pl.BlockSpec(memory_space=pltpu.VMEM)


def pairs(count):
    step = 2 if count % 2 == 0 else 1
    return [range(i, i + step) for i in range(0, count, step)]


def beside(blocks):
    return jnp.concatenate(list(blocks), axis=1)


def pack_kernel(shift, me_ref, owner_ref, row_ref, table_ref, tails_ref, tails_t_ref, cand_ref, srow_ref):
    cap = tails_ref.shape[0]
    lines = owner_ref.shape[0]
    mine = owner_ref[...] == me_ref[0]
    mine_b = onehot(mine)
    before = onehot(iota((128, 128), 0) < iota((128, 128), 1))
    rank = mm(mine_b, before)
    totals = mm(mine_b, jnp.ones((128, 128), bf16))
    upper = onehot(iota((lines, lines), 1) < iota((lines, lines), 0))
    offset = mm(upper, totals.astype(bf16))
    key = jnp.where(mine, (rank + offset).astype(i32), -1)
    code = row_ref[...] * (1 << shift) + iota((lines, 128), 0) * 128 + iota((lines, 128), 1) + 1
    code = code.astype(f32)
    slots = iota((cap, 128), 0)
    total = jnp.zeros((cap, 128), f32)
    for r in range(lines):
        total = total + jnp.where(slots == key[r : r + 1, :], code[r : r + 1, :], 0.0)
    found = jnp.sum(total, axis=1, keepdims=True).astype(i32) - 1
    live = found >= 0
    srow = jnp.where(live, lax.shift_right_arithmetic(found, shift), -1)
    cand_ref[...] = jnp.where(live, found & ((1 << shift) - 1), -1)
    srow_ref[...] = srow
    pick = onehot(iota((cap, table_ref.shape[1]), 1) == srow)
    tails_ref[...] = mm(pick, table_ref[...], NT).astype(bf16)
    tails_t_ref[0] = mm(table_ref[...], pick, NT).astype(bf16)


def pack_tails(me, tail_owners, tail_row, table_t, cap):
    cand = tail_row.shape[0]
    shift = int(math.log2(cand))
    width, rows = table_t.shape
    assert 1 << shift == cand and cand * rows < 1 << 24 and cand % 128 == 0
    return pl.pallas_call(
        functools.partial(pack_kernel, shift),
        in_specs=[SMEM] + [VMEM] * 3,
        out_shape=[
            jax.ShapeDtypeStruct((cap, width), bf16),
            jax.ShapeDtypeStruct((1, width, cap), bf16),
            jax.ShapeDtypeStruct((cap, 1), i32),
            jax.ShapeDtypeStruct((cap, 1), i32),
        ],
        compiler_params=params(mib=16),
        cost_estimate=cost(1e9, 2e6),
        name="pack_tails",
    )(me, tail_owners.reshape(-1, 128), tail_row.reshape(-1, 128), table_t)


def found_kernel(cap, me_ref, table_ref, numbers_ref, found_ref, want_ref, scr):
    count, _, queries = numbers_ref.shape
    owners = jnp.concatenate([numbers_ref[d, 0:1, :] for d in range(count)], axis=0)
    mine = owners == me_ref[0]
    before = onehot(iota((queries, queries), 0) < iota((queries, queries), 1))
    rank = mm(onehot(mine), before)
    key = jnp.where(mine, rank.astype(i32), -1)
    slots = iota((cap, queries), 0)
    for d in range(count):
        code = (numbers_ref[d, 1:2, :] + 1).astype(f32)
        picked = jnp.where(slots == key[d : d + 1, :], code, 0.0)
        scr[d * cap : (d + 1) * cap, :] = jnp.sum(picked, axis=1, keepdims=True)
    want = scr[...].astype(i32) - 1
    want_ref[...] = want
    pick = onehot(iota((count * cap, table_ref.shape[1]), 1) == want)
    found = mm(pick, table_ref[...], NT).astype(bf16)
    for d in range(count):
        found_ref[d] = found[d * cap : (d + 1) * cap, :]


def find_heads(me, numbers, table_t, cap):
    width = table_t.shape[0]
    count = numbers.shape[0]
    return pl.pallas_call(
        functools.partial(found_kernel, cap),
        in_specs=[SMEM] + [VMEM] * 2,
        out_shape=[
            jax.ShapeDtypeStruct((count, cap, width), bf16),
            jax.ShapeDtypeStruct((count * cap, 1), i32),
        ],
        scratch_shapes=[pltpu.VMEM((count * cap, 1), f32)],
        compiler_params=params(mib=16),
        cost_estimate=cost(3e8, 2e6),
        name="find_heads",
    )(me, table_t, numbers)


def pos_kernel(cap, owner_ref, pos_ref, out_ref):
    cand = owner_ref.shape[1]
    queries = pos_ref.shape[1]
    eye = iota((queries, queries), 0) == iota((queries, queries), 1)
    step = min(512, cand)
    row = pos_ref[...].astype(f32)
    pos = jnp.sum(jnp.where(eye, row, 0.0), axis=1, keepdims=True).astype(i32)
    owner = jnp.zeros((queries, step), f32)
    for c in range(0, cand, step):
        here = iota((queries, step), 1) + c
        value = owner_ref[:, c : c + step].astype(f32)
        owner = owner + jnp.where(here == pos, value, 0.0)
    owner = jnp.sum(owner, axis=1, keepdims=True).astype(i32)
    ahead = jnp.zeros((queries, step), f32)
    for c in range(0, cand, step):
        here = iota((queries, step), 1) + c
        same = (owner_ref[:, c : c + step] == owner) & (here < pos)
        ahead = ahead + jnp.where(same, 1.0, 0.0)
    ahead = jnp.sum(ahead, axis=1, keepdims=True).astype(i32)
    out_ref[...] = owner * cap + ahead


def pos_slots(tail_owners, pos_index, cap):
    queries = pos_index.shape[0]
    return pl.pallas_call(
        functools.partial(pos_kernel, cap),
        out_shape=jax.ShapeDtypeStruct((queries, 1), i32),
        compiler_params=params(mib=8),
        cost_estimate=cost(1e7, 1e5),
        name="pos_slots",
    )(tail_owners.reshape(1, -1), pos_index.reshape(1, -1))


def slot_picks(cap, slots, orow):
    count = slots // cap
    queries = orow.shape[1]
    member = iota((count, queries), 0) == orow
    before = onehot(iota((queries, queries), 0) < iota((queries, queries), 1))
    rank = mm(onehot(member), before)
    rank = jnp.sum(jnp.where(member, rank, 0.0), axis=0, keepdims=True).astype(i32)
    return onehot(iota((slots, queries), 0) == orow * cap + rank)


def front_kernel(
    cap, fetched_ref, orow_ref, rel_ref, rtab_ref, ext_ref, band_ref, w_ref,
    pre_ref, img_ref, qv_ref, vecs_ref, feats, acc, ext,
):
    s = pl.program_id(0)
    width, queries = acc.shape

    @pl.when(s == 0)
    def _():
        rows = jnp.concatenate([fetched_ref[d] for d in range(fetched_ref.shape[0])], axis=0)
        pick = slot_picks(cap, rows.shape[0], orow_ref[...])
        hvt = mm(rows, pick, TN).astype(bf16)
        for d in range(vecs_ref.shape[0]):
            vecs_ref[d, 0] = hvt
        rels = rtab_ref.shape[1]
        rvt = mm(rtab_ref[...], onehot(iota((rels, queries), 0) == rel_ref[...])).astype(bf16)
        entry = iota((width, ext_ref.shape[1]), 0)
        image = mm(onehot(entry == ext_ref[...]), hvt, TN)
        image = image + mm(onehot(entry + width == ext_ref[...]), rvt, TN)
        ext[...] = image.astype(bf16)
        for g in range(GROUPS):
            img_ref[:, g * queries : (g + 1) * queries] = ext[g * BAND_OUT : g * BAND_OUT + LANES, :]
        acc[...] = jnp.zeros_like(acc)

    units = band_ref.shape[0] // BAND_OUT
    flat = GROUPS * BAND_OUT
    pre = mm(band_ref[...], img_ref[...])
    act = (pre * sigmoid(pre)).astype(bf16)
    for f in range(units):
        for g in range(GROUPS):
            rows = slice(f * flat + g * BAND_OUT, f * flat + (g + 1) * BAND_OUT)
            part = slice(f * BAND_OUT, (f + 1) * BAND_OUT)
            lanes = slice(g * queries, (g + 1) * queries)
            pre_ref[rows, :] = pre[part, lanes]
            feats[rows, :] = act[part, lanes]
    acc[...] += mm(w_ref[...], feats[...])

    @pl.when(s == pl.num_programs(0) - 1)
    def _():
        query = acc[...]
        qv_ref[...] = query.T.astype(bf16)
        qvt = query.astype(bf16)
        for d in range(vecs_ref.shape[0]):
            vecs_ref[d, 1] = qvt


def filter_block(filts):
    return math.gcd(filts, 8)


def front(fetched, orow, rel_row, rtab_t, ext, band, weight_t, cap, copies):
    queries = orow.shape[1]
    width, flat = weight_t.shape
    filts = band.shape[0] // BAND_OUT
    units = filter_block(filts)
    cols = flat // filts * units
    return pl.pallas_call(
        functools.partial(front_kernel, cap),
        grid=(filts // units,),
        in_specs=[
            whole(fetched.shape),
            whole(orow.shape),
            whole(rel_row.shape),
            whole(rtab_t.shape),
            whole(ext.shape),
            pl.BlockSpec((units * BAND_OUT, LANES), lambda s: (s, 0)),
            pl.BlockSpec((width, cols), lambda s: (0, s)),
        ],
        out_specs=[
            pl.BlockSpec((cols, queries), lambda s: (s, 0)),
            whole((LANES, GROUPS * queries)),
            whole((queries, width)),
            whole((copies, 2, width, queries)),
        ],
        out_shape=[
            jax.ShapeDtypeStruct((flat, queries), f32),
            jax.ShapeDtypeStruct((LANES, GROUPS * queries), bf16),
            jax.ShapeDtypeStruct((queries, width), bf16),
            jax.ShapeDtypeStruct((copies, 2, width, queries), bf16),
        ],
        scratch_shapes=[
            pltpu.VMEM((cols, queries), bf16),
            pltpu.VMEM((width, queries), f32),
            pltpu.VMEM((ext.shape[1], queries), bf16),
        ],
        compiler_params=params("arbitrary", mib=24),
        cost_estimate=cost(4e9, 2.4e7, 2.5e6),
        name="front",
    )(fetched, orow, rel_row, rtab_t, ext, band, weight_t)


def score_kernel(cand, pos_ref, qv_ref, tails_ref, out_ref):
    qv = qv_ref[...]
    queries = qv.shape[0]
    owners, _, cap = tails_ref.shape
    total = jnp.zeros(qv.shape, f32)
    for b in range(owners):
        block = tails_ref[b]
        score = mm(qv, block)
        here = iota((queries, cap), 1) + b * cap
        target = jnp.where(here == pos_ref[...], 1.0 - smooth + smooth / cand, smooth / cand)
        grad = ((sigmoid(score) - target) * loss_weight).astype(bf16)
        total = total + mm(grad, block, NT)
    qgt = total.T.astype(bf16)
    for d in range(out_ref.shape[0]):
        out_ref[d] = qgt


def score_part(qv, pos, tails, cand, copies):
    queries, width = qv.shape
    return pl.pallas_call(
        functools.partial(score_kernel, cand),
        out_shape=jax.ShapeDtypeStruct((copies, width, queries), bf16),
        compiler_params=params(mib=20),
        cost_estimate=cost(1e9, 3e6, 5e5),
        name="score",
    )(pos, qv, tails)


def back_kernel(
    cap, taps, orow_ref, ext_ref, codes_ref, qgt_ref, img_ref, bandt_ref, w_ref, pre_ref,
    out_ref, sums_ref, fgrad, spread, corr, ext,
):
    s = pl.program_id(0)
    _, width, queries = qgt_ref.shape

    @pl.when(s == 0)
    def _():
        spread[...] = jnp.zeros_like(spread)

    units = bandt_ref.shape[1] // BAND_OUT
    flat = GROUPS * BAND_OUT
    linear = mm(w_ref[...], qgt_ref[0], TN)
    for f in range(units):
        cols = slice(f * flat, (f + 1) * flat)
        v = pre_ref[cols, :]
        sig = sigmoid(v)
        grad = (linear[cols, :] * (sig * (1.0 + v * (1.0 - sig)))).astype(bf16)
        for g in range(GROUPS):
            fgrad[f * BAND_OUT : (f + 1) * BAND_OUT, g * queries : (g + 1) * queries] = grad[
                g * BAND_OUT : (g + 1) * BAND_OUT, :
            ]
    spread[...] += mm(bandt_ref[...], fgrad[...])
    corr[pl.ds(s * units, units)] = mm(fgrad[...], img_ref[...], NT).reshape(units, BAND_OUT, LANES)

    @pl.when(s == pl.num_programs(0) - 1)
    def _():
        filts = corr.shape[0]
        ext[...] = jnp.zeros_like(ext)
        for g in range(GROUPS):
            ext[g * BAND_OUT : g * BAND_OUT + LANES, :] += spread[:, g * queries : (g + 1) * queries]
        entry = iota((width, ext.shape[0]), 0)
        high, low = split(ext[...])
        hpick = onehot(entry == ext_ref[...])
        rpick = onehot(entry + width == ext_ref[...])
        hgrad = (mm(hpick, high) + mm(hpick, low)).astype(bf16)
        rgrad = mm(rpick, high) + mm(rpick, low)
        total = jnp.zeros((taps, filts), f32)
        for j in range(IMG):
            rows = corr[:, j, :]
            for di in range(1, BAND):
                rows = rows + pltpu.roll(corr[:, di * IMG + j, :], LANES - di * IMG, 1)
            pick = onehot(iota((taps, LANES), 0) == codes_ref[j : j + 1, :])
            rhigh, rlow = split(rows)
            total = total + mm(pick, rhigh, NT) + mm(pick, rlow, NT)
        rest = jnp.zeros((sums_ref.shape[1] - width, queries), f32)
        for d in range(sums_ref.shape[0]):
            sums_ref[d, :width, :] = rgrad
            sums_ref[d, width:, :] = rest
            sums_ref[d, width : width + taps, :filts] = total
        blocks = out_ref.shape[0]
        pick = slot_picks(cap, blocks * cap, orow_ref[...])
        rows = mm(pick, hgrad, NT).astype(bf16)
        for d in range(blocks):
            out_ref[d] = rows[d * cap : (d + 1) * cap, :]


def sums_rows(width, taps):
    return -(-(width + taps) // 8) * 8


def back(qgt, orow, ext, codes, img, band_t, weight_t, pre, count, cap, taps, copies):
    _, width, queries = qgt.shape
    flat = weight_t.shape[1]
    filts = band_t.shape[1] // BAND_OUT
    units = filter_block(filts)
    cols = flat // filts * units
    rows = sums_rows(width, taps)
    assert filts <= queries
    return pl.pallas_call(
        functools.partial(back_kernel, cap, taps),
        grid=(filts // units,),
        in_specs=[
            whole(orow.shape),
            whole(ext.shape),
            whole(codes.shape),
            whole((1, width, queries)),
            whole(img.shape),
            pl.BlockSpec((LANES, units * BAND_OUT), lambda s: (0, s)),
            pl.BlockSpec((width, cols), lambda s: (0, s)),
            pl.BlockSpec((cols, queries), lambda s: (s, 0)),
        ],
        out_specs=[whole((count, cap, width)), whole((copies, rows, queries))],
        out_shape=[
            jax.ShapeDtypeStruct((count, cap, width), bf16),
            jax.ShapeDtypeStruct((copies, rows, queries), f32),
        ],
        scratch_shapes=[
            pltpu.VMEM((units * BAND_OUT, GROUPS * queries), bf16),
            pltpu.VMEM((LANES, GROUPS * queries), f32),
            pltpu.VMEM((filts, BAND_OUT, LANES), f32),
            pltpu.VMEM((ext.shape[1], queries), f32),
        ],
        compiler_params=params("arbitrary", mib=28),
        cost_estimate=cost(6e9, 2e7, 2.5e6),
        name="back",
    )(orow, ext, codes, qgt, img, band_t, weight_t, pre)


def tail_kernel(
    cand, core_ref, tails_ref, mate_ref, scand_ref, mcand_ref, numbers_ref, vecs_ref, own_ref, other_ref
):
    tails = jnp.concatenate([tails_ref[...], mate_ref[...]], axis=0)
    scand = jnp.concatenate([scand_ref[...], mcand_ref[...]], axis=0)
    cap = tails_ref.shape[0]
    own = jnp.zeros(own_ref.shape, f32)
    other = jnp.zeros(own_ref.shape, f32)
    for group in pairs(vecs_ref.shape[0]):
        qvt = beside(vecs_ref[p, 1] for p in group)
        pos = beside(numbers_ref[2 * p + core_ref[0], 3:4, :] for p in group)
        score = mm(tails, qvt)
        target = jnp.where(scand == pos, 1.0 - smooth + smooth / cand, smooth / cand)
        grad = ((sigmoid(score) - target) * loss_weight).astype(bf16)
        own = own + mm(qvt, grad[:cap, :], NT)
        other = other + mm(qvt, grad[cap:, :], NT)
    own_ref[...] = own
    other_ref[...] = other


def tail_part(core, tails, mate, scand, mcand, numbers, vecs, cand):
    cap, width = tails.shape
    half = jax.ShapeDtypeStruct((width, cap), f32)
    return pl.pallas_call(
        functools.partial(tail_kernel, cand),
        in_specs=[SMEM] + [VMEM] * 6,
        out_shape=[half, half],
        compiler_params=params(mib=24),
        cost_estimate=cost(2e9, 3e6, 1e6),
        name="tail_grad",
    )(core, tails, mate, scand, mcand, numbers, vecs)


def proj_kernel(
    core_ref, rtab_ref, ext_ref, band_ref, mate_ref, numbers_ref, vecs_ref, grads_ref,
    own_ref, other_ref, pick, hmat, rmat,
):
    width, rels = rtab_ref.shape
    units = band_ref.shape[0] // BAND_OUT
    flat = GROUPS * BAND_OUT
    cols = units * flat
    entry = iota((width, ext_ref.shape[1]), 0)
    for part, mat in ((0, hmat), (width, rmat)):
        pick[...] = jnp.where(entry + part == ext_ref[...], 1.0, 0.0).T.astype(bf16)
        for k, source in enumerate((band_ref, mate_ref)):
            for g in range(GROUPS):
                rows = mm(source[...], pick[g * BAND_OUT : g * BAND_OUT + LANES, :]).astype(bf16)
                for f in range(units):
                    first = k * cols + f * flat + g * BAND_OUT
                    mat[first : first + BAND_OUT, :] = rows[f * BAND_OUT : (f + 1) * BAND_OUT, :]
    for k, out in enumerate((own_ref, other_ref)):
        out[...] = jnp.zeros_like(out)
    for group in pairs(vecs_ref.shape[0]):
        hvt = beside(vecs_ref[p, 0] for p in group)
        qgt = beside(grads_ref[p] for p in group)
        rel = beside(numbers_ref[2 * p + core_ref[0], 2:3, :] for p in group)
        rvt = mm(rtab_ref[...], onehot(iota((rels, rel.shape[1]), 0) == rel)).astype(bf16)
        for k, out in enumerate((own_ref, other_ref)):
            rows = slice(k * cols, (k + 1) * cols)
            pre = mm(hmat[rows, :], hvt) + mm(rmat[rows, :], rvt)
            out[...] += mm(qgt, (pre * sigmoid(pre)).astype(bf16), NT)


def proj_part(core, rtab_t, ext, band, mate, numbers, vecs, grads):
    width = rtab_t.shape[0]
    rows = band.shape[0]
    cols = rows * GROUPS
    half = jax.ShapeDtypeStruct((width, cols), f32)
    return pl.pallas_call(
        proj_kernel,
        in_specs=[SMEM] + [VMEM] * 7,
        out_shape=[half, half],
        scratch_shapes=[
            pltpu.VMEM((ext.shape[1], width), bf16),
            pltpu.VMEM((2 * cols, width), bf16),
            pltpu.VMEM((2 * cols, width), bf16),
        ],
        compiler_params=params(mib=28),
        cost_estimate=cost(6e9, 6e6, 2.5e6),
        name="proj_grad",
    )(core, rtab_t, ext, band, mate, numbers, vecs, grads)


def proj_columns(first, cols, filters, chequer_perm, relation_table, numbers, heads, grads):
    ks = filters.shape[-1]
    rim = ks // 2
    flat = IMG * IMG
    column = first + jnp.arange(cols, dtype=i32)
    f = column // flat
    i = (column % flat) // IMG
    j = column % IMG
    spot = jnp.arange(flat, dtype=i32)
    a = (spot[:, None] // IMG - i[None, :] + rim) % IMG
    b = (spot[:, None] % IMG - j[None, :] + rim) % IMG
    tap = filters[f[None, :], jnp.minimum(a, ks - 1), jnp.minimum(b, ks - 1)]
    matrix = jnp.where((a < ks) & (b < ks), tap, jnp.zeros((), bf16))
    width = heads.shape[1]
    head = heads.transpose(0, 2, 1).reshape(-1, width)
    qg = grads.transpose(0, 2, 1).reshape(-1, width)
    joined = jnp.concatenate([head, relation_table[numbers[:, 2].reshape(-1)]], axis=1)
    pre = mm(joined[:, chequer_perm], matrix)
    return mm(qg, (pre * sigmoid(pre)).astype(bf16), TN)


def rel_kernel(width, core_ref, numbers_ref, sums_ref, rel_ref, filt_ref):
    total = jnp.zeros(rel_ref.shape, f32)
    filt = jnp.zeros(filt_ref.shape, f32)
    for group in pairs(sums_ref.shape[0]):
        rel = beside(numbers_ref[2 * p + core_ref[0], 2:3, :] for p in group)
        pick = onehot(iota((rel_ref.shape[1], rel.shape[1]), 0) == rel)
        high, low = split(beside(sums_ref[p, :width, :] for p in group))
        total = total + mm(high, pick, NT) + mm(low, pick, NT)
        for p in group:
            filt = filt + sums_ref[p, width:, :]
    rel_ref[...] = total
    filt_ref[...] = filt


def rel_part(core, numbers, sums, width, rels):
    rows, queries = sums.shape[1:]
    return pl.pallas_call(
        functools.partial(rel_kernel, width),
        in_specs=[SMEM] + [VMEM] * 2,
        out_shape=[
            jax.ShapeDtypeStruct((width, rels), f32),
            jax.ShapeDtypeStruct((rows - width, queries), f32),
        ],
        compiler_params=params(mib=24),
        cost_estimate=cost(2e9, 3e6),
        name="rel_grad",
    )(core, numbers, sums)


def entity_kernel(want_ref, srow_ref, own_ref, recv_ref, incoming_ref, out_ref):
    rows = out_ref.shape[1]
    grads = jnp.concatenate([incoming_ref[d] for d in range(incoming_ref.shape[0])], axis=0)
    total = mm(grads, onehot(iota((want_ref.shape[0], rows), 1) == want_ref[...]), TN)
    pick = onehot(iota((srow_ref.shape[0], rows), 1) == srow_ref[...])
    high, low = split(own_ref[...] + recv_ref[...])
    out_ref[...] = total + mm(high, pick) + mm(low, pick)


def entity_sum(want, srow, own, recv, incoming, rows):
    return pl.pallas_call(
        entity_kernel,
        out_shape=jax.ShapeDtypeStruct((own.shape[0], rows), f32),
        compiler_params=params(mib=24),
        cost_estimate=cost(1.5e9, 4e6),
        name="entity_grad",
    )(want, srow, own, recv, incoming)


def shards(
    entity_table,
    relation_table,
    filters,
    proj_weight,
    chequer_perm,
    head_owner,
    head_row,
    rel_ids,
    pos_index,
    tail_owner,
    tail_row,
):
    count = lax.axis_size("shard")
    me = lax.axis_index("shard")
    assert count % 2 == 0
    direct = count <= 16
    queries = head_row.shape[0]
    cand = tail_row.shape[0]
    rows, width = entity_table.shape
    rels = relation_table.shape[0]
    filts, ks, _ = filters.shape
    head_cap = 2 * queries // count
    tail_cap = 2 * cand // count
    same_core = [list(range(c, count, 2)) for c in range(2)]
    copies = count // 2 if direct else 1

    def swap(x):
        return lax.ppermute(x, "shard", [(d, d ^ 1) for d in range(count)])

    def exchange(x):
        return lax.all_to_all(x, "shard", split_axis=0, concat_axis=0, tiled=True)

    def gather_core(x):
        if direct:
            return lax.all_to_all(
                x, "shard", split_axis=0, concat_axis=0, axis_index_groups=same_core, tiled=True
            )
        return lax.all_gather(x, "shard", axis=0, axis_index_groups=same_core, tiled=True)

    me1 = me.reshape(1)
    core = (me & 1).reshape(1)
    heads = head_owner[:, 0]
    tail_owners = tail_owner[:, 0]
    table_t, rtab_t, weight_t = entity_table.T, relation_table.T, proj_weight.T
    numbers = jnp.stack([heads, head_row, rel_ids, pos_index])[None]
    numbers = exchange(jnp.broadcast_to(numbers, (count,) + numbers.shape[1:]))

    tails, tails_t, slot_cand, slot_row = pack_tails(me1, tail_owners, tail_row, table_t, tail_cap)
    all_tails = lax.all_gather(tails_t, "shard", axis=0, tiled=True)
    mate_tails, mate_cand = swap(tails), swap(slot_cand)
    found, want = find_heads(me1, numbers, table_t, head_cap)
    fetched = exchange(found)
    pos = pos_slots(tail_owners, pos_index, tail_cap)

    codes = jnp.asarray(band_codes(ks))
    band, band_t = build_band(filters, codes)
    extra = BAND_OUT * (GROUPS - 1) + LANES - IMG * IMG - BAND_OUT
    ext = jnp.concatenate([chequer_perm[-BAND_OUT:], chequer_perm, chequer_perm[:extra]])[None]
    orow = heads[None, :]
    pre, img, qv, vecs = front(
        fetched, orow, rel_ids[None, :], rtab_t, ext, band, weight_t, head_cap, copies
    )
    core_vecs = gather_core(vecs)

    qgt = score_part(qv, pos, all_tails, cand, copies)
    core_qgt = gather_core(qgt)
    outgoing, sums = back(
        qgt, orow, ext, codes, img, band_t, weight_t, pre, count, head_cap, ks * ks, copies
    )
    core_sums = gather_core(sums)
    incoming = exchange(outgoing)

    own, other = tail_part(core, tails, mate_tails, slot_cand, mate_cand, numbers, core_vecs, cand)
    entity_grad = entity_sum(want, slot_row, own, swap(other), incoming, rows).T

    cols = filts * IMG * IMG // count
    if direct and cols % (IMG * IMG) == 0:
        unit = cols // (IMG * IMG) * BAND_OUT
        mine, mate = (
            lax.dynamic_slice_in_dim(band, d * unit, unit, axis=0) for d in (me, me ^ 1)
        )
        own, other = proj_part(core, rtab_t, ext, mine, mate, numbers, core_vecs, core_qgt)
    else:
        own, other = (
            proj_columns(
                d * cols, cols, filters, chequer_perm, relation_table,
                lax.dynamic_index_in_dim(
                    numbers.reshape(count // 2, 2, 4, queries), me & 1, 1, keepdims=False
                ),
                core_vecs[:, 0], core_qgt,
            )
            for d in (me, me ^ 1)
        )
    proj_grad = (own + swap(other)).T

    part, filt = rel_part(core, numbers, core_sums, width, rels)
    relation_grad = (part + swap(part)).T
    filter_grad = (filt + swap(filt))[: ks * ks, :filts].T.reshape(filts, ks, ks)
    return (entity_grad, relation_grad, filter_grad, proj_grad)


def solution(mesh):
    placed = (
        P("shard", None),
        P(),
        P(),
        P(),
        P(),
        P(("parts", "shard"), None),
        P(("parts", "shard")),
        P(("parts", "shard")),
        P(("parts", "shard")),
        P("parts", None),
        P("parts"),
    )
    return jax.shard_map(
        shards,
        mesh=mesh,
        in_specs=placed,
        out_specs=(
            P(("parts", "shard"), None),
            P("parts", None),
            P("parts", None, None),
            P(("parts", "shard"), None),
        ),
        check_vma=False,
    )
```

time: 264 us -> 178 us (0.67)
  starting transfers between devices: 88.6 us -> 21.8 us
  waiting for transfers between devices: 81.7 us -> 35.6 us
  blocking collectives: 0 us -> 13.8 us
  between operations: 1.32 us -> 14.2 us
  Pallas kernels: 52.3 us -> 55.2 us
    ppermute x88 -> x6, starting transfers between devices: 88.6 us -> 1.27 us  [swap(): return lax.ppermute(x, 'shard', [(d, d ^ 1) for d in range(count)])]
    ppermute x88 -> x6, waiting for transfers between devices: 81.7 us -> 2.43 us  [swap(): return lax.ppermute(x, 'shard', [(d, d ^ 1) for d in range(count)])]
    all_to_all x0 -> x5, waiting for transfers between devices: none -> 30.5 us  [the longest x3 20.7 us: gather_core(): lax.all_to_all(x, 'shard', split_axis=0, concat_axis=0, axis_index_groups...]
    all_to_all x0 -> x5, starting transfers between devices: none -> 20.5 us  [the longest x3 13.2 us: gather_core(): lax.all_to_all(x, 'shard', split_axis=0, concat_axis=0, axis_index_groups...]
    all_to_all x0 -> x1, blocking collectives: none -> 13.8 us  [exchange(): return lax.all_to_all(x, 'shard', split_axis=0, concat_axis=0, tiled=True)]
    pallas_call x9, Pallas kernels: 46 us -> 48.9 us  [the longest x1 17 us: back(): pl.pallas_call(functools.partial(back_kernel, cap, taps), grid=(filts //...]
    all_gather x0 -> x1, waiting for transfers between devices: none -> 2.7 us  [shards(): all_tails = lax.all_gather(tails_t, 'shard', axis=0, tiled=True)]
    unnamed x192 -> x68, local copies, waits for them, and re-layouts: 31.9 us -> 30.9 us
  transfers between devices with their start and end apart: 88 -> 12, of which waited for: 35 -> 6; matrix products, arithmetic and copies ran while one was open for 1% -> 2% of each run, Pallas kernels for 20% -> 29%
where the time goes in v3:
time: 178 us; the launch traced here: 177 us
  Pallas kernels  55.2 us (31%)
  waiting for transfers between devices  35.6 us (20%)
  local copies, waits for them, and re-layouts  32.8 us (18%)
  starting transfers between devices  21.8 us (12%)
  between operations  14.2 us (8%)
  blocking collectives  13.8 us (8%)
  other arithmetic  3.52 us (2%)
    unnamed x68, local copies, waits for them, and re-layouts  30.9 us
    all_to_all x3, waiting for transfers between devices, gather_core(): lax.all_to_all(x, 'shard', split_axis=0, concat_axis=0, axis_index_groups...  20.7 us
    pallas_call x1, Pallas kernels, back(): pl.pallas_call(functools.partial(back_kernel, cap, taps), grid=(filts //...  17 us
    all_to_all x1, blocking collectives, exchange(): return lax.all_to_all(x, 'shard', split_axis=0, concat_axis=0, tiled=True)  13.8 us
    all_to_all x3, starting transfers between devices, gather_core(): lax.all_to_all(x, 'shard', split_axis=0, concat_axis=0, axis_index_groups...  13.2 us
    pallas_call x1, Pallas kernels, proj_part(): pl.pallas_call(proj_kernel, in_specs=[SMEM] + [VMEM] * 7, out_shape=[half...  10.2 us
    all_to_all x2, waiting for transfers between devices, exchange(): return lax.all_to_all(x, 'shard', split_axis=0, concat_axis=0, tiled=True)  9.77 us
    pallas_call x1, Pallas kernels, front(): pl.pallas_call(functools.partial(front_kernel, cap), grid=(filts // units...  7.96 us
  transfers between devices with their start and end apart: 12, of which 6 were waited for; matrix products, arithmetic and copies ran while one was open for 2% of the time, Pallas kernels for 29%

profile of v3, /device:TPU:0, one launch (start us, length us, event | category | flops | bytes accessed | tf_op | source)
XLA Modules:
  0.0 177.0 jit_solution(1458081296916275998)
XLA Ops:
  7.9 1.1 copy-done.11
  9.8 3.6 %pack_tails.1 = (bf16[512,200]{1,0:T(8,128)(2,1)S(1)}, bf16[1,200,512]{2,1,0:T(8,128)(2,1)}, s32[512,1]{1,0:T(8,128)S(1)}, s32[512,1]{1,0:T(8,128)S(1)}) custom-call(s32[1]{0:T(128)} %bitcast.me_ref, s32[32,128]{1,0:T(8,128)S(1)} %bitcast.23, s32[32,128]{1,0:T(8,128)S(1)} %bitcast.38, bf16[200,2048]{1,0:T(8,128)(2,1)S(1)} %bitcast.34), custom_call_target="tpu_custom_call" | custom-call | flops 1000000000 | bytes 2000000 | tf_op jit(solution)/shard_map/pack_tails/pallas_call | solution.py:151
  15.6 13.8 %all_to_all.30.numbers_ref = s32[16,4,128]{2,1,0:T(4,128)S(1)} all-to-all(s32[16,4,128]{2,1,0:T(4,128)S(1)} %broadcast_in_dim.4), channel_id=1, replica_groups=mesh['parts'=2,'shard'=16] {'shard'}, dimensions={0} | all-to-all | bytes 65536 | tf_op jit(solution)/shard_map/all_to_all | solution.py:648
  29.4 1.4 find_heads.1
  30.9 3.5 %all-to-all-start.1 = ((bf16[16,16,200]{2,1,0:T(8,128)(2,1)}), bf16[16,16,200]{2,1,0:T(8,128)(2,1)S(1)}, u32[]{:S(2)}, u32[]{:S(2)}) async-start(bf16[16,16,200]{2,1,0:T(8,128)(2,1)} %get-tuple-element.28), calls=%async_computation.1 | async-start | bytes 262144 | tf_op jit(solution)/shard_map/all_to_all | solution.py:648
  34.7 2.8 %band.1 = (bf16[3840,256]{1,0:T(8,128)(2,1)S(1)}, bf16[256,3840]{1,0:T(8,128)(2,1)S(1)}) custom-call(s32[20,256]{1,0:T(8,128)S(1)} %copy-done.20, bf16[48,81]{1,0:T(8,128)(2,1)S(1)} %copy.18.filt_ref), custom_call_target="tpu_custom_call" | custom-call | flops 40000000 | bytes 4000000 | tf_op jit(solution)/shard_map/band/pallas_call | solution.py:94
  37.5 1.3 copy-done.21
  38.7 4.2 %all-to-all-done.1.fetched_ref = bf16[16,16,200]{2,1,0:T(8,128)(2,1)S(1)} async-done(((bf16[16,16,200]{2,1,0:T(8,128)(2,1)}), bf16[16,16,200]{2,1,0:T(8,128)(2,1)S(1)}, u32[]{:S(2)}, u32[]{:S(2)}) %all-to-all-start.1) | async-done | bytes 102432 | tf_op jit(solution)/shard_map/all_to_all | solution.py:648
  42.9 3.2 %copy-done.9 = bf16[19200,200]{0,1:T(8,128)(2,1)S(1)} copy-done((bf16[19200,200]{0,1:T(8,128)(2,1)S(1)}, bf16[19200,200]{0,1:T(8,128)(2,1)}, u32[]{:S(2)}) %copy-start.9) | copy-done | bytes 7680024
  47.2 8.0 %front.1 = (f32[19200,128]{1,0:T(8,128)S(1)}, bf16[256,640]{1,0:T(8,128)(2,1)S(1)}, bf16[128,200]{1,0:T(8,128)(2,1)S(1)}, bf16[8,2,200,128]{3,2,1,0:T(8,128)(2,1)}) custom-call(bf16[16,16,200]{2,1,0:T(8,128)(2,1)S(1)} %all-to-all-done.1.fetched_ref, s32[1,128]{1,0:T(1,128)S(1)} %bitcast.30, s32[1,128]{1,0:T(1,128)S(1)} %bitcast.28, ...), custom_call_target="tpu_custom_call" | custom-call | flops 4000000000 | bytes 24000000 | tf_op jit(solution)/shard_map/front/pallas_call | solution.py:302
  55.2 3.8 %copy-done.23 = f32[19200,128]{1,0:T(8,128)} copy-done((f32[19200,128]{1,0:T(8,128)}, f32[19200,128]{1,0:T(8,128)S(1)}, u32[]{:S(2)}) %copy-start.23) | copy-done | bytes 9830424
  59.0 3.7 %all-to-all-start.2 = ((bf16[8,2,200,128]{3,2,1,0:T(8,128)(2,1)}), bf16[8,2,200,128]{3,2,1,0:T(8,128)(2,1)S(1)}, u32[]{:S(2)}, u32[]{:S(2)}) async-start(bf16[8,2,200,128]{3,2,1,0:T(8,128)(2,1)} %get-tuple-element.30), calls=%async_computation.2 | async-start | bytes 1638400 | tf_op jit(solution)/shard_map/all_to_all | solution.py:652
  63.4 2.7 %all-gather.2.cloned.1.call-done.tails_ref = bf16[16,200,512]{2,1,0:T(8,128)(2,1)} async-done(((bf16[1,200,512]{2,1,0:T(8,128)(2,1)}), bf16[16,200,512]{2,1,0:T(8,128)(2,1)}) %all-gather.2.cloned.1.call-update) | async-done | bytes 3276816 | tf_op jit(solution)/shard_map/all_gather | solution.py:666
  66.1 1.9 %copy-done = bf16[16,200,512]{2,1,0:T(8,128)(2,1)S(1)} copy-done((bf16[16,200,512]{2,1,0:T(8,128)(2,1)S(1)}, bf16[16,200,512]{2,1,0:T(8,128)(2,1)}, u32[]{:S(2)}) %copy-start) | copy-done | bytes 3276824
  68.1 3.3 %score.1.qgt_ref = bf16[8,200,128]{2,1,0:T(8,128)(2,1)} custom-call(s32[128,1]{1,0:T(8,128)S(1)} %pos_slots.1.pos_ref, bf16[128,200]{1,0:T(8,128)(2,1)S(1)} %get-tuple-element.33.qv_ref, bf16[16,200,512]{2,1,0:T(8,128)(2,1)S(1)} %copy-done), custom_call_target="tpu_custom_call" | custom-call | flops 1000000000 | bytes 3000000 | tf_op jit(solution)/shard_map/score/pallas_call | solution.py:356
  71.3 12.4 %all-to-all-done.2.vecs_ref = bf16[8,2,200,128]{3,2,1,0:T(8,128)(2,1)S(1)} async-done(((bf16[8,2,200,128]{3,2,1,0:T(8,128)(2,1)}), bf16[8,2,200,128]{3,2,1,0:T(8,128)(2,1)S(1)}, u32[]{:S(2)}, u32[]{:S(2)}) %all-to-all-start.2) | async-done | bytes 819232 | tf_op jit(solution)/shard_map/all_to_all | solution.py:652
  83.7 3.6 %all-to-all-start.5 = ((bf16[8,200,128]{2,1,0:T(8,128)(2,1)}), bf16[8,200,128]{2,1,0:T(8,128)(2,1)S(1)}, u32[]{:S(2)}, u32[]{:S(2)}) async-start(bf16[8,200,128]{2,1,0:T(8,128)(2,1)} %score.1.qgt_ref), calls=%async_computation.5 | async-start | bytes 819200 | tf_op jit(solution)/shard_map/all_to_all | solution.py:652
  87.4 3.2 %copy-done.10 = bf16[19200,200]{0,1:T(8,128)(2,1)S(1)} copy-done((bf16[19200,200]{0,1:T(8,128)(2,1)S(1)}, bf16[19200,200]{0,1:T(8,128)(2,1)}, u32[]{:S(2)}) %copy-start.10) | copy-done | bytes 7680024
  90.6 1.5 copy-done.22
  92.1 3.8 %copy-done.24 = f32[19200,128]{1,0:T(8,128)S(1)} copy-done((f32[19200,128]{1,0:T(8,128)S(1)}, f32[19200,128]{1,0:T(8,128)}, u32[]{:S(2)}) %copy-start.24) | copy-done | bytes 9830424
  95.9 17.0 %back.1 = (bf16[16,16,200]{2,1,0:T(8,128)(2,1)}, f32[8,288,128]{2,1,0:T(8,128)}) custom-call(s32[1,128]{1,0:T(1,128)S(1)} %bitcast.31, s32[1,576]{1,0:T(1,128)S(1)} %broadcast_in_dim.5.ext_ref, s32[20,256]{1,0:T(8,128)S(1)} %copy-done.20, bf16[8,200,128]{2,1,0:T(8,128)(2,1)} %score.1.qgt_ref, bf16[256,640]{1,0:T(8,128)(2,1)S(1)} %get-tuple-element.35.img_ref, ...), custom_call_target="tpu_custom_call" | custom-call | flops 6000000000 | bytes 20000000 | tf_op jit(solution)/shard_map/back/pallas_call | solution.py:435
  113.7 5.9 %all-to-all-start.4 = ((f32[8,288,128]{2,1,0:T(8,128)}), f32[8,288,128]{2,1,0:T(8,128)S(1)}, u32[]{:S(2)}, u32[]{:S(2)}) async-start(f32[8,288,128]{2,1,0:T(8,128)} %get-tuple-element.39), calls=%async_computation.4 | async-start | bytes 2359296 | tf_op jit(solution)/shard_map/all_to_all | solution.py:652
  122.6 10.2 %proj_grad.1 = (f32[200,1200]{1,0:T(8,128)S(1)}, f32[200,1200]{1,0:T(8,128)}) custom-call(s32[1]{0:T(128)} %bitcast.8.core_ref, bf16[200,1387]{1,0:T(8,128)(2,1)S(1)} %bitcast.37, s32[1,576]{1,0:T(1,128)S(1)} %broadcast_in_dim.5.ext_ref, bf16[240,256]{1,0:T(8,128)(2,1)S(1)} %get-tuple-element.45.band_ref, bf16[240,256]{1,0:T(8,128)(2,1)S(1)} %get-tuple-element.44.mate_ref, ...), custom_call_target="tpu_custom_call" | custom-call | flops 6000000000 | bytes 6000000 | tf_op jit(solution)/shard_map/proj_grad/pallas_call | solution.py:533
  133.4 2.4 %collective-permute-done.1.mcand_ref = s32[512,1]{1,0:T(8,128)S(1)} collective-permute-done((s32[512,1]{1,0:T(8,128)S(1)}, s32[512,1]{1,0:T(8,128)S(1)}, u32[]{:S(2)}, u32[]{:S(2)}) %collective-permute-start.1) | collective-permute-done | bytes 2080 | tf_op jit(solution)/shard_map/ppermute | solution.py:645
  135.8 2.7 %tail_grad.1 = (f32[200,512]{1,0:T(8,128)S(1)}, f32[200,512]{1,0:T(8,128)}) custom-call(s32[1]{0:T(128)} %bitcast.8.core_ref, bf16[512,200]{1,0:T(8,128)(2,1)S(1)} %copy-done.16, bf16[512,200]{1,0:T(8,128)(2,1)S(1)} %collective-permute-done.mate_ref, s32[512,1]{1,0:T(8,128)S(1)} %copy-done.18, s32[512,1]{1,0:T(8,128)S(1)} %collective-permute-done.1.mcand_ref, ...), custom_call_target="tpu_custom_call" | custom-call | flops 2000000000 | bytes 3000000 | tf_op jit(solution)/shard_map/tail_grad/pallas_call | solution.py:488
  139.6 8.3 %all-to-all-done.4.sums_ref = f32[8,288,128]{2,1,0:T(8,128)S(1)} async-done(((f32[8,288,128]{2,1,0:T(8,128)}), f32[8,288,128]{2,1,0:T(8,128)S(1)}, u32[]{:S(2)}, u32[]{:S(2)}) %all-to-all-start.4) | async-done | bytes 1179680 | tf_op jit(solution)/shard_map/all_to_all | solution.py:652
  147.9 3.8 %all-to-all-start.3 = ((bf16[16,16,200]{2,1,0:T(8,128)(2,1)}), bf16[16,16,200]{2,1,0:T(8,128)(2,1)S(1)}, u32[]{:S(2)}, u32[]{:S(2)}) async-start(bf16[16,16,200]{2,1,0:T(8,128)(2,1)} %get-tuple-element.38), calls=%async_computation.3 | async-start | bytes 262144 | tf_op jit(solution)/shard_map/all_to_all | solution.py:648
  151.7 1.9 %rel_grad.1 = (f32[200,1387]{1,0:T(8,128)S(1)}, f32[88,128]{1,0:T(8,128)S(1)}) custom-call(s32[1]{0:T(128)} %bitcast.8.core_ref, s32[16,4,128]{2,1,0:T(4,128)S(1)} %all_to_all.30.numbers_ref, f32[8,288,128]{2,1,0:T(8,128)S(1)} %all-to-all-done.4.sums_ref), custom_call_target="tpu_custom_call" | custom-call | flops 2000000000 | bytes 3000000 | tf_op jit(solution)/shard_map/rel_grad/pallas_call | solution.py:585
  153.9 5.6 %all-to-all-done.3.incoming_ref = bf16[16,16,200]{2,1,0:T(8,128)(2,1)S(1)} async-done(((bf16[16,16,200]{2,1,0:T(8,128)(2,1)}), bf16[16,16,200]{2,1,0:T(8,128)(2,1)S(1)}, u32[]{:S(2)}, u32[]{:S(2)}) %all-to-all-start.3) | async-done | bytes 102432 | tf_op jit(solution)/shard_map/all_to_all | solution.py:648
  162.3 3.7 %entity_grad.1 = f32[200,2048]{1,0:T(8,128)} custom-call(s32[256,1]{1,0:T(8,128)S(1)} %copy-done.26, s32[512,1]{1,0:T(8,128)S(1)} %copy-done.30, f32[200,512]{1,0:T(8,128)S(1)} %copy-done.28, f32[200,512]{1,0:T(8,128)} %collective-permute-done.2.recv_ref, bf16[16,16,200]{2,1,0:T(8,128)(2,1)S(1)} %all-to-all-done.3.incoming_ref), custom_call_target="tpu_custom_call" | custom-call | flops 1500000000 | bytes 4000000 | tf_op jit(solution)/shard_map/entity_grad/pallas_call | solution.py:608
  166.0 2.3 %add_bitcast_fusion.1 = f32[1200,200]{0,1:T(8,128)} fusion(f32[200,1200]{1,0:T(8,128)S(1)} %get-tuple-element.42, f32[200,1200]{1,0:T(8,128)} %collective-permute-done.5), kind=kLoop, calls=%fused_computation.1 | loop fusion | flops 240000 | bytes 2880000 | tf_op jit(solution)/shard_map/transpose | solution.py:711
  169.0 1.1 add_bitcast_fusion
  (87 shorter events, 15.1 us)
Async XLA Ops:
  7.2 59.0 %all-gather.2.cloned.1.call-start = ((), (), s32[]{:S(2)}) async-start(), calls=%async_computation.6 | async-start | bytes 3481600 | tf_op jit(solution)/shard_map/all_gather | solution.py:666
  9.8 5.8 %copy-start.6 = (s32[128]{0:T(128)S(1)}, s32[128]{0:T(128)}, u32[]{:S(2)}) copy-start(s32[128]{0:T(128)} %param.20) | copy-start | bytes 1540
  9.8 5.8 %copy-start.7 = (s32[128]{0:T(128)S(1)}, s32[128]{0:T(128)}, u32[]{:S(2)}) copy-start(s32[128]{0:T(128)} %param.19) | copy-start | bytes 1540
  9.8 5.8 %copy-start.8 = (s32[128,1]{0,1:T(1,128)S(1)}, s32[128,1]{0,1:T(1,128)}, u32[]{:S(2)}) copy-start(s32[128,1]{0,1:T(1,128)} %param.17) | copy-start | bytes 1540
  9.8 5.8 %copy-start.33 = (s32[128]{0:T(128)S(1)}, s32[128]{0:T(128)}, u32[]{:S(2)}) copy-start(s32[128]{0:T(128)} %param.18) | copy-start | bytes 1540
  9.8 19.6 %copy-start.12 = (bf16[2048,200]{0,1:T(8,128)(2,1)S(1)}, bf16[2048,200]{0,1:T(8,128)(2,1)}, u32[]{:S(2)}) copy-start(bf16[2048,200]{0,1:T(8,128)(2,1)} %param.12) | copy-start | bytes 2457604
  15.5 18.9 %copy-start.32 = (s32[400]{0:T(512)S(1)}, s32[400]{0:T(512)}, u32[]{:S(2)}) copy-start(s32[400]{0:T(512)} %param.16) | copy-start | bytes 4804
  15.5 18.9 %copy-start.31 = (bf16[48,9,9]{0,2,1:T(8,128)(2,1)S(1)}, bf16[48,9,9]{0,2,1:T(8,128)(2,1)}, u32[]{:S(2)}) copy-start(bf16[48,9,9]{0,2,1:T(8,128)(2,1)} %param.14) | copy-start | bytes 23332
  15.5 19.1 %slice-start = ((s32[400]{0:T(512)}), s32[96]{0:T(128)S(1)}, s32[]{:S(2)}) async-start(s32[400]{0:T(512)} %param.16), calls=%async_computation.7 | async-start | bytes 1024 | tf_op jit(solution)/shard_map/slice | solution.py:675
  15.5 19.2 %copy-start.20 = (s32[20,256]{1,0:T(8,128)S(1)}, s32[20,256]{1,0:T(8,128)}, u32[]{:S(2)}) copy-start(s32[20,256]{1,0:T(8,128)} %constant.14.clone.codes_ref) | copy-start | bytes 61444
  30.9 24.3 %copy-start.25 = (s32[256,1]{1,0:T(8,128)}, s32[256,1]{1,0:T(8,128)S(1)}, u32[]{:S(2)}) copy-start(s32[256,1]{1,0:T(8,128)S(1)} %get-tuple-element.24.want_ref) | copy-start | bytes 3076
  30.9 12.1 %all-to-all-start.1 = ((bf16[16,16,200]{2,1,0:T(8,128)(2,1)}), bf16[16,16,200]{2,1,0:T(8,128)(2,1)S(1)}, u32[]{:S(2)}, u32[]{:S(2)}) async-start(bf16[16,16,200]{2,1,0:T(8,128)(2,1)} %get-tuple-element.28), calls=%async_computation.1 | async-start | bytes 262144 | tf_op jit(solution)/shard_map/all_to_all | solution.py:648
  38.7 16.4 %copy-start.3 = (bf16[3840,256]{1,0:T(8,128)(2,1)}, bf16[3840,256]{1,0:T(8,128)(2,1)S(1)}, u32[]{:S(2)}) copy-start(bf16[3840,256]{1,0:T(8,128)(2,1)S(1)} %get-tuple-element.29.band_ref) | copy-start | bytes 5898244
  42.9 3.2 %copy-start.9 = (bf16[19200,200]{0,1:T(8,128)(2,1)S(1)}, bf16[19200,200]{0,1:T(8,128)(2,1)}, u32[]{:S(2)}) copy-start(bf16[19200,200]{0,1:T(8,128)(2,1)} %param.15) | copy-start | bytes 23040004
  55.2 3.8 %copy-start.23 = (f32[19200,128]{1,0:T(8,128)}, f32[19200,128]{1,0:T(8,128)S(1)}, u32[]{:S(2)}) copy-start(f32[19200,128]{1,0:T(8,128)S(1)} %get-tuple-element.37.pre_ref) | copy-start | bytes 29491204
  59.0 3.7 %copy-start.5 = (s32[4096,1]{0,1:T(1,128)S(1)}, s32[4096,1]{0,1:T(1,128)}, u32[]{:S(2)}) copy-start(s32[4096,1]{0,1:T(1,128)} %param.21) | copy-start | bytes 49156
  59.0 24.8 %all-to-all-start.2 = ((bf16[8,2,200,128]{3,2,1,0:T(8,128)(2,1)}), bf16[8,2,200,128]{3,2,1,0:T(8,128)(2,1)S(1)}, u32[]{:S(2)}, u32[]{:S(2)}) async-start(bf16[8,2,200,128]{3,2,1,0:T(8,128)(2,1)} %get-tuple-element.30), calls=%async_computation.2 | async-start | bytes 1638400 | tf_op jit(solution)/shard_map/all_to_all | solution.py:652
  66.1 1.9 %copy-start = (bf16[16,200,512]{2,1,0:T(8,128)(2,1)S(1)}, bf16[16,200,512]{2,1,0:T(8,128)(2,1)}, u32[]{:S(2)}) copy-start(bf16[16,200,512]{2,1,0:T(8,128)(2,1)} %all-gather.2.cloned.1.call-done.tails_ref) | copy-start | bytes 9830404
  83.7 29.2 %all-to-all-start.5 = ((bf16[8,200,128]{2,1,0:T(8,128)(2,1)}), bf16[8,200,128]{2,1,0:T(8,128)(2,1)S(1)}, u32[]{:S(2)}, u32[]{:S(2)}) async-start(bf16[8,200,128]{2,1,0:T(8,128)(2,1)} %score.1.qgt_ref), calls=%async_computation.5 | async-start | bytes 819200 | tf_op jit(solution)/shard_map/all_to_all | solution.py:652
  87.4 3.2 %copy-start.10 = (bf16[19200,200]{0,1:T(8,128)(2,1)S(1)}, bf16[19200,200]{0,1:T(8,128)(2,1)}, u32[]{:S(2)}) copy-start(bf16[19200,200]{0,1:T(8,128)(2,1)} %param.15) | copy-start | bytes 23040004
  90.6 1.5 copy-start.22
  92.1 3.8 %copy-start.24 = (f32[19200,128]{1,0:T(8,128)S(1)}, f32[19200,128]{1,0:T(8,128)}, u32[]{:S(2)}) copy-start(f32[19200,128]{1,0:T(8,128)} %copy-done.23) | copy-start | bytes 29491204
  113.7 34.2 %all-to-all-start.4 = ((f32[8,288,128]{2,1,0:T(8,128)}), f32[8,288,128]{2,1,0:T(8,128)S(1)}, u32[]{:S(2)}, u32[]{:S(2)}) async-start(f32[8,288,128]{2,1,0:T(8,128)} %get-tuple-element.39), calls=%async_computation.4 | async-start | bytes 2359296 | tf_op jit(solution)/shard_map/all_to_all | solution.py:652
  122.6 10.2 %copy-start.16 = (bf16[512,200]{1,0:T(8,128)(2,1)S(1)}, bf16[512,200]{1,0:T(8,128)(2,1)}, u32[]{:S(2)}) copy-start(bf16[512,200]{1,0:T(8,128)(2,1)} %copy-done.15) | copy-start | bytes 614404
  122.6 10.7 %copy-start.18 = (s32[512,1]{1,0:T(8,128)S(1)}, s32[512,1]{1,0:T(8,128)}, u32[]{:S(2)}) copy-start(s32[512,1]{1,0:T(8,128)} %copy-done.17) | copy-start | bytes 6148
  132.8 33.2 %collective-permute-start.5 = (f32[200,1200]{1,0:T(8,128)}, f32[200,1200]{1,0:T(8,128)}, u32[]{:S(2)}, u32[]{:S(2)}) collective-permute-start(f32[200,1200]{1,0:T(8,128)} %get-tuple-element.43), channel_id=1, source_target_pairs={{0,1},{1,0},{2,3},{3,2},{4,5},{5,4},{6,7},{7,6},{8,9},{9,8},{10,11... | collective-permute-start | bytes 2880008 | tf_op jit(solution)/shard_map/ppermute | solution.py:645
  132.8 3.0 %collective-permute-start = (bf16[512,200]{1,0:T(8,128)(2,1)S(1)}, bf16[512,200]{1,0:T(8,128)(2,1)S(1)}, u32[]{:S(2)}, u32[]{:S(2)}) collective-permute-start(bf16[512,200]{1,0:T(8,128)(2,1)S(1)} %copy-done.16), channel_id=1, source_target_pairs={{0,1},{1,0},{2,3},{3,2},{4,5},{5,4},{6,7},{7,6},{8,9},{9,8},{10,11... | collective-permute-start | bytes 614408 | tf_op jit(solution)/shard_map/ppermute | solution.py:645
  133.3 2.5 %collective-permute-start.1 = (s32[512,1]{1,0:T(8,128)S(1)}, s32[512,1]{1,0:T(8,128)S(1)}, u32[]{:S(2)}, u32[]{:S(2)}) collective-permute-start(s32[512,1]{1,0:T(8,128)S(1)} %copy-done.18), channel_id=1, source_target_pairs={{0,1},{1,0},{2,3},{3,2},{4,5},{5,4},{6,7},{7,6},{8,9},{9,8},{10,11... | collective-permute-start | bytes 6152 | tf_op jit(solution)/shard_map/ppermute | solution.py:645
  139.2 14.6 %collective-permute-start.2 = (f32[200,512]{1,0:T(8,128)}, f32[200,512]{1,0:T(8,128)}, u32[]{:S(2)}, u32[]{:S(2)}) collective-permute-start(f32[200,512]{1,0:T(8,128)} %get-tuple-element.32), channel_id=1, source_target_pairs={{0,1},{1,0},{2,3},{3,2},{4,5},{5,4},{6,7},{7,6},{8,9},{9,8},{10,11... | collective-permute-start | bytes 1228808 | tf_op jit(solution)/shard_map/ppermute | solution.py:645
  147.9 11.5 %all-to-all-start.3 = ((bf16[16,16,200]{2,1,0:T(8,128)(2,1)}), bf16[16,16,200]{2,1,0:T(8,128)(2,1)S(1)}, u32[]{:S(2)}, u32[]{:S(2)}) async-start(bf16[16,16,200]{2,1,0:T(8,128)(2,1)} %get-tuple-element.38), calls=%async_computation.3 | async-start | bytes 262144 | tf_op jit(solution)/shard_map/all_to_all | solution.py:648
  153.6 15.4 %collective-permute-start.3 = (f32[200,1387]{1,0:T(8,128)S(1)}, f32[200,1387]{1,0:T(8,128)S(1)}, u32[]{:S(2)}, u32[]{:S(2)}) collective-permute-start(f32[200,1387]{1,0:T(8,128)S(1)} %get-tuple-element.40), channel_id=1, source_target_pairs={{0,1},{1,0},{2,3},{3,2},{4,5},{5,4},{6,7},{7,6},{8,9},{9,8},{10,11... | collective-permute-start | bytes 3328808 | tf_op jit(solution)/shard_map/ppermute | solution.py:645
  166.0 2.3 %collective-permute-start.4 = (f32[88,128]{1,0:T(8,128)S(1)}, f32[88,128]{1,0:T(8,128)S(1)}, u32[]{:S(2)}, u32[]{:S(2)}) collective-permute-start(f32[88,128]{1,0:T(8,128)S(1)} %get-tuple-element.41), channel_id=1, source_target_pairs={{0,1},{1,0},{2,3},{3,2},{4,5},{5,4},{6,7},{7,6},{8,9},{9,8},{10,11... | collective-permute-start | bytes 135176 | tf_op jit(solution)/shard_map/ppermute | solution.py:645
  (15 other events, 13.5 us)
Sparse Core Ops, SparseCore 0:
  15.7 50.3 all-gather.1

commit v4 on v3

--- a/solution.py
+++ b/solution.py
@@ -48,9 +48,9 @@
     return 0.5 * jnp.tanh(0.5 * v) + 0.5
 
 
-def params(*semantics, mib=40):
+def params(*semantics):
     return pltpu.CompilerParams(
-        dimension_semantics=semantics or None, vmem_limit_bytes=mib << 20
+        dimension_semantics=semantics or None, vmem_limit_bytes=60 << 20
     )
 
 
@@ -98,7 +98,7 @@
             jax.ShapeDtypeStruct((LANES, count * BAND_OUT), bf16),
         ],
         scratch_shapes=[pltpu.VMEM((count, BAND_OUT, LANES), f32)],
-        compiler_params=params(mib=24),
+        compiler_params=params(),
         cost_estimate=cost(4e7, 4e6),
         name="band",
     )(codes, filters.reshape(count, ks * ks))
@@ -157,7 +157,7 @@
             jax.ShapeDtypeStruct((cap, 1), i32),
             jax.ShapeDtypeStruct((cap, 1), i32),
         ],
-        compiler_params=params(mib=16),
+        compiler_params=params(),
         cost_estimate=cost(1e9, 2e6),
         name="pack_tails",
     )(me, tail_owners.reshape(-1, 128), tail_row.reshape(-1, 128), table_t)
@@ -194,7 +194,7 @@
             jax.ShapeDtypeStruct((count * cap, 1), i32),
         ],
         scratch_shapes=[pltpu.VMEM((count * cap, 1), f32)],
-        compiler_params=params(mib=16),
+        compiler_params=params(),
         cost_estimate=cost(3e8, 2e6),
         name="find_heads",
     )(me, table_t, numbers)
@@ -227,7 +227,7 @@
     return pl.pallas_call(
         functools.partial(pos_kernel, cap),
         out_shape=jax.ShapeDtypeStruct((queries, 1), i32),
-        compiler_params=params(mib=8),
+        compiler_params=params(),
         cost_estimate=cost(1e7, 1e5),
         name="pos_slots",
     )(tail_owners.reshape(1, -1), pos_index.reshape(1, -1))
@@ -255,8 +255,7 @@
         rows = jnp.concatenate([fetched_ref[d] for d in range(fetched_ref.shape[0])], axis=0)
         pick = slot_picks(cap, rows.shape[0], orow_ref[...])
         hvt = mm(rows, pick, TN).astype(bf16)
-        for d in range(vecs_ref.shape[0]):
-            vecs_ref[d, 0] = hvt
+        vecs_ref[0] = hvt
         rels = rtab_ref.shape[1]
         rvt = mm(rtab_ref[...], onehot(iota((rels, queries), 0) == rel_ref[...])).astype(bf16)
         entry = iota((width, ext_ref.shape[1]), 0)
@@ -284,16 +283,14 @@
     def _():
         query = acc[...]
         qv_ref[...] = query.T.astype(bf16)
-        qvt = query.astype(bf16)
-        for d in range(vecs_ref.shape[0]):
-            vecs_ref[d, 1] = qvt
+        vecs_ref[1] = query.astype(bf16)
 
 
 def filter_block(filts):
     return math.gcd(filts, 8)
 
 
-def front(fetched, orow, rel_row, rtab_t, ext, band, weight_t, cap, copies):
+def front(fetched, orow, rel_row, rtab_t, ext, band, weight_t, cap):
     queries = orow.shape[1]
     width, flat = weight_t.shape
     filts = band.shape[0] // BAND_OUT
@@ -315,26 +312,26 @@
             pl.BlockSpec((cols, queries), lambda s: (s, 0)),
             whole((LANES, GROUPS * queries)),
             whole((queries, width)),
-            whole((copies, 2, width, queries)),
+            whole((2, width, queries)),
         ],
         out_shape=[
             jax.ShapeDtypeStruct((flat, queries), f32),
             jax.ShapeDtypeStruct((LANES, GROUPS * queries), bf16),
             jax.ShapeDtypeStruct((queries, width), bf16),
-            jax.ShapeDtypeStruct((copies, 2, width, queries), bf16),
+            jax.ShapeDtypeStruct((2, width, queries), bf16),
         ],
         scratch_shapes=[
             pltpu.VMEM((cols, queries), bf16),
             pltpu.VMEM((width, queries), f32),
             pltpu.VMEM((ext.shape[1], queries), bf16),
         ],
-        compiler_params=params("arbitrary", mib=24),
+        compiler_params=params("arbitrary"),
         cost_estimate=cost(4e9, 2.4e7, 2.5e6),
         name="front",
     )(fetched, orow, rel_row, rtab_t, ext, band, weight_t)
 
 
-def score_kernel(cand, pos_ref, qv_ref, tails_ref, out_ref):
+def score_kernel(cand, pos_ref, qv_ref, tails_ref, vecs_ref, out_ref):
     qv = qv_ref[...]
     queries = qv.shape[0]
     owners, _, cap = tails_ref.shape
@@ -348,26 +345,28 @@
         total = total + mm(grad, block, NT)
     qgt = total.T.astype(bf16)
     for d in range(out_ref.shape[0]):
-        out_ref[d] = qgt
-
-
-def score_part(qv, pos, tails, cand, copies):
+        out_ref[d, 0] = qgt
+        out_ref[d, 1] = vecs_ref[0]
+        out_ref[d, 2] = vecs_ref[1]
+
+
+def score_part(qv, pos, tails, vecs, cand, copies):
     queries, width = qv.shape
     return pl.pallas_call(
         functools.partial(score_kernel, cand),
-        out_shape=jax.ShapeDtypeStruct((copies, width, queries), bf16),
-        compiler_params=params(mib=20),
+        out_shape=jax.ShapeDtypeStruct((copies, 3, width, queries), bf16),
+        compiler_params=params(),
         cost_estimate=cost(1e9, 3e6, 5e5),
         name="score",
-    )(pos, qv, tails)
+    )(pos, qv, tails, vecs)
 
 
 def back_kernel(
-    cap, taps, orow_ref, ext_ref, codes_ref, qgt_ref, img_ref, bandt_ref, w_ref, pre_ref,
-    out_ref, sums_ref, fgrad, spread, corr, ext,
+    cap, orow_ref, ext_ref, qgt_ref, img_ref, bandt_ref, w_ref, pre_ref,
+    out_ref, sums_ref, corr_ref, turned, fgrad, spread, ext,
 ):
     s = pl.program_id(0)
-    _, width, queries = qgt_ref.shape
+    width, queries = qgt_ref.shape[2:]
 
     @pl.when(s == 0)
     def _():
@@ -375,7 +374,10 @@
 
     units = bandt_ref.shape[1] // BAND_OUT
     flat = GROUPS * BAND_OUT
-    linear = mm(w_ref[...], qgt_ref[0], TN)
+    eye = onehot(iota((128, 128), 0) == iota((128, 128), 1))
+    for c in range(0, turned.shape[0], 128):
+        turned[c : c + 128, :] = mm(eye, w_ref[:, c : c + 128], NT).astype(bf16)
+    linear = mm(turned[...], qgt_ref[0, 0])
     for f in range(units):
         cols = slice(f * flat, (f + 1) * flat)
         v = pre_ref[cols, :]
@@ -386,11 +388,10 @@
                 g * BAND_OUT : (g + 1) * BAND_OUT, :
             ]
     spread[...] += mm(bandt_ref[...], fgrad[...])
-    corr[pl.ds(s * units, units)] = mm(fgrad[...], img_ref[...], NT).reshape(units, BAND_OUT, LANES)
+    corr_ref[...] = mm(fgrad[...], img_ref[...], NT).reshape(units, BAND_OUT, LANES)
 
     @pl.when(s == pl.num_programs(0) - 1)
     def _():
-        filts = corr.shape[0]
         ext[...] = jnp.zeros_like(ext)
         for g in range(GROUPS):
             ext[g * BAND_OUT : g * BAND_OUT + LANES, :] += spread[:, g * queries : (g + 1) * queries]
@@ -399,20 +400,7 @@
         hpick = onehot(entry == ext_ref[...])
         rpick = onehot(entry + width == ext_ref[...])
         hgrad = (mm(hpick, high) + mm(hpick, low)).astype(bf16)
-        rgrad = mm(rpick, high) + mm(rpick, low)
-        total = jnp.zeros((taps, filts), f32)
-        for j in range(IMG):
-            rows = corr[:, j, :]
-            for di in range(1, BAND):
-                rows = rows + pltpu.roll(corr[:, di * IMG + j, :], LANES - di * IMG, 1)
-            pick = onehot(iota((taps, LANES), 0) == codes_ref[j : j + 1, :])
-            rhigh, rlow = split(rows)
-            total = total + mm(pick, rhigh, NT) + mm(pick, rlow, NT)
-        rest = jnp.zeros((sums_ref.shape[1] - width, queries), f32)
-        for d in range(sums_ref.shape[0]):
-            sums_ref[d, :width, :] = rgrad
-            sums_ref[d, width:, :] = rest
-            sums_ref[d, width : width + taps, :filts] = total
+        sums_ref[0] = mm(rpick, high) + mm(rpick, low)
         blocks = out_ref.shape[0]
         pick = slot_picks(cap, blocks * cap, orow_ref[...])
         rows = mm(pick, hgrad, NT).astype(bf16)
@@ -420,46 +408,69 @@
             out_ref[d] = rows[d * cap : (d + 1) * cap, :]
 
 
-def sums_rows(width, taps):
-    return -(-(width + taps) // 8) * 8
-
-
-def back(qgt, orow, ext, codes, img, band_t, weight_t, pre, count, cap, taps, copies):
-    _, width, queries = qgt.shape
+def back(vecs, orow, ext, img, band_t, weight_t, pre, count, cap):
+    width, queries = vecs.shape[2:]
     flat = weight_t.shape[1]
     filts = band_t.shape[1] // BAND_OUT
     units = filter_block(filts)
     cols = flat // filts * units
-    rows = sums_rows(width, taps)
-    assert filts <= queries
-    return pl.pallas_call(
-        functools.partial(back_kernel, cap, taps),
+    assert cols % 128 == 0
+    return pl.pallas_call(
+        functools.partial(back_kernel, cap),
         grid=(filts // units,),
         in_specs=[
             whole(orow.shape),
             whole(ext.shape),
-            whole(codes.shape),
-            whole((1, width, queries)),
+            whole((1, 1, width, queries)),
             whole(img.shape),
             pl.BlockSpec((LANES, units * BAND_OUT), lambda s: (0, s)),
             pl.BlockSpec((width, cols), lambda s: (0, s)),
             pl.BlockSpec((cols, queries), lambda s: (s, 0)),
         ],
-        out_specs=[whole((count, cap, width)), whole((copies, rows, queries))],
+        out_specs=[
+            whole((count, cap, width)),
+            whole((1, width, queries)),
+            pl.BlockSpec((units, BAND_OUT, LANES), lambda s: (s, 0, 0)),
+        ],
         out_shape=[
             jax.ShapeDtypeStruct((count, cap, width), bf16),
-            jax.ShapeDtypeStruct((copies, rows, queries), f32),
+            jax.ShapeDtypeStruct((1, width, queries), f32),
+            jax.ShapeDtypeStruct((filts, BAND_OUT, LANES), f32),
         ],
         scratch_shapes=[
+            pltpu.VMEM((cols, width), bf16),
             pltpu.VMEM((units * BAND_OUT, GROUPS * queries), bf16),
             pltpu.VMEM((LANES, GROUPS * queries), f32),
-            pltpu.VMEM((filts, BAND_OUT, LANES), f32),
             pltpu.VMEM((ext.shape[1], queries), f32),
         ],
-        compiler_params=params("arbitrary", mib=28),
+        compiler_params=params("arbitrary"),
         cost_estimate=cost(6e9, 2e7, 2.5e6),
         name="back",
-    )(orow, ext, codes, qgt, img, band_t, weight_t, pre)
+    )(orow, ext, vecs, img, band_t, weight_t, pre)
+
+
+def diag_kernel(taps, codes_ref, corr_ref, out_ref):
+    filts = corr_ref.shape[0]
+    total = jnp.zeros((taps, filts), f32)
+    for j in range(IMG):
+        rows = corr_ref[:, j, :]
+        for di in range(1, BAND):
+            rows = rows + pltpu.roll(corr_ref[:, di * IMG + j, :], LANES - di * IMG, 1)
+        pick = onehot(iota((taps, LANES), 0) == codes_ref[j : j + 1, :])
+        high, low = split(rows)
+        total = total + mm(pick, high, NT) + mm(pick, low, NT)
+    for d in range(out_ref.shape[0]):
+        out_ref[d] = total
+
+
+def filter_sums(corr, codes, taps, copies):
+    return pl.pallas_call(
+        functools.partial(diag_kernel, taps),
+        out_shape=jax.ShapeDtypeStruct((copies, taps, corr.shape[0]), f32),
+        compiler_params=params(),
+        cost_estimate=cost(1e8, 4e6),
+        name="filter_sums",
+    )(codes, corr)
 
 
 def tail_kernel(
@@ -471,7 +482,7 @@
     own = jnp.zeros(own_ref.shape, f32)
     other = jnp.zeros(own_ref.shape, f32)
     for group in pairs(vecs_ref.shape[0]):
-        qvt = beside(vecs_ref[p, 1] for p in group)
+        qvt = beside(vecs_ref[p, 2] for p in group)
         pos = beside(numbers_ref[2 * p + core_ref[0], 3:4, :] for p in group)
         score = mm(tails, qvt)
         target = jnp.where(scand == pos, 1.0 - smooth + smooth / cand, smooth / cand)
@@ -489,14 +500,14 @@
         functools.partial(tail_kernel, cand),
         in_specs=[SMEM] + [VMEM] * 6,
         out_shape=[half, half],
-        compiler_params=params(mib=24),
+        compiler_params=params(),
         cost_estimate=cost(2e9, 3e6, 1e6),
         name="tail_grad",
     )(core, tails, mate, scand, mcand, numbers, vecs)
 
 
 def proj_kernel(
-    core_ref, rtab_ref, ext_ref, band_ref, mate_ref, numbers_ref, vecs_ref, grads_ref,
+    core_ref, rtab_ref, ext_ref, band_ref, mate_ref, numbers_ref, vecs_ref,
     own_ref, other_ref, pick, hmat, rmat,
 ):
     width, rels = rtab_ref.shape
@@ -515,8 +526,8 @@
     for k, out in enumerate((own_ref, other_ref)):
         out[...] = jnp.zeros_like(out)
     for group in pairs(vecs_ref.shape[0]):
-        hvt = beside(vecs_ref[p, 0] for p in group)
-        qgt = beside(grads_ref[p] for p in group)
+        hvt = beside(vecs_ref[p, 1] for p in group)
+        qgt = beside(vecs_ref[p, 0] for p in group)
         rel = beside(numbers_ref[2 * p + core_ref[0], 2:3, :] for p in group)
         rvt = mm(rtab_ref[...], onehot(iota((rels, rel.shape[1]), 0) == rel)).astype(bf16)
         for k, out in enumerate((own_ref, other_ref)):
@@ -525,24 +536,24 @@
             out[...] += mm(qgt, (pre * sigmoid(pre)).astype(bf16), NT)
 
 
-def proj_part(core, rtab_t, ext, band, mate, numbers, vecs, grads):
+def proj_part(core, rtab_t, ext, band, mate, numbers, vecs):
     width = rtab_t.shape[0]
     rows = band.shape[0]
     cols = rows * GROUPS
     half = jax.ShapeDtypeStruct((width, cols), f32)
     return pl.pallas_call(
         proj_kernel,
-        in_specs=[SMEM] + [VMEM] * 7,
+        in_specs=[SMEM] + [VMEM] * 6,
         out_shape=[half, half],
         scratch_shapes=[
             pltpu.VMEM((ext.shape[1], width), bf16),
             pltpu.VMEM((2 * cols, width), bf16),
             pltpu.VMEM((2 * cols, width), bf16),
         ],
-        compiler_params=params(mib=28),
+        compiler_params=params(),
         cost_estimate=cost(6e9, 6e6, 2.5e6),
         name="proj_grad",
-    )(core, rtab_t, ext, band, mate, numbers, vecs, grads)
+    )(core, rtab_t, ext, band, mate, numbers, vecs)
 
 
 def proj_columns(first, cols, filters, chequer_perm, relation_table, numbers, heads, grads):
@@ -566,33 +577,31 @@
     return mm(qg, (pre * sigmoid(pre)).astype(bf16), TN)
 
 
-def rel_kernel(width, core_ref, numbers_ref, sums_ref, rel_ref, filt_ref):
+def rel_kernel(numbers_ref, sums_ref, filt_ref, rel_ref, out_ref):
     total = jnp.zeros(rel_ref.shape, f32)
-    filt = jnp.zeros(filt_ref.shape, f32)
     for group in pairs(sums_ref.shape[0]):
-        rel = beside(numbers_ref[2 * p + core_ref[0], 2:3, :] for p in group)
+        rel = beside(numbers_ref[p, 2:3, :] for p in group)
         pick = onehot(iota((rel_ref.shape[1], rel.shape[1]), 0) == rel)
-        high, low = split(beside(sums_ref[p, :width, :] for p in group))
+        high, low = split(beside(sums_ref[p] for p in group))
         total = total + mm(high, pick, NT) + mm(low, pick, NT)
-        for p in group:
-            filt = filt + sums_ref[p, width:, :]
     rel_ref[...] = total
-    filt_ref[...] = filt
-
-
-def rel_part(core, numbers, sums, width, rels):
-    rows, queries = sums.shape[1:]
-    return pl.pallas_call(
-        functools.partial(rel_kernel, width),
-        in_specs=[SMEM] + [VMEM] * 2,
+    filt = filt_ref[0]
+    for d in range(1, filt_ref.shape[0]):
+        filt = filt + filt_ref[d]
+    out_ref[...] = filt
+
+
+def rel_part(numbers, sums, filt, rels):
+    return pl.pallas_call(
+        rel_kernel,
         out_shape=[
-            jax.ShapeDtypeStruct((width, rels), f32),
-            jax.ShapeDtypeStruct((rows - width, queries), f32),
-        ],
-        compiler_params=params(mib=24),
+            jax.ShapeDtypeStruct((sums.shape[1], rels), f32),
+            jax.ShapeDtypeStruct(filt.shape[1:], f32),
+        ],
+        compiler_params=params(),
         cost_estimate=cost(2e9, 3e6),
         name="rel_grad",
-    )(core, numbers, sums)
+    )(numbers, sums, filt)
 
 
 def entity_kernel(want_ref, srow_ref, own_ref, recv_ref, incoming_ref, out_ref):
@@ -608,7 +617,7 @@
     return pl.pallas_call(
         entity_kernel,
         out_shape=jax.ShapeDtypeStruct((own.shape[0], rows), f32),
-        compiler_params=params(mib=24),
+        compiler_params=params(),
         cost_estimate=cost(1.5e9, 4e6),
         name="entity_grad",
     )(want, srow, own, recv, incoming)
@@ -675,17 +684,15 @@
     ext = jnp.concatenate([chequer_perm[-BAND_OUT:], chequer_perm, chequer_perm[:extra]])[None]
     orow = heads[None, :]
     pre, img, qv, vecs = front(
-        fetched, orow, rel_ids[None, :], rtab_t, ext, band, weight_t, head_cap, copies
+        fetched, orow, rel_ids[None, :], rtab_t, ext, band, weight_t, head_cap
     )
+
+    vecs = score_part(qv, pos, all_tails, vecs, cand, copies)
     core_vecs = gather_core(vecs)
-
-    qgt = score_part(qv, pos, all_tails, cand, copies)
-    core_qgt = gather_core(qgt)
-    outgoing, sums = back(
-        qgt, orow, ext, codes, img, band_t, weight_t, pre, count, head_cap, ks * ks, copies
-    )
-    core_sums = gather_core(sums)
+    outgoing, sums, corr = back(vecs, orow, ext, img, band_t, weight_t, pre, count, head_cap)
+    all_sums = lax.all_gather(sums, "shard", axis=0, tiled=True)
     incoming = exchange(outgoing)
+    filt = exchange(filter_sums(corr, codes, ks * ks, count))
 
     own, other = tail_part(core, tails, mate_tails, slot_cand, mate_cand, numbers, core_vecs, cand)
     entity_grad = entity_sum(want, slot_row, own, swap(other), incoming, rows).T
@@ -696,7 +703,7 @@
         mine, mate = (
             lax.dynamic_slice_in_dim(band, d * unit, unit, axis=0) for d in (me, me ^ 1)
         )
-        own, other = proj_part(core, rtab_t, ext, mine, mate, numbers, core_vecs, core_qgt)
+        own, other = proj_part(core, rtab_t, ext, mine, mate, numbers, core_vecs)
     else:
         own, other = (
             proj_columns(
@@ -704,16 +711,15 @@
                 lax.dynamic_index_in_dim(
                     numbers.reshape(count // 2, 2, 4, queries), me & 1, 1, keepdims=False
                 ),
-                core_vecs[:, 0], core_qgt,
+                core_vecs[:, 1], core_vecs[:, 0],
             )
             for d in (me, me ^ 1)
         )
     proj_grad = (own + swap(other)).T
 
-    part, filt = rel_part(core, numbers, core_sums, width, rels)
-    relation_grad = (part + swap(part)).T
-    filter_grad = (filt + swap(filt))[: ks * ks, :filts].T.reshape(filts, ks, ks)
-    return (entity_grad, relation_grad, filter_grad, proj_grad)
+    relation_grad, filter_grad = rel_part(numbers, all_sums, filt, rels)
+    filter_grad = filter_grad.T.reshape(filts, ks, ks)
+    return (entity_grad, relation_grad.T, filter_grad, proj_grad)
 
 
 def solution(mesh):

time: 178 us -> 163 us (0.916)
  Pallas kernels: 55.2 us -> 84.3 us
  local copies, waits for them, and re-layouts: 32.8 us -> 10.7 us
  waiting for transfers between devices: 35.6 us -> 17.8 us
  other arithmetic: 3.52 us -> 1.16 us
  starting transfers between devices: 21.8 us -> 19.5 us
    unnamed x68 -> x30, local copies, waits for them, and re-layouts: 30.9 us -> 2.91 us
    all_to_all x3 -> x1, waiting for transfers between devices: 20.7 us -> 0.48 us  [gather_core(): lax.all_to_all(x, 'shard', split_axis=0, concat_axis=0, axis_index_groups...]
    pallas_call x3 -> x4, Pallas kernels: 29.1 us -> 43.4 us  [the longest x1 20.5 us: back(): pl.pallas_call(functools.partial(back_kernel, cap), grid=(filts // units,...]
    all_to_all x3 -> x1, starting transfers between devices: 13.2 us -> 3.57 us  [gather_core(): lax.all_to_all(x, 'shard', split_axis=0, concat_axis=0, axis_index_groups...]
    all_to_all x2 -> x3, starting transfers between devices: 7.26 us -> 14.7 us  [exchange(): return lax.all_to_all(x, 'shard', split_axis=0, concat_axis=0, tiled=True)]
    all_gather x1, waiting for transfers between devices: 2.7 us -> 7.61 us  [shards(): all_tails = lax.all_gather(tails_t, 'shard', axis=0, tiled=True)]
    pallas_call x1, Pallas kernels: 7.96 us -> 12.2 us  [front(): pl.pallas_call(functools.partial(front_kernel, cap), grid=(filts // units...]
    all_to_all x2 -> x3, waiting for transfers between devices: 9.77 us -> 6.76 us  [exchange(): return lax.all_to_all(x, 'shard', split_axis=0, concat_axis=0, tiled=True)]
  transfers between devices with their start and end apart: 12 -> 10, of which waited for: 6 -> 4; matrix products, arithmetic and copies ran while one was open for 2% -> 5% of each run, Pallas kernels for 29% -> 46%
where the time goes in v4:
time: 163 us; the launch traced here: 162 us
  Pallas kernels  84.3 us (52%)
  starting transfers between devices  19.5 us (12%)
  waiting for transfers between devices  17.8 us (11%)
  between operations  14.2 us (9%)
  blocking collectives  13.9 us (9%)
  local copies, waits for them, and re-layouts  10.7 us (7%)
    pallas_call x1, Pallas kernels, back(): pl.pallas_call(functools.partial(back_kernel, cap), grid=(filts // units,...  20.5 us
    all_to_all x3, starting transfers between devices, exchange(): return lax.all_to_all(x, 'shard', split_axis=0, concat_axis=0, tiled=True)  14.7 us
    all_to_all x1, blocking collectives, exchange(): return lax.all_to_all(x, 'shard', split_axis=0, concat_axis=0, tiled=True)  13.9 us
    pallas_call x1, Pallas kernels, front(): pl.pallas_call(functools.partial(front_kernel, cap), grid=(filts // units...  12.2 us
    pallas_call x1, Pallas kernels, proj_part(): pl.pallas_call(proj_kernel, in_specs=[SMEM] + [VMEM] * 6, out_shape=[half...  11.8 us
    all_gather x1, waiting for transfers between devices, shards(): all_tails = lax.all_gather(tails_t, 'shard', axis=0, tiled=True)  7.61 us
    all_to_all x3, waiting for transfers between devices, exchange(): return lax.all_to_all(x, 'shard', split_axis=0, concat_axis=0, tiled=True)  6.76 us
    pallas_call x1, Pallas kernels, rel_part(): pl.pallas_call(rel_kernel, out_shape=[jax.ShapeDtypeStruct((sums.shape[1]...  6.23 us
  transfers between devices with their start and end apart: 10, of which 4 were waited for; matrix products, arithmetic and copies ran while one was open for 5% of the time, Pallas kernels for 46%

profile of v4, /device:TPU:0, one launch (start us, length us, event | category | flops | bytes accessed | tf_op | source)
XLA Modules:
  0.0 161.6 jit_solution(13907951287423406204)
XLA Ops:
  7.3 4.9 %pack_tails.1 = (bf16[512,200]{1,0:T(8,128)(2,1)}, bf16[1,200,512]{2,1,0:T(8,128)(2,1)}, s32[512,1]{1,0:T(8,128)}, s32[512,1]{1,0:T(8,128)}) custom-call(s32[1]{0:T(128)} %bitcast.me_ref, s32[32,128]{1,0:T(8,128)} %bitcast.22, s32[32,128]{1,0:T(8,128)} %bitcast.38, bf16[200,2048]{1,0:T(8,128)(2,1)} %bitcast.34), custom_call_target="tpu_custom_call" | custom-call | flops 1000000000 | bytes 2000000 | tf_op jit(solution)/shard_map/pack_tails/pallas_call | solution.py:151
  12.3 13.9 %all_to_all.25.numbers_ref = s32[16,4,128]{2,1,0:T(4,128)} all-to-all(s32[16,4,128]{2,1,0:T(4,128)S(1)} %broadcast_in_dim.4), channel_id=1, replica_groups=mesh['parts'=2,'shard'=16] {'shard'}, dimensions={0} | all-to-all | bytes 65536 | tf_op jit(solution)/shard_map/all_to_all | solution.py:657
  26.2 2.6 %find_heads.1 = (bf16[16,16,200]{2,1,0:T(8,128)(2,1)}, s32[256,1]{1,0:T(8,128)}) custom-call(s32[1]{0:T(128)} %bitcast.me_ref, bf16[200,2048]{1,0:T(8,128)(2,1)} %bitcast.35, s32[16,4,128]{2,1,0:T(4,128)} %all_to_all.25.numbers_ref), custom_call_target="tpu_custom_call" | custom-call | flops 300000000 | bytes 2000000 | tf_op jit(solution)/shard_map/find_heads/pallas_call | solution.py:189
  28.8 3.5 %all-to-all-start.1 = ((bf16[16,16,200]{2,1,0:T(8,128)(2,1)}), bf16[16,16,200]{2,1,0:T(8,128)(2,1)S(1)}, u32[]{:S(2)}, u32[]{:S(2)}) async-start(bf16[16,16,200]{2,1,0:T(8,128)(2,1)} %get-tuple-element.29), calls=%async_computation.1 | async-start | bytes 262144 | tf_op jit(solution)/shard_map/all_to_all | solution.py:657
  32.4 0.6 broadcast_in_dim.5.ext_ref
  33.1 0.7 copy.18.filt_ref
  33.8 2.1 %pos_slots.1.pos_ref = s32[128,1]{1,0:T(8,128)} custom-call(s32[1,4096]{1,0:T(1,128)} %bitcast.23, s32[1,128]{1,0:T(1,128)} %bitcast.24), custom_call_target="tpu_custom_call" | custom-call | flops 10000000 | bytes 100000 | tf_op jit(solution)/shard_map/pos_slots/pallas_call | solution.py:227
  35.9 5.2 %band.1 = (bf16[3840,256]{1,0:T(8,128)(2,1)}, bf16[256,3840]{1,0:T(8,128)(2,1)}) custom-call(s32[20,256]{1,0:T(8,128)} %constant.14.clone.codes_ref, bf16[48,81]{1,0:T(8,128)(2,1)} %copy.18.filt_ref), custom_call_target="tpu_custom_call" | custom-call | flops 40000000 | bytes 4000000 | tf_op jit(solution)/shard_map/band/pallas_call | solution.py:94
  41.1 0.7 copy-done.2
  41.7 12.2 %front.1 = (f32[19200,128]{1,0:T(8,128)}, bf16[256,640]{1,0:T(8,128)(2,1)}, bf16[128,200]{1,0:T(8,128)(2,1)}, bf16[2,200,128]{2,1,0:T(8,128)(2,1)}) custom-call(bf16[16,16,200]{2,1,0:T(8,128)(2,1)} %copy-done.2, s32[1,128]{1,0:T(1,128)} %bitcast.29, s32[1,128]{1,0:T(1,128)} %bitcast.27, bf16[200,1387]{1,0:T(8,128)(2,1)} %bitcast.36, ...), custom_call_target="tpu_custom_call" | custom-call | flops 4000000000 | bytes 24000000 | tf_op jit(solution)/shard_map/front/pallas_call | solution.py:299
  54.0 7.6 %all-gather.3.cloned.1.call-done.tails_ref = bf16[16,200,512]{2,1,0:T(8,128)(2,1)} async-done(((bf16[1,200,512]{2,1,0:T(8,128)(2,1)}), bf16[16,200,512]{2,1,0:T(8,128)(2,1)}) %all-gather.3.cloned.1.call-update) | async-done | bytes 3276816 | tf_op jit(solution)/shard_map/all_gather | solution.py:675
  61.6 5.6 %score.1.qgt_ref = bf16[8,3,200,128]{3,2,1,0:T(8,128)(2,1)} custom-call(s32[128,1]{1,0:T(8,128)} %pos_slots.1.pos_ref, bf16[128,200]{1,0:T(8,128)(2,1)} %get-tuple-element.31.qv_ref, bf16[16,200,512]{2,1,0:T(8,128)(2,1)} %all-gather.3.cloned.1.call-done.tails_ref, bf16[2,200,128]{2,1,0:T(8,128)(2,1)} %get-tuple-element.33.vecs_ref), custom_call_target="tpu_custom_call" | custom-call | flops 1000000000 | bytes 3000000 | tf_op jit(solution)/shard_map/score/pallas_call | solution.py:355
  67.2 3.6 %all-to-all-start.2 = ((bf16[8,3,200,128]{3,2,1,0:T(8,128)(2,1)}), bf16[8,3,200,128]{3,2,1,0:T(8,128)(2,1)S(1)}, u32[]{:S(2)}, u32[]{:S(2)}) async-start(bf16[8,3,200,128]{3,2,1,0:T(8,128)(2,1)} %score.1.qgt_ref), calls=%async_computation.2 | async-start | bytes 2457600 | tf_op jit(solution)/shard_map/all_to_all | solution.py:661
  71.0 20.5 %back.1 = (bf16[16,16,200]{2,1,0:T(8,128)(2,1)}, f32[1,200,128]{2,1,0:T(8,128)}, f32[48,80,256]{2,1,0:T(8,128)}) custom-call(s32[1,128]{1,0:T(1,128)} %bitcast.30, s32[1,576]{1,0:T(1,128)} %broadcast_in_dim.5.ext_ref, bf16[8,3,200,128]{3,2,1,0:T(8,128)(2,1)} %score.1.qgt_ref, bf16[256,640]{1,0:T(8,128)(2,1)} %get-tuple-element.36.img_ref, ...), custom_call_target="tpu_custom_call" | custom-call | flops 6000000000 | bytes 20000000 | tf_op jit(solution)/shard_map/back/pallas_call | solution.py:418
  91.8 1.7 %constant_dynamic-slice_fusion = (bf16[240,256]{1,0:T(8,128)(2,1)}, bf16[240,256]{1,0:T(8,128)(2,1)}) fusion(bf16[3840,256]{1,0:T(8,128)(2,1)} %get-tuple-element.30.band_ref, s32[]{:T(128)S(6)} %select_n.7, s32[]{:T(128)S(6)} %select_n.6), kind=kLoop, calls=%fused_computation.3 | loop fusion | bytes 491528 | tf_op jit(solution)/shard_map/dynamic_slice | solution.py:704
  93.5 4.9 %filter_sums.1 = f32[16,81,48]{2,1,0:T(8,128)} custom-call(s32[20,256]{1,0:T(8,128)} %constant.14.clone.codes_ref, f32[48,80,256]{2,1,0:T(8,128)} %get-tuple-element.41.corr_ref), custom_call_target="tpu_custom_call" | custom-call | flops 100000000 | bytes 4000000 | tf_op jit(solution)/shard_map/filter_sums/pallas_call | solution.py:467
  98.4 2.1 %copy.19 = f32[16,81,48]{1,2,0:T(8,128)} copy(f32[16,81,48]{2,1,0:T(8,128)} %filter_sums.1) | data formatting | bytes 497664 | tf_op jit(solution)/shard_map/filter_sums/pallas_call | solution.py:467
  100.5 0.5 all-to-all-done.2.vecs_ref
  101.0 5.2 %all-to-all-start.4 = ((f32[16,81,48]{1,2,0:T(8,128)}), f32[16,81,48]{1,2,0:T(8,128)S(1)}, u32[]{:S(2)}, u32[]{:S(2)}) async-start(f32[16,81,48]{1,2,0:T(8,128)} %copy.19), calls=%async_computation.4 | async-start | bytes 786432 | tf_op jit(solution)/shard_map/all_to_all | solution.py:657
  106.2 11.8 %proj_grad.1 = (f32[200,1200]{1,0:T(8,128)}, f32[200,1200]{1,0:T(8,128)}) custom-call(s32[1]{0:T(128)} %bitcast.8.core_ref, bf16[200,1387]{1,0:T(8,128)(2,1)} %bitcast.37, s32[1,576]{1,0:T(1,128)} %broadcast_in_dim.5.ext_ref, bf16[240,256]{1,0:T(8,128)(2,1)} %get-tuple-element.47.band_ref, bf16[240,256]{1,0:T(8,128)(2,1)} %get-tuple-element.46.mate_ref, ...), custom_call_target="tpu_custom_call" | custom-call | flops 6000000000 | bytes 6000000 | tf_op jit(solution)/shard_map/proj_grad/pallas_call | solution.py:544
  118.5 2.9 %collective-permute-done.1.mcand_ref = s32[512,1]{1,0:T(8,128)S(1)} collective-permute-done((s32[512,1]{1,0:T(8,128)S(1)}, s32[512,1]{1,0:T(8,128)S(1)}, u32[]{:S(2)}, u32[]{:S(2)}) %collective-permute-start.1) | collective-permute-done | bytes 2080 | tf_op jit(solution)/shard_map/ppermute | solution.py:654
  121.3 0.7 copy-done.14
  122.1 0.7 copy-done.13
  122.8 4.3 %tail_grad.1 = (f32[200,512]{1,0:T(8,128)}, f32[200,512]{1,0:T(8,128)}) custom-call(s32[1]{0:T(128)} %bitcast.8.core_ref, bf16[512,200]{1,0:T(8,128)(2,1)} %get-tuple-element.27.tails_ref, bf16[512,200]{1,0:T(8,128)(2,1)} %copy-done.13, s32[512,1]{1,0:T(8,128)} %get-tuple-element.28.scand_ref, s32[512,1]{1,0:T(8,128)} %copy-done.14, ...), custom_call_target="tpu_custom_call" | custom-call | flops 2000000000 | bytes 3000000 | tf_op jit(solution)/shard_map/tail_grad/pallas_call | solution.py:499
  127.2 6.0 %all-to-all-start.3 = ((bf16[16,16,200]{2,1,0:T(8,128)(2,1)}), bf16[16,16,200]{2,1,0:T(8,128)(2,1)S(1)}, u32[]{:S(2)}, u32[]{:S(2)}) async-start(bf16[16,16,200]{2,1,0:T(8,128)(2,1)} %get-tuple-element.39), calls=%async_computation.3 | async-start | bytes 262144 | tf_op jit(solution)/shard_map/all_to_all | solution.py:657
  133.2 1.2 copy.20.filt_ref
  134.4 6.8 %all-to-all-done.3.incoming_ref = bf16[16,16,200]{2,1,0:T(8,128)(2,1)S(1)} async-done(((bf16[16,16,200]{2,1,0:T(8,128)(2,1)}), bf16[16,16,200]{2,1,0:T(8,128)(2,1)S(1)}, u32[]{:S(2)}, u32[]{:S(2)}) %all-to-all-start.3) | async-done | bytes 102432 | tf_op jit(solution)/shard_map/all_to_all | solution.py:657
  141.2 0.6 copy-done.3
  142.0 4.0 %entity_grad.1 = f32[200,2048]{1,0:T(8,128)} custom-call(s32[256,1]{1,0:T(8,128)} %get-tuple-element.25.want_ref, s32[512,1]{1,0:T(8,128)} %get-tuple-element.26.srow_ref, f32[200,512]{1,0:T(8,128)} %get-tuple-element.34.own_ref, f32[200,512]{1,0:T(8,128)} %copy-done.10, bf16[16,16,200]{2,1,0:T(8,128)(2,1)} %copy-done.3), custom_call_target="tpu_custom_call" | custom-call | flops 1500000000 | bytes 4000000 | tf_op jit(solution)/shard_map/entity_grad/pallas_call | solution.py:617
  146.0 6.2 %rel_grad.1 = (f32[200,1387]{1,0:T(8,128)}, f32[81,48]{1,0:T(8,128)}) custom-call(s32[16,4,128]{2,1,0:T(4,128)} %all_to_all.25.numbers_ref, f32[16,200,128]{2,1,0:T(8,128)} %all-gather.5.cloned.1.call-done.sums_ref, f32[16,81,48]{2,1,0:T(8,128)} %copy.20.filt_ref), custom_call_target="tpu_custom_call" | custom-call | flops 2000000000 | bytes 3000000 | tf_op jit(solution)/shard_map/rel_grad/pallas_call | solution.py:595
  152.2 1.4 reshape.29
  153.7 1.1 add_bitcast_fusion
  (47 shorter events, 1.6 us)
Async XLA Ops:
  7.2 5.0 %copy-start.5 = (s32[128]{0:T(128)S(1)}, s32[128]{0:T(128)}, u32[]{:S(2)}) copy-start(s32[128]{0:T(128)} %param.20) | copy-start | bytes 1540
  7.2 5.0 %copy-start.8 = (s32[128]{0:T(128)S(1)}, s32[128]{0:T(128)}, u32[]{:S(2)}) copy-start(s32[128]{0:T(128)} %param.19) | copy-start | bytes 1540
  7.2 5.0 %copy-start.7 = (s32[128]{0:T(128)S(1)}, s32[128]{0:T(128)}, u32[]{:S(2)}) copy-start(s32[128]{0:T(128)} %param.18) | copy-start | bytes 1540
  7.2 5.0 %copy-start.9 = (s32[128,1]{0,1:T(1,128)S(1)}, s32[128,1]{0,1:T(1,128)}, u32[]{:S(2)}) copy-start(s32[128,1]{0,1:T(1,128)} %param.17) | copy-start | bytes 1540
  7.2 54.4 %all-gather.3.cloned.1.call-start = ((), (), s32[]{:S(2)}) async-start(), calls=%async_computation.5 | async-start | bytes 3481600 | tf_op jit(solution)/shard_map/all_gather | solution.py:675
  7.3 25.0 %copy-start.6 = (s32[400]{0:T(512)S(1)}, s32[400]{0:T(512)}, u32[]{:S(2)}) copy-start(s32[400]{0:T(512)} %param.16) | copy-start | bytes 4804
  7.3 25.1 %slice-start = ((s32[400]{0:T(512)}), s32[96]{0:T(128)S(1)}, s32[]{:S(2)}) async-start(s32[400]{0:T(512)} %param.16), calls=%async_computation.7 | async-start | bytes 1024 | tf_op jit(solution)/shard_map/slice | solution.py:684
  7.3 25.8 %copy-start.4 = (bf16[48,9,9]{0,2,1:T(8,128)(2,1)S(1)}, bf16[48,9,9]{0,2,1:T(8,128)(2,1)}, u32[]{:S(2)}) copy-start(bf16[48,9,9]{0,2,1:T(8,128)(2,1)} %param.14) | copy-start | bytes 23332
  28.8 12.3 %all-to-all-start.1 = ((bf16[16,16,200]{2,1,0:T(8,128)(2,1)}), bf16[16,16,200]{2,1,0:T(8,128)(2,1)S(1)}, u32[]{:S(2)}, u32[]{:S(2)}) async-start(bf16[16,16,200]{2,1,0:T(8,128)(2,1)} %get-tuple-element.29), calls=%async_computation.1 | async-start | bytes 262144 | tf_op jit(solution)/shard_map/all_to_all | solution.py:657
  41.1 0.7 copy-start.2
  67.2 33.8 %all-to-all-start.2 = ((bf16[8,3,200,128]{3,2,1,0:T(8,128)(2,1)}), bf16[8,3,200,128]{3,2,1,0:T(8,128)(2,1)S(1)}, u32[]{:S(2)}, u32[]{:S(2)}) async-start(bf16[8,3,200,128]{3,2,1,0:T(8,128)(2,1)} %score.1.qgt_ref), calls=%async_computation.2 | async-start | bytes 2457600 | tf_op jit(solution)/shard_map/all_to_all | solution.py:661
  70.7 75.3 %all-gather.5.cloned.1.call-start = ((), (), s32[]{:S(2)}) async-start(), calls=%async_computation.6 | async-start | bytes 1740800 | tf_op jit(solution)/shard_map/all_gather | solution.py:693
  71.0 20.5 %copy-start.11 = (bf16[512,200]{1,0:T(8,128)(2,1)S(1)}, bf16[512,200]{1,0:T(8,128)(2,1)}, u32[]{:S(2)}) copy-start(bf16[512,200]{1,0:T(8,128)(2,1)} %get-tuple-element.27.tails_ref) | copy-start | bytes 614404
  91.5 29.9 %collective-permute-start = (bf16[512,200]{1,0:T(8,128)(2,1)S(1)}, bf16[512,200]{1,0:T(8,128)(2,1)S(1)}, u32[]{:S(2)}, u32[]{:S(2)}) collective-permute-start(bf16[512,200]{1,0:T(8,128)(2,1)S(1)} %copy-done.11), channel_id=1, source_target_pairs={{0,1},{1,0},{2,3},{3,2},{4,5},{5,4},{6,7},{7,6},{8,9},{9,8},{10,11... | collective-permute-start | bytes 614408 | tf_op jit(solution)/shard_map/ppermute | solution.py:654
  101.0 5.2 %copy-start = (bf16[8,3,200,128]{3,2,1,0:T(8,128)(2,1)}, bf16[8,3,200,128]{3,2,1,0:T(8,128)(2,1)S(1)}, u32[]{:S(2)}) copy-start(bf16[8,3,200,128]{3,2,1,0:T(8,128)(2,1)S(1)} %all-to-all-done.2.vecs_ref) | copy-start | bytes 3686404
  101.0 26.2 %all-to-all-start.4 = ((f32[16,81,48]{1,2,0:T(8,128)}), f32[16,81,48]{1,2,0:T(8,128)S(1)}, u32[]{:S(2)}, u32[]{:S(2)}) async-start(f32[16,81,48]{1,2,0:T(8,128)} %copy.19), calls=%async_computation.4 | async-start | bytes 786432 | tf_op jit(solution)/shard_map/all_to_all | solution.py:657
  106.2 12.2 %copy-start.12 = (s32[512,1]{1,0:T(8,128)S(1)}, s32[512,1]{1,0:T(8,128)}, u32[]{:S(2)}) copy-start(s32[512,1]{1,0:T(8,128)} %get-tuple-element.28.scand_ref) | copy-start | bytes 6148
  118.0 35.7 %collective-permute-start.3 = (f32[200,1200]{1,0:T(8,128)}, f32[200,1200]{1,0:T(8,128)S(1)}, u32[]{:S(2)}, u32[]{:S(2)}) collective-permute-start(f32[200,1200]{1,0:T(8,128)} %get-tuple-element.45), channel_id=1, source_target_pairs={{0,1},{1,0},{2,3},{3,2},{4,5},{5,4},{6,7},{7,6},{8,9},{9,8},{10,11... | collective-permute-start | bytes 2880008 | tf_op jit(solution)/shard_map/ppermute | solution.py:654
  118.4 3.0 %collective-permute-start.1 = (s32[512,1]{1,0:T(8,128)S(1)}, s32[512,1]{1,0:T(8,128)S(1)}, u32[]{:S(2)}, u32[]{:S(2)}) collective-permute-start(s32[512,1]{1,0:T(8,128)S(1)} %copy-done.12), channel_id=1, source_target_pairs={{0,1},{1,0},{2,3},{3,2},{4,5},{5,4},{6,7},{7,6},{8,9},{9,8},{10,11... | collective-permute-start | bytes 6152 | tf_op jit(solution)/shard_map/ppermute | solution.py:654
  121.3 0.7 copy-start.14
  122.1 0.7 copy-start.13
  127.1 14.1 %collective-permute-start.2 = (f32[200,512]{1,0:T(8,128)}, f32[200,512]{1,0:T(8,128)S(1)}, u32[]{:S(2)}, u32[]{:S(2)}) collective-permute-start(f32[200,512]{1,0:T(8,128)} %get-tuple-element.35), channel_id=1, source_target_pairs={{0,1},{1,0},{2,3},{3,2},{4,5},{5,4},{6,7},{7,6},{8,9},{9,8},{10,11... | collective-permute-start | bytes 1228808 | tf_op jit(solution)/shard_map/ppermute | solution.py:654
  127.2 14.0 %all-to-all-start.3 = ((bf16[16,16,200]{2,1,0:T(8,128)(2,1)}), bf16[16,16,200]{2,1,0:T(8,128)(2,1)S(1)}, u32[]{:S(2)}, u32[]{:S(2)}) async-start(bf16[16,16,200]{2,1,0:T(8,128)(2,1)} %get-tuple-element.39), calls=%async_computation.3 | async-start | bytes 262144 | tf_op jit(solution)/shard_map/all_to_all | solution.py:657
  141.2 0.7 copy-start.3
  141.2 0.8 copy-start.10
  146.0 7.7 %copy-start.1 = (f32[200,1200]{1,0:T(8,128)S(1)}, f32[200,1200]{1,0:T(8,128)}, u32[]{:S(2)}) copy-start(f32[200,1200]{1,0:T(8,128)} %get-tuple-element.44) | copy-start | bytes 2880004
Sparse Core Ops, SparseCore 0:
  12.3 49.2 all-gather.2
  91.6 43.1 all-gather.4

commit v5 on v4

--- a/solution.py
+++ b/solution.py
@@ -116,10 +116,9 @@
     return jnp.concatenate(list(blocks), axis=1)
 
 
-def pack_kernel(shift, me_ref, owner_ref, row_ref, table_ref, tails_ref, tails_t_ref, cand_ref, srow_ref):
-    cap = tails_ref.shape[0]
-    lines = owner_ref.shape[0]
-    mine = owner_ref[...] == me_ref[0]
+def slot_values(owner, device, value, cap):
+    lines = owner.shape[0]
+    mine = owner == device
     mine_b = onehot(mine)
     before = onehot(iota((128, 128), 0) < iota((128, 128), 1))
     rank = mm(mine_b, before)
@@ -127,40 +126,54 @@
     upper = onehot(iota((lines, lines), 1) < iota((lines, lines), 0))
     offset = mm(upper, totals.astype(bf16))
     key = jnp.where(mine, (rank + offset).astype(i32), -1)
-    code = row_ref[...] * (1 << shift) + iota((lines, 128), 0) * 128 + iota((lines, 128), 1) + 1
-    code = code.astype(f32)
+    value = (value + 1).astype(f32)
     slots = iota((cap, 128), 0)
     total = jnp.zeros((cap, 128), f32)
     for r in range(lines):
-        total = total + jnp.where(slots == key[r : r + 1, :], code[r : r + 1, :], 0.0)
-    found = jnp.sum(total, axis=1, keepdims=True).astype(i32) - 1
-    live = found >= 0
-    srow = jnp.where(live, lax.shift_right_arithmetic(found, shift), -1)
-    cand_ref[...] = jnp.where(live, found & ((1 << shift) - 1), -1)
+        total = total + jnp.where(slots == key[r : r + 1, :], value[r : r + 1, :], 0.0)
+    return jnp.sum(total, axis=1, keepdims=True).astype(i32) - 1
+
+
+def pack_kernel(me_ref, owner_ref, row_ref, table_ref, tails_t_ref, srow_ref):
+    cap = srow_ref.shape[0]
+    srow = slot_values(owner_ref[...], me_ref[0], row_ref[...], cap)
     srow_ref[...] = srow
     pick = onehot(iota((cap, table_ref.shape[1]), 1) == srow)
-    tails_ref[...] = mm(pick, table_ref[...], NT).astype(bf16)
     tails_t_ref[0] = mm(table_ref[...], pick, NT).astype(bf16)
 
 
 def pack_tails(me, tail_owners, tail_row, table_t, cap):
-    cand = tail_row.shape[0]
-    shift = int(math.log2(cand))
-    width, rows = table_t.shape
-    assert 1 << shift == cand and cand * rows < 1 << 24 and cand % 128 == 0
-    return pl.pallas_call(
-        functools.partial(pack_kernel, shift),
+    assert tail_row.shape[0] % 128 == 0
+    return pl.pallas_call(
+        pack_kernel,
         in_specs=[SMEM] + [VMEM] * 3,
         out_shape=[
-            jax.ShapeDtypeStruct((cap, width), bf16),
-            jax.ShapeDtypeStruct((1, width, cap), bf16),
-            jax.ShapeDtypeStruct((cap, 1), i32),
+            jax.ShapeDtypeStruct((1, table_t.shape[0], cap), bf16),
             jax.ShapeDtypeStruct((cap, 1), i32),
         ],
         compiler_params=params(),
         cost_estimate=cost(1e9, 2e6),
         name="pack_tails",
     )(me, tail_owners.reshape(-1, 128), tail_row.reshape(-1, 128), table_t)
+
+
+def cand_kernel(me_ref, owner_ref, out_ref):
+    cap = out_ref.shape[1]
+    owner = owner_ref[...]
+    index = iota(owner.shape, 0) * 128 + iota(owner.shape, 1)
+    for k in range(2):
+        out_ref[k] = slot_values(owner, me_ref[0] ^ k, index, cap)
+
+
+def slot_cands(me, tail_owners, cap):
+    return pl.pallas_call(
+        cand_kernel,
+        in_specs=[SMEM, VMEM],
+        out_shape=jax.ShapeDtypeStruct((2, cap, 1), i32),
+        compiler_params=params(),
+        cost_estimate=cost(1e8, 1e6),
+        name="slot_cands",
+    )(me, tail_owners.reshape(-1, 128))
 
 
 def found_kernel(cap, me_ref, table_ref, numbers_ref, found_ref, want_ref, scr):
@@ -245,7 +258,7 @@
 
 def front_kernel(
     cap, fetched_ref, orow_ref, rel_ref, rtab_ref, ext_ref, band_ref, w_ref,
-    pre_ref, img_ref, qv_ref, vecs_ref, feats, acc, ext,
+    slope_ref, turned_ref, img_ref, qv_ref, vecs_ref, feats, acc, ext,
 ):
     s = pl.program_id(0)
     width, queries = acc.shape
@@ -255,7 +268,8 @@
         rows = jnp.concatenate([fetched_ref[d] for d in range(fetched_ref.shape[0])], axis=0)
         pick = slot_picks(cap, rows.shape[0], orow_ref[...])
         hvt = mm(rows, pick, TN).astype(bf16)
-        vecs_ref[0] = hvt
+        for d in range(vecs_ref.shape[0]):
+            vecs_ref[d, 0] = hvt
         rels = rtab_ref.shape[1]
         rvt = mm(rtab_ref[...], onehot(iota((rels, queries), 0) == rel_ref[...])).astype(bf16)
         entry = iota((width, ext_ref.shape[1]), 0)
@@ -269,33 +283,41 @@
     units = band_ref.shape[0] // BAND_OUT
     flat = GROUPS * BAND_OUT
     pre = mm(band_ref[...], img_ref[...])
-    act = (pre * sigmoid(pre)).astype(bf16)
+    sig = sigmoid(pre)
+    act = (pre * sig).astype(bf16)
+    slope = sig * (1.0 + pre * (1.0 - sig))
     for f in range(units):
         for g in range(GROUPS):
             rows = slice(f * flat + g * BAND_OUT, f * flat + (g + 1) * BAND_OUT)
             part = slice(f * BAND_OUT, (f + 1) * BAND_OUT)
             lanes = slice(g * queries, (g + 1) * queries)
-            pre_ref[rows, :] = pre[part, lanes]
+            slope_ref[rows, :] = slope[part, lanes]
             feats[rows, :] = act[part, lanes]
     acc[...] += mm(w_ref[...], feats[...])
+    eye = onehot(iota((128, 128), 0) == iota((128, 128), 1))
+    for c in range(0, turned_ref.shape[0], 128):
+        turned_ref[c : c + 128, :] = mm(eye, w_ref[:, c : c + 128], NT).astype(bf16)
 
     @pl.when(s == pl.num_programs(0) - 1)
     def _():
         query = acc[...]
         qv_ref[...] = query.T.astype(bf16)
-        vecs_ref[1] = query.astype(bf16)
+        qvt = query.astype(bf16)
+        for d in range(vecs_ref.shape[0]):
+            vecs_ref[d, 1] = qvt
 
 
 def filter_block(filts):
     return math.gcd(filts, 8)
 
 
-def front(fetched, orow, rel_row, rtab_t, ext, band, weight_t, cap):
+def front(fetched, orow, rel_row, rtab_t, ext, band, weight_t, cap, copies):
     queries = orow.shape[1]
     width, flat = weight_t.shape
     filts = band.shape[0] // BAND_OUT
     units = filter_block(filts)
     cols = flat // filts * units
+    assert cols % 128 == 0
     return pl.pallas_call(
         functools.partial(front_kernel, cap),
         grid=(filts // units,),
@@ -310,15 +332,17 @@
         ],
         out_specs=[
             pl.BlockSpec((cols, queries), lambda s: (s, 0)),
+            pl.BlockSpec((cols, width), lambda s: (s, 0)),
             whole((LANES, GROUPS * queries)),
             whole((queries, width)),
-            whole((2, width, queries)),
+            whole((copies, 2, width, queries)),
         ],
         out_shape=[
             jax.ShapeDtypeStruct((flat, queries), f32),
+            jax.ShapeDtypeStruct((flat, width), bf16),
             jax.ShapeDtypeStruct((LANES, GROUPS * queries), bf16),
             jax.ShapeDtypeStruct((queries, width), bf16),
-            jax.ShapeDtypeStruct((2, width, queries), bf16),
+            jax.ShapeDtypeStruct((copies, 2, width, queries), bf16),
         ],
         scratch_shapes=[
             pltpu.VMEM((cols, queries), bf16),
@@ -331,42 +355,58 @@
     )(fetched, orow, rel_row, rtab_t, ext, band, weight_t)
 
 
-def score_kernel(cand, pos_ref, qv_ref, tails_ref, vecs_ref, out_ref):
+def score_kernel(cand, pos_ref, qv_ref, tails_ref, out_ref, acc):
+    step = pl.program_id(0)
+
+    @pl.when(step == 0)
+    def _():
+        acc[...] = jnp.zeros_like(acc)
+
     qv = qv_ref[...]
     queries = qv.shape[0]
-    owners, _, cap = tails_ref.shape
-    total = jnp.zeros(qv.shape, f32)
-    for b in range(owners):
+    blocks, _, cap = tails_ref.shape
+    total = acc[...]
+    for b in range(blocks):
         block = tails_ref[b]
         score = mm(qv, block)
-        here = iota((queries, cap), 1) + b * cap
+        here = iota((queries, cap), 1) + (step * blocks + b) * cap
         target = jnp.where(here == pos_ref[...], 1.0 - smooth + smooth / cand, smooth / cand)
         grad = ((sigmoid(score) - target) * loss_weight).astype(bf16)
         total = total + mm(grad, block, NT)
-    qgt = total.T.astype(bf16)
-    for d in range(out_ref.shape[0]):
-        out_ref[d, 0] = qgt
-        out_ref[d, 1] = vecs_ref[0]
-        out_ref[d, 2] = vecs_ref[1]
-
-
-def score_part(qv, pos, tails, vecs, cand, copies):
+    acc[...] = total
+
+    @pl.when(step == pl.num_programs(0) - 1)
+    def _():
+        out_ref[0] = total.T.astype(bf16)
+
+
+def score_part(qv, pos, tails, cand):
     queries, width = qv.shape
+    owners, _, cap = tails.shape
+    blocks = math.gcd(owners, max(1, 2048 // cap))
     return pl.pallas_call(
         functools.partial(score_kernel, cand),
-        out_shape=jax.ShapeDtypeStruct((copies, 3, width, queries), bf16),
-        compiler_params=params(),
+        grid=(owners // blocks,),
+        in_specs=[
+            whole(pos.shape),
+            whole(qv.shape),
+            pl.BlockSpec((blocks, width, cap), lambda s: (s, 0, 0)),
+        ],
+        out_specs=whole((1, width, queries)),
+        out_shape=jax.ShapeDtypeStruct((1, width, queries), bf16),
+        scratch_shapes=[pltpu.VMEM((queries, width), f32)],
+        compiler_params=params("arbitrary"),
         cost_estimate=cost(1e9, 3e6, 5e5),
         name="score",
-    )(pos, qv, tails, vecs)
+    )(pos, qv, tails)
 
 
 def back_kernel(
-    cap, orow_ref, ext_ref, qgt_ref, img_ref, bandt_ref, w_ref, pre_ref,
-    out_ref, sums_ref, corr_ref, turned, fgrad, spread, ext,
+    cap, orow_ref, ext_ref, qgt_ref, img_ref, bandt_ref, w_ref, slope_ref,
+    out_ref, sums_ref, corr_ref, fgrad, spread, ext,
 ):
     s = pl.program_id(0)
-    width, queries = qgt_ref.shape[2:]
+    _, width, queries = qgt_ref.shape
 
     @pl.when(s == 0)
     def _():
@@ -374,15 +414,10 @@
 
     units = bandt_ref.shape[1] // BAND_OUT
     flat = GROUPS * BAND_OUT
-    eye = onehot(iota((128, 128), 0) == iota((128, 128), 1))
-    for c in range(0, turned.shape[0], 128):
-        turned[c : c + 128, :] = mm(eye, w_ref[:, c : c + 128], NT).astype(bf16)
-    linear = mm(turned[...], qgt_ref[0, 0])
+    qgt = qgt_ref[0]
     for f in range(units):
         cols = slice(f * flat, (f + 1) * flat)
-        v = pre_ref[cols, :]
-        sig = sigmoid(v)
-        grad = (linear[cols, :] * (sig * (1.0 + v * (1.0 - sig)))).astype(bf16)
+        grad = (mm(w_ref[cols, :], qgt) * slope_ref[cols, :]).astype(bf16)
         for g in range(GROUPS):
             fgrad[f * BAND_OUT : (f + 1) * BAND_OUT, g * queries : (g + 1) * queries] = grad[
                 g * BAND_OUT : (g + 1) * BAND_OUT, :
@@ -400,7 +435,9 @@
         hpick = onehot(entry == ext_ref[...])
         rpick = onehot(entry + width == ext_ref[...])
         hgrad = (mm(hpick, high) + mm(hpick, low)).astype(bf16)
-        sums_ref[0] = mm(rpick, high) + mm(rpick, low)
+        rgrad = mm(rpick, high) + mm(rpick, low)
+        for d in range(sums_ref.shape[0]):
+            sums_ref[d] = rgrad
         blocks = out_ref.shape[0]
         pick = slot_picks(cap, blocks * cap, orow_ref[...])
         rows = mm(pick, hgrad, NT).astype(bf16)
@@ -408,37 +445,35 @@
             out_ref[d] = rows[d * cap : (d + 1) * cap, :]
 
 
-def back(vecs, orow, ext, img, band_t, weight_t, pre, count, cap):
-    width, queries = vecs.shape[2:]
-    flat = weight_t.shape[1]
+def back(qgt, orow, ext, img, band_t, weight, slope, count, cap, copies):
+    _, width, queries = qgt.shape
+    flat = weight.shape[0]
     filts = band_t.shape[1] // BAND_OUT
     units = filter_block(filts)
     cols = flat // filts * units
-    assert cols % 128 == 0
     return pl.pallas_call(
         functools.partial(back_kernel, cap),
         grid=(filts // units,),
         in_specs=[
             whole(orow.shape),
             whole(ext.shape),
-            whole((1, 1, width, queries)),
+            whole(qgt.shape),
             whole(img.shape),
             pl.BlockSpec((LANES, units * BAND_OUT), lambda s: (0, s)),
-            pl.BlockSpec((width, cols), lambda s: (0, s)),
+            pl.BlockSpec((cols, width), lambda s: (s, 0)),
             pl.BlockSpec((cols, queries), lambda s: (s, 0)),
         ],
         out_specs=[
             whole((count, cap, width)),
-            whole((1, width, queries)),
+            whole((copies, width, queries)),
             pl.BlockSpec((units, BAND_OUT, LANES), lambda s: (s, 0, 0)),
         ],
         out_shape=[
             jax.ShapeDtypeStruct((count, cap, width), bf16),
-            jax.ShapeDtypeStruct((1, width, queries), f32),
+            jax.ShapeDtypeStruct((copies, width, queries), f32),
             jax.ShapeDtypeStruct((filts, BAND_OUT, LANES), f32),
         ],
         scratch_shapes=[
-            pltpu.VMEM((cols, width), bf16),
             pltpu.VMEM((units * BAND_OUT, GROUPS * queries), bf16),
             pltpu.VMEM((LANES, GROUPS * queries), f32),
             pltpu.VMEM((ext.shape[1], queries), f32),
@@ -446,44 +481,57 @@
         compiler_params=params("arbitrary"),
         cost_estimate=cost(6e9, 2e7, 2.5e6),
         name="back",
-    )(orow, ext, vecs, img, band_t, weight_t, pre)
-
-
-def diag_kernel(taps, codes_ref, corr_ref, out_ref):
+    )(orow, ext, qgt, img, band_t, weight, slope)
+
+
+def half_taps(taps):
+    return -(-taps // 32) * 16
+
+
+def diag_kernel(taps, codes_ref, corr_ref, rows_ref, out_ref):
     filts = corr_ref.shape[0]
-    total = jnp.zeros((taps, filts), f32)
+    cap, width = rows_ref.shape[1:]
+    half = half_taps(taps)
+    total = jnp.zeros((2 * half, filts), f32)
     for j in range(IMG):
         rows = corr_ref[:, j, :]
         for di in range(1, BAND):
             rows = rows + pltpu.roll(corr_ref[:, di * IMG + j, :], LANES - di * IMG, 1)
-        pick = onehot(iota((taps, LANES), 0) == codes_ref[j : j + 1, :])
+        pick = onehot(iota((2 * half, LANES), 0) == codes_ref[j : j + 1, :])
         high, low = split(rows)
         total = total + mm(pick, high, NT) + mm(pick, low, NT)
+    packed = jnp.zeros((half, width), f32)
+    for k in range(2):
+        for i, piece in enumerate(split(total[k * half : (k + 1) * half, :])):
+            place = onehot(iota((filts, width), 1) == iota((filts, width), 0) + (2 * k + i) * filts)
+            packed = packed + mm(piece, place)
+    packed = packed.astype(bf16)
     for d in range(out_ref.shape[0]):
-        out_ref[d] = total
-
-
-def filter_sums(corr, codes, taps, copies):
+        out_ref[d, :cap, :] = rows_ref[d]
+        out_ref[d, cap:, :] = packed
+
+
+def filter_sums(corr, codes, rows, taps):
+    count, cap, width = rows.shape
+    assert 4 * corr.shape[0] <= width
     return pl.pallas_call(
         functools.partial(diag_kernel, taps),
-        out_shape=jax.ShapeDtypeStruct((copies, taps, corr.shape[0]), f32),
+        out_shape=jax.ShapeDtypeStruct((count, cap + half_taps(taps), width), bf16),
         compiler_params=params(),
         cost_estimate=cost(1e8, 4e6),
         name="filter_sums",
-    )(codes, corr)
-
-
-def tail_kernel(
-    cand, core_ref, tails_ref, mate_ref, scand_ref, mcand_ref, numbers_ref, vecs_ref, own_ref, other_ref
-):
-    tails = jnp.concatenate([tails_ref[...], mate_ref[...]], axis=0)
-    scand = jnp.concatenate([scand_ref[...], mcand_ref[...]], axis=0)
-    cap = tails_ref.shape[0]
+    )(codes, corr, rows)
+
+
+def tail_kernel(cand, ids_ref, tails_ref, mate_ref, scand_ref, numbers_ref, vecs_ref, own_ref, other_ref):
+    cap = own_ref.shape[1]
+    tails = jnp.concatenate([ref[0].astype(f32).T for ref in (tails_ref, mate_ref)], axis=0).astype(bf16)
+    scand = jnp.concatenate([scand_ref[0], scand_ref[1]], axis=0)
     own = jnp.zeros(own_ref.shape, f32)
     other = jnp.zeros(own_ref.shape, f32)
     for group in pairs(vecs_ref.shape[0]):
-        qvt = beside(vecs_ref[p, 2] for p in group)
-        pos = beside(numbers_ref[2 * p + core_ref[0], 3:4, :] for p in group)
+        qvt = beside(vecs_ref[p, 1] for p in group)
+        pos = beside(numbers_ref[2 * p + ids_ref[2], 3:4, :] for p in group)
         score = mm(tails, qvt)
         target = jnp.where(scand == pos, 1.0 - smooth + smooth / cand, smooth / cand)
         grad = ((sigmoid(score) - target) * loss_weight).astype(bf16)
@@ -493,22 +541,32 @@
     other_ref[...] = other
 
 
-def tail_part(core, tails, mate, scand, mcand, numbers, vecs, cand):
-    cap, width = tails.shape
+def tail_part(ids, tails, scand, numbers, vecs, cand):
+    _, width, cap = tails.shape
     half = jax.ShapeDtypeStruct((width, cap), f32)
     return pl.pallas_call(
         functools.partial(tail_kernel, cand),
-        in_specs=[SMEM] + [VMEM] * 6,
+        grid_spec=pltpu.PrefetchScalarGridSpec(
+            num_scalar_prefetch=1,
+            grid=(1,),
+            in_specs=[
+                pl.BlockSpec((1, width, cap), lambda s, ids: (ids[0], 0, 0)),
+                pl.BlockSpec((1, width, cap), lambda s, ids: (ids[1], 0, 0)),
+                whole(scand.shape),
+                whole(numbers.shape),
+                whole(vecs.shape),
+            ],
+            out_specs=[whole(half.shape)] * 2,
+        ),
         out_shape=[half, half],
-        compiler_params=params(),
+        compiler_params=params("arbitrary"),
         cost_estimate=cost(2e9, 3e6, 1e6),
         name="tail_grad",
-    )(core, tails, mate, scand, mcand, numbers, vecs)
-
-
-def proj_kernel(
-    core_ref, rtab_ref, ext_ref, band_ref, mate_ref, numbers_ref, vecs_ref,
-    own_ref, other_ref, pick, hmat, rmat,
+    )(ids, tails, tails, scand, numbers, vecs)
+
+
+def feats_kernel(
+    ids_ref, rtab_ref, ext_ref, band_ref, mate_ref, numbers_ref, vecs_ref, out_ref, pick, hmat, rmat
 ):
     width, rels = rtab_ref.shape
     units = band_ref.shape[0] // BAND_OUT
@@ -523,37 +581,67 @@
                 for f in range(units):
                     first = k * cols + f * flat + g * BAND_OUT
                     mat[first : first + BAND_OUT, :] = rows[f * BAND_OUT : (f + 1) * BAND_OUT, :]
-    for k, out in enumerate((own_ref, other_ref)):
-        out[...] = jnp.zeros_like(out)
+    queries = vecs_ref.shape[3]
     for group in pairs(vecs_ref.shape[0]):
-        hvt = beside(vecs_ref[p, 1] for p in group)
-        qgt = beside(vecs_ref[p, 0] for p in group)
-        rel = beside(numbers_ref[2 * p + core_ref[0], 2:3, :] for p in group)
+        hvt = beside(vecs_ref[p, 0] for p in group)
+        rel = beside(numbers_ref[2 * p + ids_ref[2], 2:3, :] for p in group)
         rvt = mm(rtab_ref[...], onehot(iota((rels, rel.shape[1]), 0) == rel)).astype(bf16)
-        for k, out in enumerate((own_ref, other_ref)):
+        lanes = slice(group[0] * queries, (group[-1] + 1) * queries)
+        for k in range(2):
             rows = slice(k * cols, (k + 1) * cols)
             pre = mm(hmat[rows, :], hvt) + mm(rmat[rows, :], rvt)
-            out[...] += mm(qgt, (pre * sigmoid(pre)).astype(bf16), NT)
-
-
-def proj_part(core, rtab_t, ext, band, mate, numbers, vecs):
+            out_ref[rows, lanes] = (pre * sigmoid(pre)).astype(bf16)
+
+
+def column_feats(ids, rtab_t, ext, band, numbers, vecs, cols):
     width = rtab_t.shape[0]
-    rows = band.shape[0]
-    cols = rows * GROUPS
-    half = jax.ShapeDtypeStruct((width, cols), f32)
+    unit = cols // GROUPS
+    gathered, _, _, queries = vecs.shape
+    return pl.pallas_call(
+        feats_kernel,
+        grid_spec=pltpu.PrefetchScalarGridSpec(
+            num_scalar_prefetch=1,
+            grid=(1,),
+            in_specs=[
+                whole(rtab_t.shape),
+                whole(ext.shape),
+                pl.BlockSpec((unit, LANES), lambda s, ids: (ids[0], 0)),
+                pl.BlockSpec((unit, LANES), lambda s, ids: (ids[1], 0)),
+                whole(numbers.shape),
+                whole(vecs.shape),
+            ],
+            out_specs=whole((2 * cols, gathered * queries)),
+            scratch_shapes=[
+                pltpu.VMEM((ext.shape[1], width), bf16),
+                pltpu.VMEM((2 * cols, width), bf16),
+                pltpu.VMEM((2 * cols, width), bf16),
+            ],
+        ),
+        out_shape=jax.ShapeDtypeStruct((2 * cols, gathered * queries), bf16),
+        compiler_params=params("arbitrary"),
+        cost_estimate=cost(6e9, 6e6, 2.5e6),
+        name="column_feats",
+    )(ids, rtab_t, ext, band, band, numbers, vecs)
+
+
+def proj_kernel(core_ref, feats_ref, grads_ref, own_ref, other_ref):
+    count = grads_ref.shape[0]
+    cols = own_ref.shape[1]
+    qgt = beside(grads_ref[2 * p + core_ref[0]] for p in range(count // 2))
+    own_ref[...] = mm(qgt, feats_ref[:cols, :], NT)
+    other_ref[...] = mm(qgt, feats_ref[cols:, :], NT)
+
+
+def proj_part(core, feats, grads):
+    half = jax.ShapeDtypeStruct((grads.shape[1], feats.shape[0] // 2), f32)
     return pl.pallas_call(
         proj_kernel,
-        in_specs=[SMEM] + [VMEM] * 6,
+        in_specs=[SMEM] + [VMEM] * 2,
         out_shape=[half, half],
-        scratch_shapes=[
-            pltpu.VMEM((ext.shape[1], width), bf16),
-            pltpu.VMEM((2 * cols, width), bf16),
-            pltpu.VMEM((2 * cols, width), bf16),
-        ],
         compiler_params=params(),
-        cost_estimate=cost(6e9, 6e6, 2.5e6),
+        cost_estimate=cost(1e9, 8e6),
         name="proj_grad",
-    )(core, rtab_t, ext, band, mate, numbers, vecs)
+    )(core, feats, grads)
 
 
 def proj_columns(first, cols, filters, chequer_perm, relation_table, numbers, heads, grads):
@@ -577,46 +665,56 @@
     return mm(qg, (pre * sigmoid(pre)).astype(bf16), TN)
 
 
-def rel_kernel(numbers_ref, sums_ref, filt_ref, rel_ref, out_ref):
-    total = jnp.zeros(rel_ref.shape, f32)
+def rel_kernel(core_ref, numbers_ref, sums_ref, rel_ref):
+    width, rels = rel_ref.shape
+    total = jnp.zeros((2 * width, rels), f32)
     for group in pairs(sums_ref.shape[0]):
-        rel = beside(numbers_ref[p, 2:3, :] for p in group)
-        pick = onehot(iota((rel_ref.shape[1], rel.shape[1]), 0) == rel)
-        high, low = split(beside(sums_ref[p] for p in group))
-        total = total + mm(high, pick, NT) + mm(low, pick, NT)
-    rel_ref[...] = total
-    filt = filt_ref[0]
-    for d in range(1, filt_ref.shape[0]):
-        filt = filt + filt_ref[d]
-    out_ref[...] = filt
-
-
-def rel_part(numbers, sums, filt, rels):
+        rel = beside(numbers_ref[2 * p + core_ref[0], 2:3, :] for p in group)
+        pick = onehot(iota((rels, rel.shape[1]), 0) == rel)
+        parts = jnp.concatenate(split(beside(sums_ref[p] for p in group)), axis=0)
+        total = total + mm(parts, pick, NT)
+    rel_ref[...] = total[:width, :] + total[width:, :]
+
+
+def rel_part(core, numbers, sums, rels):
     return pl.pallas_call(
         rel_kernel,
-        out_shape=[
-            jax.ShapeDtypeStruct((sums.shape[1], rels), f32),
-            jax.ShapeDtypeStruct(filt.shape[1:], f32),
-        ],
+        in_specs=[SMEM] + [VMEM] * 2,
+        out_shape=jax.ShapeDtypeStruct((sums.shape[1], rels), f32),
         compiler_params=params(),
         cost_estimate=cost(2e9, 3e6),
         name="rel_grad",
-    )(numbers, sums, filt)
-
-
-def entity_kernel(want_ref, srow_ref, own_ref, recv_ref, incoming_ref, out_ref):
+    )(core, numbers, sums)
+
+
+def entity_kernel(cap, want_ref, srow_ref, own_ref, recv_ref, incoming_ref, out_ref, filt_ref):
     rows = out_ref.shape[1]
-    grads = jnp.concatenate([incoming_ref[d] for d in range(incoming_ref.shape[0])], axis=0)
+    count, _, width = incoming_ref.shape
+    half, filts = filt_ref.shape[0] // 2, filt_ref.shape[1]
+    grads = jnp.concatenate([incoming_ref[d, :cap, :] for d in range(count)], axis=0)
     total = mm(grads, onehot(iota((want_ref.shape[0], rows), 1) == want_ref[...]), TN)
     pick = onehot(iota((srow_ref.shape[0], rows), 1) == srow_ref[...])
     high, low = split(own_ref[...] + recv_ref[...])
     out_ref[...] = total + mm(high, pick) + mm(low, pick)
-
-
-def entity_sum(want, srow, own, recv, incoming, rows):
-    return pl.pallas_call(
-        entity_kernel,
-        out_shape=jax.ShapeDtypeStruct((own.shape[0], rows), f32),
+    packed = incoming_ref[0, cap:, :].astype(f32)
+    for d in range(1, count):
+        packed = packed + incoming_ref[d, cap:, :].astype(f32)
+    high, low = split(packed)
+    for k in range(2):
+        lane = iota((width, filts), 0) - 2 * k * filts
+        unit = iota((width, filts), 1)
+        place = onehot((lane == unit) | (lane == unit + filts))
+        filt_ref[k * half : (k + 1) * half, :] = mm(high, place) + mm(low, place)
+
+
+def entity_sum(want, srow, own, recv, incoming, rows, cap, filts):
+    half = incoming.shape[1] - cap
+    return pl.pallas_call(
+        functools.partial(entity_kernel, cap),
+        out_shape=[
+            jax.ShapeDtypeStruct((own.shape[0], rows), f32),
+            jax.ShapeDtypeStruct((2 * half, filts), f32),
+        ],
         compiler_params=params(),
         cost_estimate=cost(1.5e9, 4e6),
         name="entity_grad",
@@ -671,9 +769,10 @@
     numbers = jnp.stack([heads, head_row, rel_ids, pos_index])[None]
     numbers = exchange(jnp.broadcast_to(numbers, (count,) + numbers.shape[1:]))
 
-    tails, tails_t, slot_cand, slot_row = pack_tails(me1, tail_owners, tail_row, table_t, tail_cap)
+    ids = jnp.stack([me, me ^ 1, me & 1])
+    tails_t, slot_row = pack_tails(me1, tail_owners, tail_row, table_t, tail_cap)
     all_tails = lax.all_gather(tails_t, "shard", axis=0, tiled=True)
-    mate_tails, mate_cand = swap(tails), swap(slot_cand)
+    scand = slot_cands(me1, tail_owners, tail_cap)
     found, want = find_heads(me1, numbers, table_t, head_cap)
     fetched = exchange(found)
     pos = pos_slots(tail_owners, pos_index, tail_cap)
@@ -683,43 +782,46 @@
     extra = BAND_OUT * (GROUPS - 1) + LANES - IMG * IMG - BAND_OUT
     ext = jnp.concatenate([chequer_perm[-BAND_OUT:], chequer_perm, chequer_perm[:extra]])[None]
     orow = heads[None, :]
-    pre, img, qv, vecs = front(
-        fetched, orow, rel_ids[None, :], rtab_t, ext, band, weight_t, head_cap
+    slope, weight, img, qv, vecs = front(
+        fetched, orow, rel_ids[None, :], rtab_t, ext, band, weight_t, head_cap, copies
     )
-
-    vecs = score_part(qv, pos, all_tails, vecs, cand, copies)
     core_vecs = gather_core(vecs)
-    outgoing, sums, corr = back(vecs, orow, ext, img, band_t, weight_t, pre, count, head_cap)
-    all_sums = lax.all_gather(sums, "shard", axis=0, tiled=True)
-    incoming = exchange(outgoing)
-    filt = exchange(filter_sums(corr, codes, ks * ks, count))
-
-    own, other = tail_part(core, tails, mate_tails, slot_cand, mate_cand, numbers, core_vecs, cand)
-    entity_grad = entity_sum(want, slot_row, own, swap(other), incoming, rows).T
+
+    qgt = score_part(qv, pos, all_tails, cand)
+    all_qgt = lax.all_gather(qgt, "shard", axis=0, tiled=True)
+    outgoing, sums, corr = back(qgt, orow, ext, img, band_t, weight, slope, count, head_cap, copies)
+    core_sums = gather_core(sums)
+    incoming = exchange(filter_sums(corr, codes, outgoing, ks * ks))
+
+    own, other = tail_part(ids, all_tails, scand, numbers, core_vecs, cand)
+    entity_grad, filter_grad = entity_sum(
+        want, slot_row, own, swap(other), incoming, rows, head_cap, filts
+    )
+    filter_grad = filter_grad[: ks * ks].T.reshape(filts, ks, ks)
 
     cols = filts * IMG * IMG // count
     if direct and cols % (IMG * IMG) == 0:
-        unit = cols // (IMG * IMG) * BAND_OUT
-        mine, mate = (
-            lax.dynamic_slice_in_dim(band, d * unit, unit, axis=0) for d in (me, me ^ 1)
+        feats = column_feats(ids, rtab_t, ext, band, numbers, core_vecs, cols)
+        own, other = proj_part(core, feats, all_qgt)
+    else:
+        core_numbers, core_qgt = (
+            lax.dynamic_index_in_dim(
+                x.reshape((count // 2, 2) + x.shape[1:]), me & 1, 1, keepdims=False
+            )
+            for x in (numbers, all_qgt)
         )
-        own, other = proj_part(core, rtab_t, ext, mine, mate, numbers, core_vecs)
-    else:
         own, other = (
             proj_columns(
                 d * cols, cols, filters, chequer_perm, relation_table,
-                lax.dynamic_index_in_dim(
-                    numbers.reshape(count // 2, 2, 4, queries), me & 1, 1, keepdims=False
-                ),
-                core_vecs[:, 1], core_vecs[:, 0],
+                core_numbers, core_vecs[:, 0], core_qgt,
             )
             for d in (me, me ^ 1)
         )
     proj_grad = (own + swap(other)).T
 
-    relation_grad, filter_grad = rel_part(numbers, all_sums, filt, rels)
-    filter_grad = filter_grad.T.reshape(filts, ks, ks)
-    return (entity_grad, relation_grad.T, filter_grad, proj_grad)
+    part = rel_part(core, numbers, core_sums, rels)
+    relation_grad = (part + swap(part)).T
+    return (entity_grad.T, relation_grad, filter_grad, proj_grad)
 
 
 def solution(mesh):

time: 163 us -> 180 us (1.10)
  blocking collectives: 13.9 us -> 43 us
  waiting for transfers between devices: 17.8 us -> 1.43 us
  Pallas kernels: 84.3 us -> 90.9 us
  local copies, waits for them, and re-layouts: 10.7 us -> 4.55 us
  other arithmetic: 1.16 us -> 4.2 us
    all_gather x0 -> x1, blocking collectives: none -> 29.2 us  [shards(): all_qgt = lax.all_gather(qgt, 'shard', axis=0, tiled=True)]
    all_gather x1, waiting for transfers between devices: 7.61 us -> 0.01 us  [shards(): all_tails = lax.all_gather(tails_t, 'shard', axis=0, tiled=True)]
    all_to_all x1 -> x2, starting transfers between devices: 3.57 us -> 10.6 us  [gather_core(): lax.all_to_all(x, 'shard', split_axis=0, concat_axis=0, axis_index_groups...]
    pallas_call x1, Pallas kernels: 12.2 us -> 18.5 us  [front(): pl.pallas_call(functools.partial(front_kernel, cap), grid=(filts // units...]
    pallas_call x6 -> x8, Pallas kernels: 36.8 us -> 42.6 us  [the longest x1 10.4 us: column_feats(): pl.pallas_call(feats_kernel, grid_spec=pltpu.PrefetchScalarGridSpec(num_s...]
    pallas_call x1, Pallas kernels: 20.5 us -> 14.8 us  [back(): pl.pallas_call(functools.partial(back_kernel, cap), grid=(filts // units,...]
    all_to_all x3 -> x2, waiting for transfers between devices: 6.76 us -> 1.11 us  [exchange(): return lax.all_to_all(x, 'shard', split_axis=0, concat_axis=0, tiled=True)]
    all_to_all x3 -> x2, starting transfers between devices: 14.7 us -> 9.32 us  [exchange(): return lax.all_to_all(x, 'shard', split_axis=0, concat_axis=0, tiled=True)]
  transfers between devices with their start and end apart: 10 -> 8, of which waited for: 4 -> 2; matrix products, arithmetic and copies ran while one was open for 5% -> 3% of each run, Pallas kernels for 46% -> 48%
where the time goes in v5:
time: 180 us; the launch traced here: 179 us
  Pallas kernels  90.9 us (50%)
  blocking collectives  43 us (24%)
  starting transfers between devices  20.8 us (12%)
  between operations  14.2 us (8%)
  local copies, waits for them, and re-layouts  4.55 us (3%)
  other arithmetic  4.2 us (2%)
    all_gather x1, blocking collectives, shards(): all_qgt = lax.all_gather(qgt, 'shard', axis=0, tiled=True)  29.2 us
    pallas_call x1, Pallas kernels, front(): pl.pallas_call(functools.partial(front_kernel, cap), grid=(filts // units...  18.5 us
    pallas_call x1, Pallas kernels, back(): pl.pallas_call(functools.partial(back_kernel, cap), grid=(filts // units,...  14.8 us
    all_to_all x1, blocking collectives, exchange(): return lax.all_to_all(x, 'shard', split_axis=0, concat_axis=0, tiled=True)  13.8 us
    all_to_all x2, starting transfers between devices, gather_core(): lax.all_to_all(x, 'shard', split_axis=0, concat_axis=0, axis_index_groups...  10.6 us
    pallas_call x1, Pallas kernels, column_feats(): pl.pallas_call(feats_kernel, grid_spec=pltpu.PrefetchScalarGridSpec(num_s...  10.4 us
    all_to_all x2, starting transfers between devices, exchange(): return lax.all_to_all(x, 'shard', split_axis=0, concat_axis=0, tiled=True)  9.32 us
    pallas_call x1, Pallas kernels, score_part(): pl.pallas_call(functools.partial(score_kernel, cand), grid=(owners // blo...  5.59 us
  transfers between devices with their start and end apart: 8, of which 2 were waited for; matrix products, arithmetic and copies ran while one was open for 3% of the time, Pallas kernels for 48%

profile of v5, /device:TPU:0, one launch (start us, length us, event | category | flops | bytes accessed | tf_op | source)
XLA Modules:
  0.0 179.1 jit_solution(3460815668378716008)
XLA Ops:
  7.3 4.1 %pack_tails.1 = (bf16[1,200,512]{2,1,0:T(8,128)(2,1)}, s32[512,1]{1,0:T(8,128)}) custom-call(s32[1]{0:T(128)} %bitcast.me_ref, s32[32,128]{1,0:T(8,128)} %bitcast.24, s32[32,128]{1,0:T(8,128)} %bitcast.40, bf16[200,2048]{1,0:T(8,128)(2,1)} %bitcast.36), custom_call_target="tpu_custom_call" | custom-call | flops 1000000000 | bytes 2000000 | tf_op jit(solution)/shard_map/pack_tails/pallas_call | solution.py:147
  11.5 13.8 %all_to_all.25.numbers_ref = s32[16,4,128]{2,1,0:T(4,128)} all-to-all(s32[16,4,128]{2,1,0:T(4,128)S(1)} %broadcast_in_dim.4), channel_id=1, replica_groups=mesh['parts'=2,'shard'=16] {'shard'}, dimensions={0} | all-to-all | bytes 65536 | tf_op jit(solution)/shard_map/all_to_all | solution.py:755
  25.3 2.6 %find_heads.1 = (bf16[16,16,200]{2,1,0:T(8,128)(2,1)}, s32[256,1]{1,0:T(8,128)}) custom-call(s32[1]{0:T(128)} %bitcast.me_ref, bf16[200,2048]{1,0:T(8,128)(2,1)} %bitcast.37, s32[16,4,128]{2,1,0:T(4,128)} %all_to_all.25.numbers_ref), custom_call_target="tpu_custom_call" | custom-call | flops 300000000 | bytes 2000000 | tf_op jit(solution)/shard_map/find_heads/pallas_call | solution.py:202
  27.9 3.5 %all-to-all-start.1 = ((bf16[16,16,200]{2,1,0:T(8,128)(2,1)}), bf16[16,16,200]{2,1,0:T(8,128)(2,1)S(1)}, u32[]{:S(2)}, u32[]{:S(2)}) async-start(bf16[16,16,200]{2,1,0:T(8,128)(2,1)} %get-tuple-element.27), calls=%async_computation.1 | async-start | bytes 262144 | tf_op jit(solution)/shard_map/all_to_all | solution.py:755
  31.6 0.6 broadcast_in_dim.5.ext_ref
  32.2 0.7 copy.18.filt_ref
  32.9 5.3 %band.1 = (bf16[3840,256]{1,0:T(8,128)(2,1)}, bf16[256,3840]{1,0:T(8,128)(2,1)}) custom-call(s32[20,256]{1,0:T(8,128)} %constant.8.clone.codes_ref, bf16[48,81]{1,0:T(8,128)(2,1)} %copy.18.filt_ref), custom_call_target="tpu_custom_call" | custom-call | flops 40000000 | bytes 4000000 | tf_op jit(solution)/shard_map/band/pallas_call | solution.py:94
  38.2 1.1 all-to-all-done.1.fetched_ref
  39.3 0.6 copy-done.5
  39.9 18.5 %front.1 = (f32[19200,128]{1,0:T(8,128)}, bf16[19200,200]{1,0:T(8,128)(2,1)}, bf16[256,640]{1,0:T(8,128)(2,1)}, bf16[128,200]{1,0:T(8,128)(2,1)}, bf16[8,2,200,128]{3,2,1,0:T(8,128)(2,1)}) custom-call(bf16[16,16,200]{2,1,0:T(8,128)(2,1)} %copy-done.5, s32[1,128]{1,0:T(1,128)} %bitcast.32, s32[1,128]{1,0:T(1,128)} %bitcast.30, bf16[200,1387]{1,0:T(8,128)(2,1)} %bitcast.38, ...), custom_call_target="tpu_custom_call" | custom-call | flops 4000000000 | bytes 24000000 | tf_op jit(solution)/shard_map/front/pallas_call | solution.py:321
  58.5 4.6 %all-to-all-start.2 = ((bf16[8,2,200,128]{3,2,1,0:T(8,128)(2,1)}), bf16[8,2,200,128]{3,2,1,0:T(8,128)(2,1)S(1)}, u32[]{:S(2)}, u32[]{:S(2)}) async-start(bf16[8,2,200,128]{3,2,1,0:T(8,128)(2,1)} %get-tuple-element.29), calls=%async_computation.2 | async-start | bytes 1638400 | tf_op jit(solution)/shard_map/all_to_all | solution.py:759
  63.0 2.1 %pos_slots.1.pos_ref = s32[128,1]{1,0:T(8,128)} custom-call(s32[1,4096]{1,0:T(1,128)} %bitcast.25, s32[1,128]{1,0:T(1,128)} %bitcast.27), custom_call_target="tpu_custom_call" | custom-call | flops 10000000 | bytes 100000 | tf_op jit(solution)/shard_map/pos_slots/pallas_call | solution.py:240
  65.1 5.6 %score.1.qgt_ref = bf16[1,200,128]{2,1,0:T(8,128)(2,1)} custom-call(s32[128,1]{1,0:T(8,128)} %pos_slots.1.pos_ref, bf16[128,200]{1,0:T(8,128)(2,1)} %get-tuple-element.32.qv_ref, bf16[16,200,512]{2,1,0:T(8,128)(2,1)} %all-gather.2.cloned.1.call-done.tails_ref.mate_ref), custom_call_target="tpu_custom_call" | custom-call | flops 1000000000 | bytes 3000000 | tf_op jit(solution)/shard_map/score/pallas_call | solution.py:387
  70.7 14.8 %back.1 = (bf16[16,16,200]{2,1,0:T(8,128)(2,1)}, f32[8,200,128]{2,1,0:T(8,128)}, f32[48,80,256]{2,1,0:T(8,128)}) custom-call(s32[1,128]{1,0:T(1,128)} %bitcast.33, s32[1,576]{1,0:T(1,128)} %broadcast_in_dim.5.ext_ref, bf16[1,200,128]{2,1,0:T(8,128)(2,1)} %score.1.qgt_ref, bf16[256,640]{1,0:T(8,128)(2,1)} %get-tuple-element.33.img_ref, ...), custom_call_target="tpu_custom_call" | custom-call | flops 6000000000 | bytes 20000000 | tf_op jit(solution)/shard_map/back/pallas_call | solution.py:454
  85.6 6.0 %all-to-all-start.4 = ((f32[8,200,128]{2,1,0:T(8,128)}), f32[8,200,128]{2,1,0:T(8,128)S(1)}, u32[]{:S(2)}, u32[]{:S(2)}) async-start(f32[8,200,128]{2,1,0:T(8,128)} %get-tuple-element.40), calls=%async_computation.4 | async-start | bytes 1638400 | tf_op jit(solution)/shard_map/all_to_all | solution.py:759
  91.6 4.5 %slot_cands.1.scand_ref = s32[2,512,1]{2,1,0:T(8,128)} custom-call(s32[1]{0:T(128)} %bitcast.me_ref, s32[32,128]{1,0:T(8,128)} %bitcast.26), custom_call_target="tpu_custom_call" | custom-call | flops 100000000 | bytes 1000000 | tf_op jit(solution)/shard_map/slot_cands/pallas_call | solution.py:169
  96.1 0.6 pad_add_fusion.2.ids_ref
  96.7 10.4 %column_feats.1.feats_ref = bf16[2400,1024]{1,0:T(8,128)(2,1)} custom-call(s32[3]{0:T(128)} %pad_add_fusion.2.ids_ref, bf16[200,1387]{1,0:T(8,128)(2,1)} %bitcast.39, s32[1,576]{1,0:T(1,128)} %broadcast_in_dim.5.ext_ref, bf16[3840,256]{1,0:T(8,128)(2,1)} %get-tuple-element.28.band_ref.mate_ref, bf16[3840,256]{1,0:T(8,128)(2,1)} %get-tuple-element.28.band_ref.mate_ref, ...), custom_call_target="tpu_custom_call" | custom-call | flops 6000000000 | bytes 6000000 | tf_op jit(solution)/shard_map/column_feats/pallas_call | solution.py:600
  107.1 5.0 %filter_sums.1 = bf16[16,64,200]{2,1,0:T(8,128)(2,1)} custom-call(s32[20,256]{1,0:T(8,128)} %constant.8.clone.codes_ref, f32[48,80,256]{2,1,0:T(8,128)} %get-tuple-element.37.corr_ref, bf16[16,16,200]{2,1,0:T(8,128)(2,1)} %get-tuple-element.38.rows_ref), custom_call_target="tpu_custom_call" | custom-call | flops 100000000 | bytes 4000000 | tf_op jit(solution)/shard_map/filter_sums/pallas_call | solution.py:517
  112.3 5.8 %all-to-all-start.3 = ((bf16[16,64,200]{2,1,0:T(8,128)(2,1)}), bf16[16,64,200]{2,1,0:T(8,128)(2,1)S(1)}, u32[]{:S(2)}, u32[]{:S(2)}) async-start(bf16[16,64,200]{2,1,0:T(8,128)(2,1)} %filter_sums.1), calls=%async_computation.3 | async-start | bytes 1048576 | tf_op jit(solution)/shard_map/all_to_all | solution.py:755
  118.2 29.2 %all_gather.7.grads_ref = bf16[16,200,128]{2,1,0:T(8,128)(2,1)} all-gather(bf16[1,200,128]{2,1,0:T(8,128)(2,1)S(1)} %copy-done.6), channel_id=1, replica_groups=mesh['parts'=2,'shard'=16] {'shard'}, dimensions={0}, use_global_device_ids=true | all-gather | bytes 870400 | tf_op jit(solution)/shard_map/all_gather | solution.py:791
  147.4 5.2 %proj_grad.1 = (f32[200,1200]{1,0:T(8,128)}, f32[200,1200]{1,0:T(8,128)}) custom-call(s32[1]{0:T(128)} %bitcast.9.core_ref, bf16[2400,1024]{1,0:T(8,128)(2,1)} %column_feats.1.feats_ref, bf16[16,200,128]{2,1,0:T(8,128)(2,1)} %all_gather.7.grads_ref), custom_call_target="tpu_custom_call" | custom-call | flops 1000000000 | bytes 8000000 | tf_op jit(solution)/shard_map/proj_grad/pallas_call | solution.py:637
  152.6 0.4 collective-permute-start.2
  152.9 4.9 %tail_grad.1 = (f32[200,512]{1,0:T(8,128)}, f32[200,512]{1,0:T(8,128)}) custom-call(s32[3]{0:T(128)} %pad_add_fusion.2.ids_ref, bf16[16,200,512]{2,1,0:T(8,128)(2,1)} %all-gather.2.cloned.1.call-done.tails_ref.mate_ref, bf16[16,200,512]{2,1,0:T(8,128)(2,1)} %all-gather.2.cloned.1.call-done.tails_ref.mate_ref, s32[2,512,1]{2,1,0:T(8,128)} %slot_cands.1.scand_ref, ...), custom_call_target="tpu_custom_call" | custom-call | flops 2000000000 | bytes 3000000 | tf_op jit(solution)/shard_map/tail_grad/pallas_call | solution.py:547
  158.0 3.6 %rel_grad.1 = f32[200,1387]{1,0:T(8,128)} custom-call(s32[1]{0:T(128)} %bitcast.9.core_ref, s32[16,4,128]{2,1,0:T(4,128)} %all_to_all.25.numbers_ref, f32[8,200,128]{2,1,0:T(8,128)} %copy-done.3), custom_call_target="tpu_custom_call" | custom-call | flops 2000000000 | bytes 3000000 | tf_op jit(solution)/shard_map/rel_grad/pallas_call | solution.py:680
  161.7 0.4 collective-permute-start.1
  162.0 0.7 copy-done.13
  163.0 4.3 %entity_grad.1 = (f32[200,2048]{1,0:T(8,128)}, f32[96,48]{1,0:T(8,128)}) custom-call(s32[256,1]{1,0:T(8,128)} %get-tuple-element.24.want_ref, s32[512,1]{1,0:T(8,128)} %get-tuple-element.25.srow_ref, f32[200,512]{1,0:T(8,128)} %get-tuple-element.30.own_ref, f32[200,512]{1,0:T(8,128)} %copy-done.13, bf16[16,64,200]{2,1,0:T(8,128)(2,1)} %copy-done.4), custom_call_target="tpu_custom_call" | custom-call | flops 1500000000 | bytes 4000000 | tf_op jit(solution)/shard_map/entity_grad/pallas_call | solution.py:712
  167.2 0.9 slice_bitcast_fusion
  168.1 0.6 reshape.26
  168.8 2.3 %add_bitcast_fusion.1 = f32[1200,200]{0,1:T(8,128)} fusion(f32[200,1200]{1,0:T(8,128)S(1)} %copy-done.2, f32[200,1200]{1,0:T(8,128)} %collective-permute-done.2), kind=kLoop, calls=%fused_computation.1 | loop fusion | flops 240000 | bytes 2880000 | tf_op jit(solution)/shard_map/transpose | solution.py:820
  171.1 1.1 add_bitcast_fusion
  (43 shorter events, 0.9 us)
Async XLA Ops:
  7.2 4.3 %copy-start.8 = (s32[128]{0:T(128)S(1)}, s32[128]{0:T(128)}, u32[]{:S(2)}) copy-start(s32[128]{0:T(128)} %param.20) | copy-start | bytes 1540
  7.2 4.3 %copy-start.11 = (s32[128]{0:T(128)S(1)}, s32[128]{0:T(128)}, u32[]{:S(2)}) copy-start(s32[128]{0:T(128)} %param.19) | copy-start | bytes 1540
  7.2 4.3 %copy-start.10 = (s32[128]{0:T(128)S(1)}, s32[128]{0:T(128)}, u32[]{:S(2)}) copy-start(s32[128]{0:T(128)} %param.18) | copy-start | bytes 1540
  7.2 4.3 %copy-start.12 = (s32[128,1]{0,1:T(1,128)S(1)}, s32[128,1]{0,1:T(1,128)}, u32[]{:S(2)}) copy-start(s32[128,1]{0,1:T(1,128)} %param.17) | copy-start | bytes 1540
  7.2 57.9 %all-gather.2.cloned.1.call-start = ((), (), s32[]{:S(2)}) async-start(), calls=%async_computation.5 | async-start | bytes 3481600 | tf_op jit(solution)/shard_map/all_gather | solution.py:774
  7.3 24.1 %copy-start.9 = (s32[400]{0:T(512)S(1)}, s32[400]{0:T(512)}, u32[]{:S(2)}) copy-start(s32[400]{0:T(512)} %param.16) | copy-start | bytes 4804
  7.3 24.2 %slice-start = ((s32[400]{0:T(512)}), s32[96]{0:T(128)S(1)}, s32[]{:S(2)}) async-start(s32[400]{0:T(512)} %param.16), calls=%async_computation.6 | async-start | bytes 1024 | tf_op jit(solution)/shard_map/slice | solution.py:783
  7.3 24.9 %copy-start.7 = (bf16[48,9,9]{0,2,1:T(8,128)(2,1)S(1)}, bf16[48,9,9]{0,2,1:T(8,128)(2,1)}, u32[]{:S(2)}) copy-start(bf16[48,9,9]{0,2,1:T(8,128)(2,1)} %param.14) | copy-start | bytes 23332
  27.9 11.4 %all-to-all-start.1 = ((bf16[16,16,200]{2,1,0:T(8,128)(2,1)}), bf16[16,16,200]{2,1,0:T(8,128)(2,1)S(1)}, u32[]{:S(2)}, u32[]{:S(2)}) async-start(bf16[16,16,200]{2,1,0:T(8,128)(2,1)} %get-tuple-element.27), calls=%async_computation.1 | async-start | bytes 262144 | tf_op jit(solution)/shard_map/all_to_all | solution.py:755
  39.3 0.6 copy-start.5
  58.5 27.1 %all-to-all-start.2 = ((bf16[8,2,200,128]{3,2,1,0:T(8,128)(2,1)}), bf16[8,2,200,128]{3,2,1,0:T(8,128)(2,1)S(1)}, u32[]{:S(2)}, u32[]{:S(2)}) async-start(bf16[8,2,200,128]{3,2,1,0:T(8,128)(2,1)} %get-tuple-element.29), calls=%async_computation.2 | async-start | bytes 1638400 | tf_op jit(solution)/shard_map/all_to_all | solution.py:759
  85.5 11.2 %copy-start = (bf16[8,2,200,128]{3,2,1,0:T(8,128)(2,1)}, bf16[8,2,200,128]{3,2,1,0:T(8,128)(2,1)S(1)}, u32[]{:S(2)}) copy-start(bf16[8,2,200,128]{3,2,1,0:T(8,128)(2,1)S(1)} %all-to-all-done.2.vecs_ref) | copy-start | bytes 2457604
  85.6 26.8 %all-to-all-start.4 = ((f32[8,200,128]{2,1,0:T(8,128)}), f32[8,200,128]{2,1,0:T(8,128)S(1)}, u32[]{:S(2)}, u32[]{:S(2)}) async-start(f32[8,200,128]{2,1,0:T(8,128)} %get-tuple-element.40), calls=%async_computation.4 | async-start | bytes 1638400 | tf_op jit(solution)/shard_map/all_to_all | solution.py:759
  107.1 11.1 %copy-start.6 = (bf16[1,200,128]{2,1,0:T(8,128)(2,1)S(1)}, bf16[1,200,128]{2,1,0:T(8,128)(2,1)}, u32[]{:S(2)}) copy-start(bf16[1,200,128]{2,1,0:T(8,128)(2,1)} %score.1.qgt_ref) | copy-start | bytes 153604
  112.3 40.3 %copy-start.3 = (f32[8,200,128]{2,1,0:T(8,128)}, f32[8,200,128]{2,1,0:T(8,128)S(1)}, u32[]{:S(2)}) copy-start(f32[8,200,128]{2,1,0:T(8,128)S(1)} %all-to-all-done.4.sums_ref) | copy-start | bytes 2457604
  112.3 49.7 %all-to-all-start.3 = ((bf16[16,64,200]{2,1,0:T(8,128)(2,1)}), bf16[16,64,200]{2,1,0:T(8,128)(2,1)S(1)}, u32[]{:S(2)}, u32[]{:S(2)}) async-start(bf16[16,64,200]{2,1,0:T(8,128)(2,1)} %filter_sums.1), calls=%async_computation.3 | async-start | bytes 1048576 | tf_op jit(solution)/shard_map/all_to_all | solution.py:755
  152.6 16.2 %collective-permute-start.2 = (f32[200,1200]{1,0:T(8,128)}, f32[200,1200]{1,0:T(8,128)}, u32[]{:S(2)}, u32[]{:S(2)}) collective-permute-start(f32[200,1200]{1,0:T(8,128)} %get-tuple-element.43), channel_id=1, source_target_pairs={{0,1},{1,0},{2,3},{3,2},{4,5},{5,4},{6,7},{7,6},{8,9},{9,8},{10,11... | collective-permute-start | bytes 2880008 | tf_op jit(solution)/shard_map/ppermute | solution.py:752
  157.9 4.2 %collective-permute-start = (f32[200,512]{1,0:T(8,128)}, f32[200,512]{1,0:T(8,128)S(1)}, u32[]{:S(2)}, u32[]{:S(2)}) collective-permute-start(f32[200,512]{1,0:T(8,128)} %get-tuple-element.31), channel_id=1, source_target_pairs={{0,1},{1,0},{2,3},{3,2},{4,5},{5,4},{6,7},{7,6},{8,9},{9,8},{10,11... | collective-permute-start | bytes 1228808 | tf_op jit(solution)/shard_map/ppermute | solution.py:752
  161.7 9.5 %collective-permute-start.1 = (f32[200,1387]{1,0:T(8,128)}, f32[200,1387]{1,0:T(8,128)S(1)}, u32[]{:S(2)}, u32[]{:S(2)}) collective-permute-start(f32[200,1387]{1,0:T(8,128)} %rel_grad.1), channel_id=1, source_target_pairs={{0,1},{1,0},{2,3},{3,2},{4,5},{5,4},{6,7},{7,6},{8,9},{9,8},{10,11... | collective-permute-start | bytes 3328808 | tf_op jit(solution)/shard_map/ppermute | solution.py:752
  162.0 0.8 copy-start.13
  162.0 0.9 copy-start.4
  163.0 5.8 %copy-start.2 = (f32[200,1200]{1,0:T(8,128)S(1)}, f32[200,1200]{1,0:T(8,128)}, u32[]{:S(2)}) copy-start(f32[200,1200]{1,0:T(8,128)} %get-tuple-element.42) | copy-start | bytes 2880004
  167.2 3.9 %copy-start.1 = (f32[200,1387]{1,0:T(8,128)S(1)}, f32[200,1387]{1,0:T(8,128)}, u32[]{:S(2)}) copy-start(f32[200,1387]{1,0:T(8,128)} %rel_grad.1) | copy-start | bytes 3328804
Sparse Core Ops, SparseCore 0:
  11.6 49.4 all-gather.1

commit v6 on v5

--- a/solution.py
+++ b/solution.py
@@ -116,6 +116,18 @@
     return jnp.concatenate(list(blocks), axis=1)
 
 
+def spans(size, step):
+    return [slice(i, min(i + step, size)) for i in range(0, size, step)]
+
+
+def fill_picks(ref, index):
+    rows, lanes = ref.shape
+    for r in spans(rows, 64):
+        for c in spans(lanes, 256):
+            here = iota((r.stop - r.start, c.stop - c.start), 1) + c.start
+            ref[r, c] = onehot(here == index[r, :])
+
+
 def slot_values(owner, device, value, cap):
     lines = owner.shape[0]
     mine = owner == device
@@ -127,19 +139,22 @@
     offset = mm(upper, totals.astype(bf16))
     key = jnp.where(mine, (rank + offset).astype(i32), -1)
     value = (value + 1).astype(f32)
-    slots = iota((cap, 128), 0)
-    total = jnp.zeros((cap, 128), f32)
-    for r in range(lines):
-        total = total + jnp.where(slots == key[r : r + 1, :], value[r : r + 1, :], 0.0)
-    return jnp.sum(total, axis=1, keepdims=True).astype(i32) - 1
-
-
-def pack_kernel(me_ref, owner_ref, row_ref, table_ref, tails_t_ref, srow_ref):
+    found = []
+    for s in spans(cap, 128):
+        slots = iota((s.stop - s.start, 128), 0) + s.start
+        total = jnp.zeros(slots.shape, f32)
+        for r in range(lines):
+            total = total + jnp.where(slots == key[r : r + 1, :], value[r : r + 1, :], 0.0)
+        found.append(jnp.sum(total, axis=1, keepdims=True))
+    return jnp.concatenate(found, axis=0).astype(i32) - 1
+
+
+def pack_kernel(me_ref, owner_ref, row_ref, table_ref, tails_t_ref, srow_ref, picks):
     cap = srow_ref.shape[0]
     srow = slot_values(owner_ref[...], me_ref[0], row_ref[...], cap)
     srow_ref[...] = srow
-    pick = onehot(iota((cap, table_ref.shape[1]), 1) == srow)
-    tails_t_ref[0] = mm(table_ref[...], pick, NT).astype(bf16)
+    fill_picks(picks, srow)
+    tails_t_ref[0] = mm(table_ref[...], picks[...], NT).astype(bf16)
 
 
 def pack_tails(me, tail_owners, tail_row, table_t, cap):
@@ -151,6 +166,7 @@
             jax.ShapeDtypeStruct((1, table_t.shape[0], cap), bf16),
             jax.ShapeDtypeStruct((cap, 1), i32),
         ],
+        scratch_shapes=[pltpu.VMEM((cap, table_t.shape[1]), bf16)],
         compiler_params=params(),
         cost_estimate=cost(1e9, 2e6),
         name="pack_tails",
@@ -176,7 +192,7 @@
     )(me, tail_owners.reshape(-1, 128))
 
 
-def found_kernel(cap, me_ref, table_ref, numbers_ref, found_ref, want_ref, scr):
+def found_kernel(cap, me_ref, table_ref, numbers_ref, found_ref, want_ref, scr, picks):
     count, _, queries = numbers_ref.shape
     owners = jnp.concatenate([numbers_ref[d, 0:1, :] for d in range(count)], axis=0)
     mine = owners == me_ref[0]
@@ -190,8 +206,8 @@
         scr[d * cap : (d + 1) * cap, :] = jnp.sum(picked, axis=1, keepdims=True)
     want = scr[...].astype(i32) - 1
     want_ref[...] = want
-    pick = onehot(iota((count * cap, table_ref.shape[1]), 1) == want)
-    found = mm(pick, table_ref[...], NT).astype(bf16)
+    fill_picks(picks, want)
+    found = mm(picks[...], table_ref[...], NT).astype(bf16)
     for d in range(count):
         found_ref[d] = found[d * cap : (d + 1) * cap, :]
 
@@ -206,7 +222,10 @@
             jax.ShapeDtypeStruct((count, cap, width), bf16),
             jax.ShapeDtypeStruct((count * cap, 1), i32),
         ],
-        scratch_shapes=[pltpu.VMEM((count * cap, 1), f32)],
+        scratch_shapes=[
+            pltpu.VMEM((count * cap, 1), f32),
+            pltpu.VMEM((count * cap, table_t.shape[1]), bf16),
+        ],
         compiler_params=params(),
         cost_estimate=cost(3e8, 2e6),
         name="find_heads",
@@ -217,7 +236,7 @@
     cand = owner_ref.shape[1]
     queries = pos_ref.shape[1]
     eye = iota((queries, queries), 0) == iota((queries, queries), 1)
-    step = min(512, cand)
+    step = min(128, cand)
     row = pos_ref[...].astype(f32)
     pos = jnp.sum(jnp.where(eye, row, 0.0), axis=1, keepdims=True).astype(i32)
     owner = jnp.zeros((queries, step), f32)
@@ -258,7 +277,7 @@
 
 def front_kernel(
     cap, fetched_ref, orow_ref, rel_ref, rtab_ref, ext_ref, band_ref, w_ref,
-    slope_ref, turned_ref, img_ref, qv_ref, vecs_ref, feats, acc, ext,
+    img_ref, qv_ref, vecs_ref, feats, acc, ext, pre,
 ):
     s = pl.program_id(0)
     width, queries = acc.shape
@@ -282,21 +301,13 @@
 
     units = band_ref.shape[0] // BAND_OUT
     flat = GROUPS * BAND_OUT
-    pre = mm(band_ref[...], img_ref[...])
-    sig = sigmoid(pre)
-    act = (pre * sig).astype(bf16)
-    slope = sig * (1.0 + pre * (1.0 - sig))
+    pre[...] = mm(band_ref[...], img_ref[...])
     for f in range(units):
         for g in range(GROUPS):
             rows = slice(f * flat + g * BAND_OUT, f * flat + (g + 1) * BAND_OUT)
-            part = slice(f * BAND_OUT, (f + 1) * BAND_OUT)
-            lanes = slice(g * queries, (g + 1) * queries)
-            slope_ref[rows, :] = slope[part, lanes]
-            feats[rows, :] = act[part, lanes]
+            v = pre[f * BAND_OUT : (f + 1) * BAND_OUT, g * queries : (g + 1) * queries]
+            feats[rows, :] = (v * sigmoid(v)).astype(bf16)
     acc[...] += mm(w_ref[...], feats[...])
-    eye = onehot(iota((128, 128), 0) == iota((128, 128), 1))
-    for c in range(0, turned_ref.shape[0], 128):
-        turned_ref[c : c + 128, :] = mm(eye, w_ref[:, c : c + 128], NT).astype(bf16)
 
     @pl.when(s == pl.num_programs(0) - 1)
     def _():
@@ -317,7 +328,6 @@
     filts = band.shape[0] // BAND_OUT
     units = filter_block(filts)
     cols = flat // filts * units
-    assert cols % 128 == 0
     return pl.pallas_call(
         functools.partial(front_kernel, cap),
         grid=(filts // units,),
@@ -331,15 +341,11 @@
             pl.BlockSpec((width, cols), lambda s: (0, s)),
         ],
         out_specs=[
-            pl.BlockSpec((cols, queries), lambda s: (s, 0)),
-            pl.BlockSpec((cols, width), lambda s: (s, 0)),
             whole((LANES, GROUPS * queries)),
             whole((queries, width)),
             whole((copies, 2, width, queries)),
         ],
         out_shape=[
-            jax.ShapeDtypeStruct((flat, queries), f32),
-            jax.ShapeDtypeStruct((flat, width), bf16),
             jax.ShapeDtypeStruct((LANES, GROUPS * queries), bf16),
             jax.ShapeDtypeStruct((queries, width), bf16),
             jax.ShapeDtypeStruct((copies, 2, width, queries), bf16),
@@ -348,6 +354,7 @@
             pltpu.VMEM((cols, queries), bf16),
             pltpu.VMEM((width, queries), f32),
             pltpu.VMEM((ext.shape[1], queries), bf16),
+            pltpu.VMEM((units * BAND_OUT, GROUPS * queries), f32),
         ],
         compiler_params=params("arbitrary"),
         cost_estimate=cost(4e9, 2.4e7, 2.5e6),
@@ -355,7 +362,7 @@
     )(fetched, orow, rel_row, rtab_t, ext, band, weight_t)
 
 
-def score_kernel(cand, pos_ref, qv_ref, tails_ref, out_ref, acc):
+def score_kernel(cand, pos_ref, qv_ref, tails_ref, out_ref, acc, scores, grads):
     step = pl.program_id(0)
 
     @pl.when(step == 0)
@@ -368,19 +375,22 @@
     total = acc[...]
     for b in range(blocks):
         block = tails_ref[b]
-        score = mm(qv, block)
-        here = iota((queries, cap), 1) + (step * blocks + b) * cap
-        target = jnp.where(here == pos_ref[...], 1.0 - smooth + smooth / cand, smooth / cand)
-        grad = ((sigmoid(score) - target) * loss_weight).astype(bf16)
-        total = total + mm(grad, block, NT)
+        scores[b] = mm(qv, block)
+        for r in spans(queries, 16):
+            here = iota((r.stop - r.start, cap), 1) + (step * blocks + b) * cap
+            target = jnp.where(here == pos_ref[r, :], 1.0 - smooth + smooth / cand, smooth / cand)
+            grads[b, r, :] = ((sigmoid(scores[b, r, :]) - target) * loss_weight).astype(bf16)
+        total = total + mm(grads[b], block, NT)
     acc[...] = total
 
     @pl.when(step == pl.num_programs(0) - 1)
     def _():
-        out_ref[0] = total.T.astype(bf16)
-
-
-def score_part(qv, pos, tails, cand):
+        qgt = total.T.astype(bf16)
+        for d in range(out_ref.shape[0]):
+            out_ref[d] = qgt
+
+
+def score_part(qv, pos, tails, cand, copies):
     queries, width = qv.shape
     owners, _, cap = tails.shape
     blocks = math.gcd(owners, max(1, 2048 // cap))
@@ -392,9 +402,13 @@
             whole(qv.shape),
             pl.BlockSpec((blocks, width, cap), lambda s: (s, 0, 0)),
         ],
-        out_specs=whole((1, width, queries)),
-        out_shape=jax.ShapeDtypeStruct((1, width, queries), bf16),
-        scratch_shapes=[pltpu.VMEM((queries, width), f32)],
+        out_specs=whole((copies, width, queries)),
+        out_shape=jax.ShapeDtypeStruct((copies, width, queries), bf16),
+        scratch_shapes=[
+            pltpu.VMEM((queries, width), f32),
+            pltpu.VMEM((blocks, queries, cap), f32),
+            pltpu.VMEM((blocks, queries, cap), bf16),
+        ],
         compiler_params=params("arbitrary"),
         cost_estimate=cost(1e9, 3e6, 5e5),
         name="score",
@@ -402,8 +416,8 @@
 
 
 def back_kernel(
-    cap, orow_ref, ext_ref, qgt_ref, img_ref, bandt_ref, w_ref, slope_ref,
-    out_ref, sums_ref, corr_ref, fgrad, spread, ext,
+    cap, orow_ref, ext_ref, qgt_ref, img_ref, band_ref, bandt_ref, w_ref,
+    out_ref, sums_ref, corr_ref, fgrad, spread, ext, pre, linear,
 ):
     s = pl.program_id(0)
     _, width, queries = qgt_ref.shape
@@ -414,14 +428,16 @@
 
     units = bandt_ref.shape[1] // BAND_OUT
     flat = GROUPS * BAND_OUT
-    qgt = qgt_ref[0]
+    pre[...] = mm(band_ref[...], img_ref[...])
+    linear[...] = mm(w_ref[...], qgt_ref[0], TN)
     for f in range(units):
-        cols = slice(f * flat, (f + 1) * flat)
-        grad = (mm(w_ref[cols, :], qgt) * slope_ref[cols, :]).astype(bf16)
         for g in range(GROUPS):
-            fgrad[f * BAND_OUT : (f + 1) * BAND_OUT, g * queries : (g + 1) * queries] = grad[
-                g * BAND_OUT : (g + 1) * BAND_OUT, :
-            ]
+            rows = slice(f * flat + g * BAND_OUT, f * flat + (g + 1) * BAND_OUT)
+            part = slice(f * BAND_OUT, (f + 1) * BAND_OUT)
+            lanes = slice(g * queries, (g + 1) * queries)
+            v = pre[part, lanes]
+            sig = sigmoid(v)
+            fgrad[part, lanes] = (linear[rows, :] * (sig * (1.0 + v * (1.0 - sig)))).astype(bf16)
     spread[...] += mm(bandt_ref[...], fgrad[...])
     corr_ref[...] = mm(fgrad[...], img_ref[...], NT).reshape(units, BAND_OUT, LANES)
 
@@ -436,8 +452,7 @@
         rpick = onehot(entry + width == ext_ref[...])
         hgrad = (mm(hpick, high) + mm(hpick, low)).astype(bf16)
         rgrad = mm(rpick, high) + mm(rpick, low)
-        for d in range(sums_ref.shape[0]):
-            sums_ref[d] = rgrad
+        sums_ref[0] = rgrad
         blocks = out_ref.shape[0]
         pick = slot_picks(cap, blocks * cap, orow_ref[...])
         rows = mm(pick, hgrad, NT).astype(bf16)
@@ -445,9 +460,9 @@
             out_ref[d] = rows[d * cap : (d + 1) * cap, :]
 
 
-def back(qgt, orow, ext, img, band_t, weight, slope, count, cap, copies):
+def back(qgt, orow, ext, img, band, band_t, weight_t, count, cap):
     _, width, queries = qgt.shape
-    flat = weight.shape[0]
+    flat = weight_t.shape[1]
     filts = band_t.shape[1] // BAND_OUT
     units = filter_block(filts)
     cols = flat // filts * units
@@ -457,31 +472,33 @@
         in_specs=[
             whole(orow.shape),
             whole(ext.shape),
-            whole(qgt.shape),
+            whole((1, width, queries)),
             whole(img.shape),
+            pl.BlockSpec((units * BAND_OUT, LANES), lambda s: (s, 0)),
             pl.BlockSpec((LANES, units * BAND_OUT), lambda s: (0, s)),
-            pl.BlockSpec((cols, width), lambda s: (s, 0)),
-            pl.BlockSpec((cols, queries), lambda s: (s, 0)),
+            pl.BlockSpec((width, cols), lambda s: (0, s)),
         ],
         out_specs=[
             whole((count, cap, width)),
-            whole((copies, width, queries)),
+            whole((1, width, queries)),
             pl.BlockSpec((units, BAND_OUT, LANES), lambda s: (s, 0, 0)),
         ],
         out_shape=[
             jax.ShapeDtypeStruct((count, cap, width), bf16),
-            jax.ShapeDtypeStruct((copies, width, queries), f32),
+            jax.ShapeDtypeStruct((1, width, queries), f32),
             jax.ShapeDtypeStruct((filts, BAND_OUT, LANES), f32),
         ],
         scratch_shapes=[
             pltpu.VMEM((units * BAND_OUT, GROUPS * queries), bf16),
             pltpu.VMEM((LANES, GROUPS * queries), f32),
             pltpu.VMEM((ext.shape[1], queries), f32),
+            pltpu.VMEM((units * BAND_OUT, GROUPS * queries), f32),
+            pltpu.VMEM((cols, queries), f32),
         ],
         compiler_params=params("arbitrary"),
         cost_estimate=cost(6e9, 2e7, 2.5e6),
         name="back",
-    )(orow, ext, qgt, img, band_t, weight, slope)
+    )(orow, ext, qgt, img, band, band_t, weight_t)
 
 
 def half_taps(taps):
@@ -523,18 +540,22 @@
     )(codes, corr, rows)
 
 
-def tail_kernel(cand, ids_ref, tails_ref, mate_ref, scand_ref, numbers_ref, vecs_ref, own_ref, other_ref):
+def tail_kernel(
+    cand, ids_ref, tails_ref, mate_ref, scand_ref, numbers_ref, vecs_ref, own_ref, other_ref, scores, grads
+):
     cap = own_ref.shape[1]
     tails = jnp.concatenate([ref[0].astype(f32).T for ref in (tails_ref, mate_ref)], axis=0).astype(bf16)
     scand = jnp.concatenate([scand_ref[0], scand_ref[1]], axis=0)
     own = jnp.zeros(own_ref.shape, f32)
     other = jnp.zeros(own_ref.shape, f32)
-    for group in pairs(vecs_ref.shape[0]):
+    for i, group in enumerate(pairs(vecs_ref.shape[0])):
         qvt = beside(vecs_ref[p, 1] for p in group)
         pos = beside(numbers_ref[2 * p + ids_ref[2], 3:4, :] for p in group)
-        score = mm(tails, qvt)
-        target = jnp.where(scand == pos, 1.0 - smooth + smooth / cand, smooth / cand)
-        grad = ((sigmoid(score) - target) * loss_weight).astype(bf16)
+        score, grad = scores.at[i % 2], grads.at[i % 2]
+        score[...] = mm(tails, qvt)
+        for r in spans(2 * cap, 64):
+            target = jnp.where(scand[r, :] == pos, 1.0 - smooth + smooth / cand, smooth / cand)
+            grad[r, :] = ((sigmoid(score[r, :]) - target) * loss_weight).astype(bf16)
         own = own + mm(qvt, grad[:cap, :], NT)
         other = other + mm(qvt, grad[cap:, :], NT)
     own_ref[...] = own
@@ -557,6 +578,10 @@
                 whole(vecs.shape),
             ],
             out_specs=[whole(half.shape)] * 2,
+            scratch_shapes=[
+                pltpu.VMEM((2, 2 * cap, 2 * vecs.shape[3]), f32),
+                pltpu.VMEM((2, 2 * cap, 2 * vecs.shape[3]), bf16),
+            ],
         ),
         out_shape=[half, half],
         compiler_params=params("arbitrary"),
@@ -566,7 +591,7 @@
 
 
 def feats_kernel(
-    ids_ref, rtab_ref, ext_ref, band_ref, mate_ref, numbers_ref, vecs_ref, out_ref, pick, hmat, rmat
+    ids_ref, rtab_ref, ext_ref, band_ref, mate_ref, numbers_ref, vecs_ref, out_ref, pick, hmat, rmat, pre, rpick
 ):
     width, rels = rtab_ref.shape
     units = band_ref.shape[0] // BAND_OUT
@@ -585,12 +610,16 @@
     for group in pairs(vecs_ref.shape[0]):
         hvt = beside(vecs_ref[p, 0] for p in group)
         rel = beside(numbers_ref[2 * p + ids_ref[2], 2:3, :] for p in group)
-        rvt = mm(rtab_ref[...], onehot(iota((rels, rel.shape[1]), 0) == rel)).astype(bf16)
+        for r in spans(rels, 64):
+            rpick[r, :] = onehot(iota((r.stop - r.start, rel.shape[1]), 0) + r.start == rel)
+        rvt = mm(rtab_ref[...], rpick[...]).astype(bf16)
         lanes = slice(group[0] * queries, (group[-1] + 1) * queries)
         for k in range(2):
             rows = slice(k * cols, (k + 1) * cols)
-            pre = mm(hmat[rows, :], hvt) + mm(rmat[rows, :], rvt)
-            out_ref[rows, lanes] = (pre * sigmoid(pre)).astype(bf16)
+            pre[k] = mm(hmat[rows, :], hvt) + mm(rmat[rows, :], rvt)
+            for r in spans(cols, 80):
+                v = pre[k, r, :]
+                out_ref[k * cols + r.start : k * cols + r.stop, lanes] = (v * sigmoid(v)).astype(bf16)
 
 
 def column_feats(ids, rtab_t, ext, band, numbers, vecs, cols):
@@ -615,6 +644,8 @@
                 pltpu.VMEM((ext.shape[1], width), bf16),
                 pltpu.VMEM((2 * cols, width), bf16),
                 pltpu.VMEM((2 * cols, width), bf16),
+                pltpu.VMEM((2, cols, 2 * queries), f32),
+                pltpu.VMEM((rtab_t.shape[1], 2 * queries), bf16),
             ],
         ),
         out_shape=jax.ShapeDtypeStruct((2 * cols, gathered * queries), bf16),
@@ -624,24 +655,22 @@
     )(ids, rtab_t, ext, band, band, numbers, vecs)
 
 
-def proj_kernel(core_ref, feats_ref, grads_ref, own_ref, other_ref):
-    count = grads_ref.shape[0]
+def proj_kernel(feats_ref, grads_ref, own_ref, other_ref):
     cols = own_ref.shape[1]
-    qgt = beside(grads_ref[2 * p + core_ref[0]] for p in range(count // 2))
+    qgt = beside(grads_ref[p] for p in range(grads_ref.shape[0]))
     own_ref[...] = mm(qgt, feats_ref[:cols, :], NT)
     other_ref[...] = mm(qgt, feats_ref[cols:, :], NT)
 
 
-def proj_part(core, feats, grads):
+def proj_part(feats, grads):
     half = jax.ShapeDtypeStruct((grads.shape[1], feats.shape[0] // 2), f32)
     return pl.pallas_call(
         proj_kernel,
-        in_specs=[SMEM] + [VMEM] * 2,
         out_shape=[half, half],
         compiler_params=params(),
         cost_estimate=cost(1e9, 8e6),
         name="proj_grad",
-    )(core, feats, grads)
+    )(feats, grads)
 
 
 def proj_columns(first, cols, filters, chequer_perm, relation_table, numbers, heads, grads):
@@ -665,26 +694,33 @@
     return mm(qg, (pre * sigmoid(pre)).astype(bf16), TN)
 
 
-def rel_kernel(core_ref, numbers_ref, sums_ref, rel_ref):
+def rel_kernel(numbers_ref, sums_ref, rel_ref, picks):
     width, rels = rel_ref.shape
-    total = jnp.zeros((2 * width, rels), f32)
-    for group in pairs(sums_ref.shape[0]):
-        rel = beside(numbers_ref[2 * p + core_ref[0], 2:3, :] for p in group)
-        pick = onehot(iota((rels, rel.shape[1]), 0) == rel)
-        parts = jnp.concatenate(split(beside(sums_ref[p] for p in group)), axis=0)
-        total = total + mm(parts, pick, NT)
+    queries = sums_ref.shape[2]
+    total = None
+    for block in spans(sums_ref.shape[0], picks.shape[1] // queries):
+        members = range(block.start, block.stop)
+        for i, p in enumerate(members):
+            rel = numbers_ref[p, 2:3, :]
+            for r in spans(rels, 128):
+                here = iota((r.stop - r.start, queries), 0) + r.start
+                picks[r, i * queries : (i + 1) * queries] = onehot(here == rel)
+        parts = jnp.concatenate(split(beside(sums_ref[p] for p in members)), axis=0)
+        part = mm(parts, picks[...], NT)
+        total = part if total is None else total + part
     rel_ref[...] = total[:width, :] + total[width:, :]
 
 
-def rel_part(core, numbers, sums, rels):
+def rel_part(numbers, sums, rels):
+    count, width, queries = sums.shape
     return pl.pallas_call(
         rel_kernel,
-        in_specs=[SMEM] + [VMEM] * 2,
-        out_shape=jax.ShapeDtypeStruct((sums.shape[1], rels), f32),
+        out_shape=jax.ShapeDtypeStruct((width, rels), f32),
+        scratch_shapes=[pltpu.VMEM((rels, math.gcd(count, 16) * queries), bf16)],
         compiler_params=params(),
         cost_estimate=cost(2e9, 3e6),
         name="rel_grad",
-    )(core, numbers, sums)
+    )(numbers, sums)
 
 
 def entity_kernel(cap, want_ref, srow_ref, own_ref, recv_ref, incoming_ref, out_ref, filt_ref):
@@ -692,10 +728,14 @@
     count, _, width = incoming_ref.shape
     half, filts = filt_ref.shape[0] // 2, filt_ref.shape[1]
     grads = jnp.concatenate([incoming_ref[d, :cap, :] for d in range(count)], axis=0)
-    total = mm(grads, onehot(iota((want_ref.shape[0], rows), 1) == want_ref[...]), TN)
-    pick = onehot(iota((srow_ref.shape[0], rows), 1) == srow_ref[...])
+    turned = grads.astype(f32).T.astype(bf16)
     high, low = split(own_ref[...] + recv_ref[...])
-    out_ref[...] = total + mm(high, pick) + mm(low, pick)
+    for c in spans(rows, 256):
+        here = iota((want_ref.shape[0], c.stop - c.start), 1) + c.start
+        total = mm(turned, onehot(here == want_ref[...]))
+        here = iota((srow_ref.shape[0], c.stop - c.start), 1) + c.start
+        pick = onehot(here == srow_ref[...])
+        out_ref[:, c] = total + mm(high, pick) + mm(low, pick)
     packed = incoming_ref[0, cap:, :].astype(f32)
     for d in range(1, count):
         packed = packed + incoming_ref[d, cap:, :].astype(f32)
@@ -762,7 +802,6 @@
         return lax.all_gather(x, "shard", axis=0, axis_index_groups=same_core, tiled=True)
 
     me1 = me.reshape(1)
-    core = (me & 1).reshape(1)
     heads = head_owner[:, 0]
     tail_owners = tail_owner[:, 0]
     table_t, rtab_t, weight_t = entity_table.T, relation_table.T, proj_weight.T
@@ -782,15 +821,16 @@
     extra = BAND_OUT * (GROUPS - 1) + LANES - IMG * IMG - BAND_OUT
     ext = jnp.concatenate([chequer_perm[-BAND_OUT:], chequer_perm, chequer_perm[:extra]])[None]
     orow = heads[None, :]
-    slope, weight, img, qv, vecs = front(
+    img, qv, vecs = front(
         fetched, orow, rel_ids[None, :], rtab_t, ext, band, weight_t, head_cap, copies
     )
     core_vecs = gather_core(vecs)
 
-    qgt = score_part(qv, pos, all_tails, cand)
-    all_qgt = lax.all_gather(qgt, "shard", axis=0, tiled=True)
-    outgoing, sums, corr = back(qgt, orow, ext, img, band_t, weight, slope, count, head_cap, copies)
-    core_sums = gather_core(sums)
+    qgt = score_part(qv, pos, all_tails, cand, copies)
+    outgoing, sums, corr = back(qgt, orow, ext, img, band, band_t, weight_t, count, head_cap)
+    all_sums = lax.all_gather(sums, "shard", axis=0, tiled=True)
+    qgt, _ = lax.optimization_barrier((qgt, outgoing))
+    core_qgt = gather_core(qgt)
     incoming = exchange(filter_sums(corr, codes, outgoing, ks * ks))
 
     own, other = tail_part(ids, all_tails, scand, numbers, core_vecs, cand)
@@ -802,13 +842,10 @@
     cols = filts * IMG * IMG // count
     if direct and cols % (IMG * IMG) == 0:
         feats = column_feats(ids, rtab_t, ext, band, numbers, core_vecs, cols)
-        own, other = proj_part(core, feats, all_qgt)
+        own, other = proj_part(feats, core_qgt)
     else:
-        core_numbers, core_qgt = (
-            lax.dynamic_index_in_dim(
-                x.reshape((count // 2, 2) + x.shape[1:]), me & 1, 1, keepdims=False
-            )
-            for x in (numbers, all_qgt)
+        core_numbers = lax.dynamic_index_in_dim(
+            numbers.reshape(count // 2, 2, 4, queries), me & 1, 1, keepdims=False
         )
         own, other = (
             proj_columns(
@@ -819,8 +856,7 @@
         )
     proj_grad = (own + swap(other)).T
 
-    part = rel_part(core, numbers, core_sums, rels)
-    relation_grad = (part + swap(part)).T
+    relation_grad = rel_part(numbers, all_sums, rels).T
     return (entity_grad.T, relation_grad, filter_grad, proj_grad)
 
 

time: 180 us -> 155 us (0.86)
  blocking collectives: 43 us -> 13.9 us
  waiting for transfers between devices: 1.43 us -> 13.2 us
  Pallas kernels: 90.9 us -> 87.4 us
  starting transfers between devices: 20.8 us -> 18.4 us
  other arithmetic: 4.2 us -> 1.82 us
    all_gather x1 -> x0, blocking collectives: 29.2 us -> none  [shards(): all_qgt = lax.all_gather(qgt, 'shard', axis=0, tiled=True)]
    pallas_call x1, Pallas kernels: 18.5 us -> 10.7 us  [front(): pl.pallas_call(functools.partial(front_kernel, cap), grid=(filts // units...]
    all_to_all x2, waiting for transfers between devices: 0.29 us -> 5.62 us  [gather_core(): lax.all_to_all(x, 'shard', split_axis=0, concat_axis=0, axis_index_groups...]
    all_gather x1, waiting for transfers between devices: 0.01 us -> 4.54 us  [shards(): all_tails = lax.all_gather(tails_t, 'shard', axis=0, tiled=True)]
    pallas_call x1, Pallas kernels: 14.8 us -> 18.2 us  [back(): pl.pallas_call(functools.partial(back_kernel, cap), grid=(filts // units,...]
    all_to_all x2, starting transfers between devices: 9.32 us -> 7.1 us  [exchange(): return lax.all_to_all(x, 'shard', split_axis=0, concat_axis=0, tiled=True)]
    ppermute x3 -> x2, waiting for transfers between devices: 0.01 us -> 1.84 us  [swap(): return lax.ppermute(x, 'shard', [(d, d ^ 1) for d in range(count)])]
  transfers between devices with their start and end apart: 8 -> 8, of which waited for: 2 -> 4; matrix products, arithmetic and copies ran while one was open for 3% -> 3% of each run, Pallas kernels for 48% -> 51%
where the time goes in v6:
time: 155 us; the launch traced here: 153 us
  Pallas kernels  87.4 us (56%)
  starting transfers between devices  18.4 us (12%)
  between operations  14.2 us (9%)
  blocking collectives  13.9 us (9%)
  waiting for transfers between devices  13.2 us (9%)
  local copies, waits for them, and re-layouts  4.43 us (3%)
  other arithmetic  1.82 us (1%)
    pallas_call x1, Pallas kernels, back(): pl.pallas_call(functools.partial(back_kernel, cap), grid=(filts // units,...  18.2 us
    all_to_all x1, blocking collectives, exchange(): return lax.all_to_all(x, 'shard', split_axis=0, concat_axis=0, tiled=True)  13.9 us
    pallas_call x1, Pallas kernels, front(): pl.pallas_call(functools.partial(front_kernel, cap), grid=(filts // units...  10.7 us
    all_to_all x2, starting transfers between devices, gather_core(): lax.all_to_all(x, 'shard', split_axis=0, concat_axis=0, axis_index_groups...  10.7 us
    pallas_call x1, Pallas kernels, column_feats(): pl.pallas_call(feats_kernel, grid_spec=pltpu.PrefetchScalarGridSpec(num_s...  10.4 us
    all_to_all x2, starting transfers between devices, exchange(): return lax.all_to_all(x, 'shard', split_axis=0, concat_axis=0, tiled=True)  7.1 us
    pallas_call x1, Pallas kernels, score_part(): pl.pallas_call(functools.partial(score_kernel, cand), grid=(owners // blo...  5.73 us
    all_to_all x2, waiting for transfers between devices, gather_core(): lax.all_to_all(x, 'shard', split_axis=0, concat_axis=0, axis_index_groups...  5.62 us
  transfers between devices with their start and end apart: 8, of which 4 were waited for; matrix products, arithmetic and copies ran while one was open for 3% of the time, Pallas kernels for 51%

profile of v6, /device:TPU:0, one launch (start us, length us, event | category | flops | bytes accessed | tf_op | source)
XLA Modules:
  0.0 153.4 jit_solution(10723697955847388398)
XLA Ops:
  7.3 4.0 %pack_tails.1 = (bf16[1,200,512]{2,1,0:T(8,128)(2,1)}, s32[512,1]{1,0:T(8,128)}) custom-call(s32[1]{0:T(128)} %bitcast.me_ref, s32[32,128]{1,0:T(8,128)} %bitcast.23, s32[32,128]{1,0:T(8,128)} %bitcast.40, bf16[200,2048]{1,0:T(8,128)(2,1)} %bitcast.36), custom_call_target="tpu_custom_call" | custom-call | flops 1000000000 | bytes 2000000 | tf_op jit(solution)/shard_map/pack_tails/pallas_call | solution.py:162
  11.4 13.9 %all_to_all.25.numbers_ref = s32[16,4,128]{2,1,0:T(4,128)} all-to-all(s32[16,4,128]{2,1,0:T(4,128)S(1)} %broadcast_in_dim.4), channel_id=1, replica_groups=mesh['parts'=2,'shard'=16] {'shard'}, dimensions={0} | all-to-all | bytes 65536 | tf_op jit(solution)/shard_map/all_to_all | solution.py:795
  25.3 2.6 %find_heads.1 = (bf16[16,16,200]{2,1,0:T(8,128)(2,1)}, s32[256,1]{1,0:T(8,128)}) custom-call(s32[1]{0:T(128)} %bitcast.me_ref, bf16[200,2048]{1,0:T(8,128)(2,1)} %bitcast.37, s32[16,4,128]{2,1,0:T(4,128)} %all_to_all.25.numbers_ref), custom_call_target="tpu_custom_call" | custom-call | flops 300000000 | bytes 2000000 | tf_op jit(solution)/shard_map/find_heads/pallas_call | solution.py:218
  27.9 3.5 %all-to-all-start.1 = ((bf16[16,16,200]{2,1,0:T(8,128)(2,1)}), bf16[16,16,200]{2,1,0:T(8,128)(2,1)S(1)}, u32[]{:S(2)}, u32[]{:S(2)}) async-start(bf16[16,16,200]{2,1,0:T(8,128)(2,1)} %get-tuple-element.26), calls=%async_computation.1 | async-start | bytes 262144 | tf_op jit(solution)/shard_map/all_to_all | solution.py:795
  31.5 0.6 broadcast_in_dim.5.ext_ref
  32.2 0.7 copy.18.filt_ref
  32.9 5.2 %band.1 = (bf16[3840,256]{1,0:T(8,128)(2,1)}, bf16[256,3840]{1,0:T(8,128)(2,1)}) custom-call(s32[20,256]{1,0:T(8,128)} %constant.8.clone.codes_ref, bf16[48,81]{1,0:T(8,128)(2,1)} %copy.18.filt_ref), custom_call_target="tpu_custom_call" | custom-call | flops 40000000 | bytes 4000000 | tf_op jit(solution)/shard_map/band/pallas_call | solution.py:94
  38.1 1.2 all-to-all-done.1.fetched_ref
  39.3 0.6 copy-done.4
  39.9 10.7 %front.1 = (bf16[256,640]{1,0:T(8,128)(2,1)}, bf16[128,200]{1,0:T(8,128)(2,1)}, bf16[8,2,200,128]{3,2,1,0:T(8,128)(2,1)}) custom-call(bf16[16,16,200]{2,1,0:T(8,128)(2,1)} %copy-done.4, s32[1,128]{1,0:T(1,128)} %bitcast.31, s32[1,128]{1,0:T(1,128)} %bitcast.29, bf16[200,1387]{1,0:T(8,128)(2,1)} %bitcast.38, s32[1,576]{1,0:T(1,128)} %broadcast_in_dim.5.ext_ref, ...), custom_call_target="tpu_custom_call" | custom-call | flops 4000000000 | bytes 24000000 | tf_op jit(solution)/shard_map/front/pallas_call | solution.py:331
  50.6 4.3 %all-to-all-start.2 = ((bf16[8,2,200,128]{3,2,1,0:T(8,128)(2,1)}), bf16[8,2,200,128]{3,2,1,0:T(8,128)(2,1)S(1)}, u32[]{:S(2)}, u32[]{:S(2)}) async-start(bf16[8,2,200,128]{3,2,1,0:T(8,128)(2,1)} %get-tuple-element.28), calls=%async_computation.2 | async-start | bytes 1638400 | tf_op jit(solution)/shard_map/all_to_all | solution.py:799
  55.0 2.2 %pos_slots.1.pos_ref = s32[128,1]{1,0:T(8,128)} custom-call(s32[1,4096]{1,0:T(1,128)} %bitcast.24, s32[1,128]{1,0:T(1,128)} %bitcast.26), custom_call_target="tpu_custom_call" | custom-call | flops 10000000 | bytes 100000 | tf_op jit(solution)/shard_map/pos_slots/pallas_call | solution.py:259
  57.2 4.5 %all-gather.3.cloned.1.call-done.tails_ref.mate_ref = bf16[16,200,512]{2,1,0:T(8,128)(2,1)} async-done(((bf16[1,200,512]{2,1,0:T(8,128)(2,1)}), bf16[16,200,512]{2,1,0:T(8,128)(2,1)}) %all-gather.3.cloned.1.call-update) | async-done | bytes 3276816 | tf_op jit(solution)/shard_map/all_gather | solution.py:813
  61.7 5.7 %score.1.qgt_ref = bf16[8,200,128]{2,1,0:T(8,128)(2,1)} custom-call(s32[128,1]{1,0:T(8,128)} %pos_slots.1.pos_ref, bf16[128,200]{1,0:T(8,128)(2,1)} %get-tuple-element.31.qv_ref, bf16[16,200,512]{2,1,0:T(8,128)(2,1)} %all-gather.3.cloned.1.call-done.tails_ref.mate_ref), custom_call_target="tpu_custom_call" | custom-call | flops 1000000000 | bytes 3000000 | tf_op jit(solution)/shard_map/score/pallas_call | solution.py:397
  67.4 18.2 %back.1 = (bf16[16,16,200]{2,1,0:T(8,128)(2,1)}, f32[1,200,128]{2,1,0:T(8,128)}, f32[48,80,256]{2,1,0:T(8,128)}) custom-call(s32[1,128]{1,0:T(1,128)} %bitcast.32, s32[1,576]{1,0:T(1,128)} %broadcast_in_dim.5.ext_ref, bf16[8,200,128]{2,1,0:T(8,128)(2,1)} %score.1.qgt_ref, bf16[256,640]{1,0:T(8,128)(2,1)} %get-tuple-element.32.img_ref, ...), custom_call_target="tpu_custom_call" | custom-call | flops 6000000000 | bytes 20000000 | tf_op jit(solution)/shard_map/back/pallas_call | solution.py:469
  85.6 6.4 %all-to-all-start.4 = ((bf16[8,200,128]{2,1,0:T(8,128)(2,1)}), bf16[8,200,128]{2,1,0:T(8,128)(2,1)S(1)}, u32[]{:S(2)}, u32[]{:S(2)}) async-start(bf16[8,200,128]{2,1,0:T(8,128)(2,1)} %score.1.qgt_ref), calls=%async_computation.4 | async-start | bytes 819200 | tf_op jit(solution)/shard_map/all_to_all | solution.py:799
  92.0 3.9 %slot_cands.1.scand_ref = s32[2,512,1]{2,1,0:T(8,128)} custom-call(s32[1]{0:T(128)} %bitcast.me_ref, s32[32,128]{1,0:T(8,128)} %bitcast.25), custom_call_target="tpu_custom_call" | custom-call | flops 100000000 | bytes 1000000 | tf_op jit(solution)/shard_map/slot_cands/pallas_call | solution.py:185
  95.9 0.7 pad_add_fusion.2.ids_ref
  96.6 4.9 %filter_sums.1 = bf16[16,64,200]{2,1,0:T(8,128)(2,1)} custom-call(s32[20,256]{1,0:T(8,128)} %constant.8.clone.codes_ref, f32[48,80,256]{2,1,0:T(8,128)} %get-tuple-element.34.corr_ref, bf16[16,16,200]{2,1,0:T(8,128)(2,1)} %get-tuple-element.35.rows_ref), custom_call_target="tpu_custom_call" | custom-call | flops 100000000 | bytes 4000000 | tf_op jit(solution)/shard_map/filter_sums/pallas_call | solution.py:534
  101.5 5.6 %all-to-all-done.4.grads_ref = bf16[8,200,128]{2,1,0:T(8,128)(2,1)S(1)} async-done(((bf16[8,200,128]{2,1,0:T(8,128)(2,1)}), bf16[8,200,128]{2,1,0:T(8,128)(2,1)S(1)}, u32[]{:S(2)}, u32[]{:S(2)}) %all-to-all-start.4) | async-done | bytes 409632 | tf_op jit(solution)/shard_map/all_to_all | solution.py:799
  107.1 3.6 %all-to-all-start.3 = ((bf16[16,64,200]{2,1,0:T(8,128)(2,1)}), bf16[16,64,200]{2,1,0:T(8,128)(2,1)S(1)}, u32[]{:S(2)}, u32[]{:S(2)}) async-start(bf16[16,64,200]{2,1,0:T(8,128)(2,1)} %filter_sums.1), calls=%async_computation.3 | async-start | bytes 1048576 | tf_op jit(solution)/shard_map/all_to_all | solution.py:795
  110.7 10.4 %column_feats.1.feats_ref = bf16[2400,1024]{1,0:T(8,128)(2,1)} custom-call(s32[3]{0:T(128)} %pad_add_fusion.2.ids_ref, bf16[200,1387]{1,0:T(8,128)(2,1)} %bitcast.39, s32[1,576]{1,0:T(1,128)} %broadcast_in_dim.5.ext_ref, bf16[3840,256]{1,0:T(8,128)(2,1)} %get-tuple-element.27.band_ref.mate_ref, bf16[3840,256]{1,0:T(8,128)(2,1)} %get-tuple-element.27.band_ref.mate_ref, ...), custom_call_target="tpu_custom_call" | custom-call | flops 6000000000 | bytes 6000000 | tf_op jit(solution)/shard_map/column_feats/pallas_call | solution.py:629
  121.1 5.0 %proj_grad.1 = (f32[200,1200]{1,0:T(8,128)}, f32[200,1200]{1,0:T(8,128)}) custom-call(bf16[2400,1024]{1,0:T(8,128)(2,1)} %column_feats.1.feats_ref, bf16[8,200,128]{2,1,0:T(8,128)(2,1)} %copy-done.1), custom_call_target="tpu_custom_call" | custom-call | flops 1000000000 | bytes 8000000 | tf_op jit(solution)/shard_map/proj_grad/pallas_call | solution.py:667
  126.2 0.4 collective-permute-start.1
  126.6 5.0 %tail_grad.1 = (f32[200,512]{1,0:T(8,128)}, f32[200,512]{1,0:T(8,128)}) custom-call(s32[3]{0:T(128)} %pad_add_fusion.2.ids_ref, bf16[16,200,512]{2,1,0:T(8,128)(2,1)} %all-gather.3.cloned.1.call-done.tails_ref.mate_ref, bf16[16,200,512]{2,1,0:T(8,128)(2,1)} %all-gather.3.cloned.1.call-done.tails_ref.mate_ref, s32[2,512,1]{2,1,0:T(8,128)} %slot_cands.1.scand_ref, ...), custom_call_target="tpu_custom_call" | custom-call | flops 2000000000 | bytes 3000000 | tf_op jit(solution)/shard_map/tail_grad/pallas_call | solution.py:568
  131.7 1.8 %collective-permute-done.recv_ref = f32[200,512]{1,0:T(8,128)S(1)} collective-permute-done((f32[200,512]{1,0:T(8,128)}, f32[200,512]{1,0:T(8,128)S(1)}, u32[]{:S(2)}, u32[]{:S(2)}) %collective-permute-start) | collective-permute-done | bytes 409632 | tf_op jit(solution)/shard_map/ppermute | solution.py:792
  133.5 0.8 copy-done.11
  134.4 4.2 %entity_grad.1 = (f32[200,2048]{1,0:T(8,128)}, f32[96,48]{1,0:T(8,128)}) custom-call(s32[256,1]{1,0:T(8,128)} %get-tuple-element.23.want_ref, s32[512,1]{1,0:T(8,128)} %get-tuple-element.24.srow_ref, f32[200,512]{1,0:T(8,128)} %get-tuple-element.29.own_ref, f32[200,512]{1,0:T(8,128)} %copy-done.11, bf16[16,64,200]{2,1,0:T(8,128)(2,1)} %copy-done.3), custom_call_target="tpu_custom_call" | custom-call | flops 1500000000 | bytes 4000000 | tf_op jit(solution)/shard_map/entity_grad/pallas_call | solution.py:752
  138.7 0.8 slice_bitcast_fusion
  139.5 0.6 reshape.25
  140.1 1.1 add_bitcast_fusion
  141.2 5.4 %rel_grad.1 = f32[200,1387]{1,0:T(8,128)} custom-call(s32[16,4,128]{2,1,0:T(4,128)} %all_to_all.25.numbers_ref, f32[16,200,128]{2,1,0:T(8,128)} %all-gather.5.cloned.1.call-done.sums_ref), custom_call_target="tpu_custom_call" | custom-call | flops 2000000000 | bytes 3000000 | tf_op jit(solution)/shard_map/rel_grad/pallas_call | solution.py:716
  (38 shorter events, 0.6 us)
Async XLA Ops:
  7.2 4.1 %copy-start.6 = (s32[128]{0:T(128)S(1)}, s32[128]{0:T(128)}, u32[]{:S(2)}) copy-start(s32[128]{0:T(128)} %param.20) | copy-start | bytes 1540
  7.2 4.1 %copy-start.9 = (s32[128]{0:T(128)S(1)}, s32[128]{0:T(128)}, u32[]{:S(2)}) copy-start(s32[128]{0:T(128)} %param.19) | copy-start | bytes 1540
  7.2 4.1 %copy-start.8 = (s32[128]{0:T(128)S(1)}, s32[128]{0:T(128)}, u32[]{:S(2)}) copy-start(s32[128]{0:T(128)} %param.18) | copy-start | bytes 1540
  7.2 4.1 %copy-start.10 = (s32[128,1]{0,1:T(1,128)S(1)}, s32[128,1]{0,1:T(1,128)}, u32[]{:S(2)}) copy-start(s32[128,1]{0,1:T(1,128)} %param.17) | copy-start | bytes 1540
  7.2 54.5 %all-gather.3.cloned.1.call-start = ((), (), s32[]{:S(2)}) async-start(), calls=%async_computation.5 | async-start | bytes 3481600 | tf_op jit(solution)/shard_map/all_gather | solution.py:813
  7.3 24.1 %copy-start.7 = (s32[400]{0:T(512)S(1)}, s32[400]{0:T(512)}, u32[]{:S(2)}) copy-start(s32[400]{0:T(512)} %param.16) | copy-start | bytes 4804
  7.3 24.2 %slice-start = ((s32[400]{0:T(512)}), s32[96]{0:T(128)S(1)}, s32[]{:S(2)}) async-start(s32[400]{0:T(512)} %param.16), calls=%async_computation.7 | async-start | bytes 1024 | tf_op jit(solution)/shard_map/slice | solution.py:822
  7.3 24.9 %copy-start.5 = (bf16[48,9,9]{0,2,1:T(8,128)(2,1)S(1)}, bf16[48,9,9]{0,2,1:T(8,128)(2,1)}, u32[]{:S(2)}) copy-start(bf16[48,9,9]{0,2,1:T(8,128)(2,1)} %param.14) | copy-start | bytes 23332
  27.9 11.4 %all-to-all-start.1 = ((bf16[16,16,200]{2,1,0:T(8,128)(2,1)}), bf16[16,16,200]{2,1,0:T(8,128)(2,1)S(1)}, u32[]{:S(2)}, u32[]{:S(2)}) async-start(bf16[16,16,200]{2,1,0:T(8,128)(2,1)} %get-tuple-element.26), calls=%async_computation.1 | async-start | bytes 262144 | tf_op jit(solution)/shard_map/all_to_all | solution.py:795
  39.3 0.6 copy-start.4
  50.6 35.0 %all-to-all-start.2 = ((bf16[8,2,200,128]{3,2,1,0:T(8,128)(2,1)}), bf16[8,2,200,128]{3,2,1,0:T(8,128)(2,1)S(1)}, u32[]{:S(2)}, u32[]{:S(2)}) async-start(bf16[8,2,200,128]{3,2,1,0:T(8,128)(2,1)} %get-tuple-element.28), calls=%async_computation.2 | async-start | bytes 1638400 | tf_op jit(solution)/shard_map/all_to_all | solution.py:799
  54.9 86.2 %all-gather.5.cloned.1.call-start = ((), (), s32[]{:S(2)}) async-start(), calls=%async_computation.6 | async-start | bytes 1740800 | tf_op jit(solution)/shard_map/all_gather | solution.py:831
  85.6 15.9 %copy-start = (bf16[8,2,200,128]{3,2,1,0:T(8,128)(2,1)}, bf16[8,2,200,128]{3,2,1,0:T(8,128)(2,1)S(1)}, u32[]{:S(2)}) copy-start(bf16[8,2,200,128]{3,2,1,0:T(8,128)(2,1)S(1)} %all-to-all-done.2.vecs_ref) | copy-start | bytes 2457604
  85.6 21.5 %all-to-all-start.4 = ((bf16[8,200,128]{2,1,0:T(8,128)(2,1)}), bf16[8,200,128]{2,1,0:T(8,128)(2,1)S(1)}, u32[]{:S(2)}, u32[]{:S(2)}) async-start(bf16[8,200,128]{2,1,0:T(8,128)(2,1)} %score.1.qgt_ref), calls=%async_computation.4 | async-start | bytes 819200 | tf_op jit(solution)/shard_map/all_to_all | solution.py:799
  107.1 14.0 %copy-start.1 = (bf16[8,200,128]{2,1,0:T(8,128)(2,1)}, bf16[8,200,128]{2,1,0:T(8,128)(2,1)S(1)}, u32[]{:S(2)}) copy-start(bf16[8,200,128]{2,1,0:T(8,128)(2,1)S(1)} %all-to-all-done.4.grads_ref) | copy-start | bytes 1228804
  107.1 26.4 %all-to-all-start.3 = ((bf16[16,64,200]{2,1,0:T(8,128)(2,1)}), bf16[16,64,200]{2,1,0:T(8,128)(2,1)S(1)}, u32[]{:S(2)}, u32[]{:S(2)}) async-start(bf16[16,64,200]{2,1,0:T(8,128)(2,1)} %filter_sums.1), calls=%async_computation.3 | async-start | bytes 1048576 | tf_op jit(solution)/shard_map/all_to_all | solution.py:795
  126.2 13.9 %collective-permute-start.1 = (f32[200,1200]{1,0:T(8,128)}, f32[200,1200]{1,0:T(8,128)S(1)}, u32[]{:S(2)}, u32[]{:S(2)}) collective-permute-start(f32[200,1200]{1,0:T(8,128)} %get-tuple-element.41), channel_id=1, source_target_pairs={{0,1},{1,0},{2,3},{3,2},{4,5},{5,4},{6,7},{7,6},{8,9},{9,8},{10,11... | collective-permute-start | bytes 2880008 | tf_op jit(solution)/shard_map/ppermute | solution.py:792
  131.5 2.0 %collective-permute-start = (f32[200,512]{1,0:T(8,128)}, f32[200,512]{1,0:T(8,128)S(1)}, u32[]{:S(2)}, u32[]{:S(2)}) collective-permute-start(f32[200,512]{1,0:T(8,128)} %get-tuple-element.30), channel_id=1, source_target_pairs={{0,1},{1,0},{2,3},{3,2},{4,5},{5,4},{6,7},{7,6},{8,9},{9,8},{10,11... | collective-permute-start | bytes 1228808 | tf_op jit(solution)/shard_map/ppermute | solution.py:792
  133.5 0.8 copy-start.11
  133.5 0.9 copy-start.3
  134.4 5.7 %copy-start.2 = (f32[200,1200]{1,0:T(8,128)S(1)}, f32[200,1200]{1,0:T(8,128)}, u32[]{:S(2)}) copy-start(f32[200,1200]{1,0:T(8,128)} %get-tuple-element.40) | copy-start | bytes 2880004
Sparse Core Ops, SparseCore 0:
  11.4 50.2 all-gather.2
  85.7 46.7 all-gather.4

commit v7 on v6

--- a/solution.py
+++ b/solution.py
@@ -126,6 +126,11 @@
         for c in spans(lanes, 256):
             here = iota((r.stop - r.start, c.stop - c.start), 1) + c.start
             ref[r, c] = onehot(here == index[r, :])
+
+
+def field(ref, d, k):
+    queries = ref.shape[2] // 4
+    return ref[d, :, k * queries : (k + 1) * queries]
 
 
 def slot_values(owner, device, value, cap):
@@ -173,35 +178,17 @@
     )(me, tail_owners.reshape(-1, 128), tail_row.reshape(-1, 128), table_t)
 
 
-def cand_kernel(me_ref, owner_ref, out_ref):
-    cap = out_ref.shape[1]
-    owner = owner_ref[...]
-    index = iota(owner.shape, 0) * 128 + iota(owner.shape, 1)
-    for k in range(2):
-        out_ref[k] = slot_values(owner, me_ref[0] ^ k, index, cap)
-
-
-def slot_cands(me, tail_owners, cap):
-    return pl.pallas_call(
-        cand_kernel,
-        in_specs=[SMEM, VMEM],
-        out_shape=jax.ShapeDtypeStruct((2, cap, 1), i32),
-        compiler_params=params(),
-        cost_estimate=cost(1e8, 1e6),
-        name="slot_cands",
-    )(me, tail_owners.reshape(-1, 128))
-
-
 def found_kernel(cap, me_ref, table_ref, numbers_ref, found_ref, want_ref, scr, picks):
-    count, _, queries = numbers_ref.shape
-    owners = jnp.concatenate([numbers_ref[d, 0:1, :] for d in range(count)], axis=0)
+    count = numbers_ref.shape[0]
+    owners = jnp.concatenate([field(numbers_ref, d, 0) for d in range(count)], axis=0)
+    queries = owners.shape[1]
     mine = owners == me_ref[0]
     before = onehot(iota((queries, queries), 0) < iota((queries, queries), 1))
     rank = mm(onehot(mine), before)
     key = jnp.where(mine, rank.astype(i32), -1)
     slots = iota((cap, queries), 0)
     for d in range(count):
-        code = (numbers_ref[d, 1:2, :] + 1).astype(f32)
+        code = (field(numbers_ref, d, 1) + 1).astype(f32)
         picked = jnp.where(slots == key[d : d + 1, :], code, 0.0)
         scr[d * cap : (d + 1) * cap, :] = jnp.sum(picked, axis=1, keepdims=True)
     want = scr[...].astype(i32) - 1
@@ -232,37 +219,42 @@
     )(me, table_t, numbers)
 
 
-def pos_kernel(cap, owner_ref, pos_ref, out_ref):
-    cand = owner_ref.shape[1]
+def slots_kernel(me_ref, owner_ref, row_ref, pos_ref, cand_ref, out_ref):
+    cap = cand_ref.shape[1]
+    owner = owner_ref[...]
+    index = iota(owner.shape, 0) * 128 + iota(owner.shape, 1)
+    for k in range(2):
+        cand_ref[k] = slot_values(owner, me_ref[0] ^ k, index, cap)
     queries = pos_ref.shape[1]
     eye = iota((queries, queries), 0) == iota((queries, queries), 1)
-    step = min(128, cand)
     row = pos_ref[...].astype(f32)
     pos = jnp.sum(jnp.where(eye, row, 0.0), axis=1, keepdims=True).astype(i32)
-    owner = jnp.zeros((queries, step), f32)
-    for c in range(0, cand, step):
-        here = iota((queries, step), 1) + c
-        value = owner_ref[:, c : c + step].astype(f32)
-        owner = owner + jnp.where(here == pos, value, 0.0)
+    lanes = spans(row_ref.shape[1], 128)
+    owner = jnp.zeros((queries, 128), f32)
+    for c in lanes:
+        here = iota((queries, 128), 1) + c.start
+        owner = owner + jnp.where(here == pos, row_ref[:, c].astype(f32), 0.0)
     owner = jnp.sum(owner, axis=1, keepdims=True).astype(i32)
-    ahead = jnp.zeros((queries, step), f32)
-    for c in range(0, cand, step):
-        here = iota((queries, step), 1) + c
-        same = (owner_ref[:, c : c + step] == owner) & (here < pos)
-        ahead = ahead + jnp.where(same, 1.0, 0.0)
+    ahead = jnp.zeros((queries, 128), f32)
+    for c in lanes:
+        here = iota((queries, 128), 1) + c.start
+        ahead = ahead + jnp.where((row_ref[:, c] == owner) & (here < pos), 1.0, 0.0)
     ahead = jnp.sum(ahead, axis=1, keepdims=True).astype(i32)
     out_ref[...] = owner * cap + ahead
 
 
-def pos_slots(tail_owners, pos_index, cap):
-    queries = pos_index.shape[0]
-    return pl.pallas_call(
-        functools.partial(pos_kernel, cap),
-        out_shape=jax.ShapeDtypeStruct((queries, 1), i32),
+def slot_tables(me, tail_owners, pos_index, cap):
+    return pl.pallas_call(
+        slots_kernel,
+        in_specs=[SMEM] + [VMEM] * 3,
+        out_shape=[
+            jax.ShapeDtypeStruct((2, cap, 1), i32),
+            jax.ShapeDtypeStruct((pos_index.shape[0], 1), i32),
+        ],
         compiler_params=params(),
-        cost_estimate=cost(1e7, 1e5),
-        name="pos_slots",
-    )(tail_owners.reshape(1, -1), pos_index.reshape(1, -1))
+        cost_estimate=cost(1e9, 1e6),
+        name="slot_tables",
+    )(me, tail_owners.reshape(-1, 128), tail_owners.reshape(1, -1), pos_index.reshape(1, -1))
 
 
 def slot_picks(cap, slots, orow):
@@ -277,7 +269,7 @@
 
 def front_kernel(
     cap, fetched_ref, orow_ref, rel_ref, rtab_ref, ext_ref, band_ref, w_ref,
-    img_ref, qv_ref, vecs_ref, feats, acc, ext, pre,
+    slope_ref, img_ref, qv_ref, vecs_ref, feats, acc, ext, pre,
 ):
     s = pl.program_id(0)
     width, queries = acc.shape
@@ -306,7 +298,9 @@
         for g in range(GROUPS):
             rows = slice(f * flat + g * BAND_OUT, f * flat + (g + 1) * BAND_OUT)
             v = pre[f * BAND_OUT : (f + 1) * BAND_OUT, g * queries : (g + 1) * queries]
-            feats[rows, :] = (v * sigmoid(v)).astype(bf16)
+            sig = sigmoid(v)
+            feats[rows, :] = (v * sig).astype(bf16)
+            slope_ref[rows, :] = sig * (1.0 + v * (1.0 - sig))
     acc[...] += mm(w_ref[...], feats[...])
 
     @pl.when(s == pl.num_programs(0) - 1)
@@ -341,11 +335,13 @@
             pl.BlockSpec((width, cols), lambda s: (0, s)),
         ],
         out_specs=[
+            pl.BlockSpec((cols, queries), lambda s: (s, 0)),
             whole((LANES, GROUPS * queries)),
             whole((queries, width)),
             whole((copies, 2, width, queries)),
         ],
         out_shape=[
+            jax.ShapeDtypeStruct((flat, queries), f32),
             jax.ShapeDtypeStruct((LANES, GROUPS * queries), bf16),
             jax.ShapeDtypeStruct((queries, width), bf16),
             jax.ShapeDtypeStruct((copies, 2, width, queries), bf16),
@@ -385,12 +381,10 @@
 
     @pl.when(step == pl.num_programs(0) - 1)
     def _():
-        qgt = total.T.astype(bf16)
-        for d in range(out_ref.shape[0]):
-            out_ref[d] = qgt
-
-
-def score_part(qv, pos, tails, cand, copies):
+        out_ref[0] = total.T
+
+
+def score_part(qv, pos, tails, cand):
     queries, width = qv.shape
     owners, _, cap = tails.shape
     blocks = math.gcd(owners, max(1, 2048 // cap))
@@ -402,8 +396,8 @@
             whole(qv.shape),
             pl.BlockSpec((blocks, width, cap), lambda s: (s, 0, 0)),
         ],
-        out_specs=whole((copies, width, queries)),
-        out_shape=jax.ShapeDtypeStruct((copies, width, queries), bf16),
+        out_specs=whole((1, width, queries)),
+        out_shape=jax.ShapeDtypeStruct((1, width, queries), f32),
         scratch_shapes=[
             pltpu.VMEM((queries, width), f32),
             pltpu.VMEM((blocks, queries, cap), f32),
@@ -416,8 +410,8 @@
 
 
 def back_kernel(
-    cap, orow_ref, ext_ref, qgt_ref, img_ref, band_ref, bandt_ref, w_ref,
-    out_ref, sums_ref, corr_ref, fgrad, spread, ext, pre, linear,
+    cap, orow_ref, ext_ref, qgt_ref, bandt_ref, w_ref, slope_ref,
+    out_ref, sums_ref, fgrad_ref, spread, ext, linear,
 ):
     s = pl.program_id(0)
     _, width, queries = qgt_ref.shape
@@ -428,18 +422,14 @@
 
     units = bandt_ref.shape[1] // BAND_OUT
     flat = GROUPS * BAND_OUT
-    pre[...] = mm(band_ref[...], img_ref[...])
-    linear[...] = mm(w_ref[...], qgt_ref[0], TN)
+    linear[...] = mm(w_ref[...], qgt_ref[0].astype(bf16), TN)
     for f in range(units):
         for g in range(GROUPS):
             rows = slice(f * flat + g * BAND_OUT, f * flat + (g + 1) * BAND_OUT)
             part = slice(f * BAND_OUT, (f + 1) * BAND_OUT)
             lanes = slice(g * queries, (g + 1) * queries)
-            v = pre[part, lanes]
-            sig = sigmoid(v)
-            fgrad[part, lanes] = (linear[rows, :] * (sig * (1.0 + v * (1.0 - sig)))).astype(bf16)
-    spread[...] += mm(bandt_ref[...], fgrad[...])
-    corr_ref[...] = mm(fgrad[...], img_ref[...], NT).reshape(units, BAND_OUT, LANES)
+            fgrad_ref[part, lanes] = (linear[rows, :] * slope_ref[rows, :]).astype(bf16)
+    spread[...] += mm(bandt_ref[...], fgrad_ref[...])
 
     @pl.when(s == pl.num_programs(0) - 1)
     def _():
@@ -452,7 +442,8 @@
         rpick = onehot(entry + width == ext_ref[...])
         hgrad = (mm(hpick, high) + mm(hpick, low)).astype(bf16)
         rgrad = mm(rpick, high) + mm(rpick, low)
-        sums_ref[0] = rgrad
+        for d in range(sums_ref.shape[0]):
+            sums_ref[d] = rgrad
         blocks = out_ref.shape[0]
         pick = slot_picks(cap, blocks * cap, orow_ref[...])
         rows = mm(pick, hgrad, NT).astype(bf16)
@@ -460,11 +451,11 @@
             out_ref[d] = rows[d * cap : (d + 1) * cap, :]
 
 
-def back(qgt, orow, ext, img, band, band_t, weight_t, count, cap):
+def back(qgt, orow, ext, band_t, weight_t, slope, count, cap, copies):
     _, width, queries = qgt.shape
     flat = weight_t.shape[1]
     filts = band_t.shape[1] // BAND_OUT
-    units = filter_block(filts)
+    units = math.gcd(filts, 16)
     cols = flat // filts * units
     return pl.pallas_call(
         functools.partial(back_kernel, cap),
@@ -472,40 +463,48 @@
         in_specs=[
             whole(orow.shape),
             whole(ext.shape),
-            whole((1, width, queries)),
-            whole(img.shape),
-            pl.BlockSpec((units * BAND_OUT, LANES), lambda s: (s, 0)),
+            whole(qgt.shape),
             pl.BlockSpec((LANES, units * BAND_OUT), lambda s: (0, s)),
             pl.BlockSpec((width, cols), lambda s: (0, s)),
+            pl.BlockSpec((cols, queries), lambda s: (s, 0)),
         ],
         out_specs=[
             whole((count, cap, width)),
-            whole((1, width, queries)),
-            pl.BlockSpec((units, BAND_OUT, LANES), lambda s: (s, 0, 0)),
+            whole((copies, width, queries)),
+            pl.BlockSpec((units * BAND_OUT, GROUPS * queries), lambda s: (s, 0)),
         ],
         out_shape=[
             jax.ShapeDtypeStruct((count, cap, width), bf16),
-            jax.ShapeDtypeStruct((1, width, queries), f32),
-            jax.ShapeDtypeStruct((filts, BAND_OUT, LANES), f32),
+            jax.ShapeDtypeStruct((copies, width, queries), f32),
+            jax.ShapeDtypeStruct((filts * BAND_OUT, GROUPS * queries), bf16),
         ],
         scratch_shapes=[
-            pltpu.VMEM((units * BAND_OUT, GROUPS * queries), bf16),
             pltpu.VMEM((LANES, GROUPS * queries), f32),
             pltpu.VMEM((ext.shape[1], queries), f32),
-            pltpu.VMEM((units * BAND_OUT, GROUPS * queries), f32),
             pltpu.VMEM((cols, queries), f32),
         ],
         compiler_params=params("arbitrary"),
-        cost_estimate=cost(6e9, 2e7, 2.5e6),
+        cost_estimate=cost(6e9, 2e7),
         name="back",
-    )(orow, ext, qgt, img, band, band_t, weight_t)
+    )(orow, ext, qgt, band_t, weight_t, slope)
 
 
 def half_taps(taps):
     return -(-taps // 32) * 16
 
 
-def diag_kernel(taps, codes_ref, corr_ref, rows_ref, out_ref):
+def diag_kernel(taps, codes_ref, fgrad_ref, img_ref, rows_ref, out_ref, corr_ref):
+    s = pl.program_id(0)
+    units = fgrad_ref.shape[0] // BAND_OUT
+    part = mm(fgrad_ref[...], img_ref[...], NT)
+    corr_ref[pl.ds(s * units, units)] = part.reshape(units, BAND_OUT, LANES)
+
+    @pl.when(s == pl.num_programs(0) - 1)
+    def _():
+        diag_sums(taps, codes_ref, corr_ref, rows_ref, out_ref)
+
+
+def diag_sums(taps, codes_ref, corr_ref, rows_ref, out_ref):
     filts = corr_ref.shape[0]
     cap, width = rows_ref.shape[1:]
     half = half_taps(taps)
@@ -528,16 +527,28 @@
         out_ref[d, cap:, :] = packed
 
 
-def filter_sums(corr, codes, rows, taps):
+def filter_sums(fgrad, img, codes, rows, taps):
     count, cap, width = rows.shape
-    assert 4 * corr.shape[0] <= width
+    filts = fgrad.shape[0] // BAND_OUT
+    units = filter_block(filts)
+    assert 4 * filts <= width
+    out = (count, cap + half_taps(taps), width)
     return pl.pallas_call(
         functools.partial(diag_kernel, taps),
-        out_shape=jax.ShapeDtypeStruct((count, cap + half_taps(taps), width), bf16),
-        compiler_params=params(),
-        cost_estimate=cost(1e8, 4e6),
+        grid=(filts // units,),
+        in_specs=[
+            whole(codes.shape),
+            pl.BlockSpec((units * BAND_OUT, fgrad.shape[1]), lambda s: (s, 0)),
+            whole(img.shape),
+            whole(rows.shape),
+        ],
+        out_specs=whole(out),
+        out_shape=jax.ShapeDtypeStruct(out, bf16),
+        scratch_shapes=[pltpu.VMEM((filts, BAND_OUT, LANES), f32)],
+        compiler_params=params("arbitrary"),
+        cost_estimate=cost(2e9, 6e6),
         name="filter_sums",
-    )(codes, corr, rows)
+    )(codes, fgrad, img, rows)
 
 
 def tail_kernel(
@@ -550,7 +561,7 @@
     other = jnp.zeros(own_ref.shape, f32)
     for i, group in enumerate(pairs(vecs_ref.shape[0])):
         qvt = beside(vecs_ref[p, 1] for p in group)
-        pos = beside(numbers_ref[2 * p + ids_ref[2], 3:4, :] for p in group)
+        pos = beside(field(numbers_ref, 2 * p + ids_ref[2], 3) for p in group)
         score, grad = scores.at[i % 2], grads.at[i % 2]
         score[...] = mm(tails, qvt)
         for r in spans(2 * cap, 64):
@@ -591,39 +602,37 @@
 
 
 def feats_kernel(
-    ids_ref, rtab_ref, ext_ref, band_ref, mate_ref, numbers_ref, vecs_ref, out_ref, pick, hmat, rmat, pre, rpick
+    ids_ref, rtab_ref, ext_ref, band_ref, mate_ref, numbers_ref, vecs_ref, out_ref, hpick, rpick, rels_hot, ext, pre
 ):
     width, rels = rtab_ref.shape
     units = band_ref.shape[0] // BAND_OUT
     flat = GROUPS * BAND_OUT
     cols = units * flat
     entry = iota((width, ext_ref.shape[1]), 0)
-    for part, mat in ((0, hmat), (width, rmat)):
-        pick[...] = jnp.where(entry + part == ext_ref[...], 1.0, 0.0).T.astype(bf16)
+    hpick[...] = jnp.where(entry == ext_ref[...], 1.0, 0.0).T.astype(bf16)
+    rpick[...] = jnp.where(entry + width == ext_ref[...], 1.0, 0.0).T.astype(bf16)
+    queries = vecs_ref.shape[3]
+    for i, group in enumerate(pairs(vecs_ref.shape[0])):
+        hvt = beside(vecs_ref[p, 0] for p in group)
+        rel = beside(field(numbers_ref, 2 * p + ids_ref[2], 2) for p in group)
+        for r in spans(rels, 64):
+            rels_hot[r, :] = onehot(iota((r.stop - r.start, rel.shape[1]), 0) + r.start == rel)
+        rvt = mm(rtab_ref[...], rels_hot[...]).astype(bf16)
+        image = ext.at[i % 2]
+        image[...] = (mm(hpick[...], hvt) + mm(rpick[...], rvt)).astype(bf16)
+        lanes = slice(group[0] * queries, (group[-1] + 1) * queries)
         for k, source in enumerate((band_ref, mate_ref)):
             for g in range(GROUPS):
-                rows = mm(source[...], pick[g * BAND_OUT : g * BAND_OUT + LANES, :]).astype(bf16)
+                slot = (k * GROUPS + g) % 2
+                pre[slot] = mm(source[...], image[g * BAND_OUT : g * BAND_OUT + LANES, :])
                 for f in range(units):
+                    v = pre[slot, f * BAND_OUT : (f + 1) * BAND_OUT, :]
                     first = k * cols + f * flat + g * BAND_OUT
-                    mat[first : first + BAND_OUT, :] = rows[f * BAND_OUT : (f + 1) * BAND_OUT, :]
-    queries = vecs_ref.shape[3]
-    for group in pairs(vecs_ref.shape[0]):
-        hvt = beside(vecs_ref[p, 0] for p in group)
-        rel = beside(numbers_ref[2 * p + ids_ref[2], 2:3, :] for p in group)
-        for r in spans(rels, 64):
-            rpick[r, :] = onehot(iota((r.stop - r.start, rel.shape[1]), 0) + r.start == rel)
-        rvt = mm(rtab_ref[...], rpick[...]).astype(bf16)
-        lanes = slice(group[0] * queries, (group[-1] + 1) * queries)
-        for k in range(2):
-            rows = slice(k * cols, (k + 1) * cols)
-            pre[k] = mm(hmat[rows, :], hvt) + mm(rmat[rows, :], rvt)
-            for r in spans(cols, 80):
-                v = pre[k, r, :]
-                out_ref[k * cols + r.start : k * cols + r.stop, lanes] = (v * sigmoid(v)).astype(bf16)
+                    out_ref[first : first + BAND_OUT, lanes] = (v * sigmoid(v)).astype(bf16)
 
 
 def column_feats(ids, rtab_t, ext, band, numbers, vecs, cols):
-    width = rtab_t.shape[0]
+    width, rels = rtab_t.shape
     unit = cols // GROUPS
     gathered, _, _, queries = vecs.shape
     return pl.pallas_call(
@@ -642,35 +651,37 @@
             out_specs=whole((2 * cols, gathered * queries)),
             scratch_shapes=[
                 pltpu.VMEM((ext.shape[1], width), bf16),
-                pltpu.VMEM((2 * cols, width), bf16),
-                pltpu.VMEM((2 * cols, width), bf16),
-                pltpu.VMEM((2, cols, 2 * queries), f32),
-                pltpu.VMEM((rtab_t.shape[1], 2 * queries), bf16),
+                pltpu.VMEM((ext.shape[1], width), bf16),
+                pltpu.VMEM((rels, 2 * queries), bf16),
+                pltpu.VMEM((2, ext.shape[1], 2 * queries), bf16),
+                pltpu.VMEM((2, unit, 2 * queries), f32),
             ],
         ),
         out_shape=jax.ShapeDtypeStruct((2 * cols, gathered * queries), bf16),
         compiler_params=params("arbitrary"),
-        cost_estimate=cost(6e9, 6e6, 2.5e6),
+        cost_estimate=cost(5e9, 6e6, 2.5e6),
         name="column_feats",
     )(ids, rtab_t, ext, band, band, numbers, vecs)
 
 
-def proj_kernel(feats_ref, grads_ref, own_ref, other_ref):
+def proj_kernel(core_ref, feats_ref, grads_ref, own_ref, other_ref):
     cols = own_ref.shape[1]
-    qgt = beside(grads_ref[p] for p in range(grads_ref.shape[0]))
+    count = grads_ref.shape[0] // 2
+    qgt = beside(grads_ref[2 * p + core_ref[0]].astype(bf16) for p in range(count))
     own_ref[...] = mm(qgt, feats_ref[:cols, :], NT)
     other_ref[...] = mm(qgt, feats_ref[cols:, :], NT)
 
 
-def proj_part(feats, grads):
+def proj_part(core, feats, grads):
     half = jax.ShapeDtypeStruct((grads.shape[1], feats.shape[0] // 2), f32)
     return pl.pallas_call(
         proj_kernel,
+        in_specs=[SMEM] + [VMEM] * 2,
         out_shape=[half, half],
         compiler_params=params(),
         cost_estimate=cost(1e9, 8e6),
         name="proj_grad",
-    )(feats, grads)
+    )(core, feats, grads)
 
 
 def proj_columns(first, cols, filters, chequer_perm, relation_table, numbers, heads, grads):
@@ -694,14 +705,14 @@
     return mm(qg, (pre * sigmoid(pre)).astype(bf16), TN)
 
 
-def rel_kernel(numbers_ref, sums_ref, rel_ref, picks):
+def rel_kernel(core_ref, numbers_ref, sums_ref, rel_ref, picks):
     width, rels = rel_ref.shape
     queries = sums_ref.shape[2]
     total = None
     for block in spans(sums_ref.shape[0], picks.shape[1] // queries):
         members = range(block.start, block.stop)
         for i, p in enumerate(members):
-            rel = numbers_ref[p, 2:3, :]
+            rel = field(numbers_ref, 2 * p + core_ref[0], 2)
             for r in spans(rels, 128):
                 here = iota((r.stop - r.start, queries), 0) + r.start
                 picks[r, i * queries : (i + 1) * queries] = onehot(here == rel)
@@ -711,16 +722,17 @@
     rel_ref[...] = total[:width, :] + total[width:, :]
 
 
-def rel_part(numbers, sums, rels):
+def rel_part(core, numbers, sums, rels):
     count, width, queries = sums.shape
     return pl.pallas_call(
         rel_kernel,
+        in_specs=[SMEM] + [VMEM] * 2,
         out_shape=jax.ShapeDtypeStruct((width, rels), f32),
-        scratch_shapes=[pltpu.VMEM((rels, math.gcd(count, 16) * queries), bf16)],
+        scratch_shapes=[pltpu.VMEM((rels, math.gcd(count, 8) * queries), bf16)],
         compiler_params=params(),
         cost_estimate=cost(2e9, 3e6),
         name="rel_grad",
-    )(numbers, sums)
+    )(core, numbers, sums)
 
 
 def entity_kernel(cap, want_ref, srow_ref, own_ref, recv_ref, incoming_ref, out_ref, filt_ref):
@@ -802,36 +814,35 @@
         return lax.all_gather(x, "shard", axis=0, axis_index_groups=same_core, tiled=True)
 
     me1 = me.reshape(1)
+    core = (me & 1).reshape(1)
     heads = head_owner[:, 0]
     tail_owners = tail_owner[:, 0]
     table_t, rtab_t, weight_t = entity_table.T, relation_table.T, proj_weight.T
-    numbers = jnp.stack([heads, head_row, rel_ids, pos_index])[None]
-    numbers = exchange(jnp.broadcast_to(numbers, (count,) + numbers.shape[1:]))
+    numbers = jnp.concatenate([heads, head_row, rel_ids, pos_index])
+    numbers = exchange(jnp.broadcast_to(numbers, (count, 1, 4 * queries)))
 
     ids = jnp.stack([me, me ^ 1, me & 1])
     tails_t, slot_row = pack_tails(me1, tail_owners, tail_row, table_t, tail_cap)
     all_tails = lax.all_gather(tails_t, "shard", axis=0, tiled=True)
-    scand = slot_cands(me1, tail_owners, tail_cap)
+    scand, pos = slot_tables(me1, tail_owners, pos_index, tail_cap)
     found, want = find_heads(me1, numbers, table_t, head_cap)
     fetched = exchange(found)
-    pos = pos_slots(tail_owners, pos_index, tail_cap)
 
     codes = jnp.asarray(band_codes(ks))
     band, band_t = build_band(filters, codes)
     extra = BAND_OUT * (GROUPS - 1) + LANES - IMG * IMG - BAND_OUT
     ext = jnp.concatenate([chequer_perm[-BAND_OUT:], chequer_perm, chequer_perm[:extra]])[None]
     orow = heads[None, :]
-    img, qv, vecs = front(
+    slope, img, qv, vecs = front(
         fetched, orow, rel_ids[None, :], rtab_t, ext, band, weight_t, head_cap, copies
     )
     core_vecs = gather_core(vecs)
 
-    qgt = score_part(qv, pos, all_tails, cand, copies)
-    outgoing, sums, corr = back(qgt, orow, ext, img, band, band_t, weight_t, count, head_cap)
-    all_sums = lax.all_gather(sums, "shard", axis=0, tiled=True)
-    qgt, _ = lax.optimization_barrier((qgt, outgoing))
-    core_qgt = gather_core(qgt)
-    incoming = exchange(filter_sums(corr, codes, outgoing, ks * ks))
+    qgt = score_part(qv, pos, all_tails, cand)
+    all_qgt = lax.all_gather(qgt, "shard", axis=0, tiled=True)
+    outgoing, sums, fgrad = back(qgt, orow, ext, band_t, weight_t, slope, count, head_cap, copies)
+    core_sums = gather_core(sums)
+    incoming = exchange(filter_sums(fgrad, img, codes, outgoing, ks * ks))
 
     own, other = tail_part(ids, all_tails, scand, numbers, core_vecs, cand)
     entity_grad, filter_grad = entity_sum(
@@ -842,10 +853,13 @@
     cols = filts * IMG * IMG // count
     if direct and cols % (IMG * IMG) == 0:
         feats = column_feats(ids, rtab_t, ext, band, numbers, core_vecs, cols)
-        own, other = proj_part(feats, core_qgt)
+        own, other = proj_part(core, feats, all_qgt)
     else:
-        core_numbers = lax.dynamic_index_in_dim(
-            numbers.reshape(count // 2, 2, 4, queries), me & 1, 1, keepdims=False
+        core_numbers, core_qgt = (
+            lax.dynamic_index_in_dim(
+                x.reshape((count // 2, 2) + x.shape[1:]), me & 1, 1, keepdims=False
+            )
+            for x in (numbers.reshape(count, 4, queries), all_qgt.astype(bf16))
         )
         own, other = (
             proj_columns(
@@ -856,7 +870,8 @@
         )
     proj_grad = (own + swap(other)).T
 
-    relation_grad = rel_part(numbers, all_sums, rels).T
+    part = rel_part(core, numbers, core_sums, rels)
+    relation_grad = (part + swap(part)).T
     return (entity_grad.T, relation_grad, filter_grad, proj_grad)
 
 

time: 155 us -> 179 us (1.15)
  waiting for transfers between devices: 13.2 us -> 47.3 us
  blocking collectives: 13.9 us -> 0 us
  starting transfers between devices: 18.4 us -> 22.6 us
  Pallas kernels: 87.4 us -> 85.1 us
    all_to_all x2, waiting for transfers between devices: 5.62 us -> 37.5 us  [gather_core(): lax.all_to_all(x, 'shard', split_axis=0, concat_axis=0, axis_index_groups...]
    all_to_all x1 -> x0, blocking collectives: 13.9 us -> none  [exchange(): return lax.all_to_all(x, 'shard', split_axis=0, concat_axis=0, tiled=True)]
    all_to_all x2 -> x3, starting transfers between devices: 7.1 us -> 14.6 us  [exchange(): return lax.all_to_all(x, 'shard', split_axis=0, concat_axis=0, tiled=True)]
    all_to_all x2 -> x3, waiting for transfers between devices: 1.2 us -> 6.58 us  [exchange(): return lax.all_to_all(x, 'shard', split_axis=0, concat_axis=0, tiled=True)]
    pallas_call x1, Pallas kernels: 18.2 us -> 14.4 us  [back(): pl.pallas_call(functools.partial(back_kernel, cap), grid=(filts // units,...]
    all_to_all x2, starting transfers between devices: 10.7 us -> 7.32 us  [gather_core(): lax.all_to_all(x, 'shard', split_axis=0, concat_axis=0, axis_index_groups...]
    pallas_call x1, Pallas kernels: 10.7 us -> 12.8 us  [front(): pl.pallas_call(functools.partial(front_kernel, cap), grid=(filts // units...]
    all_gather x1, waiting for transfers between devices: 4.54 us -> 2.52 us  [shards(): all_tails = lax.all_gather(tails_t, 'shard', axis=0, tiled=True)]
  transfers between devices with their start and end apart: 8 -> 10, of which waited for: 4 -> 4; matrix products, arithmetic and copies ran while one was open for 3% -> 3% of each run, Pallas kernels for 51% -> 34%
where the time goes in v7:
time: 179 us; the launch traced here: 178 us
  Pallas kernels  85.1 us (48%)
  waiting for transfers between devices  47.3 us (26%)
  starting transfers between devices  22.6 us (13%)
  between operations  14.2 us (8%)
  local copies, waits for them, and re-layouts  6.04 us (3%)
  other arithmetic  2.95 us (2%)
    all_to_all x2, waiting for transfers between devices, gather_core(): lax.all_to_all(x, 'shard', split_axis=0, concat_axis=0, axis_index_groups...  37.5 us
    all_to_all x3, starting transfers between devices, exchange(): return lax.all_to_all(x, 'shard', split_axis=0, concat_axis=0, tiled=True)  14.6 us
    pallas_call x1, Pallas kernels, back(): pl.pallas_call(functools.partial(back_kernel, cap), grid=(filts // units,...  14.4 us
    pallas_call x1, Pallas kernels, front(): pl.pallas_call(functools.partial(front_kernel, cap), grid=(filts // units...  12.8 us
    pallas_call x1, Pallas kernels, column_feats(): pl.pallas_call(feats_kernel, grid_spec=pltpu.PrefetchScalarGridSpec(num_s...  9.21 us
    pallas_call x1, Pallas kernels, filter_sums(): pl.pallas_call(functools.partial(diag_kernel, taps), grid=(filts // units...  8.38 us
    all_to_all x2, starting transfers between devices, gather_core(): lax.all_to_all(x, 'shard', split_axis=0, concat_axis=0, axis_index_groups...  7.32 us
    all_to_all x3, waiting for transfers between devices, exchange(): return lax.all_to_all(x, 'shard', split_axis=0, concat_axis=0, tiled=True)  6.58 us
  transfers between devices with their start and end apart: 10, of which 4 were waited for; matrix products, arithmetic and copies ran while one was open for 3% of the time, Pallas kernels for 34%

profile of v7, /device:TPU:0, one launch (start us, length us, event | category | flops | bytes accessed | tf_op | source)
XLA Modules:
  0.0 178.2 jit_solution(4687597562999718679)
XLA Ops:
  7.3 4.0 %pack_tails.1 = (bf16[1,200,512]{2,1,0:T(8,128)(2,1)}, s32[512,1]{1,0:T(8,128)}) custom-call(s32[1]{0:T(128)} %bitcast.me_ref, s32[32,128]{1,0:T(8,128)} %bitcast.36, s32[32,128]{1,0:T(8,128)} %bitcast.35, bf16[200,2048]{1,0:T(8,128)(2,1)} %bitcast.31), custom_call_target="tpu_custom_call" | custom-call | flops 1000000000 | bytes 2000000 | tf_op jit(solution)/shard_map/pack_tails/pallas_call | solution.py:167
  11.4 0.6 broadcast_in_dim.9
  12.0 7.3 %all-to-all-start = ((s32[16,1,512]{2,1,0:T(1,128)}), s32[16,1,512]{2,1,0:T(1,128)S(1)}, u32[]{:S(2)}, u32[]{:S(2)}) async-start(s32[16,1,512]{2,1,0:T(1,128)} %broadcast_in_dim.9), calls=%async_computation | async-start | bytes 65536 | tf_op jit(solution)/shard_map/all_to_all | solution.py:807
  19.4 6.6 %all-to-all-done.numbers_ref = s32[16,1,512]{2,1,0:T(1,128)S(1)} async-done(((s32[16,1,512]{2,1,0:T(1,128)}), s32[16,1,512]{2,1,0:T(1,128)S(1)}, u32[]{:S(2)}, u32[]{:S(2)}) %all-to-all-start) | async-done | bytes 32800 | tf_op jit(solution)/shard_map/all_to_all | solution.py:807
  26.6 2.6 %find_heads.1 = (bf16[16,16,200]{2,1,0:T(8,128)(2,1)}, s32[256,1]{1,0:T(8,128)}) custom-call(s32[1]{0:T(128)} %bitcast.me_ref, bf16[200,2048]{1,0:T(8,128)(2,1)} %bitcast.32, s32[16,1,512]{2,1,0:T(1,128)} %copy-done.5), custom_call_target="tpu_custom_call" | custom-call | flops 300000000 | bytes 2000000 | tf_op jit(solution)/shard_map/find_heads/pallas_call | solution.py:205
  29.2 3.7 %all-to-all-start.1 = ((bf16[16,16,200]{2,1,0:T(8,128)(2,1)}), bf16[16,16,200]{2,1,0:T(8,128)(2,1)S(1)}, u32[]{:S(2)}, u32[]{:S(2)}) async-start(bf16[16,16,200]{2,1,0:T(8,128)(2,1)} %get-tuple-element.29), calls=%async_computation.1 | async-start | bytes 262144 | tf_op jit(solution)/shard_map/all_to_all | solution.py:807
  33.6 0.7 copy.18.filt_ref
  34.3 5.3 %band.1 = (bf16[3840,256]{1,0:T(8,128)(2,1)}, bf16[256,3840]{1,0:T(8,128)(2,1)}) custom-call(s32[20,256]{1,0:T(8,128)} %constant.8.clone.codes_ref, bf16[48,81]{1,0:T(8,128)(2,1)} %copy.18.filt_ref), custom_call_target="tpu_custom_call" | custom-call | flops 40000000 | bytes 4000000 | tf_op jit(solution)/shard_map/band/pallas_call | solution.py:94
  39.5 4.4 %slot_tables.1 = (s32[2,512,1]{2,1,0:T(8,128)}, s32[128,1]{1,0:T(8,128)}) custom-call(s32[1]{0:T(128)} %bitcast.me_ref, s32[32,128]{1,0:T(8,128)} %bitcast.37, s32[1,4096]{1,0:T(1,128)} %bitcast.38, s32[1,128]{1,0:T(1,128)} %bitcast.24), custom_call_target="tpu_custom_call" | custom-call | flops 1000000000 | bytes 1000000 | tf_op jit(solution)/shard_map/slot_tables/pallas_call | solution.py:247
  43.9 0.7 copy-done.6
  44.6 12.8 %front.1 = (f32[19200,128]{1,0:T(8,128)}, bf16[256,640]{1,0:T(8,128)(2,1)}, bf16[128,200]{1,0:T(8,128)(2,1)}, bf16[8,2,200,128]{3,2,1,0:T(8,128)(2,1)}) custom-call(bf16[16,16,200]{2,1,0:T(8,128)(2,1)} %copy-done.6, s32[1,128]{1,0:T(1,128)} %bitcast.26, s32[1,128]{1,0:T(1,128)} %bitcast.25, bf16[200,1387]{1,0:T(8,128)(2,1)} %bitcast.33, ...), custom_call_target="tpu_custom_call" | custom-call | flops 4000000000 | bytes 24000000 | tf_op jit(solution)/shard_map/front/pallas_call | solution.py:325
  57.4 2.5 %all-gather.3.cloned.1.call-done.tails_ref.mate_ref = bf16[16,200,512]{2,1,0:T(8,128)(2,1)} async-done(((bf16[1,200,512]{2,1,0:T(8,128)(2,1)}), bf16[16,200,512]{2,1,0:T(8,128)(2,1)}) %all-gather.3.cloned.1.call-update) | async-done | bytes 3276816 | tf_op jit(solution)/shard_map/all_gather | solution.py:826
  59.9 5.6 %score.1.qgt_ref = f32[1,200,128]{2,1,0:T(8,128)} custom-call(s32[128,1]{1,0:T(8,128)} %get-tuple-element.34.pos_ref, bf16[128,200]{1,0:T(8,128)(2,1)} %get-tuple-element.35.qv_ref, bf16[16,200,512]{2,1,0:T(8,128)(2,1)} %all-gather.3.cloned.1.call-done.tails_ref.mate_ref), custom_call_target="tpu_custom_call" | custom-call | flops 1000000000 | bytes 3000000 | tf_op jit(solution)/shard_map/score/pallas_call | solution.py:391
  65.6 14.4 %back.1 = (bf16[16,16,200]{2,1,0:T(8,128)(2,1)}, f32[8,200,128]{2,1,0:T(8,128)}, bf16[3840,640]{1,0:T(8,128)(2,1)}) custom-call(s32[1,128]{1,0:T(1,128)} %bitcast.27, s32[1,576]{1,0:T(1,128)} %broadcast_in_dim.11.ext_ref, f32[1,200,128]{2,1,0:T(8,128)} %score.1.qgt_ref, bf16[256,3840]{1,0:T(8,128)(2,1)} %get-tuple-element.36.bandt_ref, ...), custom_call_target="tpu_custom_call" | custom-call | flops 6000000000 | bytes 20000000 | tf_op jit(solution)/shard_map/back/pallas_call | solution.py:460
  80.0 3.5 %all-to-all-start.4 = ((f32[8,200,128]{2,1,0:T(8,128)}), f32[8,200,128]{2,1,0:T(8,128)S(1)}, u32[]{:S(2)}, u32[]{:S(2)}) async-start(f32[8,200,128]{2,1,0:T(8,128)} %get-tuple-element.42), calls=%async_computation.4 | async-start | bytes 1638400 | tf_op jit(solution)/shard_map/all_to_all | solution.py:811
  83.6 0.7 all-gather.5.cloned.1.call-update
  84.3 23.2 %all-to-all-done.4.sums_ref = f32[8,200,128]{2,1,0:T(8,128)S(1)} async-done(((f32[8,200,128]{2,1,0:T(8,128)}), f32[8,200,128]{2,1,0:T(8,128)S(1)}, u32[]{:S(2)}, u32[]{:S(2)}) %all-to-all-start.4) | async-done | bytes 819232 | tf_op jit(solution)/shard_map/all_to_all | solution.py:811
  107.5 3.8 %all-to-all-start.2 = ((bf16[8,2,200,128]{3,2,1,0:T(8,128)(2,1)}), bf16[8,2,200,128]{3,2,1,0:T(8,128)(2,1)S(1)}, u32[]{:S(2)}, u32[]{:S(2)}) async-start(bf16[8,2,200,128]{3,2,1,0:T(8,128)(2,1)} %get-tuple-element.31), calls=%async_computation.2 | async-start | bytes 1638400 | tf_op jit(solution)/shard_map/all_to_all | solution.py:811
  111.3 0.6 pad_add_fusion.2.ids_ref
  111.9 8.4 %filter_sums.1 = bf16[16,64,200]{2,1,0:T(8,128)(2,1)} custom-call(s32[20,256]{1,0:T(8,128)} %constant.8.clone.codes_ref, bf16[3840,640]{1,0:T(8,128)(2,1)} %get-tuple-element.38.fgrad_ref, bf16[256,640]{1,0:T(8,128)(2,1)} %get-tuple-element.39.img_ref, bf16[16,16,200]{2,1,0:T(8,128)(2,1)} %get-tuple-element.40.rows_ref), custom_call_target="tpu_custom_call" | custom-call | flops 2000000000 | bytes 6000000 | tf_op jit(solution)/shard_map/filter_sums/pallas_call | solution.py:536
  120.3 3.8 %rel_grad.1 = f32[200,1387]{1,0:T(8,128)} custom-call(s32[1]{0:T(128)} %bitcast.6.core_ref, s32[16,1,512]{2,1,0:T(1,128)} %copy-done.5, f32[8,200,128]{2,1,0:T(8,128)} %copy-done.3), custom_call_target="tpu_custom_call" | custom-call | flops 2000000000 | bytes 3000000 | tf_op jit(solution)/shard_map/rel_grad/pallas_call | solution.py:727
  124.1 14.3 %all-to-all-done.2.vecs_ref = bf16[8,2,200,128]{3,2,1,0:T(8,128)(2,1)S(1)} async-done(((bf16[8,2,200,128]{3,2,1,0:T(8,128)(2,1)}), bf16[8,2,200,128]{3,2,1,0:T(8,128)(2,1)S(1)}, u32[]{:S(2)}, u32[]{:S(2)}) %all-to-all-start.2) | async-done | bytes 819232 | tf_op jit(solution)/shard_map/all_to_all | solution.py:811
  138.4 3.6 %all-to-all-start.3 = ((bf16[16,64,200]{2,1,0:T(8,128)(2,1)}), bf16[16,64,200]{2,1,0:T(8,128)(2,1)S(1)}, u32[]{:S(2)}, u32[]{:S(2)}) async-start(bf16[16,64,200]{2,1,0:T(8,128)(2,1)} %filter_sums.1), calls=%async_computation.3 | async-start | bytes 1048576 | tf_op jit(solution)/shard_map/all_to_all | solution.py:807
  142.0 4.9 %tail_grad.1 = (f32[200,512]{1,0:T(8,128)}, f32[200,512]{1,0:T(8,128)}) custom-call(s32[3]{0:T(128)} %pad_add_fusion.2.ids_ref, bf16[16,200,512]{2,1,0:T(8,128)(2,1)} %all-gather.3.cloned.1.call-done.tails_ref.mate_ref, bf16[16,200,512]{2,1,0:T(8,128)(2,1)} %all-gather.3.cloned.1.call-done.tails_ref.mate_ref, s32[2,512,1]{2,1,0:T(8,128)} %get-tuple-element.28.scand_ref, ...), custom_call_target="tpu_custom_call" | custom-call | flops 2000000000 | bytes 3000000 | tf_op jit(solution)/shard_map/tail_grad/pallas_call | solution.py:579
  147.3 9.2 %column_feats.1.feats_ref = bf16[2400,1024]{1,0:T(8,128)(2,1)} custom-call(s32[3]{0:T(128)} %pad_add_fusion.2.ids_ref, bf16[200,1387]{1,0:T(8,128)(2,1)} %bitcast.34, s32[1,576]{1,0:T(1,128)} %broadcast_in_dim.11.ext_ref, bf16[3840,256]{1,0:T(8,128)(2,1)} %get-tuple-element.30.band_ref.mate_ref, bf16[3840,256]{1,0:T(8,128)(2,1)} %get-tuple-element.30.band_ref.mate_ref, ...), custom_call_target="tpu_custom_call" | custom-call | flops 5000000000 | bytes 6000000 | tf_op jit(solution)/shard_map/column_feats/pallas_call | solution.py:638
  156.5 5.5 %proj_grad.1 = (f32[200,1200]{1,0:T(8,128)}, f32[200,1200]{1,0:T(8,128)}) custom-call(s32[1]{0:T(128)} %bitcast.6.core_ref, bf16[2400,1024]{1,0:T(8,128)(2,1)} %column_feats.1.feats_ref, f32[16,200,128]{2,1,0:T(8,128)} %all-gather.5.cloned.1.call-done.grads_ref), custom_call_target="tpu_custom_call" | custom-call | flops 1000000000 | bytes 8000000 | tf_op jit(solution)/shard_map/proj_grad/pallas_call | solution.py:677
  162.1 0.8 copy-done.13
  163.1 4.2 %entity_grad.1 = (f32[200,2048]{1,0:T(8,128)}, f32[96,48]{1,0:T(8,128)}) custom-call(s32[256,1]{1,0:T(8,128)} %get-tuple-element.25.want_ref, s32[512,1]{1,0:T(8,128)} %get-tuple-element.26.srow_ref, f32[200,512]{1,0:T(8,128)} %get-tuple-element.32.own_ref, f32[200,512]{1,0:T(8,128)} %copy-done.13, bf16[16,64,200]{2,1,0:T(8,128)(2,1)} %copy-done.4), custom_call_target="tpu_custom_call" | custom-call | flops 1500000000 | bytes 4000000 | tf_op jit(solution)/shard_map/entity_grad/pallas_call | solution.py:764
  167.3 0.8 slice_bitcast_fusion
  168.1 0.6 reshape.28
  168.7 1.2 add_bitcast_fusion
  170.3 1.1 add_bitcast_fusion.1
  (45 shorter events, 2.6 us)
Async XLA Ops:
  7.2 52.8 %all-gather.3.cloned.1.call-start = ((), (), s32[]{:S(2)}) async-start(), calls=%async_computation.5 | async-start | bytes 3481600 | tf_op jit(solution)/shard_map/all_gather | solution.py:826
  7.2 4.1 %copy-start.9 = (s32[128]{0:T(128)S(1)}, s32[128]{0:T(128)}, u32[]{:S(2)}) copy-start(s32[128]{0:T(128)} %param.18) | copy-start | bytes 1540
  7.2 4.1 %copy-start.10 = (s32[128]{0:T(128)S(1)}, s32[128]{0:T(128)}, u32[]{:S(2)}) copy-start(s32[128]{0:T(128)} %param.20) | copy-start | bytes 1540
  7.2 4.1 %copy-start.11 = (s32[128]{0:T(128)S(1)}, s32[128]{0:T(128)}, u32[]{:S(2)}) copy-start(s32[128]{0:T(128)} %param.19) | copy-start | bytes 1540
  7.2 4.1 %copy-start.12 = (s32[128,1]{0,1:T(1,128)S(1)}, s32[128,1]{0,1:T(1,128)}, u32[]{:S(2)}) copy-start(s32[128,1]{0,1:T(1,128)} %param.17) | copy-start | bytes 1540
  7.3 12.1 %copy-start.8 = (s32[400]{0:T(512)S(1)}, s32[400]{0:T(512)}, u32[]{:S(2)}) copy-start(s32[400]{0:T(512)} %param.16) | copy-start | bytes 4804
  11.3 21.6 %slice-start = ((s32[400]{0:T(512)}), s32[96]{0:T(128)S(1)}, s32[]{:S(2)}) async-start(s32[400]{0:T(512)} %param.16), calls=%async_computation.7 | async-start | bytes 1024 | tf_op jit(solution)/shard_map/slice | solution.py:834
  11.3 22.3 %copy-start.7 = (bf16[48,9,9]{0,2,1:T(8,128)(2,1)S(1)}, bf16[48,9,9]{0,2,1:T(8,128)(2,1)}, u32[]{:S(2)}) copy-start(bf16[48,9,9]{0,2,1:T(8,128)(2,1)} %param.14) | copy-start | bytes 23332
  12.0 14.0 %all-to-all-start = ((s32[16,1,512]{2,1,0:T(1,128)}), s32[16,1,512]{2,1,0:T(1,128)S(1)}, u32[]{:S(2)}, u32[]{:S(2)}) async-start(s32[16,1,512]{2,1,0:T(1,128)} %broadcast_in_dim.9), calls=%async_computation | async-start | bytes 65536 | tf_op jit(solution)/shard_map/all_to_all | solution.py:807
  26.0 0.6 copy-start.5
  29.2 14.7 %all-to-all-start.1 = ((bf16[16,16,200]{2,1,0:T(8,128)(2,1)}), bf16[16,16,200]{2,1,0:T(8,128)(2,1)S(1)}, u32[]{:S(2)}, u32[]{:S(2)}) async-start(bf16[16,16,200]{2,1,0:T(8,128)(2,1)} %get-tuple-element.29), calls=%async_computation.1 | async-start | bytes 262144 | tf_op jit(solution)/shard_map/all_to_all | solution.py:807
  43.9 0.7 copy-start.6
  80.0 27.5 %all-to-all-start.4 = ((f32[8,200,128]{2,1,0:T(8,128)}), f32[8,200,128]{2,1,0:T(8,128)S(1)}, u32[]{:S(2)}, u32[]{:S(2)}) async-start(f32[8,200,128]{2,1,0:T(8,128)} %get-tuple-element.42), calls=%async_computation.4 | async-start | bytes 1638400 | tf_op jit(solution)/shard_map/all_to_all | solution.py:811
  83.5 73.0 %all-gather.5.cloned.1.call-start = ((), (), s32[]{:S(2)}) async-start(), calls=%async_computation.6 | async-start | bytes 1740800 | tf_op jit(solution)/shard_map/all_gather | solution.py:842
  107.5 12.8 %copy-start.3 = (f32[8,200,128]{2,1,0:T(8,128)}, f32[8,200,128]{2,1,0:T(8,128)S(1)}, u32[]{:S(2)}) copy-start(f32[8,200,128]{2,1,0:T(8,128)S(1)} %all-to-all-done.4.sums_ref) | copy-start | bytes 2457604
  107.5 30.9 %all-to-all-start.2 = ((bf16[8,2,200,128]{3,2,1,0:T(8,128)(2,1)}), bf16[8,2,200,128]{3,2,1,0:T(8,128)(2,1)S(1)}, u32[]{:S(2)}, u32[]{:S(2)}) async-start(bf16[8,2,200,128]{3,2,1,0:T(8,128)(2,1)} %get-tuple-element.31), calls=%async_computation.2 | async-start | bytes 1638400 | tf_op jit(solution)/shard_map/all_to_all | solution.py:811
  124.1 44.7 %collective-permute-start.1 = (f32[200,1387]{1,0:T(8,128)}, f32[200,1387]{1,0:T(8,128)S(1)}, u32[]{:S(2)}, u32[]{:S(2)}) collective-permute-start(f32[200,1387]{1,0:T(8,128)} %rel_grad.1), channel_id=1, source_target_pairs={{0,1},{1,0},{2,3},{3,2},{4,5},{5,4},{6,7},{7,6},{8,9},{9,8},{10,11... | collective-permute-start | bytes 3328808 | tf_op jit(solution)/shard_map/ppermute | solution.py:804
  138.4 3.6 %copy-start = (bf16[8,2,200,128]{3,2,1,0:T(8,128)(2,1)}, bf16[8,2,200,128]{3,2,1,0:T(8,128)(2,1)S(1)}, u32[]{:S(2)}) copy-start(bf16[8,2,200,128]{3,2,1,0:T(8,128)(2,1)S(1)} %all-to-all-done.2.vecs_ref) | copy-start | bytes 2457604
  138.4 23.7 %all-to-all-start.3 = ((bf16[16,64,200]{2,1,0:T(8,128)(2,1)}), bf16[16,64,200]{2,1,0:T(8,128)(2,1)S(1)}, u32[]{:S(2)}, u32[]{:S(2)}) async-start(bf16[16,64,200]{2,1,0:T(8,128)(2,1)} %filter_sums.1), calls=%async_computation.3 | async-start | bytes 1048576 | tf_op jit(solution)/shard_map/all_to_all | solution.py:807
  146.9 15.2 %collective-permute-start = (f32[200,512]{1,0:T(8,128)}, f32[200,512]{1,0:T(8,128)S(1)}, u32[]{:S(2)}, u32[]{:S(2)}) collective-permute-start(f32[200,512]{1,0:T(8,128)} %get-tuple-element.33), channel_id=1, source_target_pairs={{0,1},{1,0},{2,3},{3,2},{4,5},{5,4},{6,7},{7,6},{8,9},{9,8},{10,11... | collective-permute-start | bytes 1228808 | tf_op jit(solution)/shard_map/ppermute | solution.py:804
  162.0 7.9 %collective-permute-start.2 = (f32[200,1200]{1,0:T(8,128)}, f32[200,1200]{1,0:T(8,128)S(1)}, u32[]{:S(2)}, u32[]{:S(2)}) collective-permute-start(f32[200,1200]{1,0:T(8,128)} %get-tuple-element.45), channel_id=1, source_target_pairs={{0,1},{1,0},{2,3},{3,2},{4,5},{5,4},{6,7},{7,6},{8,9},{9,8},{10,11... | collective-permute-start | bytes 2880008 | tf_op jit(solution)/shard_map/ppermute | solution.py:804
  162.1 0.8 copy-start.13
  162.1 0.9 copy-start.4
  163.1 5.7 %copy-start.1 = (f32[200,1387]{1,0:T(8,128)S(1)}, f32[200,1387]{1,0:T(8,128)}, u32[]{:S(2)}) copy-start(f32[200,1387]{1,0:T(8,128)} %rel_grad.1) | copy-start | bytes 3328804
  168.7 1.5 copy-start.2
Sparse Core Ops, SparseCore 0:
  11.4 48.4 all-gather.2
  86.5 50.8 all-gather.4

commit v8 on v7

--- a/solution.py
+++ b/solution.py
@@ -358,135 +358,135 @@
     )(fetched, orow, rel_row, rtab_t, ext, band, weight_t)
 
 
-def score_kernel(cand, pos_ref, qv_ref, tails_ref, out_ref, acc, scores, grads):
-    step = pl.program_id(0)
-
-    @pl.when(step == 0)
-    def _():
-        acc[...] = jnp.zeros_like(acc)
+def middle_kernel(
+    cap, cand, pos_ref, qv_ref, orow_ref, ext_ref, bandt_ref, tails_hbm, w_hbm, slope_hbm,
+    out_ref, sums_ref, qgt_ref, fgrad_hbm,
+    tails, w, slope, fgrad, scores, grads, spread, ext, linear, tail_sems, w_sems, slope_sems, out_sems,
+):
+    owners, width, slots = tails.shape
+    steps, _, cols = w.shape
+    queries = qv_ref.shape[0]
+    chunks = tail_sems.shape[0]
+    blocks = owners // chunks
+    part_rows = fgrad.shape[1]
+
+    def tail_copy(i):
+        span = pl.ds(i * blocks, blocks)
+        return pltpu.make_async_copy(tails_hbm.at[span], tails.at[span], tail_sems.at[i])
+
+    def w_copy(k):
+        return pltpu.make_async_copy(w_hbm.at[:, pl.ds(k * cols, cols)], w.at[k], w_sems.at[k])
+
+    def slope_copy(k):
+        return pltpu.make_async_copy(slope_hbm.at[pl.ds(k * cols, cols)], slope.at[k], slope_sems.at[k])
+
+    def out_copy(k):
+        span = pl.ds(k * part_rows, part_rows)
+        return pltpu.make_async_copy(fgrad.at[k], fgrad_hbm.at[span], out_sems.at[k])
+
+    for i in range(chunks):
+        tail_copy(i).start()
+    for k in range(steps):
+        w_copy(k).start()
+        slope_copy(k).start()
 
     qv = qv_ref[...]
-    queries = qv.shape[0]
-    blocks, _, cap = tails_ref.shape
-    total = acc[...]
-    for b in range(blocks):
-        block = tails_ref[b]
-        scores[b] = mm(qv, block)
-        for r in spans(queries, 16):
-            here = iota((r.stop - r.start, cap), 1) + (step * blocks + b) * cap
-            target = jnp.where(here == pos_ref[r, :], 1.0 - smooth + smooth / cand, smooth / cand)
-            grads[b, r, :] = ((sigmoid(scores[b, r, :]) - target) * loss_weight).astype(bf16)
-        total = total + mm(grads[b], block, NT)
-    acc[...] = total
-
-    @pl.when(step == pl.num_programs(0) - 1)
-    def _():
-        out_ref[0] = total.T
-
-
-def score_part(qv, pos, tails, cand):
+    total = jnp.zeros((queries, width), f32)
+    for i in range(chunks):
+        tail_copy(i).wait()
+        for b in range(blocks):
+            o = i * blocks + b
+            block = tails[o]
+            slot = o % scores.shape[0]
+            scores[slot] = mm(qv, block)
+            for r in spans(queries, 16):
+                here = iota((r.stop - r.start, slots), 1) + o * slots
+                target = jnp.where(here == pos_ref[r, :], 1.0 - smooth + smooth / cand, smooth / cand)
+                grads[slot, r, :] = ((sigmoid(scores[slot, r, :]) - target) * loss_weight).astype(bf16)
+            total = total + mm(grads[slot], block, NT)
+    qgt = total.T.astype(bf16)
+    for d in range(qgt_ref.shape[0]):
+        qgt_ref[d] = qgt
+
+    units = part_rows // BAND_OUT
+    flat = GROUPS * BAND_OUT
+    for k in range(steps):
+        lin = linear.at[k % 2]
+        w_copy(k).wait()
+        lin[...] = mm(w[k], qgt, TN)
+        slope_copy(k).wait()
+        for f in range(units):
+            for g in range(GROUPS):
+                rows = slice(f * flat + g * BAND_OUT, f * flat + (g + 1) * BAND_OUT)
+                part = slice(f * BAND_OUT, (f + 1) * BAND_OUT)
+                lanes = slice(g * queries, (g + 1) * queries)
+                fgrad[k, part, lanes] = (lin[rows, :] * slope[k, rows, :]).astype(bf16)
+        out_copy(k).start()
+        spread_k = mm(bandt_ref[:, k * part_rows : (k + 1) * part_rows], fgrad[k])
+        if k == 0:
+            spread[...] = spread_k
+        else:
+            spread[...] += spread_k
+
+    ext[...] = jnp.zeros_like(ext)
+    for g in range(GROUPS):
+        ext[g * BAND_OUT : g * BAND_OUT + LANES, :] += spread[:, g * queries : (g + 1) * queries]
+    entry = iota((width, ext.shape[0]), 0)
+    high, low = split(ext[...])
+    hpick = onehot(entry == ext_ref[...])
+    rpick = onehot(entry + width == ext_ref[...])
+    hgrad = (mm(hpick, high) + mm(hpick, low)).astype(bf16)
+    sums_ref[0] = mm(rpick, high) + mm(rpick, low)
+    count = out_ref.shape[0]
+    pick = slot_picks(cap, count * cap, orow_ref[...])
+    rows = mm(pick, hgrad, NT).astype(bf16)
+    for d in range(count):
+        out_ref[d] = rows[d * cap : (d + 1) * cap, :]
+    for k in range(steps):
+        out_copy(k).wait()
+
+
+def middle(pos, qv, orow, ext, band_t, tails, weight_t, slope, cand, cap, copies):
     queries, width = qv.shape
-    owners, _, cap = tails.shape
-    blocks = math.gcd(owners, max(1, 2048 // cap))
-    return pl.pallas_call(
-        functools.partial(score_kernel, cand),
-        grid=(owners // blocks,),
-        in_specs=[
-            whole(pos.shape),
-            whole(qv.shape),
-            pl.BlockSpec((blocks, width, cap), lambda s: (s, 0, 0)),
-        ],
-        out_specs=whole((1, width, queries)),
-        out_shape=jax.ShapeDtypeStruct((1, width, queries), f32),
-        scratch_shapes=[
-            pltpu.VMEM((queries, width), f32),
-            pltpu.VMEM((blocks, queries, cap), f32),
-            pltpu.VMEM((blocks, queries, cap), bf16),
-        ],
-        compiler_params=params("arbitrary"),
-        cost_estimate=cost(1e9, 3e6, 5e5),
-        name="score",
-    )(pos, qv, tails)
-
-
-def back_kernel(
-    cap, orow_ref, ext_ref, qgt_ref, bandt_ref, w_ref, slope_ref,
-    out_ref, sums_ref, fgrad_ref, spread, ext, linear,
-):
-    s = pl.program_id(0)
-    _, width, queries = qgt_ref.shape
-
-    @pl.when(s == 0)
-    def _():
-        spread[...] = jnp.zeros_like(spread)
-
-    units = bandt_ref.shape[1] // BAND_OUT
-    flat = GROUPS * BAND_OUT
-    linear[...] = mm(w_ref[...], qgt_ref[0].astype(bf16), TN)
-    for f in range(units):
-        for g in range(GROUPS):
-            rows = slice(f * flat + g * BAND_OUT, f * flat + (g + 1) * BAND_OUT)
-            part = slice(f * BAND_OUT, (f + 1) * BAND_OUT)
-            lanes = slice(g * queries, (g + 1) * queries)
-            fgrad_ref[part, lanes] = (linear[rows, :] * slope_ref[rows, :]).astype(bf16)
-    spread[...] += mm(bandt_ref[...], fgrad_ref[...])
-
-    @pl.when(s == pl.num_programs(0) - 1)
-    def _():
-        ext[...] = jnp.zeros_like(ext)
-        for g in range(GROUPS):
-            ext[g * BAND_OUT : g * BAND_OUT + LANES, :] += spread[:, g * queries : (g + 1) * queries]
-        entry = iota((width, ext.shape[0]), 0)
-        high, low = split(ext[...])
-        hpick = onehot(entry == ext_ref[...])
-        rpick = onehot(entry + width == ext_ref[...])
-        hgrad = (mm(hpick, high) + mm(hpick, low)).astype(bf16)
-        rgrad = mm(rpick, high) + mm(rpick, low)
-        for d in range(sums_ref.shape[0]):
-            sums_ref[d] = rgrad
-        blocks = out_ref.shape[0]
-        pick = slot_picks(cap, blocks * cap, orow_ref[...])
-        rows = mm(pick, hgrad, NT).astype(bf16)
-        for d in range(blocks):
-            out_ref[d] = rows[d * cap : (d + 1) * cap, :]
-
-
-def back(qgt, orow, ext, band_t, weight_t, slope, count, cap, copies):
-    _, width, queries = qgt.shape
+    owners, _, slots = tails.shape
     flat = weight_t.shape[1]
     filts = band_t.shape[1] // BAND_OUT
     units = math.gcd(filts, 16)
-    cols = flat // filts * units
-    return pl.pallas_call(
-        functools.partial(back_kernel, cap),
-        grid=(filts // units,),
-        in_specs=[
-            whole(orow.shape),
-            whole(ext.shape),
-            whole(qgt.shape),
-            pl.BlockSpec((LANES, units * BAND_OUT), lambda s: (0, s)),
-            pl.BlockSpec((width, cols), lambda s: (0, s)),
-            pl.BlockSpec((cols, queries), lambda s: (s, 0)),
-        ],
-        out_specs=[
-            whole((count, cap, width)),
-            whole((copies, width, queries)),
-            pl.BlockSpec((units * BAND_OUT, GROUPS * queries), lambda s: (s, 0)),
-        ],
+    steps = filts // units
+    cols = flat // steps
+    rows = units * BAND_OUT
+    blocks = math.gcd(owners, max(1, 2048 // slots))
+    ring = min(owners, 4)
+    hbm = pl.BlockSpec(memory_space=pl.ANY)
+    return pl.pallas_call(
+        functools.partial(middle_kernel, cap, cand),
+        in_specs=[VMEM] * 5 + [hbm] * 3,
+        out_specs=[VMEM] * 3 + [hbm],
         out_shape=[
-            jax.ShapeDtypeStruct((count, cap, width), bf16),
-            jax.ShapeDtypeStruct((copies, width, queries), f32),
+            jax.ShapeDtypeStruct((owners, cap, width), bf16),
+            jax.ShapeDtypeStruct((1, width, queries), f32),
+            jax.ShapeDtypeStruct((copies, width, queries), bf16),
             jax.ShapeDtypeStruct((filts * BAND_OUT, GROUPS * queries), bf16),
         ],
         scratch_shapes=[
+            pltpu.VMEM(tails.shape, bf16),
+            pltpu.VMEM((steps, width, cols), bf16),
+            pltpu.VMEM((steps, cols, queries), f32),
+            pltpu.VMEM((steps, rows, GROUPS * queries), bf16),
+            pltpu.VMEM((ring, queries, slots), f32),
+            pltpu.VMEM((ring, queries, slots), bf16),
             pltpu.VMEM((LANES, GROUPS * queries), f32),
             pltpu.VMEM((ext.shape[1], queries), f32),
-            pltpu.VMEM((cols, queries), f32),
-        ],
-        compiler_params=params("arbitrary"),
-        cost_estimate=cost(6e9, 2e7),
-        name="back",
-    )(orow, ext, qgt, band_t, weight_t, slope)
+            pltpu.VMEM((2, cols, queries), f32),
+            pltpu.SemaphoreType.DMA((owners // blocks,)),
+            pltpu.SemaphoreType.DMA((steps,)),
+            pltpu.SemaphoreType.DMA((steps,)),
+            pltpu.SemaphoreType.DMA((steps,)),
+        ],
+        compiler_params=params(),
+        cost_estimate=cost(6e9, 2.5e7, 5e5),
+        name="middle",
+    )(pos, qv, orow, ext, band_t, tails, weight_t, slope)
 
 
 def half_taps(taps):
@@ -664,24 +664,22 @@
     )(ids, rtab_t, ext, band, band, numbers, vecs)
 
 
-def proj_kernel(core_ref, feats_ref, grads_ref, own_ref, other_ref):
+def proj_kernel(feats_ref, grads_ref, own_ref, other_ref):
     cols = own_ref.shape[1]
-    count = grads_ref.shape[0] // 2
-    qgt = beside(grads_ref[2 * p + core_ref[0]].astype(bf16) for p in range(count))
+    qgt = beside(grads_ref[p] for p in range(grads_ref.shape[0]))
     own_ref[...] = mm(qgt, feats_ref[:cols, :], NT)
     other_ref[...] = mm(qgt, feats_ref[cols:, :], NT)
 
 
-def proj_part(core, feats, grads):
+def proj_part(feats, grads):
     half = jax.ShapeDtypeStruct((grads.shape[1], feats.shape[0] // 2), f32)
     return pl.pallas_call(
         proj_kernel,
-        in_specs=[SMEM] + [VMEM] * 2,
         out_shape=[half, half],
         compiler_params=params(),
         cost_estimate=cost(1e9, 8e6),
         name="proj_grad",
-    )(core, feats, grads)
+    )(feats, grads)
 
 
 def proj_columns(first, cols, filters, chequer_perm, relation_table, numbers, heads, grads):
@@ -705,14 +703,14 @@
     return mm(qg, (pre * sigmoid(pre)).astype(bf16), TN)
 
 
-def rel_kernel(core_ref, numbers_ref, sums_ref, rel_ref, picks):
+def rel_kernel(numbers_ref, sums_ref, rel_ref, picks):
     width, rels = rel_ref.shape
     queries = sums_ref.shape[2]
     total = None
     for block in spans(sums_ref.shape[0], picks.shape[1] // queries):
         members = range(block.start, block.stop)
         for i, p in enumerate(members):
-            rel = field(numbers_ref, 2 * p + core_ref[0], 2)
+            rel = field(numbers_ref, p, 2)
             for r in spans(rels, 128):
                 here = iota((r.stop - r.start, queries), 0) + r.start
                 picks[r, i * queries : (i + 1) * queries] = onehot(here == rel)
@@ -722,17 +720,16 @@
     rel_ref[...] = total[:width, :] + total[width:, :]
 
 
-def rel_part(core, numbers, sums, rels):
+def rel_part(numbers, sums, rels):
     count, width, queries = sums.shape
     return pl.pallas_call(
         rel_kernel,
-        in_specs=[SMEM] + [VMEM] * 2,
         out_shape=jax.ShapeDtypeStruct((width, rels), f32),
-        scratch_shapes=[pltpu.VMEM((rels, math.gcd(count, 8) * queries), bf16)],
+        scratch_shapes=[pltpu.VMEM((rels, math.gcd(count, 16) * queries), bf16)],
         compiler_params=params(),
         cost_estimate=cost(2e9, 3e6),
         name="rel_grad",
-    )(core, numbers, sums)
+    )(numbers, sums)
 
 
 def entity_kernel(cap, want_ref, srow_ref, own_ref, recv_ref, incoming_ref, out_ref, filt_ref):
@@ -814,7 +811,6 @@
         return lax.all_gather(x, "shard", axis=0, axis_index_groups=same_core, tiled=True)
 
     me1 = me.reshape(1)
-    core = (me & 1).reshape(1)
     heads = head_owner[:, 0]
     tail_owners = tail_owner[:, 0]
     table_t, rtab_t, weight_t = entity_table.T, relation_table.T, proj_weight.T
@@ -838,11 +834,15 @@
     )
     core_vecs = gather_core(vecs)
 
-    qgt = score_part(qv, pos, all_tails, cand)
-    all_qgt = lax.all_gather(qgt, "shard", axis=0, tiled=True)
-    outgoing, sums, fgrad = back(qgt, orow, ext, band_t, weight_t, slope, count, head_cap, copies)
-    core_sums = gather_core(sums)
-    incoming = exchange(filter_sums(fgrad, img, codes, outgoing, ks * ks))
+    outgoing, sums, qgt, fgrad = middle(
+        pos, qv, orow, ext, band_t, all_tails, weight_t, slope, cand, head_cap, copies
+    )
+    all_sums = lax.all_gather(sums, "shard", axis=0, tiled=True)
+    qgt, core_vecs = lax.optimization_barrier((qgt, core_vecs))
+    core_qgt = gather_core(qgt)
+    outgoing = filter_sums(fgrad, img, codes, outgoing, ks * ks)
+    outgoing, core_qgt = lax.optimization_barrier((outgoing, core_qgt))
+    incoming = exchange(outgoing)
 
     own, other = tail_part(ids, all_tails, scand, numbers, core_vecs, cand)
     entity_grad, filter_grad = entity_sum(
@@ -853,13 +853,10 @@
     cols = filts * IMG * IMG // count
     if direct and cols % (IMG * IMG) == 0:
         feats = column_feats(ids, rtab_t, ext, band, numbers, core_vecs, cols)
-        own, other = proj_part(core, feats, all_qgt)
+        own, other = proj_part(feats, core_qgt)
     else:
-        core_numbers, core_qgt = (
-            lax.dynamic_index_in_dim(
-                x.reshape((count // 2, 2) + x.shape[1:]), me & 1, 1, keepdims=False
-            )
-            for x in (numbers.reshape(count, 4, queries), all_qgt.astype(bf16))
+        core_numbers = lax.dynamic_index_in_dim(
+            numbers.reshape(count // 2, 2, 4, queries), me & 1, 1, keepdims=False
         )
         own, other = (
             proj_columns(
@@ -870,8 +867,7 @@
         )
     proj_grad = (own + swap(other)).T
 
-    part = rel_part(core, numbers, core_sums, rels)
-    relation_grad = (part + swap(part)).T
+    relation_grad = rel_part(numbers, all_sums, rels).T
     return (entity_grad.T, relation_grad, filter_grad, proj_grad)
 
 

time: 179 us -> 147 us (0.82)
  waiting for transfers between devices: 47.3 us -> 8.34 us
  blocking collectives: 0 us -> 13.9 us
  starting transfers between devices: 22.6 us -> 17.9 us
    all_to_all x2, waiting for transfers between devices: 37.5 us -> 5.35 us  [gather_core(): lax.all_to_all(x, 'shard', split_axis=0, concat_axis=0, axis_index_groups...]
    all_to_all x0 -> x1, blocking collectives: none -> 13.9 us  [exchange(): return lax.all_to_all(x, 'shard', split_axis=0, concat_axis=0, tiled=True)]
    all_to_all x3 -> x2, starting transfers between devices: 14.6 us -> 7.08 us  [exchange(): return lax.all_to_all(x, 'shard', split_axis=0, concat_axis=0, tiled=True)]
    all_to_all x3 -> x2, waiting for transfers between devices: 6.58 us -> 1.16 us  [exchange(): return lax.all_to_all(x, 'shard', split_axis=0, concat_axis=0, tiled=True)]
    all_to_all x2, starting transfers between devices: 7.32 us -> 10.1 us  [gather_core(): lax.all_to_all(x, 'shard', split_axis=0, concat_axis=0, axis_index_groups...]
    all_gather x1, waiting for transfers between devices: 2.52 us -> 0.01 us  [shards(): all_tails = lax.all_gather(tails_t, 'shard', axis=0, tiled=True)]
    pallas_call x4 -> x3, Pallas kernels: 29.3 us -> 28.8 us  [the longest x1 18.4 us: middle(): pl.pallas_call(functools.partial(middle_kernel, cap, cand), in_specs=[VME...]
  transfers between devices with their start and end apart: 10 -> 8, of which waited for: 4 -> 3; matrix products, arithmetic and copies ran while one was open for 3% -> 3% of each run, Pallas kernels for 34% -> 52%
where the time goes in v8:
time: 147 us; the launch traced here: 145 us
  Pallas kernels  84.9 us (58%)
  starting transfers between devices  17.9 us (12%)
  between operations  14.2 us (10%)
  blocking collectives  13.9 us (9%)
  waiting for transfers between devices  8.34 us (6%)
  local copies, waits for them, and re-layouts  4.45 us (3%)
  other arithmetic  1.71 us (1%)
    pallas_call x1, Pallas kernels, middle(): pl.pallas_call(functools.partial(middle_kernel, cap, cand), in_specs=[VME...  18.4 us
    all_to_all x1, blocking collectives, exchange(): return lax.all_to_all(x, 'shard', split_axis=0, concat_axis=0, tiled=True)  13.9 us
    pallas_call x1, Pallas kernels, front(): pl.pallas_call(functools.partial(front_kernel, cap), grid=(filts // units...  13.2 us
    all_to_all x2, starting transfers between devices, gather_core(): lax.all_to_all(x, 'shard', split_axis=0, concat_axis=0, axis_index_groups...  10.1 us
    pallas_call x1, Pallas kernels, column_feats(): pl.pallas_call(feats_kernel, grid_spec=pltpu.PrefetchScalarGridSpec(num_s...  9.2 us
    pallas_call x1, Pallas kernels, filter_sums(): pl.pallas_call(functools.partial(diag_kernel, taps), grid=(filts // units...  8.36 us
    all_to_all x2, starting transfers between devices, exchange(): return lax.all_to_all(x, 'shard', split_axis=0, concat_axis=0, tiled=True)  7.08 us
    pallas_call x1, Pallas kernels, rel_part(): pl.pallas_call(rel_kernel, out_shape=jax.ShapeDtypeStruct((width, rels),...  5.41 us
  transfers between devices with their start and end apart: 8, of which 3 were waited for; matrix products, arithmetic and copies ran while one was open for 3% of the time, Pallas kernels for 52%

profile of v8, /device:TPU:0, one launch (start us, length us, event | category | flops | bytes accessed | tf_op | source)
XLA Modules:
  0.0 145.5 jit_solution(2848805993990146254)
XLA Ops:
  7.3 4.0 %pack_tails.1 = (bf16[1,200,512]{2,1,0:T(8,128)(2,1)}, s32[512,1]{1,0:T(8,128)}) custom-call(s32[1]{0:T(128)} %bitcast.me_ref, s32[32,128]{1,0:T(8,128)} %bitcast.35, s32[32,128]{1,0:T(8,128)} %bitcast.34, bf16[200,2048]{1,0:T(8,128)(2,1)} %bitcast.30), custom_call_target="tpu_custom_call" | custom-call | flops 1000000000 | bytes 2000000 | tf_op jit(solution)/shard_map/pack_tails/pallas_call | solution.py:167
  11.4 13.9 %all_to_all.25.numbers_ref = s32[16,1,512]{2,1,0:T(1,128)} all-to-all(s32[16,1,512]{2,1,0:T(1,128)S(1)} %broadcast_in_dim.9), channel_id=1, replica_groups=mesh['parts'=2,'shard'=16] {'shard'}, dimensions={0} | all-to-all | bytes 65536 | tf_op jit(solution)/shard_map/all_to_all | solution.py:804
  25.3 2.6 %find_heads.1 = (bf16[16,16,200]{2,1,0:T(8,128)(2,1)}, s32[256,1]{1,0:T(8,128)}) custom-call(s32[1]{0:T(128)} %bitcast.me_ref, bf16[200,2048]{1,0:T(8,128)(2,1)} %bitcast.31, s32[16,1,512]{2,1,0:T(1,128)} %all_to_all.25.numbers_ref), custom_call_target="tpu_custom_call" | custom-call | flops 300000000 | bytes 2000000 | tf_op jit(solution)/shard_map/find_heads/pallas_call | solution.py:205
  27.9 3.5 %all-to-all-start.1 = ((bf16[16,16,200]{2,1,0:T(8,128)(2,1)}), bf16[16,16,200]{2,1,0:T(8,128)(2,1)S(1)}, u32[]{:S(2)}, u32[]{:S(2)}) async-start(bf16[16,16,200]{2,1,0:T(8,128)(2,1)} %get-tuple-element.35), calls=%async_computation.1 | async-start | bytes 262144 | tf_op jit(solution)/shard_map/all_to_all | solution.py:804
  31.6 0.6 broadcast_in_dim.11.ext_ref
  32.2 0.7 copy.18.filt_ref
  32.9 5.3 %band.1 = (bf16[3840,256]{1,0:T(8,128)(2,1)}, bf16[256,3840]{1,0:T(8,128)(2,1)}) custom-call(s32[20,256]{1,0:T(8,128)} %constant.8.clone.codes_ref, bf16[48,81]{1,0:T(8,128)(2,1)} %copy.18.filt_ref), custom_call_target="tpu_custom_call" | custom-call | flops 40000000 | bytes 4000000 | tf_op jit(solution)/shard_map/band/pallas_call | solution.py:94
  38.1 1.2 all-to-all-done.1.fetched_ref
  39.3 0.7 copy-done.4
  39.9 13.2 %front.1 = (f32[19200,128]{1,0:T(8,128)}, bf16[256,640]{1,0:T(8,128)(2,1)}, bf16[128,200]{1,0:T(8,128)(2,1)}, bf16[8,2,200,128]{3,2,1,0:T(8,128)(2,1)}) custom-call(bf16[16,16,200]{2,1,0:T(8,128)(2,1)} %copy-done.4, s32[1,128]{1,0:T(1,128)} %bitcast.25, s32[1,128]{1,0:T(1,128)} %bitcast.28, bf16[200,1387]{1,0:T(8,128)(2,1)} %bitcast.32, ...), custom_call_target="tpu_custom_call" | custom-call | flops 4000000000 | bytes 24000000 | tf_op jit(solution)/shard_map/front/pallas_call | solution.py:325
  53.2 4.3 %all-to-all-start.2 = ((bf16[8,2,200,128]{3,2,1,0:T(8,128)(2,1)}), bf16[8,2,200,128]{3,2,1,0:T(8,128)(2,1)S(1)}, u32[]{:S(2)}, u32[]{:S(2)}) async-start(bf16[8,2,200,128]{3,2,1,0:T(8,128)(2,1)} %get-tuple-element.41), calls=%async_computation.2 | async-start | bytes 1638400 | tf_op jit(solution)/shard_map/all_to_all | solution.py:808
  57.5 0.2 all-gather.5.cloned.1.call-start
  57.7 4.4 %slot_tables.1 = (s32[2,512,1]{2,1,0:T(8,128)}, s32[128,1]{1,0:T(8,128)}) custom-call(s32[1]{0:T(128)} %bitcast.me_ref, s32[32,128]{1,0:T(8,128)} %bitcast.36, s32[1,4096]{1,0:T(1,128)} %bitcast.37, s32[1,128]{1,0:T(1,128)} %bitcast.29), custom_call_target="tpu_custom_call" | custom-call | flops 1000000000 | bytes 1000000 | tf_op jit(solution)/shard_map/slot_tables/pallas_call | solution.py:247
  62.1 18.4 %middle.1 = (bf16[16,16,200]{2,1,0:T(8,128)(2,1)}, f32[1,200,128]{2,1,0:T(8,128)}, bf16[8,200,128]{2,1,0:T(8,128)(2,1)}, bf16[3840,640]{1,0:T(8,128)(2,1)}) custom-call(s32[128,1]{1,0:T(8,128)} %get-tuple-element.34.pos_ref, bf16[128,200]{1,0:T(8,128)(2,1)} %get-tuple-element.37.qv_ref, s32[1,128]{1,0:T(1,128)} %bitcast.26, ...), custom_call_target="tpu_custom_call" | custom-call | flops 6000000000 | bytes 25000000 | tf_op jit(solution)/shard_map/middle/pallas_call | solution.py:461
  80.5 5.8 %all-to-all-start.3 = ((bf16[8,200,128]{2,1,0:T(8,128)(2,1)}), bf16[8,200,128]{2,1,0:T(8,128)(2,1)S(1)}, u32[]{:S(2)}, u32[]{:S(2)}) async-start(bf16[8,200,128]{2,1,0:T(8,128)(2,1)} %get-tuple-element.48), calls=%async_computation.3 | async-start | bytes 819200 | tf_op jit(solution)/shard_map/all_to_all | solution.py:808
  86.3 0.6 pad_add_fusion.2.ids_ref
  86.8 8.4 %filter_sums.1 = bf16[16,64,200]{2,1,0:T(8,128)(2,1)} custom-call(s32[20,256]{1,0:T(8,128)} %constant.8.clone.codes_ref, bf16[3840,640]{1,0:T(8,128)(2,1)} %get-tuple-element.45.fgrad_ref, bf16[256,640]{1,0:T(8,128)(2,1)} %get-tuple-element.46.img_ref, bf16[16,16,200]{2,1,0:T(8,128)(2,1)} %get-tuple-element.47.rows_ref), custom_call_target="tpu_custom_call" | custom-call | flops 2000000000 | bytes 6000000 | tf_op jit(solution)/shard_map/filter_sums/pallas_call | solution.py:536
  95.2 5.3 %all-to-all-done.3.grads_ref = bf16[8,200,128]{2,1,0:T(8,128)(2,1)S(1)} async-done(((bf16[8,200,128]{2,1,0:T(8,128)(2,1)}), bf16[8,200,128]{2,1,0:T(8,128)(2,1)S(1)}, u32[]{:S(2)}, u32[]{:S(2)}) %all-to-all-start.3) | async-done | bytes 409632 | tf_op jit(solution)/shard_map/all_to_all | solution.py:808
  100.6 3.6 %all-to-all-start.4 = ((bf16[16,64,200]{2,1,0:T(8,128)(2,1)}), bf16[16,64,200]{2,1,0:T(8,128)(2,1)S(1)}, u32[]{:S(2)}, u32[]{:S(2)}) async-start(bf16[16,64,200]{2,1,0:T(8,128)(2,1)} %filter_sums.1), calls=%async_computation.4 | async-start | bytes 1048576 | tf_op jit(solution)/shard_map/all_to_all | solution.py:804
  104.1 9.2 %column_feats.1.feats_ref = bf16[2400,1024]{1,0:T(8,128)(2,1)} custom-call(s32[3]{0:T(128)} %pad_add_fusion.2.ids_ref, bf16[200,1387]{1,0:T(8,128)(2,1)} %bitcast.33, s32[1,576]{1,0:T(1,128)} %broadcast_in_dim.11.ext_ref, bf16[3840,256]{1,0:T(8,128)(2,1)} %get-tuple-element.36.band_ref.mate_ref, bf16[3840,256]{1,0:T(8,128)(2,1)} %get-tuple-element.36.band_ref.mate_ref, ...), custom_call_target="tpu_custom_call" | custom-call | flops 5000000000 | bytes 6000000 | tf_op jit(solution)/shard_map/column_feats/pallas_call | solution.py:638
  113.3 5.1 %proj_grad.1 = (f32[200,1200]{1,0:T(8,128)}, f32[200,1200]{1,0:T(8,128)}) custom-call(bf16[2400,1024]{1,0:T(8,128)(2,1)} %column_feats.1.feats_ref, bf16[8,200,128]{2,1,0:T(8,128)(2,1)} %copy-done.1), custom_call_target="tpu_custom_call" | custom-call | flops 1000000000 | bytes 8000000 | tf_op jit(solution)/shard_map/proj_grad/pallas_call | solution.py:676
  118.4 0.3 collective-permute-start.1
  118.7 4.9 %tail_grad.1 = (f32[200,512]{1,0:T(8,128)}, f32[200,512]{1,0:T(8,128)}) custom-call(s32[3]{0:T(128)} %pad_add_fusion.2.ids_ref, bf16[16,200,512]{2,1,0:T(8,128)(2,1)} %all-gather.3.cloned.1.call-done.tails_hbm.tails_ref.mate_ref, bf16[16,200,512]{2,1,0:T(8,128)(2,1)} %all-gather.3.cloned.1.call-done.tails_hbm.tails_ref.mate_ref, ...), custom_call_target="tpu_custom_call" | custom-call | flops 2000000000 | bytes 3000000 | tf_op jit(solution)/shard_map/tail_grad/pallas_call | solution.py:579
  123.6 0.2 collective-permute-start
  123.8 1.8 %collective-permute-done.recv_ref = f32[200,512]{1,0:T(8,128)S(1)} collective-permute-done((f32[200,512]{1,0:T(8,128)}, f32[200,512]{1,0:T(8,128)S(1)}, u32[]{:S(2)}, u32[]{:S(2)}) %collective-permute-start) | collective-permute-done | bytes 409632 | tf_op jit(solution)/shard_map/ppermute | solution.py:801
  125.6 0.8 copy-done.11
  126.4 0.2 copy-done.3
  126.5 4.2 %entity_grad.1 = (f32[200,2048]{1,0:T(8,128)}, f32[96,48]{1,0:T(8,128)}) custom-call(s32[256,1]{1,0:T(8,128)} %get-tuple-element.30.want_ref, s32[512,1]{1,0:T(8,128)} %get-tuple-element.31.srow_ref, f32[200,512]{1,0:T(8,128)} %get-tuple-element.43.own_ref, f32[200,512]{1,0:T(8,128)} %copy-done.11, bf16[16,64,200]{2,1,0:T(8,128)(2,1)} %copy-done.3), custom_call_target="tpu_custom_call" | custom-call | flops 1500000000 | bytes 4000000 | tf_op jit(solution)/shard_map/entity_grad/pallas_call | solution.py:761
  130.7 0.8 slice_bitcast_fusion
  131.5 0.6 reshape.27
  132.1 1.1 add_bitcast_fusion
  133.2 5.4 %rel_grad.1 = f32[200,1387]{1,0:T(8,128)} custom-call(s32[16,1,512]{2,1,0:T(1,128)} %all_to_all.25.numbers_ref, f32[16,200,128]{2,1,0:T(8,128)} %all-gather.5.cloned.1.call-done.sums_ref), custom_call_target="tpu_custom_call" | custom-call | flops 2000000000 | bytes 3000000 | tf_op jit(solution)/shard_map/rel_grad/pallas_call | solution.py:725
  (36 shorter events, 0.3 us)
Async XLA Ops:
  7.2 4.1 %copy-start.10 = (s32[128]{0:T(128)S(1)}, s32[128]{0:T(128)}, u32[]{:S(2)}) copy-start(s32[128]{0:T(128)} %param.20) | copy-start | bytes 1540
  7.2 4.1 %copy-start.9 = (s32[128]{0:T(128)S(1)}, s32[128]{0:T(128)}, u32[]{:S(2)}) copy-start(s32[128]{0:T(128)} %param.19) | copy-start | bytes 1540
  7.2 4.1 %copy-start.6 = (s32[128,1]{0,1:T(1,128)S(1)}, s32[128,1]{0,1:T(1,128)}, u32[]{:S(2)}) copy-start(s32[128,1]{0,1:T(1,128)} %param.17) | copy-start | bytes 1540
  7.2 4.1 %copy-start.8 = (s32[128]{0:T(128)S(1)}, s32[128]{0:T(128)}, u32[]{:S(2)}) copy-start(s32[128]{0:T(128)} %param.18) | copy-start | bytes 1540
  7.2 24.2 %copy-start.7 = (s32[400]{0:T(512)S(1)}, s32[400]{0:T(512)}, u32[]{:S(2)}) copy-start(s32[400]{0:T(512)} %param.16) | copy-start | bytes 4804
  7.2 24.3 %slice-start = ((s32[400]{0:T(512)}), s32[96]{0:T(128)S(1)}, s32[]{:S(2)}) async-start(s32[400]{0:T(512)} %param.16), calls=%async_computation.7 | async-start | bytes 1024 | tf_op jit(solution)/shard_map/slice | solution.py:830
  7.2 24.9 %copy-start.5 = (bf16[48,9,9]{0,2,1:T(8,128)(2,1)S(1)}, bf16[48,9,9]{0,2,1:T(8,128)(2,1)}, u32[]{:S(2)}) copy-start(bf16[48,9,9]{0,2,1:T(8,128)(2,1)} %param.14) | copy-start | bytes 23332
  7.2 54.8 %all-gather.3.cloned.1.call-start = ((), (), s32[]{:S(2)}) async-start(), calls=%async_computation.5 | async-start | bytes 3481600 | tf_op jit(solution)/shard_map/all_gather | solution.py:822
  27.9 11.4 %all-to-all-start.1 = ((bf16[16,16,200]{2,1,0:T(8,128)(2,1)}), bf16[16,16,200]{2,1,0:T(8,128)(2,1)S(1)}, u32[]{:S(2)}, u32[]{:S(2)}) async-start(bf16[16,16,200]{2,1,0:T(8,128)(2,1)} %get-tuple-element.35), calls=%async_computation.1 | async-start | bytes 262144 | tf_op jit(solution)/shard_map/all_to_all | solution.py:804
  39.3 0.7 copy-start.4
  53.2 27.3 %all-to-all-start.2 = ((bf16[8,2,200,128]{3,2,1,0:T(8,128)(2,1)}), bf16[8,2,200,128]{3,2,1,0:T(8,128)(2,1)S(1)}, u32[]{:S(2)}, u32[]{:S(2)}) async-start(bf16[8,2,200,128]{3,2,1,0:T(8,128)(2,1)} %get-tuple-element.41), calls=%async_computation.2 | async-start | bytes 1638400 | tf_op jit(solution)/shard_map/all_to_all | solution.py:808
  57.5 75.7 %all-gather.5.cloned.1.call-start = ((), (), s32[]{:S(2)}) async-start(), calls=%async_computation.6 | async-start | bytes 1740800 | tf_op jit(solution)/shard_map/all_gather | solution.py:840
  80.5 14.7 %copy-start = (bf16[8,2,200,128]{3,2,1,0:T(8,128)(2,1)}, bf16[8,2,200,128]{3,2,1,0:T(8,128)(2,1)S(1)}, u32[]{:S(2)}) copy-start(bf16[8,2,200,128]{3,2,1,0:T(8,128)(2,1)S(1)} %all-to-all-done.2.vecs_ref) | copy-start | bytes 2457604
  80.5 20.1 %all-to-all-start.3 = ((bf16[8,200,128]{2,1,0:T(8,128)(2,1)}), bf16[8,200,128]{2,1,0:T(8,128)(2,1)S(1)}, u32[]{:S(2)}, u32[]{:S(2)}) async-start(bf16[8,200,128]{2,1,0:T(8,128)(2,1)} %get-tuple-element.48), calls=%async_computation.3 | async-start | bytes 819200 | tf_op jit(solution)/shard_map/all_to_all | solution.py:808
  100.6 12.8 %copy-start.1 = (bf16[8,200,128]{2,1,0:T(8,128)(2,1)}, bf16[8,200,128]{2,1,0:T(8,128)(2,1)S(1)}, u32[]{:S(2)}) copy-start(bf16[8,200,128]{2,1,0:T(8,128)(2,1)S(1)} %all-to-all-done.3.grads_ref) | copy-start | bytes 1228804
  100.6 25.1 %all-to-all-start.4 = ((bf16[16,64,200]{2,1,0:T(8,128)(2,1)}), bf16[16,64,200]{2,1,0:T(8,128)(2,1)S(1)}, u32[]{:S(2)}, u32[]{:S(2)}) async-start(bf16[16,64,200]{2,1,0:T(8,128)(2,1)} %filter_sums.1), calls=%async_computation.4 | async-start | bytes 1048576 | tf_op jit(solution)/shard_map/all_to_all | solution.py:804
  118.4 13.7 %collective-permute-start.1 = (f32[200,1200]{1,0:T(8,128)}, f32[200,1200]{1,0:T(8,128)S(1)}, u32[]{:S(2)}, u32[]{:S(2)}) collective-permute-start(f32[200,1200]{1,0:T(8,128)} %get-tuple-element.55), channel_id=1, source_target_pairs={{0,1},{1,0},{2,3},{3,2},{4,5},{5,4},{6,7},{7,6},{8,9},{9,8},{10,11... | collective-permute-start | bytes 2880008 | tf_op jit(solution)/shard_map/ppermute | solution.py:801
  123.6 8.5 %copy-start.2 = (f32[200,1200]{1,0:T(8,128)S(1)}, f32[200,1200]{1,0:T(8,128)}, u32[]{:S(2)}) copy-start(f32[200,1200]{1,0:T(8,128)} %get-tuple-element.54) | copy-start | bytes 2880004
  123.6 2.0 %collective-permute-start = (f32[200,512]{1,0:T(8,128)}, f32[200,512]{1,0:T(8,128)S(1)}, u32[]{:S(2)}, u32[]{:S(2)}) collective-permute-start(f32[200,512]{1,0:T(8,128)} %get-tuple-element.44), channel_id=1, source_target_pairs={{0,1},{1,0},{2,3},{3,2},{4,5},{5,4},{6,7},{7,6},{8,9},{9,8},{10,11... | collective-permute-start | bytes 1228808 | tf_op jit(solution)/shard_map/ppermute | solution.py:801
  125.6 0.8 copy-start.11
  125.6 0.9 copy-start.3
Sparse Core Ops, SparseCore 0:
  11.4 49.2 all-gather.2
  80.6 45.3 all-gather.4

commit v9 on v8

--- a/solution.py
+++ b/solution.py
@@ -359,9 +359,10 @@
 
 
 def middle_kernel(
-    cap, cand, pos_ref, qv_ref, orow_ref, ext_ref, bandt_ref, tails_hbm, w_hbm, slope_hbm,
+    cap, cand, pos_ref, qv_ref, orow_ref, ext_ref, bandt_hbm, tails_hbm, w_hbm, slope_hbm,
     out_ref, sums_ref, qgt_ref, fgrad_hbm,
-    tails, w, slope, fgrad, scores, grads, spread, ext, linear, tail_sems, w_sems, slope_sems, out_sems,
+    bandt, tails, w, slope, fgrad, scores, grads, spread, ext, linear,
+    band_sem, tail_sems, w_sems, slope_sems, out_sems,
 ):
     owners, width, slots = tails.shape
     steps, _, cols = w.shape
@@ -386,9 +387,12 @@
 
     for i in range(chunks):
         tail_copy(i).start()
+    band_copy = pltpu.make_async_copy(bandt_hbm, bandt, band_sem)
     for k in range(steps):
         w_copy(k).start()
         slope_copy(k).start()
+        if k == 0:
+            band_copy.start()
 
     qv = qv_ref[...]
     total = jnp.zeros((queries, width), f32)
@@ -422,7 +426,9 @@
                 lanes = slice(g * queries, (g + 1) * queries)
                 fgrad[k, part, lanes] = (lin[rows, :] * slope[k, rows, :]).astype(bf16)
         out_copy(k).start()
-        spread_k = mm(bandt_ref[:, k * part_rows : (k + 1) * part_rows], fgrad[k])
+        if k == 0:
+            band_copy.wait()
+        spread_k = mm(bandt[:, k * part_rows : (k + 1) * part_rows], fgrad[k])
         if k == 0:
             spread[...] = spread_k
         else:
@@ -460,7 +466,7 @@
     hbm = pl.BlockSpec(memory_space=pl.ANY)
     return pl.pallas_call(
         functools.partial(middle_kernel, cap, cand),
-        in_specs=[VMEM] * 5 + [hbm] * 3,
+        in_specs=[VMEM] * 4 + [hbm] * 4,
         out_specs=[VMEM] * 3 + [hbm],
         out_shape=[
             jax.ShapeDtypeStruct((owners, cap, width), bf16),
@@ -469,6 +475,7 @@
             jax.ShapeDtypeStruct((filts * BAND_OUT, GROUPS * queries), bf16),
         ],
         scratch_shapes=[
+            pltpu.VMEM(band_t.shape, bf16),
             pltpu.VMEM(tails.shape, bf16),
             pltpu.VMEM((steps, width, cols), bf16),
             pltpu.VMEM((steps, cols, queries), f32),
@@ -478,6 +485,7 @@
             pltpu.VMEM((LANES, GROUPS * queries), f32),
             pltpu.VMEM((ext.shape[1], queries), f32),
             pltpu.VMEM((2, cols, queries), f32),
+            pltpu.SemaphoreType.DMA,
             pltpu.SemaphoreType.DMA((owners // blocks,)),
             pltpu.SemaphoreType.DMA((steps,)),
             pltpu.SemaphoreType.DMA((steps,)),
@@ -601,8 +609,9 @@
     )(ids, tails, tails, scand, numbers, vecs)
 
 
-def feats_kernel(
-    ids_ref, rtab_ref, ext_ref, band_ref, mate_ref, numbers_ref, vecs_ref, out_ref, hpick, rpick, rels_hot, ext, pre
+def proj_kernel(
+    ids_ref, rtab_ref, ext_ref, band_ref, mate_ref, numbers_ref, vecs_ref, grads_ref,
+    own_ref, other_ref, feats, hpick, rpick, rels_hot, ext, pre,
 ):
     width, rels = rtab_ref.shape
     units = band_ref.shape[0] // BAND_OUT
@@ -628,15 +637,19 @@
                 for f in range(units):
                     v = pre[slot, f * BAND_OUT : (f + 1) * BAND_OUT, :]
                     first = k * cols + f * flat + g * BAND_OUT
-                    out_ref[first : first + BAND_OUT, lanes] = (v * sigmoid(v)).astype(bf16)
-
-
-def column_feats(ids, rtab_t, ext, band, numbers, vecs, cols):
+                    feats[first : first + BAND_OUT, lanes] = (v * sigmoid(v)).astype(bf16)
+    qgt = beside(grads_ref[p] for p in range(grads_ref.shape[0]))
+    own_ref[...] = mm(qgt, feats[:cols, :], NT)
+    other_ref[...] = mm(qgt, feats[cols:, :], NT)
+
+
+def proj_part(ids, rtab_t, ext, band, numbers, vecs, grads, cols):
     width, rels = rtab_t.shape
     unit = cols // GROUPS
     gathered, _, _, queries = vecs.shape
-    return pl.pallas_call(
-        feats_kernel,
+    half = jax.ShapeDtypeStruct((width, cols), f32)
+    return pl.pallas_call(
+        proj_kernel,
         grid_spec=pltpu.PrefetchScalarGridSpec(
             num_scalar_prefetch=1,
             grid=(1,),
@@ -647,9 +660,11 @@
                 pl.BlockSpec((unit, LANES), lambda s, ids: (ids[1], 0)),
                 whole(numbers.shape),
                 whole(vecs.shape),
+                whole(grads.shape),
             ],
-            out_specs=whole((2 * cols, gathered * queries)),
+            out_specs=[whole(half.shape)] * 2,
             scratch_shapes=[
+                pltpu.VMEM((2 * cols, gathered * queries), bf16),
                 pltpu.VMEM((ext.shape[1], width), bf16),
                 pltpu.VMEM((ext.shape[1], width), bf16),
                 pltpu.VMEM((rels, 2 * queries), bf16),
@@ -657,29 +672,11 @@
                 pltpu.VMEM((2, unit, 2 * queries), f32),
             ],
         ),
-        out_shape=jax.ShapeDtypeStruct((2 * cols, gathered * queries), bf16),
+        out_shape=[half, half],
         compiler_params=params("arbitrary"),
-        cost_estimate=cost(5e9, 6e6, 2.5e6),
-        name="column_feats",
-    )(ids, rtab_t, ext, band, band, numbers, vecs)
-
-
-def proj_kernel(feats_ref, grads_ref, own_ref, other_ref):
-    cols = own_ref.shape[1]
-    qgt = beside(grads_ref[p] for p in range(grads_ref.shape[0]))
-    own_ref[...] = mm(qgt, feats_ref[:cols, :], NT)
-    other_ref[...] = mm(qgt, feats_ref[cols:, :], NT)
-
-
-def proj_part(feats, grads):
-    half = jax.ShapeDtypeStruct((grads.shape[1], feats.shape[0] // 2), f32)
-    return pl.pallas_call(
-        proj_kernel,
-        out_shape=[half, half],
-        compiler_params=params(),
-        cost_estimate=cost(1e9, 8e6),
+        cost_estimate=cost(6e9, 6e6, 2.5e6),
         name="proj_grad",
-    )(feats, grads)
+    )(ids, rtab_t, ext, band, band, numbers, vecs, grads)
 
 
 def proj_columns(first, cols, filters, chequer_perm, relation_table, numbers, heads, grads):
@@ -703,7 +700,9 @@
     return mm(qg, (pre * sigmoid(pre)).astype(bf16), TN)
 
 
-def rel_kernel(numbers_ref, sums_ref, rel_ref, picks):
+def rel_kernel(numbers_ref, sums_hbm, rel_ref, sums_ref, picks, sem):
+    copy = pltpu.make_async_copy(sums_hbm, sums_ref, sem)
+    copy.start()
     width, rels = rel_ref.shape
     queries = sums_ref.shape[2]
     total = None
@@ -714,6 +713,8 @@
             for r in spans(rels, 128):
                 here = iota((r.stop - r.start, queries), 0) + r.start
                 picks[r, i * queries : (i + 1) * queries] = onehot(here == rel)
+        if block.start == 0:
+            copy.wait()
         parts = jnp.concatenate(split(beside(sums_ref[p] for p in members)), axis=0)
         part = mm(parts, picks[...], NT)
         total = part if total is None else total + part
@@ -724,8 +725,13 @@
     count, width, queries = sums.shape
     return pl.pallas_call(
         rel_kernel,
+        in_specs=[VMEM, pl.BlockSpec(memory_space=pl.ANY)],
         out_shape=jax.ShapeDtypeStruct((width, rels), f32),
-        scratch_shapes=[pltpu.VMEM((rels, math.gcd(count, 16) * queries), bf16)],
+        scratch_shapes=[
+            pltpu.VMEM(sums.shape, f32),
+            pltpu.VMEM((rels, math.gcd(count, 16) * queries), bf16),
+            pltpu.SemaphoreType.DMA,
+        ],
         compiler_params=params(),
         cost_estimate=cost(2e9, 3e6),
         name="rel_grad",
@@ -821,11 +827,12 @@
     tails_t, slot_row = pack_tails(me1, tail_owners, tail_row, table_t, tail_cap)
     all_tails = lax.all_gather(tails_t, "shard", axis=0, tiled=True)
     scand, pos = slot_tables(me1, tail_owners, pos_index, tail_cap)
+    codes = jnp.asarray(band_codes(ks))
+    band, band_t = build_band(filters, codes)
+    numbers, scand, pos, band, band_t = lax.optimization_barrier((numbers, scand, pos, band, band_t))
     found, want = find_heads(me1, numbers, table_t, head_cap)
     fetched = exchange(found)
 
-    codes = jnp.asarray(band_codes(ks))
-    band, band_t = build_band(filters, codes)
     extra = BAND_OUT * (GROUPS - 1) + LANES - IMG * IMG - BAND_OUT
     ext = jnp.concatenate([chequer_perm[-BAND_OUT:], chequer_perm, chequer_perm[:extra]])[None]
     orow = heads[None, :]
@@ -852,8 +859,7 @@
 
     cols = filts * IMG * IMG // count
     if direct and cols % (IMG * IMG) == 0:
-        feats = column_feats(ids, rtab_t, ext, band, numbers, core_vecs, cols)
-        own, other = proj_part(feats, core_qgt)
+        own, other = proj_part(ids, rtab_t, ext, band, numbers, core_vecs, core_qgt, cols)
     else:
         core_numbers = lax.dynamic_index_in_dim(
             numbers.reshape(count // 2, 2, 4, queries), me & 1, 1, keepdims=False

time: 147 us -> 153 us (1.041)
  waiting for transfers between devices: 8.34 us -> 24.9 us
  blocking collectives: 13.9 us -> 0 us
  starting transfers between devices: 17.9 us -> 25.1 us
  Pallas kernels: 84.9 us -> 79.9 us
    all_to_all x1 -> x0, blocking collectives: 13.9 us -> none  [exchange(): return lax.all_to_all(x, 'shard', split_axis=0, concat_axis=0, tiled=True)]
    all_to_all x2 -> x3, waiting for transfers between devices: 1.16 us -> 13.3 us  [exchange(): return lax.all_to_all(x, 'shard', split_axis=0, concat_axis=0, tiled=True)]
    all_to_all x2 -> x3, starting transfers between devices: 7.08 us -> 17.2 us  [exchange(): return lax.all_to_all(x, 'shard', split_axis=0, concat_axis=0, tiled=True)]
    all_to_all x2, waiting for transfers between devices: 5.35 us -> 9.9 us  [gather_core(): lax.all_to_all(x, 'shard', split_axis=0, concat_axis=0, axis_index_groups...]
    pallas_call x3 -> x2, Pallas kernels: 19.7 us -> 15.7 us  [the longest x1 9.47 us: proj_part(): pl.pallas_call(proj_kernel, grid_spec=pltpu.PrefetchScalarGridSpec(num_sc...]
    all_to_all x2, starting transfers between devices: 10.1 us -> 7.21 us  [gather_core(): lax.all_to_all(x, 'shard', split_axis=0, concat_axis=0, axis_index_groups...]
  transfers between devices with their start and end apart: 8 -> 9, of which waited for: 3 -> 5; matrix products, arithmetic and copies ran while one was open for 3% -> 3% of each run, Pallas kernels for 52% -> 46%
where the time goes in v9:
time: 153 us; the launch traced here: 151 us
  Pallas kernels  79.9 us (52%)
  starting transfers between devices  25.1 us (16%)
  waiting for transfers between devices  24.9 us (16%)
  between operations  14.2 us (9%)
  local copies, waits for them, and re-layouts  5.55 us (4%)
  other arithmetic  1.82 us (1%)
    pallas_call x1, Pallas kernels, middle(): pl.pallas_call(functools.partial(middle_kernel, cap, cand), in_specs=[VME...  17.6 us
    all_to_all x3, starting transfers between devices, exchange(): return lax.all_to_all(x, 'shard', split_axis=0, concat_axis=0, tiled=True)  17.2 us
    all_to_all x3, waiting for transfers between devices, exchange(): return lax.all_to_all(x, 'shard', split_axis=0, concat_axis=0, tiled=True)  13.3 us
    pallas_call x1, Pallas kernels, front(): pl.pallas_call(functools.partial(front_kernel, cap), grid=(filts // units...  12.8 us
    all_to_all x2, waiting for transfers between devices, gather_core(): lax.all_to_all(x, 'shard', split_axis=0, concat_axis=0, axis_index_groups...  9.9 us
    pallas_call x1, Pallas kernels, proj_part(): pl.pallas_call(proj_kernel, grid_spec=pltpu.PrefetchScalarGridSpec(num_sc...  9.47 us
    pallas_call x1, Pallas kernels, filter_sums(): pl.pallas_call(functools.partial(diag_kernel, taps), grid=(filts // units...  8.36 us
    all_to_all x2, starting transfers between devices, gather_core(): lax.all_to_all(x, 'shard', split_axis=0, concat_axis=0, axis_index_groups...  7.21 us
  transfers between devices with their start and end apart: 9, of which 5 were waited for; matrix products, arithmetic and copies ran while one was open for 3% of the time, Pallas kernels for 46%

profile of v9, /device:TPU:0, one launch (start us, length us, event | category | flops | bytes accessed | tf_op | source)
XLA Modules:
  0.0 151.4 jit_solution(15285280419706151557)
XLA Ops:
  7.3 4.0 %pack_tails.1 = (bf16[1,200,512]{2,1,0:T(8,128)(2,1)}, s32[512,1]{1,0:T(8,128)}) custom-call(s32[1]{0:T(128)} %bitcast.me_ref, s32[32,128]{1,0:T(8,128)} %bitcast.35, s32[32,128]{1,0:T(8,128)} %bitcast.34, bf16[200,2048]{1,0:T(8,128)(2,1)} %bitcast.30), custom_call_target="tpu_custom_call" | custom-call | flops 1000000000 | bytes 2000000 | tf_op jit(solution)/shard_map/pack_tails/pallas_call | solution.py:167
  11.3 0.6 broadcast_in_dim.9
  12.0 7.4 %all-to-all-start = ((s32[16,1,512]{2,1,0:T(1,128)}), s32[16,1,512]{2,1,0:T(1,128)S(1)}, u32[]{:S(2)}, u32[]{:S(2)}) async-start(s32[16,1,512]{2,1,0:T(1,128)} %broadcast_in_dim.9), calls=%async_computation | async-start | bytes 65536 | tf_op jit(solution)/shard_map/all_to_all | solution.py:810
  19.4 0.7 copy.18.filt_ref
  20.1 5.3 %band.1 = (bf16[3840,256]{1,0:T(8,128)(2,1)}, bf16[256,3840]{1,0:T(8,128)(2,1)}) custom-call(s32[20,256]{1,0:T(8,128)} %constant.8.clone.codes_ref, bf16[48,81]{1,0:T(8,128)(2,1)} %copy.18.filt_ref), custom_call_target="tpu_custom_call" | custom-call | flops 40000000 | bytes 4000000 | tf_op jit(solution)/shard_map/band/pallas_call | solution.py:94
  25.3 4.4 %slot_tables.1 = (s32[2,512,1]{2,1,0:T(8,128)}, s32[128,1]{1,0:T(8,128)}) custom-call(s32[1]{0:T(128)} %bitcast.me_ref, s32[32,128]{1,0:T(8,128)} %bitcast.36, s32[1,4096]{1,0:T(1,128)} %bitcast.37, s32[1,128]{1,0:T(1,128)} %bitcast.28), custom_call_target="tpu_custom_call" | custom-call | flops 1000000000 | bytes 1000000 | tf_op jit(solution)/shard_map/slot_tables/pallas_call | solution.py:247
  29.7 0.6 copy-done.4
  30.3 2.6 %find_heads.1 = (bf16[16,16,200]{2,1,0:T(8,128)(2,1)}, s32[256,1]{1,0:T(8,128)}) custom-call(s32[1]{0:T(128)} %bitcast.me_ref, bf16[200,2048]{1,0:T(8,128)(2,1)} %bitcast.31, s32[16,1,512]{2,1,0:T(1,128)} %copy-done.4), custom_call_target="tpu_custom_call" | custom-call | flops 300000000 | bytes 2000000 | tf_op jit(solution)/shard_map/find_heads/pallas_call | solution.py:205
  32.9 6.0 %all-to-all-start.1 = ((bf16[16,16,200]{2,1,0:T(8,128)(2,1)}), bf16[16,16,200]{2,1,0:T(8,128)(2,1)S(1)}, u32[]{:S(2)}, u32[]{:S(2)}) async-start(bf16[16,16,200]{2,1,0:T(8,128)(2,1)} %get-tuple-element.45), calls=%async_computation.1 | async-start | bytes 262144 | tf_op jit(solution)/shard_map/all_to_all | solution.py:810
  39.1 0.6 broadcast_in_dim.11.ext_ref
  39.7 9.3 %all-to-all-done.1.fetched_ref = bf16[16,16,200]{2,1,0:T(8,128)(2,1)S(1)} async-done(((bf16[16,16,200]{2,1,0:T(8,128)(2,1)}), bf16[16,16,200]{2,1,0:T(8,128)(2,1)S(1)}, u32[]{:S(2)}, u32[]{:S(2)}) %all-to-all-start.1) | async-done | bytes 102432 | tf_op jit(solution)/shard_map/all_to_all | solution.py:810
  49.0 0.7 copy-done.5
  49.6 12.8 %front.1 = (f32[19200,128]{1,0:T(8,128)}, bf16[256,640]{1,0:T(8,128)(2,1)}, bf16[128,200]{1,0:T(8,128)(2,1)}, bf16[8,2,200,128]{3,2,1,0:T(8,128)(2,1)}) custom-call(bf16[16,16,200]{2,1,0:T(8,128)(2,1)} %copy-done.5, s32[1,128]{1,0:T(1,128)} %bitcast.25, s32[1,128]{1,0:T(1,128)} %bitcast.29, bf16[200,1387]{1,0:T(8,128)(2,1)} %bitcast.32, ...), custom_call_target="tpu_custom_call" | custom-call | flops 4000000000 | bytes 24000000 | tf_op jit(solution)/shard_map/front/pallas_call | solution.py:325
  62.5 3.6 %all-to-all-start.2 = ((bf16[8,2,200,128]{3,2,1,0:T(8,128)(2,1)}), bf16[8,2,200,128]{3,2,1,0:T(8,128)(2,1)S(1)}, u32[]{:S(2)}, u32[]{:S(2)}) async-start(bf16[8,2,200,128]{3,2,1,0:T(8,128)(2,1)} %get-tuple-element.51), calls=%async_computation.2 | async-start | bytes 1638400 | tf_op jit(solution)/shard_map/all_to_all | solution.py:814
  66.3 17.6 %middle.1 = (bf16[16,16,200]{2,1,0:T(8,128)(2,1)}, f32[1,200,128]{2,1,0:T(8,128)}, bf16[8,200,128]{2,1,0:T(8,128)(2,1)}, bf16[3840,640]{1,0:T(8,128)(2,1)}) custom-call(s32[128,1]{1,0:T(8,128)} %get-tuple-element.44.pos_ref, bf16[128,200]{1,0:T(8,128)(2,1)} %get-tuple-element.47.qv_ref, s32[1,128]{1,0:T(1,128)} %bitcast.26, ...), custom_call_target="tpu_custom_call" | custom-call | flops 6000000000 | bytes 25000000 | tf_op jit(solution)/shard_map/middle/pallas_call | solution.py:467
  84.0 3.5 %all-to-all-done.2.vecs_ref = bf16[8,2,200,128]{3,2,1,0:T(8,128)(2,1)S(1)} async-done(((bf16[8,2,200,128]{3,2,1,0:T(8,128)(2,1)}), bf16[8,2,200,128]{3,2,1,0:T(8,128)(2,1)S(1)}, u32[]{:S(2)}, u32[]{:S(2)}) %all-to-all-start.2) | async-done | bytes 819232 | tf_op jit(solution)/shard_map/all_to_all | solution.py:814
  87.5 3.6 %all-to-all-start.3 = ((bf16[8,200,128]{2,1,0:T(8,128)(2,1)}), bf16[8,200,128]{2,1,0:T(8,128)(2,1)S(1)}, u32[]{:S(2)}, u32[]{:S(2)}) async-start(bf16[8,200,128]{2,1,0:T(8,128)(2,1)} %get-tuple-element.58), calls=%async_computation.3 | async-start | bytes 819200 | tf_op jit(solution)/shard_map/all_to_all | solution.py:814
  91.1 0.7 pad_add_fusion.2.ids_ref
  91.8 8.4 %filter_sums.1 = bf16[16,64,200]{2,1,0:T(8,128)(2,1)} custom-call(s32[20,256]{1,0:T(8,128)} %constant.8.clone.codes_ref, bf16[3840,640]{1,0:T(8,128)(2,1)} %get-tuple-element.55.fgrad_ref, bf16[256,640]{1,0:T(8,128)(2,1)} %get-tuple-element.56.img_ref, bf16[16,16,200]{2,1,0:T(8,128)(2,1)} %get-tuple-element.57.rows_ref), custom_call_target="tpu_custom_call" | custom-call | flops 2000000000 | bytes 6000000 | tf_op jit(solution)/shard_map/filter_sums/pallas_call | solution.py:544
  100.2 6.4 %all-to-all-done.3.grads_ref = bf16[8,200,128]{2,1,0:T(8,128)(2,1)S(1)} async-done(((bf16[8,200,128]{2,1,0:T(8,128)(2,1)}), bf16[8,200,128]{2,1,0:T(8,128)(2,1)S(1)}, u32[]{:S(2)}, u32[]{:S(2)}) %all-to-all-start.3) | async-done | bytes 409632 | tf_op jit(solution)/shard_map/all_to_all | solution.py:814
  106.5 3.8 %all-to-all-start.4 = ((bf16[16,64,200]{2,1,0:T(8,128)(2,1)}), bf16[16,64,200]{2,1,0:T(8,128)(2,1)S(1)}, u32[]{:S(2)}, u32[]{:S(2)}) async-start(bf16[16,64,200]{2,1,0:T(8,128)(2,1)} %filter_sums.1), calls=%async_computation.4 | async-start | bytes 1048576 | tf_op jit(solution)/shard_map/all_to_all | solution.py:810
  110.4 9.5 %proj_grad.1 = (f32[200,1200]{1,0:T(8,128)}, f32[200,1200]{1,0:T(8,128)}) custom-call(s32[3]{0:T(128)} %pad_add_fusion.2.ids_ref, bf16[200,1387]{1,0:T(8,128)(2,1)} %bitcast.33, s32[1,576]{1,0:T(1,128)} %broadcast_in_dim.11.ext_ref, bf16[3840,256]{1,0:T(8,128)(2,1)} %get-tuple-element.46.band_ref.mate_ref, ...), custom_call_target="tpu_custom_call" | custom-call | flops 6000000000 | bytes 6000000 | tf_op jit(solution)/shard_map/proj_grad/pallas_call | solution.py:651
  119.9 4.9 %tail_grad.1 = (f32[200,512]{1,0:T(8,128)}, f32[200,512]{1,0:T(8,128)}) custom-call(s32[3]{0:T(128)} %pad_add_fusion.2.ids_ref, bf16[16,200,512]{2,1,0:T(8,128)(2,1)} %all-gather.3.cloned.1.call-done.tails_hbm.tails_ref.mate_ref, bf16[16,200,512]{2,1,0:T(8,128)(2,1)} %all-gather.3.cloned.1.call-done.tails_hbm.tails_ref.mate_ref, ...), custom_call_target="tpu_custom_call" | custom-call | flops 2000000000 | bytes 3000000 | tf_op jit(solution)/shard_map/tail_grad/pallas_call | solution.py:587
  124.8 0.4 collective-permute-start
  125.2 1.6 %collective-permute-done.recv_ref = f32[200,512]{1,0:T(8,128)S(1)} collective-permute-done((f32[200,512]{1,0:T(8,128)}, f32[200,512]{1,0:T(8,128)S(1)}, u32[]{:S(2)}, u32[]{:S(2)}) %collective-permute-start) | collective-permute-done | bytes 409632 | tf_op jit(solution)/shard_map/ppermute | solution.py:807
  126.8 4.0 %all-to-all-done.4.incoming_ref = bf16[16,64,200]{2,1,0:T(8,128)(2,1)S(1)} async-done(((bf16[16,64,200]{2,1,0:T(8,128)(2,1)}), bf16[16,64,200]{2,1,0:T(8,128)(2,1)S(1)}, u32[]{:S(2)}, u32[]{:S(2)}) %all-to-all-start.4) | async-done | bytes 409632 | tf_op jit(solution)/shard_map/all_to_all | solution.py:810
  130.9 0.8 copy-done.2
  131.7 4.2 %entity_grad.1 = (f32[200,2048]{1,0:T(8,128)}, f32[96,48]{1,0:T(8,128)}) custom-call(s32[256,1]{1,0:T(8,128)} %get-tuple-element.40.want_ref, s32[512,1]{1,0:T(8,128)} %get-tuple-element.41.srow_ref, f32[200,512]{1,0:T(8,128)} %get-tuple-element.53.own_ref, f32[200,512]{1,0:T(8,128)} %copy-done.12, bf16[16,64,200]{2,1,0:T(8,128)(2,1)} %copy-done.2), custom_call_target="tpu_custom_call" | custom-call | flops 1500000000 | bytes 4000000 | tf_op jit(solution)/shard_map/entity_grad/pallas_call | solution.py:767
  135.9 0.8 slice_bitcast_fusion
  136.7 0.6 reshape.27
  137.3 1.1 add_bitcast_fusion
  138.4 6.2 %rel_grad.1 = f32[200,1387]{1,0:T(8,128)} custom-call(s32[16,1,512]{2,1,0:T(1,128)} %copy-done.4, f32[16,200,128]{2,1,0:T(8,128)} %all-gather.5.cloned.1.call-done.sums_hbm), custom_call_target="tpu_custom_call" | custom-call | flops 2000000000 | bytes 3000000 | tf_op jit(solution)/shard_map/rel_grad/pallas_call | solution.py:726
  (38 shorter events, 0.6 us)
Async XLA Ops:
  7.2 4.1 %copy-start.10 = (s32[128]{0:T(128)S(1)}, s32[128]{0:T(128)}, u32[]{:S(2)}) copy-start(s32[128]{0:T(128)} %param.20) | copy-start | bytes 1540
  7.2 4.1 %copy-start.11 = (s32[128]{0:T(128)S(1)}, s32[128]{0:T(128)}, u32[]{:S(2)}) copy-start(s32[128]{0:T(128)} %param.19) | copy-start | bytes 1540
  7.2 4.1 %copy-start.7 = (s32[128,1]{0,1:T(1,128)S(1)}, s32[128,1]{0,1:T(1,128)}, u32[]{:S(2)}) copy-start(s32[128,1]{0,1:T(1,128)} %param.17) | copy-start | bytes 1540
  7.2 4.1 %copy-start.9 = (s32[128]{0:T(128)S(1)}, s32[128]{0:T(128)}, u32[]{:S(2)}) copy-start(s32[128]{0:T(128)} %param.18) | copy-start | bytes 1540
  7.2 59.1 %all-gather.3.cloned.1.call-start = ((), (), s32[]{:S(2)}) async-start(), calls=%async_computation.5 | async-start | bytes 3481600 | tf_op jit(solution)/shard_map/all_gather | solution.py:828
  7.3 12.1 %copy-start.6 = (bf16[48,9,9]{0,2,1:T(8,128)(2,1)S(1)}, bf16[48,9,9]{0,2,1:T(8,128)(2,1)}, u32[]{:S(2)}) copy-start(bf16[48,9,9]{0,2,1:T(8,128)(2,1)} %param.14) | copy-start | bytes 23332
  12.0 17.7 %all-to-all-start = ((s32[16,1,512]{2,1,0:T(1,128)}), s32[16,1,512]{2,1,0:T(1,128)S(1)}, u32[]{:S(2)}, u32[]{:S(2)}) async-start(s32[16,1,512]{2,1,0:T(1,128)} %broadcast_in_dim.9), calls=%async_computation | async-start | bytes 65536 | tf_op jit(solution)/shard_map/all_to_all | solution.py:810
  25.3 13.6 %copy-start.8 = (s32[400]{0:T(512)S(1)}, s32[400]{0:T(512)}, u32[]{:S(2)}) copy-start(s32[400]{0:T(512)} %param.16) | copy-start | bytes 4804
  25.3 13.7 %slice-start = ((s32[400]{0:T(512)}), s32[96]{0:T(128)S(1)}, s32[]{:S(2)}) async-start(s32[400]{0:T(512)} %param.16), calls=%async_computation.7 | async-start | bytes 1024 | tf_op jit(solution)/shard_map/slice | solution.py:837
  29.7 0.6 copy-start.4
  32.9 16.1 %all-to-all-start.1 = ((bf16[16,16,200]{2,1,0:T(8,128)(2,1)}), bf16[16,16,200]{2,1,0:T(8,128)(2,1)S(1)}, u32[]{:S(2)}, u32[]{:S(2)}) async-start(bf16[16,16,200]{2,1,0:T(8,128)(2,1)} %get-tuple-element.45), calls=%async_computation.1 | async-start | bytes 262144 | tf_op jit(solution)/shard_map/all_to_all | solution.py:810
  49.0 0.7 copy-start.5
  62.5 25.0 %all-to-all-start.2 = ((bf16[8,2,200,128]{3,2,1,0:T(8,128)(2,1)}), bf16[8,2,200,128]{3,2,1,0:T(8,128)(2,1)S(1)}, u32[]{:S(2)}, u32[]{:S(2)}) async-start(bf16[8,2,200,128]{3,2,1,0:T(8,128)(2,1)} %get-tuple-element.51), calls=%async_computation.2 | async-start | bytes 1638400 | tf_op jit(solution)/shard_map/all_to_all | solution.py:814
  66.0 72.4 %all-gather.5.cloned.1.call-start = ((), (), s32[]{:S(2)}) async-start(), calls=%async_computation.6 | async-start | bytes 1740800 | tf_op jit(solution)/shard_map/all_gather | solution.py:847
  87.5 12.7 %copy-start = (bf16[8,2,200,128]{3,2,1,0:T(8,128)(2,1)}, bf16[8,2,200,128]{3,2,1,0:T(8,128)(2,1)S(1)}, u32[]{:S(2)}) copy-start(bf16[8,2,200,128]{3,2,1,0:T(8,128)(2,1)S(1)} %all-to-all-done.2.vecs_ref) | copy-start | bytes 2457604
  87.5 19.0 %all-to-all-start.3 = ((bf16[8,200,128]{2,1,0:T(8,128)(2,1)}), bf16[8,200,128]{2,1,0:T(8,128)(2,1)S(1)}, u32[]{:S(2)}, u32[]{:S(2)}) async-start(bf16[8,200,128]{2,1,0:T(8,128)(2,1)} %get-tuple-element.58), calls=%async_computation.3 | async-start | bytes 819200 | tf_op jit(solution)/shard_map/all_to_all | solution.py:814
  106.5 3.8 %copy-start.3 = (bf16[8,200,128]{2,1,0:T(8,128)(2,1)}, bf16[8,200,128]{2,1,0:T(8,128)(2,1)S(1)}, u32[]{:S(2)}) copy-start(bf16[8,200,128]{2,1,0:T(8,128)(2,1)S(1)} %all-to-all-done.3.grads_ref) | copy-start | bytes 1228804
  106.5 24.3 %all-to-all-start.4 = ((bf16[16,64,200]{2,1,0:T(8,128)(2,1)}), bf16[16,64,200]{2,1,0:T(8,128)(2,1)S(1)}, u32[]{:S(2)}, u32[]{:S(2)}) async-start(bf16[16,64,200]{2,1,0:T(8,128)(2,1)} %filter_sums.1), calls=%async_computation.4 | async-start | bytes 1048576 | tf_op jit(solution)/shard_map/all_to_all | solution.py:810
  119.8 17.5 %collective-permute-start.1 = (f32[200,1200]{1,0:T(8,128)}, f32[200,1200]{1,0:T(8,128)S(1)}, u32[]{:S(2)}, u32[]{:S(2)}) collective-permute-start(f32[200,1200]{1,0:T(8,128)} %get-tuple-element.65), channel_id=1, source_target_pairs={{0,1},{1,0},{2,3},{3,2},{4,5},{5,4},{6,7},{7,6},{8,9},{9,8},{10,11... | collective-permute-start | bytes 2880008 | tf_op jit(solution)/shard_map/ppermute | solution.py:807
  124.8 2.0 %collective-permute-start = (f32[200,512]{1,0:T(8,128)}, f32[200,512]{1,0:T(8,128)S(1)}, u32[]{:S(2)}, u32[]{:S(2)}) collective-permute-start(f32[200,512]{1,0:T(8,128)} %get-tuple-element.54), channel_id=1, source_target_pairs={{0,1},{1,0},{2,3},{3,2},{4,5},{5,4},{6,7},{7,6},{8,9},{9,8},{10,11... | collective-permute-start | bytes 1228808 | tf_op jit(solution)/shard_map/ppermute | solution.py:807
  126.8 4.0 %copy-start.12 = (f32[200,512]{1,0:T(8,128)}, f32[200,512]{1,0:T(8,128)S(1)}, u32[]{:S(2)}) copy-start(f32[200,512]{1,0:T(8,128)S(1)} %collective-permute-done.recv_ref) | copy-start | bytes 1228804
  130.8 0.8 copy-start.2
  131.7 5.7 %copy-start.1 = (f32[200,1200]{1,0:T(8,128)S(1)}, f32[200,1200]{1,0:T(8,128)}, u32[]{:S(2)}) copy-start(f32[200,1200]{1,0:T(8,128)} %get-tuple-element.64) | copy-start | bytes 2880004
Sparse Core Ops, SparseCore 0:
  11.4 49.7 all-gather.2
  84.1 47.7 all-gather.4

commit v10 on v9

--- a/solution.py
+++ b/solution.py
@@ -154,24 +154,31 @@
     return jnp.concatenate(found, axis=0).astype(i32) - 1
 
 
-def pack_kernel(me_ref, owner_ref, row_ref, table_ref, tails_t_ref, srow_ref, picks):
+def pack_kernel(me_ref, owner_ref, row_ref, table_hbm, tails_t_ref, srow_ref, picks, table, sem):
+    copy = pltpu.make_async_copy(table_hbm, table, sem)
+    copy.start()
     cap = srow_ref.shape[0]
     srow = slot_values(owner_ref[...], me_ref[0], row_ref[...], cap)
     srow_ref[...] = srow
     fill_picks(picks, srow)
-    tails_t_ref[0] = mm(table_ref[...], picks[...], NT).astype(bf16)
+    copy.wait()
+    tails_t_ref[0] = mm(table[...], picks[...], NT).astype(bf16)
 
 
 def pack_tails(me, tail_owners, tail_row, table_t, cap):
     assert tail_row.shape[0] % 128 == 0
     return pl.pallas_call(
         pack_kernel,
-        in_specs=[SMEM] + [VMEM] * 3,
+        in_specs=[SMEM, VMEM, VMEM, pl.BlockSpec(memory_space=pl.ANY)],
         out_shape=[
             jax.ShapeDtypeStruct((1, table_t.shape[0], cap), bf16),
             jax.ShapeDtypeStruct((cap, 1), i32),
         ],
-        scratch_shapes=[pltpu.VMEM((cap, table_t.shape[1]), bf16)],
+        scratch_shapes=[
+            pltpu.VMEM((cap, table_t.shape[1]), bf16),
+            pltpu.VMEM(table_t.shape, bf16),
+            pltpu.SemaphoreType.DMA,
+        ],
         compiler_params=params(),
         cost_estimate=cost(1e9, 2e6),
         name="pack_tails",
@@ -219,12 +226,26 @@
     )(me, table_t, numbers)
 
 
-def slots_kernel(me_ref, owner_ref, row_ref, pos_ref, cand_ref, out_ref):
-    cap = cand_ref.shape[1]
+def cand_kernel(me_ref, owner_ref, out_ref):
+    cap = out_ref.shape[1]
     owner = owner_ref[...]
     index = iota(owner.shape, 0) * 128 + iota(owner.shape, 1)
     for k in range(2):
-        cand_ref[k] = slot_values(owner, me_ref[0] ^ k, index, cap)
+        out_ref[k] = slot_values(owner, me_ref[0] ^ k, index, cap)
+
+
+def slot_cands(me, tail_owners, cap):
+    return pl.pallas_call(
+        cand_kernel,
+        in_specs=[SMEM, VMEM],
+        out_shape=jax.ShapeDtypeStruct((2, cap, 1), i32),
+        compiler_params=params(),
+        cost_estimate=cost(1e8, 1e6),
+        name="slot_cands",
+    )(me, tail_owners.reshape(-1, 128))
+
+
+def pos_kernel(cap, row_ref, pos_ref, out_ref):
     queries = pos_ref.shape[1]
     eye = iota((queries, queries), 0) == iota((queries, queries), 1)
     row = pos_ref[...].astype(f32)
@@ -243,18 +264,14 @@
     out_ref[...] = owner * cap + ahead
 
 
-def slot_tables(me, tail_owners, pos_index, cap):
-    return pl.pallas_call(
-        slots_kernel,
-        in_specs=[SMEM] + [VMEM] * 3,
-        out_shape=[
-            jax.ShapeDtypeStruct((2, cap, 1), i32),
-            jax.ShapeDtypeStruct((pos_index.shape[0], 1), i32),
-        ],
+def pos_slots(tail_owners, pos_index, cap):
+    return pl.pallas_call(
+        functools.partial(pos_kernel, cap),
+        out_shape=jax.ShapeDtypeStruct((pos_index.shape[0], 1), i32),
         compiler_params=params(),
-        cost_estimate=cost(1e9, 1e6),
-        name="slot_tables",
-    )(me, tail_owners.reshape(-1, 128), tail_owners.reshape(1, -1), pos_index.reshape(1, -1))
+        cost_estimate=cost(1e8, 1e5),
+        name="pos_slots",
+    )(tail_owners.reshape(1, -1), pos_index.reshape(1, -1))
 
 
 def slot_picks(cap, slots, orow):
@@ -359,9 +376,9 @@
 
 
 def middle_kernel(
-    cap, cand, pos_ref, qv_ref, orow_ref, ext_ref, bandt_hbm, tails_hbm, w_hbm, slope_hbm,
-    out_ref, sums_ref, qgt_ref, fgrad_hbm,
-    bandt, tails, w, slope, fgrad, scores, grads, spread, ext, linear,
+    cand, pos_ref, qv_ref, ext_ref, bandt_hbm, tails_hbm, w_hbm, slope_hbm,
+    ext, sums_ref, qgt_ref, fgrad_hbm,
+    bandt, tails, w, slope, fgrad, scores, grads, spread, linear,
     band_sem, tail_sems, w_sems, slope_sems, out_sems,
 ):
     owners, width, slots = tails.shape
@@ -437,22 +454,14 @@
     ext[...] = jnp.zeros_like(ext)
     for g in range(GROUPS):
         ext[g * BAND_OUT : g * BAND_OUT + LANES, :] += spread[:, g * queries : (g + 1) * queries]
-    entry = iota((width, ext.shape[0]), 0)
     high, low = split(ext[...])
-    hpick = onehot(entry == ext_ref[...])
-    rpick = onehot(entry + width == ext_ref[...])
-    hgrad = (mm(hpick, high) + mm(hpick, low)).astype(bf16)
+    rpick = onehot(iota((width, ext.shape[0]), 0) + width == ext_ref[...])
     sums_ref[0] = mm(rpick, high) + mm(rpick, low)
-    count = out_ref.shape[0]
-    pick = slot_picks(cap, count * cap, orow_ref[...])
-    rows = mm(pick, hgrad, NT).astype(bf16)
-    for d in range(count):
-        out_ref[d] = rows[d * cap : (d + 1) * cap, :]
     for k in range(steps):
         out_copy(k).wait()
 
 
-def middle(pos, qv, orow, ext, band_t, tails, weight_t, slope, cand, cap, copies):
+def middle(pos, qv, ext, band_t, tails, weight_t, slope, cand, copies):
     queries, width = qv.shape
     owners, _, slots = tails.shape
     flat = weight_t.shape[1]
@@ -465,11 +474,11 @@
     ring = min(owners, 4)
     hbm = pl.BlockSpec(memory_space=pl.ANY)
     return pl.pallas_call(
-        functools.partial(middle_kernel, cap, cand),
-        in_specs=[VMEM] * 4 + [hbm] * 4,
+        functools.partial(middle_kernel, cand),
+        in_specs=[VMEM] * 3 + [hbm] * 4,
         out_specs=[VMEM] * 3 + [hbm],
         out_shape=[
-            jax.ShapeDtypeStruct((owners, cap, width), bf16),
+            jax.ShapeDtypeStruct((ext.shape[1], queries), f32),
             jax.ShapeDtypeStruct((1, width, queries), f32),
             jax.ShapeDtypeStruct((copies, width, queries), bf16),
             jax.ShapeDtypeStruct((filts * BAND_OUT, GROUPS * queries), bf16),
@@ -483,7 +492,6 @@
             pltpu.VMEM((ring, queries, slots), f32),
             pltpu.VMEM((ring, queries, slots), bf16),
             pltpu.VMEM((LANES, GROUPS * queries), f32),
-            pltpu.VMEM((ext.shape[1], queries), f32),
             pltpu.VMEM((2, cols, queries), f32),
             pltpu.SemaphoreType.DMA,
             pltpu.SemaphoreType.DMA((owners // blocks,)),
@@ -494,14 +502,16 @@
         compiler_params=params(),
         cost_estimate=cost(6e9, 2.5e7, 5e5),
         name="middle",
-    )(pos, qv, orow, ext, band_t, tails, weight_t, slope)
+    )(pos, qv, ext, band_t, tails, weight_t, slope)
 
 
 def half_taps(taps):
     return -(-taps // 32) * 16
 
 
-def diag_kernel(taps, codes_ref, fgrad_ref, img_ref, rows_ref, out_ref, corr_ref):
+def diag_kernel(
+    cap, taps, codes_ref, orow_ref, ext_ref, spread_ref, fgrad_ref, img_ref, out_ref, corr_ref
+):
     s = pl.program_id(0)
     units = fgrad_ref.shape[0] // BAND_OUT
     part = mm(fgrad_ref[...], img_ref[...], NT)
@@ -509,20 +519,26 @@
 
     @pl.when(s == pl.num_programs(0) - 1)
     def _():
-        diag_sums(taps, codes_ref, corr_ref, rows_ref, out_ref)
-
-
-def diag_sums(taps, codes_ref, corr_ref, rows_ref, out_ref):
+        width = out_ref.shape[2]
+        high, low = split(spread_ref[...])
+        hpick = onehot(iota((width, spread_ref.shape[0]), 0) == ext_ref[...])
+        hgrad = (mm(hpick, high) + mm(hpick, low)).astype(bf16)
+        pick = slot_picks(cap, out_ref.shape[0] * cap, orow_ref[...])
+        rows = mm(pick, hgrad, NT).astype(bf16)
+        diag_sums(cap, taps, codes_ref, corr_ref, rows, out_ref)
+
+
+def diag_sums(cap, taps, codes_ref, corr_ref, rows, out_ref):
     filts = corr_ref.shape[0]
-    cap, width = rows_ref.shape[1:]
+    width = out_ref.shape[2]
     half = half_taps(taps)
     total = jnp.zeros((2 * half, filts), f32)
     for j in range(IMG):
-        rows = corr_ref[:, j, :]
+        line = corr_ref[:, j, :]
         for di in range(1, BAND):
-            rows = rows + pltpu.roll(corr_ref[:, di * IMG + j, :], LANES - di * IMG, 1)
+            line = line + pltpu.roll(corr_ref[:, di * IMG + j, :], LANES - di * IMG, 1)
         pick = onehot(iota((2 * half, LANES), 0) == codes_ref[j : j + 1, :])
-        high, low = split(rows)
+        high, low = split(line)
         total = total + mm(pick, high, NT) + mm(pick, low, NT)
     packed = jnp.zeros((half, width), f32)
     for k in range(2):
@@ -531,24 +547,25 @@
             packed = packed + mm(piece, place)
     packed = packed.astype(bf16)
     for d in range(out_ref.shape[0]):
-        out_ref[d, :cap, :] = rows_ref[d]
+        out_ref[d, :cap, :] = rows[d * cap : (d + 1) * cap, :]
         out_ref[d, cap:, :] = packed
 
 
-def filter_sums(fgrad, img, codes, rows, taps):
-    count, cap, width = rows.shape
+def filter_sums(fgrad, img, codes, orow, ext, spread, count, width, cap, taps):
     filts = fgrad.shape[0] // BAND_OUT
     units = filter_block(filts)
     assert 4 * filts <= width
     out = (count, cap + half_taps(taps), width)
     return pl.pallas_call(
-        functools.partial(diag_kernel, taps),
+        functools.partial(diag_kernel, cap, taps),
         grid=(filts // units,),
         in_specs=[
             whole(codes.shape),
+            whole(orow.shape),
+            whole(ext.shape),
+            whole(spread.shape),
             pl.BlockSpec((units * BAND_OUT, fgrad.shape[1]), lambda s: (s, 0)),
             whole(img.shape),
-            whole(rows.shape),
         ],
         out_specs=whole(out),
         out_shape=jax.ShapeDtypeStruct(out, bf16),
@@ -556,7 +573,7 @@
         compiler_params=params("arbitrary"),
         cost_estimate=cost(2e9, 6e6),
         name="filter_sums",
-    )(codes, fgrad, img, rows)
+    )(codes, orow, ext, spread, fgrad, img)
 
 
 def tail_kernel(
@@ -700,9 +717,7 @@
     return mm(qg, (pre * sigmoid(pre)).astype(bf16), TN)
 
 
-def rel_kernel(numbers_ref, sums_hbm, rel_ref, sums_ref, picks, sem):
-    copy = pltpu.make_async_copy(sums_hbm, sums_ref, sem)
-    copy.start()
+def rel_kernel(numbers_ref, sums_ref, rel_ref, picks):
     width, rels = rel_ref.shape
     queries = sums_ref.shape[2]
     total = None
@@ -713,8 +728,6 @@
             for r in spans(rels, 128):
                 here = iota((r.stop - r.start, queries), 0) + r.start
                 picks[r, i * queries : (i + 1) * queries] = onehot(here == rel)
-        if block.start == 0:
-            copy.wait()
         parts = jnp.concatenate(split(beside(sums_ref[p] for p in members)), axis=0)
         part = mm(parts, picks[...], NT)
         total = part if total is None else total + part
@@ -725,13 +738,8 @@
     count, width, queries = sums.shape
     return pl.pallas_call(
         rel_kernel,
-        in_specs=[VMEM, pl.BlockSpec(memory_space=pl.ANY)],
         out_shape=jax.ShapeDtypeStruct((width, rels), f32),
-        scratch_shapes=[
-            pltpu.VMEM(sums.shape, f32),
-            pltpu.VMEM((rels, math.gcd(count, 16) * queries), bf16),
-            pltpu.SemaphoreType.DMA,
-        ],
+        scratch_shapes=[pltpu.VMEM((rels, math.gcd(count, 16) * queries), bf16)],
         compiler_params=params(),
         cost_estimate=cost(2e9, 3e6),
         name="rel_grad",
@@ -826,13 +834,13 @@
     ids = jnp.stack([me, me ^ 1, me & 1])
     tails_t, slot_row = pack_tails(me1, tail_owners, tail_row, table_t, tail_cap)
     all_tails = lax.all_gather(tails_t, "shard", axis=0, tiled=True)
-    scand, pos = slot_tables(me1, tail_owners, pos_index, tail_cap)
+    scand = slot_cands(me1, tail_owners, tail_cap)
+    found, want = find_heads(me1, numbers, table_t, head_cap)
+    fetched = exchange(found)
+    pos = pos_slots(tail_owners, pos_index, tail_cap)
+
     codes = jnp.asarray(band_codes(ks))
     band, band_t = build_band(filters, codes)
-    numbers, scand, pos, band, band_t = lax.optimization_barrier((numbers, scand, pos, band, band_t))
-    found, want = find_heads(me1, numbers, table_t, head_cap)
-    fetched = exchange(found)
-
     extra = BAND_OUT * (GROUPS - 1) + LANES - IMG * IMG - BAND_OUT
     ext = jnp.concatenate([chequer_perm[-BAND_OUT:], chequer_perm, chequer_perm[:extra]])[None]
     orow = heads[None, :]
@@ -841,17 +849,18 @@
     )
     core_vecs = gather_core(vecs)
 
-    outgoing, sums, qgt, fgrad = middle(
-        pos, qv, orow, ext, band_t, all_tails, weight_t, slope, cand, head_cap, copies
+    spread, sums, qgt, fgrad = middle(
+        pos, qv, ext, band_t, all_tails, weight_t, slope, cand, copies
     )
     all_sums = lax.all_gather(sums, "shard", axis=0, tiled=True)
     qgt, core_vecs = lax.optimization_barrier((qgt, core_vecs))
     core_qgt = gather_core(qgt)
-    outgoing = filter_sums(fgrad, img, codes, outgoing, ks * ks)
-    outgoing, core_qgt = lax.optimization_barrier((outgoing, core_qgt))
+    outgoing = filter_sums(
+        fgrad, img, codes, orow, ext, spread, count, width, head_cap, ks * ks
+    )
+    own, other = tail_part(ids, all_tails, scand, numbers, core_vecs, cand)
+    outgoing, core_qgt, own, other = lax.optimization_barrier((outgoing, core_qgt, own, other))
     incoming = exchange(outgoing)
-
-    own, other = tail_part(ids, all_tails, scand, numbers, core_vecs, cand)
     entity_grad, filter_grad = entity_sum(
         want, slot_row, own, swap(other), incoming, rows, head_cap, filts
     )

time: 153 us -> 147 us (0.961)
  waiting for transfers between devices: 24.9 us -> 10.6 us
  blocking collectives: 0 us -> 13.9 us
  starting transfers between devices: 25.1 us -> 19.3 us
    all_to_all x0 -> x1, blocking collectives: none -> 13.9 us  [exchange(): return lax.all_to_all(x, 'shard', split_axis=0, concat_axis=0, tiled=True)]
    all_to_all x2, waiting for transfers between devices: 9.9 us -> 0.38 us  [gather_core(): lax.all_to_all(x, 'shard', split_axis=0, concat_axis=0, axis_index_groups...]
    all_to_all x3 -> x2, starting transfers between devices: 17.2 us -> 9.64 us  [exchange(): return lax.all_to_all(x, 'shard', split_axis=0, concat_axis=0, tiled=True)]
    all_to_all x3 -> x2, waiting for transfers between devices: 13.3 us -> 6.48 us  [exchange(): return lax.all_to_all(x, 'shard', split_axis=0, concat_axis=0, tiled=True)]
    all_to_all x2, starting transfers between devices: 7.21 us -> 8.93 us  [gather_core(): lax.all_to_all(x, 'shard', split_axis=0, concat_axis=0, axis_index_groups...]
    pallas_call x5 -> x6, Pallas kernels: 40.6 us -> 41.6 us  [the longest x1 17.5 us: middle(): pl.pallas_call(functools.partial(middle_kernel, cand), in_specs=[VMEM] *...]
  transfers between devices with their start and end apart: 9 -> 8, of which waited for: 5 -> 5; matrix products, arithmetic and copies ran while one was open for 3% -> 3% of each run, Pallas kernels for 46% -> 49%
where the time goes in v10:
time: 147 us; the launch traced here: 145 us
  Pallas kernels  81.2 us (55%)
  starting transfers between devices  19.3 us (13%)
  between operations  14.2 us (10%)
  blocking collectives  13.9 us (9%)
  waiting for transfers between devices  10.6 us (7%)
  local copies, waits for them, and re-layouts  4.35 us (3%)
  other arithmetic  1.82 us (1%)
    pallas_call x1, Pallas kernels, middle(): pl.pallas_call(functools.partial(middle_kernel, cand), in_specs=[VMEM] *...  17.5 us
    all_to_all x1, blocking collectives, exchange(): return lax.all_to_all(x, 'shard', split_axis=0, concat_axis=0, tiled=True)  13.9 us
    pallas_call x1, Pallas kernels, front(): pl.pallas_call(functools.partial(front_kernel, cap), grid=(filts // units...  13.2 us
    all_to_all x2, starting transfers between devices, exchange(): return lax.all_to_all(x, 'shard', split_axis=0, concat_axis=0, tiled=True)  9.64 us
    pallas_call x1, Pallas kernels, proj_part(): pl.pallas_call(proj_kernel, grid_spec=pltpu.PrefetchScalarGridSpec(num_sc...  9.41 us
    all_to_all x2, starting transfers between devices, gather_core(): lax.all_to_all(x, 'shard', split_axis=0, concat_axis=0, axis_index_groups...  8.93 us
    pallas_call x1, Pallas kernels, filter_sums(): pl.pallas_call(functools.partial(diag_kernel, cap, taps), grid=(filts //...  8.69 us
    all_to_all x2, waiting for transfers between devices, exchange(): return lax.all_to_all(x, 'shard', split_axis=0, concat_axis=0, tiled=True)  6.48 us
  transfers between devices with their start and end apart: 8, of which 5 were waited for; matrix products, arithmetic and copies ran while one was open for 3% of the time, Pallas kernels for 49%

profile of v10, /device:TPU:0, one launch (start us, length us, event | category | flops | bytes accessed | tf_op | source)
XLA Modules:
  0.0 145.4 jit_solution(17452901379952975164)
XLA Ops:
  7.3 3.9 %pack_tails.1 = (bf16[1,200,512]{2,1,0:T(8,128)(2,1)}, s32[512,1]{1,0:T(8,128)}) custom-call(s32[1]{0:T(128)} %bitcast.me_ref, s32[32,128]{1,0:T(8,128)} %bitcast.25, s32[32,128]{1,0:T(8,128)} %bitcast.37, bf16[200,2048]{1,0:T(8,128)(2,1)} %bitcast.33), custom_call_target="tpu_custom_call" | custom-call | flops 1000000000 | bytes 2000000 | tf_op jit(solution)/shard_map/pack_tails/pallas_call | solution.py:170
  11.3 13.9 %all_to_all.25.numbers_ref = s32[16,1,512]{2,1,0:T(1,128)} all-to-all(s32[16,1,512]{2,1,0:T(1,128)S(1)} %broadcast_in_dim.9), channel_id=1, replica_groups=mesh['parts'=2,'shard'=16] {'shard'}, dimensions={0} | all-to-all | bytes 65536 | tf_op jit(solution)/shard_map/all_to_all | solution.py:818
  25.2 2.6 %find_heads.1 = (bf16[16,16,200]{2,1,0:T(8,128)(2,1)}, s32[256,1]{1,0:T(8,128)}) custom-call(s32[1]{0:T(128)} %bitcast.me_ref, bf16[200,2048]{1,0:T(8,128)(2,1)} %bitcast.34, s32[16,1,512]{2,1,0:T(1,128)} %all_to_all.25.numbers_ref), custom_call_target="tpu_custom_call" | custom-call | flops 300000000 | bytes 2000000 | tf_op jit(solution)/shard_map/find_heads/pallas_call | solution.py:212
  27.8 3.5 %all-to-all-start.1 = ((bf16[16,16,200]{2,1,0:T(8,128)(2,1)}), bf16[16,16,200]{2,1,0:T(8,128)(2,1)S(1)}, u32[]{:S(2)}, u32[]{:S(2)}) async-start(bf16[16,16,200]{2,1,0:T(8,128)(2,1)} %get-tuple-element.32), calls=%async_computation.1 | async-start | bytes 262144 | tf_op jit(solution)/shard_map/all_to_all | solution.py:818
  31.5 0.6 broadcast_in_dim.10.ext_ref
  32.1 0.7 copy.18.filt_ref
  32.8 5.3 %band.1 = (bf16[3840,256]{1,0:T(8,128)(2,1)}, bf16[256,3840]{1,0:T(8,128)(2,1)}) custom-call(s32[20,256]{1,0:T(8,128)} %constant.8.clone.codes_ref, bf16[48,81]{1,0:T(8,128)(2,1)} %copy.18.filt_ref), custom_call_target="tpu_custom_call" | custom-call | flops 40000000 | bytes 4000000 | tf_op jit(solution)/shard_map/band/pallas_call | solution.py:94
  38.1 1.1 all-to-all-done.1.fetched_ref
  39.2 0.7 copy-done.4
  39.9 13.2 %front.1 = (f32[19200,128]{1,0:T(8,128)}, bf16[256,640]{1,0:T(8,128)(2,1)}, bf16[128,200]{1,0:T(8,128)(2,1)}, bf16[8,2,200,128]{3,2,1,0:T(8,128)(2,1)}) custom-call(bf16[16,16,200]{2,1,0:T(8,128)(2,1)} %copy-done.4, s32[1,128]{1,0:T(1,128)} %bitcast.30, s32[1,128]{1,0:T(1,128)} %bitcast.28, bf16[200,1387]{1,0:T(8,128)(2,1)} %bitcast.35, ...), custom_call_target="tpu_custom_call" | custom-call | flops 4000000000 | bytes 24000000 | tf_op jit(solution)/shard_map/front/pallas_call | solution.py:342
  53.1 4.3 %all-to-all-start.2 = ((bf16[8,2,200,128]{3,2,1,0:T(8,128)(2,1)}), bf16[8,2,200,128]{3,2,1,0:T(8,128)(2,1)S(1)}, u32[]{:S(2)}, u32[]{:S(2)}) async-start(bf16[8,2,200,128]{3,2,1,0:T(8,128)(2,1)} %get-tuple-element.42), calls=%async_computation.2 | async-start | bytes 1638400 | tf_op jit(solution)/shard_map/all_to_all | solution.py:822
  57.4 0.2 all-gather.5.cloned.1.call-start
  57.6 2.2 %pos_slots.1.pos_ref = s32[128,1]{1,0:T(8,128)} custom-call(s32[1,4096]{1,0:T(1,128)} %bitcast.26, s32[1,128]{1,0:T(1,128)} %bitcast.29), custom_call_target="tpu_custom_call" | custom-call | flops 100000000 | bytes 100000 | tf_op jit(solution)/shard_map/pos_slots/pallas_call | solution.py:268
  59.8 0.8 all-gather.3.cloned.1.call-done.tails_hbm.tails_ref.mate_ref
  60.6 17.5 %middle.1 = (f32[576,128]{1,0:T(8,128)}, f32[1,200,128]{2,1,0:T(8,128)}, bf16[8,200,128]{2,1,0:T(8,128)(2,1)}, bf16[3840,640]{1,0:T(8,128)(2,1)}) custom-call(s32[128,1]{1,0:T(8,128)} %pos_slots.1.pos_ref, bf16[128,200]{1,0:T(8,128)(2,1)} %get-tuple-element.34.qv_ref, s32[1,576]{1,0:T(1,128)} %broadcast_in_dim.10.ext_ref, ...), custom_call_target="tpu_custom_call" | custom-call | flops 6000000000 | bytes 25000000 | tf_op jit(solution)/shard_map/middle/pallas_call | solution.py:476
  78.2 0.4 all-to-all-done.2.vecs_ref
  78.6 4.6 %all-to-all-start.3 = ((bf16[8,200,128]{2,1,0:T(8,128)(2,1)}), bf16[8,200,128]{2,1,0:T(8,128)(2,1)S(1)}, u32[]{:S(2)}, u32[]{:S(2)}) async-start(bf16[8,200,128]{2,1,0:T(8,128)(2,1)} %get-tuple-element.43), calls=%async_computation.3 | async-start | bytes 819200 | tf_op jit(solution)/shard_map/all_to_all | solution.py:822
  83.2 3.8 %slot_cands.1.scand_ref = s32[2,512,1]{2,1,0:T(8,128)} custom-call(s32[1]{0:T(128)} %bitcast.me_ref, s32[32,128]{1,0:T(8,128)} %bitcast.27), custom_call_target="tpu_custom_call" | custom-call | flops 100000000 | bytes 1000000 | tf_op jit(solution)/shard_map/slot_cands/pallas_call | solution.py:238
  87.0 0.7 pad_add_fusion.2.ids_ref
  87.7 8.7 %filter_sums.1 = bf16[16,64,200]{2,1,0:T(8,128)(2,1)} custom-call(s32[20,256]{1,0:T(8,128)} %constant.8.clone.codes_ref, s32[1,128]{1,0:T(1,128)} %bitcast.31, s32[1,576]{1,0:T(1,128)} %broadcast_in_dim.10.ext_ref, f32[576,128]{1,0:T(8,128)} %get-tuple-element.38.spread_ref, bf16[3840,640]{1,0:T(8,128)(2,1)} %get-tuple-element.39.fgrad_ref, ...), custom_call_target="tpu_custom_call" | custom-call | flops 2000000000 | bytes 6000000 | tf_op jit(solution)/shard_map/filter_sums/pallas_call | solution.py:559
  96.4 4.9 %tail_grad.1 = (f32[200,512]{1,0:T(8,128)}, f32[200,512]{1,0:T(8,128)}) custom-call(s32[3]{0:T(128)} %pad_add_fusion.2.ids_ref, bf16[16,200,512]{2,1,0:T(8,128)(2,1)} %all-gather.3.cloned.1.call-done.tails_hbm.tails_ref.mate_ref, bf16[16,200,512]{2,1,0:T(8,128)(2,1)} %all-gather.3.cloned.1.call-done.tails_hbm.tails_ref.mate_ref, ...), custom_call_target="tpu_custom_call" | custom-call | flops 2000000000 | bytes 3000000 | tf_op jit(solution)/shard_map/tail_grad/pallas_call | solution.py:604
  101.3 6.1 %all-to-all-start.4 = ((bf16[16,64,200]{2,1,0:T(8,128)(2,1)}), bf16[16,64,200]{2,1,0:T(8,128)(2,1)S(1)}, u32[]{:S(2)}, u32[]{:S(2)}) async-start(bf16[16,64,200]{2,1,0:T(8,128)(2,1)} %filter_sums.1), calls=%async_computation.4 | async-start | bytes 1048576 | tf_op jit(solution)/shard_map/all_to_all | solution.py:818
  107.5 9.4 %proj_grad.1 = (f32[200,1200]{1,0:T(8,128)}, f32[200,1200]{1,0:T(8,128)}) custom-call(s32[3]{0:T(128)} %pad_add_fusion.2.ids_ref, bf16[200,1387]{1,0:T(8,128)(2,1)} %bitcast.36, s32[1,576]{1,0:T(1,128)} %broadcast_in_dim.10.ext_ref, bf16[3840,256]{1,0:T(8,128)(2,1)} %get-tuple-element.33.band_ref.mate_ref, ...), custom_call_target="tpu_custom_call" | custom-call | flops 6000000000 | bytes 6000000 | tf_op jit(solution)/shard_map/proj_grad/pallas_call | solution.py:668
  116.9 0.4 collective-permute-start.1
  117.4 2.8 %collective-permute-done.recv_ref = f32[200,512]{1,0:T(8,128)S(1)} collective-permute-done((f32[200,512]{1,0:T(8,128)S(1)}, f32[200,512]{1,0:T(8,128)S(1)}, u32[]{:S(2)}, u32[]{:S(2)}) %collective-permute-start) | collective-permute-done | bytes 409632 | tf_op jit(solution)/shard_map/ppermute | solution.py:815
  120.2 5.3 %all-to-all-done.4.incoming_ref = bf16[16,64,200]{2,1,0:T(8,128)(2,1)S(1)} async-done(((bf16[16,64,200]{2,1,0:T(8,128)(2,1)}), bf16[16,64,200]{2,1,0:T(8,128)(2,1)S(1)}, u32[]{:S(2)}, u32[]{:S(2)}) %all-to-all-start.4) | async-done | bytes 409632 | tf_op jit(solution)/shard_map/all_to_all | solution.py:818
  125.6 0.8 copy-done.2
  126.4 4.2 %entity_grad.1 = (f32[200,2048]{1,0:T(8,128)}, f32[96,48]{1,0:T(8,128)}) custom-call(s32[256,1]{1,0:T(8,128)} %get-tuple-element.30.want_ref, s32[512,1]{1,0:T(8,128)} %get-tuple-element.31.srow_ref, f32[200,512]{1,0:T(8,128)} %get-tuple-element.47.own_ref, f32[200,512]{1,0:T(8,128)} %copy-done.12, bf16[16,64,200]{2,1,0:T(8,128)(2,1)} %copy-done.2), custom_call_target="tpu_custom_call" | custom-call | flops 1500000000 | bytes 4000000 | tf_op jit(solution)/shard_map/entity_grad/pallas_call | solution.py:775
  130.6 0.8 slice_bitcast_fusion
  131.4 0.6 reshape.27
  132.1 1.1 add_bitcast_fusion
  133.1 5.4 %rel_grad.1 = f32[200,1387]{1,0:T(8,128)} custom-call(s32[16,1,512]{2,1,0:T(1,128)} %all_to_all.25.numbers_ref, f32[16,200,128]{2,1,0:T(8,128)} %all-gather.5.cloned.1.call-done.sums_ref), custom_call_target="tpu_custom_call" | custom-call | flops 2000000000 | bytes 3000000 | tf_op jit(solution)/shard_map/rel_grad/pallas_call | solution.py:739
  (38 shorter events, 0.4 us)
Async XLA Ops:
  7.2 4.1 %copy-start.9 = (s32[128]{0:T(128)S(1)}, s32[128]{0:T(128)}, u32[]{:S(2)}) copy-start(s32[128]{0:T(128)} %param.20) | copy-start | bytes 1540
  7.2 4.1 %copy-start.8 = (s32[128]{0:T(128)S(1)}, s32[128]{0:T(128)}, u32[]{:S(2)}) copy-start(s32[128]{0:T(128)} %param.19) | copy-start | bytes 1540
  7.2 4.1 %copy-start.7 = (s32[128]{0:T(128)S(1)}, s32[128]{0:T(128)}, u32[]{:S(2)}) copy-start(s32[128]{0:T(128)} %param.18) | copy-start | bytes 1540
  7.2 4.1 %copy-start.10 = (s32[128,1]{0,1:T(1,128)S(1)}, s32[128,1]{0,1:T(1,128)}, u32[]{:S(2)}) copy-start(s32[128,1]{0,1:T(1,128)} %param.17) | copy-start | bytes 1540
  7.2 53.4 %all-gather.3.cloned.1.call-start = ((), (), s32[]{:S(2)}) async-start(), calls=%async_computation.5 | async-start | bytes 3481600 | tf_op jit(solution)/shard_map/all_gather | solution.py:836
  7.3 24.1 %copy-start.6 = (s32[400]{0:T(512)S(1)}, s32[400]{0:T(512)}, u32[]{:S(2)}) copy-start(s32[400]{0:T(512)} %param.16) | copy-start | bytes 4804
  7.3 24.1 %slice-start = ((s32[400]{0:T(512)}), s32[96]{0:T(128)S(1)}, s32[]{:S(2)}) async-start(s32[400]{0:T(512)} %param.16), calls=%async_computation.7 | async-start | bytes 1024 | tf_op jit(solution)/shard_map/slice | solution.py:845
  7.3 24.8 %copy-start.5 = (bf16[48,9,9]{0,2,1:T(8,128)(2,1)S(1)}, bf16[48,9,9]{0,2,1:T(8,128)(2,1)}, u32[]{:S(2)}) copy-start(bf16[48,9,9]{0,2,1:T(8,128)(2,1)} %param.14) | copy-start | bytes 23332
  27.8 11.4 %all-to-all-start.1 = ((bf16[16,16,200]{2,1,0:T(8,128)(2,1)}), bf16[16,16,200]{2,1,0:T(8,128)(2,1)S(1)}, u32[]{:S(2)}, u32[]{:S(2)}) async-start(bf16[16,16,200]{2,1,0:T(8,128)(2,1)} %get-tuple-element.32), calls=%async_computation.1 | async-start | bytes 262144 | tf_op jit(solution)/shard_map/all_to_all | solution.py:818
  39.2 0.7 copy-start.4
  53.1 25.5 %all-to-all-start.2 = ((bf16[8,2,200,128]{3,2,1,0:T(8,128)(2,1)}), bf16[8,2,200,128]{3,2,1,0:T(8,128)(2,1)S(1)}, u32[]{:S(2)}, u32[]{:S(2)}) async-start(bf16[8,2,200,128]{3,2,1,0:T(8,128)(2,1)} %get-tuple-element.42), calls=%async_computation.2 | async-start | bytes 1638400 | tf_op jit(solution)/shard_map/all_to_all | solution.py:822
  57.4 75.7 %all-gather.5.cloned.1.call-start = ((), (), s32[]{:S(2)}) async-start(), calls=%async_computation.6 | async-start | bytes 1740800 | tf_op jit(solution)/shard_map/all_gather | solution.py:855
  78.6 17.8 %copy-start = (bf16[8,2,200,128]{3,2,1,0:T(8,128)(2,1)}, bf16[8,2,200,128]{3,2,1,0:T(8,128)(2,1)S(1)}, u32[]{:S(2)}) copy-start(bf16[8,2,200,128]{3,2,1,0:T(8,128)(2,1)S(1)} %all-to-all-done.2.vecs_ref) | copy-start | bytes 2457604
  78.6 22.7 %all-to-all-start.3 = ((bf16[8,200,128]{2,1,0:T(8,128)(2,1)}), bf16[8,200,128]{2,1,0:T(8,128)(2,1)S(1)}, u32[]{:S(2)}, u32[]{:S(2)}) async-start(bf16[8,200,128]{2,1,0:T(8,128)(2,1)} %get-tuple-element.43), calls=%async_computation.3 | async-start | bytes 819200 | tf_op jit(solution)/shard_map/all_to_all | solution.py:822
  101.3 6.1 %copy-start.3 = (bf16[8,200,128]{2,1,0:T(8,128)(2,1)}, bf16[8,200,128]{2,1,0:T(8,128)(2,1)S(1)}, u32[]{:S(2)}) copy-start(bf16[8,200,128]{2,1,0:T(8,128)(2,1)S(1)} %all-to-all-done.3.grads_ref) | copy-start | bytes 1228804
  101.3 24.3 %all-to-all-start.4 = ((bf16[16,64,200]{2,1,0:T(8,128)(2,1)}), bf16[16,64,200]{2,1,0:T(8,128)(2,1)S(1)}, u32[]{:S(2)}, u32[]{:S(2)}) async-start(bf16[16,64,200]{2,1,0:T(8,128)(2,1)} %filter_sums.1), calls=%async_computation.4 | async-start | bytes 1048576 | tf_op jit(solution)/shard_map/all_to_all | solution.py:818
  107.4 9.8 %copy-start.11 = (f32[200,512]{1,0:T(8,128)S(1)}, f32[200,512]{1,0:T(8,128)}, u32[]{:S(2)}) copy-start(f32[200,512]{1,0:T(8,128)} %get-tuple-element.48) | copy-start | bytes 1228804
  116.9 15.2 %collective-permute-start.1 = (f32[200,1200]{1,0:T(8,128)}, f32[200,1200]{1,0:T(8,128)S(1)}, u32[]{:S(2)}, u32[]{:S(2)}) collective-permute-start(f32[200,1200]{1,0:T(8,128)} %get-tuple-element.55), channel_id=1, source_target_pairs={{0,1},{1,0},{2,3},{3,2},{4,5},{5,4},{6,7},{7,6},{8,9},{9,8},{10,11... | collective-permute-start | bytes 2880008 | tf_op jit(solution)/shard_map/ppermute | solution.py:815
  117.3 2.9 %collective-permute-start = (f32[200,512]{1,0:T(8,128)S(1)}, f32[200,512]{1,0:T(8,128)S(1)}, u32[]{:S(2)}, u32[]{:S(2)}) collective-permute-start(f32[200,512]{1,0:T(8,128)S(1)} %copy-done.11), channel_id=1, source_target_pairs={{0,1},{1,0},{2,3},{3,2},{4,5},{5,4},{6,7},{7,6},{8,9},{9,8},{10,11... | collective-permute-start | bytes 1228808 | tf_op jit(solution)/shard_map/ppermute | solution.py:815
  120.2 5.3 %copy-start.12 = (f32[200,512]{1,0:T(8,128)}, f32[200,512]{1,0:T(8,128)S(1)}, u32[]{:S(2)}) copy-start(f32[200,512]{1,0:T(8,128)S(1)} %collective-permute-done.recv_ref) | copy-start | bytes 1228804
  125.6 0.8 copy-start.2
  126.4 5.7 %copy-start.1 = (f32[200,1200]{1,0:T(8,128)S(1)}, f32[200,1200]{1,0:T(8,128)}, u32[]{:S(2)}) copy-start(f32[200,1200]{1,0:T(8,128)} %get-tuple-element.54) | copy-start | bytes 2880004
Sparse Core Ops, SparseCore 0:
  11.4 49.2 all-gather.2
  78.3 47.1 all-gather.4

commit v11 on v10

--- a/solution.py
+++ b/solution.py
@@ -746,42 +746,79 @@
     )(numbers, sums)
 
 
-def entity_kernel(cap, want_ref, srow_ref, own_ref, recv_ref, incoming_ref, out_ref, filt_ref):
-    rows = out_ref.shape[1]
+def owned_kernel(srow_ref, own_ref, recv_ref, out_ref, parts):
+    slots = srow_ref.shape[0]
+    width, lanes = out_ref.shape
+    s = pl.program_id(0)
+
+    @pl.when(s == 0)
+    def _():
+        parts[:width, :], parts[width:, :] = split(own_ref[...] + recv_ref[...])
+
+    here = iota((slots, lanes), 1) + s * lanes
+    total = mm(parts[...], onehot(here == srow_ref[...]))
+    out_ref[...] = total[:width, :] + total[width:, :]
+
+
+def owned_sum(srow, own, recv, rows):
+    width, slots = own.shape
+    lanes = math.gcd(rows, 512)
+    return pl.pallas_call(
+        owned_kernel,
+        grid=(rows // lanes,),
+        in_specs=[whole(srow.shape), whole(own.shape), whole(recv.shape)],
+        out_specs=pl.BlockSpec((width, lanes), lambda s: (0, s)),
+        out_shape=jax.ShapeDtypeStruct((width, rows), f32),
+        scratch_shapes=[pltpu.VMEM((2 * width, slots), bf16)],
+        compiler_params=params("arbitrary"),
+        cost_estimate=cost(1.5e9, 4e6),
+        name="owned_grad",
+    )(srow, own, recv)
+
+
+def entity_kernel(cap, want_ref, incoming_ref, base_ref, out_ref, filt_ref, turned):
+    lanes = out_ref.shape[1]
     count, _, width = incoming_ref.shape
     half, filts = filt_ref.shape[0] // 2, filt_ref.shape[1]
-    grads = jnp.concatenate([incoming_ref[d, :cap, :] for d in range(count)], axis=0)
-    turned = grads.astype(f32).T.astype(bf16)
-    high, low = split(own_ref[...] + recv_ref[...])
-    for c in spans(rows, 256):
-        here = iota((want_ref.shape[0], c.stop - c.start), 1) + c.start
-        total = mm(turned, onehot(here == want_ref[...]))
-        here = iota((srow_ref.shape[0], c.stop - c.start), 1) + c.start
-        pick = onehot(here == srow_ref[...])
-        out_ref[:, c] = total + mm(high, pick) + mm(low, pick)
-    packed = incoming_ref[0, cap:, :].astype(f32)
-    for d in range(1, count):
-        packed = packed + incoming_ref[d, cap:, :].astype(f32)
-    high, low = split(packed)
-    for k in range(2):
-        lane = iota((width, filts), 0) - 2 * k * filts
-        unit = iota((width, filts), 1)
-        place = onehot((lane == unit) | (lane == unit + filts))
-        filt_ref[k * half : (k + 1) * half, :] = mm(high, place) + mm(low, place)
-
-
-def entity_sum(want, srow, own, recv, incoming, rows, cap, filts):
+    s = pl.program_id(0)
+
+    @pl.when(s == 0)
+    def _():
+        grads = jnp.concatenate([incoming_ref[d, :cap, :] for d in range(count)], axis=0)
+        turned[...] = grads.astype(f32).T.astype(bf16)
+        packed = incoming_ref[0, cap:, :].astype(f32)
+        for d in range(1, count):
+            packed = packed + incoming_ref[d, cap:, :].astype(f32)
+        high, low = split(packed)
+        for k in range(2):
+            lane = iota((width, filts), 0) - 2 * k * filts
+            unit = iota((width, filts), 1)
+            place = onehot((lane == unit) | (lane == unit + filts))
+            filt_ref[k * half : (k + 1) * half, :] = mm(high, place) + mm(low, place)
+
+    here = iota((want_ref.shape[0], lanes), 1) + s * lanes
+    out_ref[...] = base_ref[...] + mm(turned[...], onehot(here == want_ref[...]))
+
+
+def entity_sum(want, incoming, base, cap, filts):
     half = incoming.shape[1] - cap
+    width, rows = base.shape
+    lanes = math.gcd(rows, 512)
+    block = pl.BlockSpec((width, lanes), lambda s: (0, s))
     return pl.pallas_call(
         functools.partial(entity_kernel, cap),
+        grid=(rows // lanes,),
+        in_specs=[whole(want.shape), whole(incoming.shape), block],
+        out_specs=[block, whole((2 * half, filts))],
         out_shape=[
-            jax.ShapeDtypeStruct((own.shape[0], rows), f32),
+            jax.ShapeDtypeStruct(base.shape, f32),
             jax.ShapeDtypeStruct((2 * half, filts), f32),
         ],
-        compiler_params=params(),
-        cost_estimate=cost(1.5e9, 4e6),
+        scratch_shapes=[pltpu.VMEM((width, want.shape[0]), bf16)],
+        compiler_params=params("arbitrary"),
+        cost_estimate=cost(1e9, 4e6),
         name="entity_grad",
-    )(want, srow, own, recv, incoming)
+    )(want, incoming, base)
 
 
 def shards(
@@ -858,12 +895,12 @@
     outgoing = filter_sums(
         fgrad, img, codes, orow, ext, spread, count, width, head_cap, ks * ks
     )
+    outgoing, core_qgt, scand = lax.optimization_barrier((outgoing, core_qgt, scand))
+    incoming = exchange(outgoing)
     own, other = tail_part(ids, all_tails, scand, numbers, core_vecs, cand)
-    outgoing, core_qgt, own, other = lax.optimization_barrier((outgoing, core_qgt, own, other))
-    incoming = exchange(outgoing)
-    entity_grad, filter_grad = entity_sum(
-        want, slot_row, own, swap(other), incoming, rows, head_cap, filts
-    )
+    core_qgt, own, other = lax.optimization_barrier((core_qgt, own, other))
+    base = owned_sum(slot_row, own, swap(other), rows)
+    entity_grad, filter_grad = entity_sum(want, incoming, base, head_cap, filts)
     filter_grad = filter_grad[: ks * ks].T.reshape(filts, ks, ks)
 
     cols = filts * IMG * IMG // count

time: 147 us -> 146 us (level)
  Pallas kernels: 81.2 us -> 85.7 us
  waiting for transfers between devices: 10.6 us -> 6.26 us
    all_to_all x2, waiting for transfers between devices: 6.48 us -> 1.15 us  [exchange(): return lax.all_to_all(x, 'shard', split_axis=0, concat_axis=0, tiled=True)]
    pallas_call x1 -> x2, Pallas kernels: 4.24 us -> 8.73 us  [the longest x1 4.51 us: entity_sum(): pl.pallas_call(functools.partial(entity_kernel, cap), grid=(rows // lanes...]
  transfers between devices with their start and end apart: 8 -> 8, of which waited for: 5 -> 5; matrix products, arithmetic and copies ran while one was open for 3% -> 3% of each run, Pallas kernels for 49% -> 53%
where the time goes in v11:
time: 146 us; the launch traced here: 145 us
  Pallas kernels  85.7 us (59%)
  starting transfers between devices  18.2 us (12%)
  between operations  14.2 us (10%)
  blocking collectives  13.9 us (10%)
  waiting for transfers between devices  6.26 us (4%)
  local copies, waits for them, and re-layouts  5.08 us (3%)
  other arithmetic  1.79 us (1%)
    pallas_call x1, Pallas kernels, middle(): pl.pallas_call(functools.partial(middle_kernel, cand), in_specs=[VMEM] *...  17.5 us
    all_to_all x1, blocking collectives, exchange(): return lax.all_to_all(x, 'shard', split_axis=0, concat_axis=0, tiled=True)  13.9 us
    pallas_call x1, Pallas kernels, front(): pl.pallas_call(functools.partial(front_kernel, cap), grid=(filts // units...  13.2 us
    pallas_call x1, Pallas kernels, proj_part(): pl.pallas_call(proj_kernel, grid_spec=pltpu.PrefetchScalarGridSpec(num_sc...  9.4 us
    all_to_all x2, starting transfers between devices, gather_core(): lax.all_to_all(x, 'shard', split_axis=0, concat_axis=0, axis_index_groups...  8.93 us
    pallas_call x1, Pallas kernels, filter_sums(): pl.pallas_call(functools.partial(diag_kernel, cap, taps), grid=(filts //...  8.68 us
    all_to_all x2, starting transfers between devices, exchange(): return lax.all_to_all(x, 'shard', split_axis=0, concat_axis=0, tiled=True)  8.52 us
    pallas_call x1, Pallas kernels, rel_part(): pl.pallas_call(rel_kernel, out_shape=jax.ShapeDtypeStruct((width, rels),...  5.41 us
  transfers between devices with their start and end apart: 8, of which 5 were waited for; matrix products, arithmetic and copies ran while one was open for 3% of the time, Pallas kernels for 53%

profile of v11, /device:TPU:0, one launch (start us, length us, event | category | flops | bytes accessed | tf_op | source)
XLA Modules:
  0.0 145.1 jit_solution(9161507355656532370)
XLA Ops:
  7.3 3.9 %pack_tails.1 = (bf16[1,200,512]{2,1,0:T(8,128)(2,1)}, s32[512,1]{1,0:T(8,128)}) custom-call(s32[1]{0:T(128)} %bitcast.me_ref, s32[32,128]{1,0:T(8,128)} %bitcast.25, s32[32,128]{1,0:T(8,128)} %bitcast.37, bf16[200,2048]{1,0:T(8,128)(2,1)} %bitcast.33), custom_call_target="tpu_custom_call" | custom-call | flops 1000000000 | bytes 2000000 | tf_op jit(solution)/shard_map/pack_tails/pallas_call | solution.py:170
  11.3 13.9 %all_to_all.25.numbers_ref = s32[16,1,512]{2,1,0:T(1,128)} all-to-all(s32[16,1,512]{2,1,0:T(1,128)S(1)} %broadcast_in_dim.9), channel_id=1, replica_groups=mesh['parts'=2,'shard'=16] {'shard'}, dimensions={0} | all-to-all | bytes 65536 | tf_op jit(solution)/shard_map/all_to_all | solution.py:855
  25.2 2.6 %find_heads.1 = (bf16[16,16,200]{2,1,0:T(8,128)(2,1)}, s32[256,1]{1,0:T(8,128)}) custom-call(s32[1]{0:T(128)} %bitcast.me_ref, bf16[200,2048]{1,0:T(8,128)(2,1)} %bitcast.34, s32[16,1,512]{2,1,0:T(1,128)} %all_to_all.25.numbers_ref), custom_call_target="tpu_custom_call" | custom-call | flops 300000000 | bytes 2000000 | tf_op jit(solution)/shard_map/find_heads/pallas_call | solution.py:212
  27.8 3.5 %all-to-all-start.1 = ((bf16[16,16,200]{2,1,0:T(8,128)(2,1)}), bf16[16,16,200]{2,1,0:T(8,128)(2,1)S(1)}, u32[]{:S(2)}, u32[]{:S(2)}) async-start(bf16[16,16,200]{2,1,0:T(8,128)(2,1)} %get-tuple-element.33), calls=%async_computation.1 | async-start | bytes 262144 | tf_op jit(solution)/shard_map/all_to_all | solution.py:855
  31.5 0.6 broadcast_in_dim.10.ext_ref
  32.1 0.7 copy.18.filt_ref
  32.8 5.3 %band.1 = (bf16[3840,256]{1,0:T(8,128)(2,1)}, bf16[256,3840]{1,0:T(8,128)(2,1)}) custom-call(s32[20,256]{1,0:T(8,128)} %constant.8.clone.codes_ref, bf16[48,81]{1,0:T(8,128)(2,1)} %copy.18.filt_ref), custom_call_target="tpu_custom_call" | custom-call | flops 40000000 | bytes 4000000 | tf_op jit(solution)/shard_map/band/pallas_call | solution.py:94
  38.1 1.1 all-to-all-done.1.fetched_ref
  39.2 0.7 copy-done.4
  39.9 13.2 %front.1 = (f32[19200,128]{1,0:T(8,128)}, bf16[256,640]{1,0:T(8,128)(2,1)}, bf16[128,200]{1,0:T(8,128)(2,1)}, bf16[8,2,200,128]{3,2,1,0:T(8,128)(2,1)}) custom-call(bf16[16,16,200]{2,1,0:T(8,128)(2,1)} %copy-done.4, s32[1,128]{1,0:T(1,128)} %bitcast.30, s32[1,128]{1,0:T(1,128)} %bitcast.28, bf16[200,1387]{1,0:T(8,128)(2,1)} %bitcast.35, ...), custom_call_target="tpu_custom_call" | custom-call | flops 4000000000 | bytes 24000000 | tf_op jit(solution)/shard_map/front/pallas_call | solution.py:342
  53.1 4.3 %all-to-all-start.2 = ((bf16[8,2,200,128]{3,2,1,0:T(8,128)(2,1)}), bf16[8,2,200,128]{3,2,1,0:T(8,128)(2,1)S(1)}, u32[]{:S(2)}, u32[]{:S(2)}) async-start(bf16[8,2,200,128]{3,2,1,0:T(8,128)(2,1)} %get-tuple-element.43), calls=%async_computation.2 | async-start | bytes 1638400 | tf_op jit(solution)/shard_map/all_to_all | solution.py:859
  57.6 2.2 %pos_slots.1.pos_ref = s32[128,1]{1,0:T(8,128)} custom-call(s32[1,4096]{1,0:T(1,128)} %bitcast.26, s32[1,128]{1,0:T(1,128)} %bitcast.29), custom_call_target="tpu_custom_call" | custom-call | flops 100000000 | bytes 100000 | tf_op jit(solution)/shard_map/pos_slots/pallas_call | solution.py:268
  59.8 0.8 all-gather.3.cloned.1.call-done.tails_hbm.tails_ref.mate_ref
  60.6 17.5 %middle.1 = (f32[576,128]{1,0:T(8,128)}, f32[1,200,128]{2,1,0:T(8,128)}, bf16[8,200,128]{2,1,0:T(8,128)(2,1)}, bf16[3840,640]{1,0:T(8,128)(2,1)}) custom-call(s32[128,1]{1,0:T(8,128)} %pos_slots.1.pos_ref, bf16[128,200]{1,0:T(8,128)(2,1)} %get-tuple-element.35.qv_ref, s32[1,576]{1,0:T(1,128)} %broadcast_in_dim.10.ext_ref, ...), custom_call_target="tpu_custom_call" | custom-call | flops 6000000000 | bytes 25000000 | tf_op jit(solution)/shard_map/middle/pallas_call | solution.py:476
  78.6 4.6 %all-to-all-start.3 = ((bf16[8,200,128]{2,1,0:T(8,128)(2,1)}), bf16[8,200,128]{2,1,0:T(8,128)(2,1)S(1)}, u32[]{:S(2)}, u32[]{:S(2)}) async-start(bf16[8,200,128]{2,1,0:T(8,128)(2,1)} %get-tuple-element.44), calls=%async_computation.3 | async-start | bytes 819200 | tf_op jit(solution)/shard_map/all_to_all | solution.py:859
  83.2 3.8 %slot_cands.1.scand_ref = s32[2,512,1]{2,1,0:T(8,128)} custom-call(s32[1]{0:T(128)} %bitcast.me_ref, s32[32,128]{1,0:T(8,128)} %bitcast.27), custom_call_target="tpu_custom_call" | custom-call | flops 100000000 | bytes 1000000 | tf_op jit(solution)/shard_map/slot_cands/pallas_call | solution.py:238
  87.0 0.6 pad_add_fusion.2.ids_ref
  87.7 8.7 %filter_sums.1 = bf16[16,64,200]{2,1,0:T(8,128)(2,1)} custom-call(s32[20,256]{1,0:T(8,128)} %constant.8.clone.codes_ref, s32[1,128]{1,0:T(1,128)} %bitcast.31, s32[1,576]{1,0:T(1,128)} %broadcast_in_dim.10.ext_ref, f32[576,128]{1,0:T(8,128)} %get-tuple-element.39.spread_ref, bf16[3840,640]{1,0:T(8,128)(2,1)} %get-tuple-element.40.fgrad_ref, ...), custom_call_target="tpu_custom_call" | custom-call | flops 2000000000 | bytes 6000000 | tf_op jit(solution)/shard_map/filter_sums/pallas_call | solution.py:559
  96.4 1.1 all-to-all-done.3.grads_ref
  97.5 5.0 %all-to-all-start.4 = ((bf16[16,64,200]{2,1,0:T(8,128)(2,1)}), bf16[16,64,200]{2,1,0:T(8,128)(2,1)S(1)}, u32[]{:S(2)}, u32[]{:S(2)}) async-start(bf16[16,64,200]{2,1,0:T(8,128)(2,1)} %filter_sums.1), calls=%async_computation.4 | async-start | bytes 1048576 | tf_op jit(solution)/shard_map/all_to_all | solution.py:855
  102.5 4.9 %tail_grad.1 = (f32[200,512]{1,0:T(8,128)}, f32[200,512]{1,0:T(8,128)}) custom-call(s32[3]{0:T(128)} %pad_add_fusion.2.ids_ref, bf16[16,200,512]{2,1,0:T(8,128)(2,1)} %all-gather.3.cloned.1.call-done.tails_hbm.tails_ref.mate_ref, bf16[16,200,512]{2,1,0:T(8,128)(2,1)} %all-gather.3.cloned.1.call-done.tails_hbm.tails_ref.mate_ref, ...), custom_call_target="tpu_custom_call" | custom-call | flops 2000000000 | bytes 3000000 | tf_op jit(solution)/shard_map/tail_grad/pallas_call | solution.py:604
  107.4 9.4 %proj_grad.1 = (f32[200,1200]{1,0:T(8,128)}, f32[200,1200]{1,0:T(8,128)}) custom-call(s32[3]{0:T(128)} %pad_add_fusion.2.ids_ref, bf16[200,1387]{1,0:T(8,128)(2,1)} %bitcast.36, s32[1,576]{1,0:T(1,128)} %broadcast_in_dim.10.ext_ref, bf16[3840,256]{1,0:T(8,128)(2,1)} %get-tuple-element.34.band_ref.mate_ref, ...), custom_call_target="tpu_custom_call" | custom-call | flops 6000000000 | bytes 6000000 | tf_op jit(solution)/shard_map/proj_grad/pallas_call | solution.py:668
  116.8 0.4 collective-permute-start.1
  117.3 2.8 %collective-permute-done.recv_ref = f32[200,512]{1,0:T(8,128)S(1)} collective-permute-done((f32[200,512]{1,0:T(8,128)S(1)}, f32[200,512]{1,0:T(8,128)S(1)}, u32[]{:S(2)}, u32[]{:S(2)}) %collective-permute-start) | collective-permute-done | bytes 409632 | tf_op jit(solution)/shard_map/ppermute | solution.py:852
  120.1 0.7 copy-done.12
  120.9 4.2 %owned_grad.1.base_ref = f32[200,2048]{1,0:T(8,128)} custom-call(s32[512,1]{1,0:T(8,128)} %get-tuple-element.46.srow_ref, f32[200,512]{1,0:T(8,128)} %get-tuple-element.52.own_ref, f32[200,512]{1,0:T(8,128)} %copy-done.12), custom_call_target="tpu_custom_call" | custom-call | flops 1500000000 | bytes 4000000 | tf_op jit(solution)/shard_map/owned_grad/pallas_call | solution.py:766
  125.1 0.8 copy-done.2
  125.9 4.5 %entity_grad.1 = (f32[200,2048]{1,0:T(8,128)}, f32[96,48]{1,0:T(8,128)}) custom-call(s32[256,1]{1,0:T(8,128)} %get-tuple-element.32.want_ref, bf16[16,64,200]{2,1,0:T(8,128)(2,1)} %copy-done.2, f32[200,2048]{1,0:T(8,128)} %owned_grad.1.base_ref), custom_call_target="tpu_custom_call" | custom-call | flops 1000000000 | bytes 4000000 | tf_op jit(solution)/shard_map/entity_grad/pallas_call | solution.py:808
  130.4 0.8 slice_bitcast_fusion
  131.2 0.6 reshape.27
  131.8 1.1 add_bitcast_fusion
  132.9 5.4 %rel_grad.1 = f32[200,1387]{1,0:T(8,128)} custom-call(s32[16,1,512]{2,1,0:T(1,128)} %all_to_all.25.numbers_ref, f32[16,200,128]{2,1,0:T(8,128)} %all-gather.5.cloned.1.call-done.sums_ref), custom_call_target="tpu_custom_call" | custom-call | flops 2000000000 | bytes 3000000 | tf_op jit(solution)/shard_map/rel_grad/pallas_call | solution.py:739
  (39 shorter events, 1.0 us)
Async XLA Ops:
  7.2 4.1 %copy-start.9 = (s32[128]{0:T(128)S(1)}, s32[128]{0:T(128)}, u32[]{:S(2)}) copy-start(s32[128]{0:T(128)} %param.20) | copy-start | bytes 1540
  7.2 4.1 %copy-start.8 = (s32[128]{0:T(128)S(1)}, s32[128]{0:T(128)}, u32[]{:S(2)}) copy-start(s32[128]{0:T(128)} %param.19) | copy-start | bytes 1540
  7.2 4.1 %copy-start.7 = (s32[128]{0:T(128)S(1)}, s32[128]{0:T(128)}, u32[]{:S(2)}) copy-start(s32[128]{0:T(128)} %param.18) | copy-start | bytes 1540
  7.2 4.1 %copy-start.10 = (s32[128,1]{0,1:T(1,128)S(1)}, s32[128,1]{0,1:T(1,128)}, u32[]{:S(2)}) copy-start(s32[128,1]{0,1:T(1,128)} %param.17) | copy-start | bytes 1540
  7.2 53.4 %all-gather.3.cloned.1.call-start = ((), (), s32[]{:S(2)}) async-start(), calls=%async_computation.5 | async-start | bytes 3481600 | tf_op jit(solution)/shard_map/all_gather | solution.py:873
  7.3 24.1 %copy-start.6 = (s32[400]{0:T(512)S(1)}, s32[400]{0:T(512)}, u32[]{:S(2)}) copy-start(s32[400]{0:T(512)} %param.16) | copy-start | bytes 4804
  7.3 24.1 %slice-start = ((s32[400]{0:T(512)}), s32[96]{0:T(128)S(1)}, s32[]{:S(2)}) async-start(s32[400]{0:T(512)} %param.16), calls=%async_computation.7 | async-start | bytes 1024 | tf_op jit(solution)/shard_map/slice | solution.py:882
  7.3 24.8 %copy-start.5 = (bf16[48,9,9]{0,2,1:T(8,128)(2,1)S(1)}, bf16[48,9,9]{0,2,1:T(8,128)(2,1)}, u32[]{:S(2)}) copy-start(bf16[48,9,9]{0,2,1:T(8,128)(2,1)} %param.14) | copy-start | bytes 23332
  27.8 11.4 %all-to-all-start.1 = ((bf16[16,16,200]{2,1,0:T(8,128)(2,1)}), bf16[16,16,200]{2,1,0:T(8,128)(2,1)S(1)}, u32[]{:S(2)}, u32[]{:S(2)}) async-start(bf16[16,16,200]{2,1,0:T(8,128)(2,1)} %get-tuple-element.33), calls=%async_computation.1 | async-start | bytes 262144 | tf_op jit(solution)/shard_map/all_to_all | solution.py:855
  39.2 0.7 copy-start.4
  53.1 25.5 %all-to-all-start.2 = ((bf16[8,2,200,128]{3,2,1,0:T(8,128)(2,1)}), bf16[8,2,200,128]{3,2,1,0:T(8,128)(2,1)S(1)}, u32[]{:S(2)}, u32[]{:S(2)}) async-start(bf16[8,2,200,128]{3,2,1,0:T(8,128)(2,1)} %get-tuple-element.43), calls=%async_computation.2 | async-start | bytes 1638400 | tf_op jit(solution)/shard_map/all_to_all | solution.py:859
  57.4 75.5 %all-gather.5.cloned.1.call-start = ((), (), s32[]{:S(2)}) async-start(), calls=%async_computation.6 | async-start | bytes 1740800 | tf_op jit(solution)/shard_map/all_gather | solution.py:892
  78.6 17.8 %copy-start = (bf16[8,2,200,128]{3,2,1,0:T(8,128)(2,1)}, bf16[8,2,200,128]{3,2,1,0:T(8,128)(2,1)S(1)}, u32[]{:S(2)}) copy-start(bf16[8,2,200,128]{3,2,1,0:T(8,128)(2,1)S(1)} %all-to-all-done.2.vecs_ref) | copy-start | bytes 2457604
  78.6 18.9 %all-to-all-start.3 = ((bf16[8,200,128]{2,1,0:T(8,128)(2,1)}), bf16[8,200,128]{2,1,0:T(8,128)(2,1)S(1)}, u32[]{:S(2)}, u32[]{:S(2)}) async-start(bf16[8,200,128]{2,1,0:T(8,128)(2,1)} %get-tuple-element.44), calls=%async_computation.3 | async-start | bytes 819200 | tf_op jit(solution)/shard_map/all_to_all | solution.py:859
  97.5 9.9 %copy-start.3 = (bf16[8,200,128]{2,1,0:T(8,128)(2,1)}, bf16[8,200,128]{2,1,0:T(8,128)(2,1)S(1)}, u32[]{:S(2)}) copy-start(bf16[8,200,128]{2,1,0:T(8,128)(2,1)S(1)} %all-to-all-done.3.grads_ref) | copy-start | bytes 1228804
  97.5 27.6 %all-to-all-start.4 = ((bf16[16,64,200]{2,1,0:T(8,128)(2,1)}), bf16[16,64,200]{2,1,0:T(8,128)(2,1)S(1)}, u32[]{:S(2)}, u32[]{:S(2)}) async-start(bf16[16,64,200]{2,1,0:T(8,128)(2,1)} %filter_sums.1), calls=%async_computation.4 | async-start | bytes 1048576 | tf_op jit(solution)/shard_map/all_to_all | solution.py:855
  107.4 9.8 %copy-start.11 = (f32[200,512]{1,0:T(8,128)S(1)}, f32[200,512]{1,0:T(8,128)}, u32[]{:S(2)}) copy-start(f32[200,512]{1,0:T(8,128)} %get-tuple-element.53) | copy-start | bytes 1228804
  116.8 15.0 %collective-permute-start.1 = (f32[200,1200]{1,0:T(8,128)}, f32[200,1200]{1,0:T(8,128)S(1)}, u32[]{:S(2)}, u32[]{:S(2)}) collective-permute-start(f32[200,1200]{1,0:T(8,128)} %get-tuple-element.59), channel_id=1, source_target_pairs={{0,1},{1,0},{2,3},{3,2},{4,5},{5,4},{6,7},{7,6},{8,9},{9,8},{10,11... | collective-permute-start | bytes 2880008 | tf_op jit(solution)/shard_map/ppermute | solution.py:852
  117.2 2.9 %collective-permute-start = (f32[200,512]{1,0:T(8,128)S(1)}, f32[200,512]{1,0:T(8,128)S(1)}, u32[]{:S(2)}, u32[]{:S(2)}) collective-permute-start(f32[200,512]{1,0:T(8,128)S(1)} %copy-done.11), channel_id=1, source_target_pairs={{0,1},{1,0},{2,3},{3,2},{4,5},{5,4},{6,7},{7,6},{8,9},{9,8},{10,11... | collective-permute-start | bytes 1228808 | tf_op jit(solution)/shard_map/ppermute | solution.py:852
  120.1 0.8 copy-start.12
  125.1 6.7 %copy-start.1 = (f32[200,1200]{1,0:T(8,128)S(1)}, f32[200,1200]{1,0:T(8,128)}, u32[]{:S(2)}) copy-start(f32[200,1200]{1,0:T(8,128)} %get-tuple-element.58) | copy-start | bytes 2880004
  125.1 0.8 copy-start.2
Sparse Core Ops, SparseCore 0:
  11.4 49.2 all-gather.2
  78.3 46.0 all-gather.4

commit v12 on v10

--- a/solution.py
+++ b/solution.py
@@ -154,24 +154,33 @@
     return jnp.concatenate(found, axis=0).astype(i32) - 1
 
 
-def pack_kernel(me_ref, owner_ref, row_ref, table_hbm, tails_t_ref, srow_ref, picks, table, sem):
+def pack_kernel(
+    shift, me_ref, owner_ref, row_ref, table_hbm, tails_t_ref, srow_ref, cand_ref, picks, table, sem
+):
     copy = pltpu.make_async_copy(table_hbm, table, sem)
     copy.start()
     cap = srow_ref.shape[0]
-    srow = slot_values(owner_ref[...], me_ref[0], row_ref[...], cap)
+    lines = owner_ref.shape[0]
+    index = iota((lines, 128), 0) * 128 + iota((lines, 128), 1)
+    found = slot_values(owner_ref[...], me_ref[0], row_ref[...] * (1 << shift) + index, cap)
+    srow = lax.shift_right_arithmetic(found, shift)
     srow_ref[...] = srow
+    cand_ref[...] = jnp.where(found < 0, -1, found & ((1 << shift) - 1))
     fill_picks(picks, srow)
     copy.wait()
     tails_t_ref[0] = mm(table[...], picks[...], NT).astype(bf16)
 
 
 def pack_tails(me, tail_owners, tail_row, table_t, cap):
-    assert tail_row.shape[0] % 128 == 0
-    return pl.pallas_call(
-        pack_kernel,
+    shift = int(math.log2(tail_row.shape[0]))
+    assert shift >= 7 and 1 << shift == tail_row.shape[0]
+    assert table_t.shape[1] << shift < 1 << 24
+    return pl.pallas_call(
+        functools.partial(pack_kernel, shift),
         in_specs=[SMEM, VMEM, VMEM, pl.BlockSpec(memory_space=pl.ANY)],
         out_shape=[
             jax.ShapeDtypeStruct((1, table_t.shape[0], cap), bf16),
+            jax.ShapeDtypeStruct((cap, 1), i32),
             jax.ShapeDtypeStruct((cap, 1), i32),
         ],
         scratch_shapes=[
@@ -227,21 +236,19 @@
 
 
 def cand_kernel(me_ref, owner_ref, out_ref):
-    cap = out_ref.shape[1]
     owner = owner_ref[...]
     index = iota(owner.shape, 0) * 128 + iota(owner.shape, 1)
-    for k in range(2):
-        out_ref[k] = slot_values(owner, me_ref[0] ^ k, index, cap)
-
-
-def slot_cands(me, tail_owners, cap):
+    out_ref[...] = slot_values(owner, me_ref[0] ^ 1, index, out_ref.shape[0])
+
+
+def mate_cands(me, tail_owners, cap):
     return pl.pallas_call(
         cand_kernel,
         in_specs=[SMEM, VMEM],
-        out_shape=jax.ShapeDtypeStruct((2, cap, 1), i32),
+        out_shape=jax.ShapeDtypeStruct((cap, 1), i32),
         compiler_params=params(),
         cost_estimate=cost(1e8, 1e6),
-        name="slot_cands",
+        name="mate_cands",
     )(me, tail_owners.reshape(-1, 128))
 
 
@@ -577,11 +584,11 @@
 
 
 def tail_kernel(
-    cand, ids_ref, tails_ref, mate_ref, scand_ref, numbers_ref, vecs_ref, own_ref, other_ref, scores, grads
+    cand, ids_ref, tails_ref, mate_ref, scand_ref, mcand_ref, numbers_ref, vecs_ref, own_ref, other_ref, scores, grads
 ):
     cap = own_ref.shape[1]
     tails = jnp.concatenate([ref[0].astype(f32).T for ref in (tails_ref, mate_ref)], axis=0).astype(bf16)
-    scand = jnp.concatenate([scand_ref[0], scand_ref[1]], axis=0)
+    scand = jnp.concatenate([scand_ref[...], mcand_ref[...]], axis=0)
     own = jnp.zeros(own_ref.shape, f32)
     other = jnp.zeros(own_ref.shape, f32)
     for i, group in enumerate(pairs(vecs_ref.shape[0])):
@@ -598,7 +605,7 @@
     other_ref[...] = other
 
 
-def tail_part(ids, tails, scand, numbers, vecs, cand):
+def tail_part(ids, tails, scand, mcand, numbers, vecs, cand):
     _, width, cap = tails.shape
     half = jax.ShapeDtypeStruct((width, cap), f32)
     return pl.pallas_call(
@@ -610,6 +617,7 @@
                 pl.BlockSpec((1, width, cap), lambda s, ids: (ids[0], 0, 0)),
                 pl.BlockSpec((1, width, cap), lambda s, ids: (ids[1], 0, 0)),
                 whole(scand.shape),
+                whole(mcand.shape),
                 whole(numbers.shape),
                 whole(vecs.shape),
             ],
@@ -623,7 +631,7 @@
         compiler_params=params("arbitrary"),
         cost_estimate=cost(2e9, 3e6, 1e6),
         name="tail_grad",
-    )(ids, tails, tails, scand, numbers, vecs)
+    )(ids, tails, tails, scand, mcand, numbers, vecs)
 
 
 def proj_kernel(
@@ -746,10 +754,11 @@
     )(numbers, sums)
 
 
-def entity_kernel(cap, want_ref, srow_ref, own_ref, recv_ref, incoming_ref, out_ref, filt_ref):
+def entity_kernel(cap, want_ref, srow_ref, own_ref, recv_ref, incoming_ref, out_ref, filt_ref, sums):
     rows = out_ref.shape[1]
     count, _, width = incoming_ref.shape
-    half, filts = filt_ref.shape[0] // 2, filt_ref.shape[1]
+    half = incoming_ref.shape[1] - cap
+    ks, _, filts = filt_ref.shape
     grads = jnp.concatenate([incoming_ref[d, :cap, :] for d in range(count)], axis=0)
     turned = grads.astype(f32).T.astype(bf16)
     high, low = split(own_ref[...] + recv_ref[...])
@@ -767,17 +776,20 @@
         lane = iota((width, filts), 0) - 2 * k * filts
         unit = iota((width, filts), 1)
         place = onehot((lane == unit) | (lane == unit + filts))
-        filt_ref[k * half : (k + 1) * half, :] = mm(high, place) + mm(low, place)
-
-
-def entity_sum(want, srow, own, recv, incoming, rows, cap, filts):
+        sums[k * half : (k + 1) * half, :] = mm(high, place) + mm(low, place)
+    for a in range(ks):
+        filt_ref[a] = sums[a * ks : (a + 1) * ks, :]
+
+
+def entity_sum(want, srow, own, recv, incoming, rows, cap, filts, ks):
     half = incoming.shape[1] - cap
     return pl.pallas_call(
         functools.partial(entity_kernel, cap),
         out_shape=[
             jax.ShapeDtypeStruct((own.shape[0], rows), f32),
-            jax.ShapeDtypeStruct((2 * half, filts), f32),
-        ],
+            jax.ShapeDtypeStruct((ks, ks, filts), f32),
+        ],
+        scratch_shapes=[pltpu.VMEM((2 * half, filts), f32)],
         compiler_params=params(),
         cost_estimate=cost(1.5e9, 4e6),
         name="entity_grad",
@@ -832,9 +844,9 @@
     numbers = exchange(jnp.broadcast_to(numbers, (count, 1, 4 * queries)))
 
     ids = jnp.stack([me, me ^ 1, me & 1])
-    tails_t, slot_row = pack_tails(me1, tail_owners, tail_row, table_t, tail_cap)
+    tails_t, slot_row, scand = pack_tails(me1, tail_owners, tail_row, table_t, tail_cap)
     all_tails = lax.all_gather(tails_t, "shard", axis=0, tiled=True)
-    scand = slot_cands(me1, tail_owners, tail_cap)
+    mcand = mate_cands(me1, tail_owners, tail_cap)
     found, want = find_heads(me1, numbers, table_t, head_cap)
     fetched = exchange(found)
     pos = pos_slots(tail_owners, pos_index, tail_cap)
@@ -858,13 +870,14 @@
     outgoing = filter_sums(
         fgrad, img, codes, orow, ext, spread, count, width, head_cap, ks * ks
     )
-    own, other = tail_part(ids, all_tails, scand, numbers, core_vecs, cand)
-    outgoing, core_qgt, own, other = lax.optimization_barrier((outgoing, core_qgt, own, other))
+    outgoing, core_qgt, mcand = lax.optimization_barrier((outgoing, core_qgt, mcand))
     incoming = exchange(outgoing)
+    own, other = tail_part(ids, all_tails, scand, mcand, numbers, core_vecs, cand)
+    core_qgt, own, other = lax.optimization_barrier((core_qgt, own, other))
     entity_grad, filter_grad = entity_sum(
-        want, slot_row, own, swap(other), incoming, rows, head_cap, filts
+        want, slot_row, own, swap(other), incoming, rows, head_cap, filts, ks
     )
-    filter_grad = filter_grad[: ks * ks].T.reshape(filts, ks, ks)
+    filter_grad = filter_grad.transpose(2, 0, 1)
 
     cols = filts * IMG * IMG // count
     if direct and cols % (IMG * IMG) == 0:

time: 147 us -> 150 us (1.020)
  waiting for transfers between devices: 10.6 us -> 18.5 us
  starting transfers between devices: 19.3 us -> 17.3 us
    all_to_all x2, waiting for transfers between devices: 6.48 us -> 13.8 us  [exchange(): return lax.all_to_all(x, 'shard', split_axis=0, concat_axis=0, tiled=True)]
    all_to_all x2, waiting for transfers between devices: 0.38 us -> 2.53 us  [gather_core(): lax.all_to_all(x, 'shard', split_axis=0, concat_axis=0, axis_index_groups...]
    all_to_all x2, starting transfers between devices: 9.64 us -> 7.61 us  [exchange(): return lax.all_to_all(x, 'shard', split_axis=0, concat_axis=0, tiled=True)]
  transfers between devices with their start and end apart: 8 -> 8, of which waited for: 5 -> 6; matrix products, arithmetic and copies ran while one was open for 3% -> 2% of each run, Pallas kernels for 49% -> 48%
where the time goes in v12:
time: 150 us; the launch traced here: 149 us
  Pallas kernels  80.2 us (53%)
  waiting for transfers between devices  18.5 us (12%)
  starting transfers between devices  17.3 us (12%)
  between operations  14.2 us (9%)
  blocking collectives  13.9 us (9%)
  local copies, waits for them, and re-layouts  2.92 us (2%)
  other arithmetic  1.82 us (1%)
    pallas_call x1, Pallas kernels, middle(): pl.pallas_call(functools.partial(middle_kernel, cand), in_specs=[VMEM] *...  17.5 us
    all_to_all x1, blocking collectives, exchange(): return lax.all_to_all(x, 'shard', split_axis=0, concat_axis=0, tiled=True)  13.9 us
    all_to_all x2, waiting for transfers between devices, exchange(): return lax.all_to_all(x, 'shard', split_axis=0, concat_axis=0, tiled=True)  13.8 us
    pallas_call x1, Pallas kernels, front(): pl.pallas_call(functools.partial(front_kernel, cap), grid=(filts // units...  13.2 us
    pallas_call x1, Pallas kernels, proj_part(): pl.pallas_call(proj_kernel, grid_spec=pltpu.PrefetchScalarGridSpec(num_sc...  9.41 us
    all_to_all x2, starting transfers between devices, gather_core(): lax.all_to_all(x, 'shard', split_axis=0, concat_axis=0, axis_index_groups...  8.94 us
    pallas_call x1, Pallas kernels, filter_sums(): pl.pallas_call(functools.partial(diag_kernel, cap, taps), grid=(filts //...  8.71 us
    all_to_all x2, starting transfers between devices, exchange(): return lax.all_to_all(x, 'shard', split_axis=0, concat_axis=0, tiled=True)  7.61 us
  transfers between devices with their start and end apart: 8, of which 6 were waited for; matrix products, arithmetic and copies ran while one was open for 2% of the time, Pallas kernels for 48%

profile of v12, /device:TPU:0, one launch (start us, length us, event | category | flops | bytes accessed | tf_op | source)
XLA Modules:
  0.0 148.8 jit_solution(8617244652163894422)
XLA Ops:
  7.3 3.9 %pack_tails.1 = (bf16[1,200,512]{2,1,0:T(8,128)(2,1)}, s32[512,1]{1,0:T(8,128)}, s32[512,1]{1,0:T(8,128)}) custom-call(s32[1]{0:T(128)} %bitcast.me_ref, s32[32,128]{1,0:T(8,128)} %bitcast.32, s32[32,128]{1,0:T(8,128)} %bitcast.31, bf16[200,2048]{1,0:T(8,128)(2,1)} %bitcast.27), custom_call_target="tpu_custom_call" | custom-call | flops 1000000000 | bytes 2000000 | tf_op jit(solution)/shard_map/pack_tails/pallas_call | solution.py:178
  11.3 13.9 %all_to_all.25.numbers_ref = s32[16,1,512]{2,1,0:T(1,128)} all-to-all(s32[16,1,512]{2,1,0:T(1,128)S(1)} %broadcast_in_dim.9), channel_id=1, replica_groups=mesh['parts'=2,'shard'=16] {'shard'}, dimensions={0} | all-to-all | bytes 65536 | tf_op jit(solution)/shard_map/all_to_all | solution.py:830
  25.2 2.6 %find_heads.1 = (bf16[16,16,200]{2,1,0:T(8,128)(2,1)}, s32[256,1]{1,0:T(8,128)}) custom-call(s32[1]{0:T(128)} %bitcast.me_ref, bf16[200,2048]{1,0:T(8,128)(2,1)} %bitcast.28, s32[16,1,512]{2,1,0:T(1,128)} %all_to_all.25.numbers_ref), custom_call_target="tpu_custom_call" | custom-call | flops 300000000 | bytes 2000000 | tf_op jit(solution)/shard_map/find_heads/pallas_call | solution.py:221
  27.8 3.5 %all-to-all-start.1 = ((bf16[16,16,200]{2,1,0:T(8,128)(2,1)}), bf16[16,16,200]{2,1,0:T(8,128)(2,1)S(1)}, u32[]{:S(2)}, u32[]{:S(2)}) async-start(bf16[16,16,200]{2,1,0:T(8,128)(2,1)} %get-tuple-element.35), calls=%async_computation.1 | async-start | bytes 262144 | tf_op jit(solution)/shard_map/all_to_all | solution.py:830
  31.4 0.1 pad_add_fusion
  31.5 0.6 broadcast_in_dim.10.ext_ref
  32.1 0.7 copy.18.filt_ref
  32.8 5.3 %band.1 = (bf16[3840,256]{1,0:T(8,128)(2,1)}, bf16[256,3840]{1,0:T(8,128)(2,1)}) custom-call(s32[20,256]{1,0:T(8,128)} %constant.8.clone.codes_ref, bf16[48,81]{1,0:T(8,128)(2,1)} %copy.18.filt_ref), custom_call_target="tpu_custom_call" | custom-call | flops 40000000 | bytes 4000000 | tf_op jit(solution)/shard_map/band/pallas_call | solution.py:94
  38.1 1.1 all-to-all-done.1.fetched_ref
  39.2 0.7 copy-done.4
  39.9 13.2 %front.1 = (f32[19200,128]{1,0:T(8,128)}, bf16[256,640]{1,0:T(8,128)(2,1)}, bf16[128,200]{1,0:T(8,128)(2,1)}, bf16[8,2,200,128]{3,2,1,0:T(8,128)(2,1)}) custom-call(bf16[16,16,200]{2,1,0:T(8,128)(2,1)} %copy-done.4, s32[1,128]{1,0:T(1,128)} %bitcast.24, s32[1,128]{1,0:T(1,128)} %bitcast.22, bf16[200,1387]{1,0:T(8,128)(2,1)} %bitcast.29, ...), custom_call_target="tpu_custom_call" | custom-call | flops 4000000000 | bytes 24000000 | tf_op jit(solution)/shard_map/front/pallas_call | solution.py:349
  53.1 4.3 %all-to-all-start.2 = ((bf16[8,2,200,128]{3,2,1,0:T(8,128)(2,1)}), bf16[8,2,200,128]{3,2,1,0:T(8,128)(2,1)S(1)}, u32[]{:S(2)}, u32[]{:S(2)}) async-start(bf16[8,2,200,128]{3,2,1,0:T(8,128)(2,1)} %get-tuple-element.45), calls=%async_computation.2 | async-start | bytes 1638400 | tf_op jit(solution)/shard_map/all_to_all | solution.py:834
  57.4 0.2 all-gather.5.cloned.1.call-start
  57.6 2.2 %pos_slots.1.pos_ref = s32[128,1]{1,0:T(8,128)} custom-call(s32[1,4096]{1,0:T(1,128)} %bitcast.33, s32[1,128]{1,0:T(1,128)} %bitcast.23), custom_call_target="tpu_custom_call" | custom-call | flops 100000000 | bytes 100000 | tf_op jit(solution)/shard_map/pos_slots/pallas_call | solution.py:275
  59.8 0.8 all-gather.3.cloned.1.call-done.tails_hbm.tails_ref.mate_ref
  60.6 17.5 %middle.1 = (f32[576,128]{1,0:T(8,128)}, f32[1,200,128]{2,1,0:T(8,128)}, bf16[8,200,128]{2,1,0:T(8,128)(2,1)}, bf16[3840,640]{1,0:T(8,128)(2,1)}) custom-call(s32[128,1]{1,0:T(8,128)} %pos_slots.1.pos_ref, bf16[128,200]{1,0:T(8,128)(2,1)} %get-tuple-element.37.qv_ref, s32[1,576]{1,0:T(1,128)} %broadcast_in_dim.10.ext_ref, ...), custom_call_target="tpu_custom_call" | custom-call | flops 6000000000 | bytes 25000000 | tf_op jit(solution)/shard_map/middle/pallas_call | solution.py:483
  78.2 0.4 all-to-all-done.2.vecs_ref
  78.6 4.6 %all-to-all-start.3 = ((bf16[8,200,128]{2,1,0:T(8,128)(2,1)}), bf16[8,200,128]{2,1,0:T(8,128)(2,1)S(1)}, u32[]{:S(2)}, u32[]{:S(2)}) async-start(bf16[8,200,128]{2,1,0:T(8,128)(2,1)} %get-tuple-element.46), calls=%async_computation.3 | async-start | bytes 819200 | tf_op jit(solution)/shard_map/all_to_all | solution.py:834
  83.2 2.8 %mate_cands.1.mcand_ref = s32[512,1]{1,0:T(8,128)} custom-call(s32[1]{0:T(128)} %bitcast.me_ref, s32[32,128]{1,0:T(8,128)} %bitcast.34), custom_call_target="tpu_custom_call" | custom-call | flops 100000000 | bytes 1000000 | tf_op jit(solution)/shard_map/mate_cands/pallas_call | solution.py:245
  86.0 0.7 pad_add_fusion.2.ids_ref
  86.6 8.7 %filter_sums.1 = bf16[16,64,200]{2,1,0:T(8,128)(2,1)} custom-call(s32[20,256]{1,0:T(8,128)} %constant.8.clone.codes_ref, s32[1,128]{1,0:T(1,128)} %bitcast.25, s32[1,576]{1,0:T(1,128)} %broadcast_in_dim.10.ext_ref, f32[576,128]{1,0:T(8,128)} %get-tuple-element.41.spread_ref, bf16[3840,640]{1,0:T(8,128)(2,1)} %get-tuple-element.42.fgrad_ref, ...), custom_call_target="tpu_custom_call" | custom-call | flops 2000000000 | bytes 6000000 | tf_op jit(solution)/shard_map/filter_sums/pallas_call | solution.py:566
  95.3 2.1 %all-to-all-done.3.grads_ref = bf16[8,200,128]{2,1,0:T(8,128)(2,1)S(1)} async-done(((bf16[8,200,128]{2,1,0:T(8,128)(2,1)}), bf16[8,200,128]{2,1,0:T(8,128)(2,1)S(1)}, u32[]{:S(2)}, u32[]{:S(2)}) %all-to-all-start.3) | async-done | bytes 409632 | tf_op jit(solution)/shard_map/all_to_all | solution.py:834
  97.5 4.9 %tail_grad.1 = (f32[200,512]{1,0:T(8,128)}, f32[200,512]{1,0:T(8,128)}) custom-call(s32[3]{0:T(128)} %pad_add_fusion.2.ids_ref, bf16[16,200,512]{2,1,0:T(8,128)(2,1)} %all-gather.3.cloned.1.call-done.tails_hbm.tails_ref.mate_ref, bf16[16,200,512]{2,1,0:T(8,128)(2,1)} %all-gather.3.cloned.1.call-done.tails_hbm.tails_ref.mate_ref, ...), custom_call_target="tpu_custom_call" | custom-call | flops 2000000000 | bytes 3000000 | tf_op jit(solution)/shard_map/tail_grad/pallas_call | solution.py:611
  102.4 9.4 %proj_grad.1 = (f32[200,1200]{1,0:T(8,128)}, f32[200,1200]{1,0:T(8,128)}) custom-call(s32[3]{0:T(128)} %pad_add_fusion.2.ids_ref, bf16[200,1387]{1,0:T(8,128)(2,1)} %bitcast.30, s32[1,576]{1,0:T(1,128)} %broadcast_in_dim.10.ext_ref, bf16[3840,256]{1,0:T(8,128)(2,1)} %get-tuple-element.36.band_ref.mate_ref, ...), custom_call_target="tpu_custom_call" | custom-call | flops 6000000000 | bytes 6000000 | tf_op jit(solution)/shard_map/proj_grad/pallas_call | solution.py:676
  111.8 4.1 %all-to-all-start.4 = ((bf16[16,64,200]{2,1,0:T(8,128)(2,1)}), bf16[16,64,200]{2,1,0:T(8,128)(2,1)S(1)}, u32[]{:S(2)}, u32[]{:S(2)}) async-start(bf16[16,64,200]{2,1,0:T(8,128)(2,1)} %filter_sums.1), calls=%async_computation.4 | async-start | bytes 1048576 | tf_op jit(solution)/shard_map/all_to_all | solution.py:830
  115.9 0.5 collective-permute-start
  116.4 1.4 collective-permute-done.recv_ref
  117.8 12.6 %all-to-all-done.4.incoming_ref = bf16[16,64,200]{2,1,0:T(8,128)(2,1)S(1)} async-done(((bf16[16,64,200]{2,1,0:T(8,128)(2,1)}), bf16[16,64,200]{2,1,0:T(8,128)(2,1)S(1)}, u32[]{:S(2)}, u32[]{:S(2)}) %all-to-all-start.4) | async-done | bytes 409632 | tf_op jit(solution)/shard_map/all_to_all | solution.py:830
  130.4 0.8 copy-done.2
  131.2 4.3 %entity_grad.1 = (f32[200,2048]{1,0:T(8,128)}, f32[9,9,48]{2,1,0:T(8,128)}) custom-call(s32[256,1]{1,0:T(8,128)} %get-tuple-element.33.want_ref, s32[512,1]{1,0:T(8,128)} %get-tuple-element.34.srow_ref, f32[200,512]{1,0:T(8,128)} %get-tuple-element.53.own_ref, f32[200,512]{1,0:T(8,128)} %copy-done.12, bf16[16,64,200]{2,1,0:T(8,128)(2,1)} %copy-done.2), custom_call_target="tpu_custom_call" | custom-call | flops 1500000000 | bytes 4000000 | tf_op jit(solution)/shard_map/entity_grad/pallas_call | solution.py:786
  135.4 1.1 add_bitcast_fusion
  136.5 5.4 %rel_grad.1 = f32[200,1387]{1,0:T(8,128)} custom-call(s32[16,1,512]{2,1,0:T(1,128)} %all_to_all.25.numbers_ref, f32[16,200,128]{2,1,0:T(8,128)} %all-gather.5.cloned.1.call-done.sums_ref), custom_call_target="tpu_custom_call" | custom-call | flops 2000000000 | bytes 3000000 | tf_op jit(solution)/shard_map/rel_grad/pallas_call | solution.py:747
  (36 shorter events, 0.3 us)
Async XLA Ops:
  7.2 4.1 %copy-start.9 = (s32[128]{0:T(128)S(1)}, s32[128]{0:T(128)}, u32[]{:S(2)}) copy-start(s32[128]{0:T(128)} %param.20) | copy-start | bytes 1540
  7.2 4.1 %copy-start.8 = (s32[128]{0:T(128)S(1)}, s32[128]{0:T(128)}, u32[]{:S(2)}) copy-start(s32[128]{0:T(128)} %param.19) | copy-start | bytes 1540
  7.2 4.1 %copy-start.7 = (s32[128]{0:T(128)S(1)}, s32[128]{0:T(128)}, u32[]{:S(2)}) copy-start(s32[128]{0:T(128)} %param.18) | copy-start | bytes 1540
  7.2 4.1 %copy-start.10 = (s32[128,1]{0,1:T(1,128)S(1)}, s32[128,1]{0,1:T(1,128)}, u32[]{:S(2)}) copy-start(s32[128,1]{0,1:T(1,128)} %param.17) | copy-start | bytes 1540
  7.2 53.4 %all-gather.3.cloned.1.call-start = ((), (), s32[]{:S(2)}) async-start(), calls=%async_computation.5 | async-start | bytes 3481600 | tf_op jit(solution)/shard_map/all_gather | solution.py:848
  7.3 24.1 %copy-start.6 = (s32[400]{0:T(512)S(1)}, s32[400]{0:T(512)}, u32[]{:S(2)}) copy-start(s32[400]{0:T(512)} %param.16) | copy-start | bytes 4804
  7.3 24.1 %slice-start = ((s32[400]{0:T(512)}), s32[96]{0:T(128)S(1)}, s32[]{:S(2)}) async-start(s32[400]{0:T(512)} %param.16), calls=%async_computation.7 | async-start | bytes 1024 | tf_op jit(solution)/shard_map/slice | solution.py:857
  7.3 24.8 %copy-start.5 = (bf16[48,9,9]{0,2,1:T(8,128)(2,1)S(1)}, bf16[48,9,9]{0,2,1:T(8,128)(2,1)}, u32[]{:S(2)}) copy-start(bf16[48,9,9]{0,2,1:T(8,128)(2,1)} %param.14) | copy-start | bytes 23332
  27.8 11.4 %all-to-all-start.1 = ((bf16[16,16,200]{2,1,0:T(8,128)(2,1)}), bf16[16,16,200]{2,1,0:T(8,128)(2,1)S(1)}, u32[]{:S(2)}, u32[]{:S(2)}) async-start(bf16[16,16,200]{2,1,0:T(8,128)(2,1)} %get-tuple-element.35), calls=%async_computation.1 | async-start | bytes 262144 | tf_op jit(solution)/shard_map/all_to_all | solution.py:830
  39.2 0.7 copy-start.4
  53.1 25.5 %all-to-all-start.2 = ((bf16[8,2,200,128]{3,2,1,0:T(8,128)(2,1)}), bf16[8,2,200,128]{3,2,1,0:T(8,128)(2,1)S(1)}, u32[]{:S(2)}, u32[]{:S(2)}) async-start(bf16[8,2,200,128]{3,2,1,0:T(8,128)(2,1)} %get-tuple-element.45), calls=%async_computation.2 | async-start | bytes 1638400 | tf_op jit(solution)/shard_map/all_to_all | solution.py:834
  57.4 79.1 %all-gather.5.cloned.1.call-start = ((), (), s32[]{:S(2)}) async-start(), calls=%async_computation.6 | async-start | bytes 1740800 | tf_op jit(solution)/shard_map/all_gather | solution.py:867
  78.6 16.8 %copy-start = (bf16[8,2,200,128]{3,2,1,0:T(8,128)(2,1)}, bf16[8,2,200,128]{3,2,1,0:T(8,128)(2,1)S(1)}, u32[]{:S(2)}) copy-start(bf16[8,2,200,128]{3,2,1,0:T(8,128)(2,1)S(1)} %all-to-all-done.2.vecs_ref) | copy-start | bytes 2457604
  78.6 18.9 %all-to-all-start.3 = ((bf16[8,200,128]{2,1,0:T(8,128)(2,1)}), bf16[8,200,128]{2,1,0:T(8,128)(2,1)S(1)}, u32[]{:S(2)}, u32[]{:S(2)}) async-start(bf16[8,200,128]{2,1,0:T(8,128)(2,1)} %get-tuple-element.46), calls=%async_computation.3 | async-start | bytes 819200 | tf_op jit(solution)/shard_map/all_to_all | solution.py:834
  97.5 4.9 %copy-start.3 = (bf16[8,200,128]{2,1,0:T(8,128)(2,1)}, bf16[8,200,128]{2,1,0:T(8,128)(2,1)S(1)}, u32[]{:S(2)}) copy-start(bf16[8,200,128]{2,1,0:T(8,128)(2,1)S(1)} %all-to-all-done.3.grads_ref) | copy-start | bytes 1228804
  102.4 13.5 %copy-start.11 = (f32[200,512]{1,0:T(8,128)S(1)}, f32[200,512]{1,0:T(8,128)}, u32[]{:S(2)}) copy-start(f32[200,512]{1,0:T(8,128)} %get-tuple-element.54) | copy-start | bytes 1228804
  111.8 23.6 %collective-permute-start.1 = (f32[200,1200]{1,0:T(8,128)}, f32[200,1200]{1,0:T(8,128)S(1)}, u32[]{:S(2)}, u32[]{:S(2)}) collective-permute-start(f32[200,1200]{1,0:T(8,128)} %get-tuple-element.61), channel_id=1, source_target_pairs={{0,1},{1,0},{2,3},{3,2},{4,5},{5,4},{6,7},{7,6},{8,9},{9,8},{10,11... | collective-permute-start | bytes 2880008 | tf_op jit(solution)/shard_map/ppermute | solution.py:827
  111.8 18.6 %all-to-all-start.4 = ((bf16[16,64,200]{2,1,0:T(8,128)(2,1)}), bf16[16,64,200]{2,1,0:T(8,128)(2,1)S(1)}, u32[]{:S(2)}, u32[]{:S(2)}) async-start(bf16[16,64,200]{2,1,0:T(8,128)(2,1)} %filter_sums.1), calls=%async_computation.4 | async-start | bytes 1048576 | tf_op jit(solution)/shard_map/all_to_all | solution.py:830
  115.9 1.8 %collective-permute-start = (f32[200,512]{1,0:T(8,128)S(1)}, f32[200,512]{1,0:T(8,128)S(1)}, u32[]{:S(2)}, u32[]{:S(2)}) collective-permute-start(f32[200,512]{1,0:T(8,128)S(1)} %copy-done.11), channel_id=1, source_target_pairs={{0,1},{1,0},{2,3},{3,2},{4,5},{5,4},{6,7},{7,6},{8,9},{9,8},{10,11... | collective-permute-start | bytes 1228808 | tf_op jit(solution)/shard_map/ppermute | solution.py:827
  117.8 12.6 %copy-start.12 = (f32[200,512]{1,0:T(8,128)}, f32[200,512]{1,0:T(8,128)S(1)}, u32[]{:S(2)}) copy-start(f32[200,512]{1,0:T(8,128)S(1)} %collective-permute-done.recv_ref) | copy-start | bytes 1228804
  130.4 0.8 copy-start.2
  131.2 4.3 %copy-start.1 = (f32[200,1200]{1,0:T(8,128)S(1)}, f32[200,1200]{1,0:T(8,128)}, u32[]{:S(2)}) copy-start(f32[200,1200]{1,0:T(8,128)} %get-tuple-element.60) | copy-start | bytes 2880004
Sparse Core Ops, SparseCore 0:
  11.4 49.2 all-gather.2
  78.3 42.4 all-gather.4
